TPU v7x, 256 devices: a whole 4x4x8 slice. The times are simulated.
256 devices in a mesh: section: 8 (over z), ep: 32 (over x, y, core).
Axes of the slice: x: 4, y: 4, z: 8, core: 2. Of those that a mesh axis runs over, the one named last changes fastest.
Arguments:
- flight_a: bfloat16 [8, 4096, 3584], P('section', 'ep'), may hold values from -6 to 6
- flight_b: bfloat16 [8, 4096, 3584], P('section', 'ep'), may hold values from -6 to 6
- routes_a: int32 [8, 1, 4096, 1], P('section', None, 'ep'), may hold values from 0 to 7; in each aligned block of 128 rows (0 to 127, 128 to 255, ..., all dimensions but the last counted through in order) at most 18 rows name the same one
- routes_b: int32 [8, 1, 4096, 1], P('section', None, 'ep'), may hold values from 0 to 7; in each aligned block of 128 rows (0 to 127, 128 to 255, ..., all dimensions but the last counted through in order) at most 18 rows name the same one
- scores_a: float32 [8, 1, 4096, 1], P('section', None, 'ep'), may hold values from 0.5 to 1.5
- scores_b: float32 [8, 1, 4096, 1], P('section', None, 'ep'), may hold values from 0.5 to 1.5
- norm_gain: float32 [8, 3584], P('section'), may hold values from 0.1 to 1.9
- w_gate: bfloat16 [8, 3584, 8192], P('section', None, 'ep'), may hold values from -0.09375 to 0.09375
- w_up: bfloat16 [8, 3584, 8192], P('section', None, 'ep'), may hold values from -0.09375 to 0.09375
- w_down: bfloat16 [8, 8192, 3584], P('section', 'ep'), may hold values from -0.1875 to 0.1875
Outputs:
- out_a: bfloat16 [8, 4096, 3584], P('section', 'ep')
- out_b: bfloat16 [8, 4096, 3584], P('section', 'ep')
Inputs may be any that keep to these rules, and one draw needn't show every extreme that they name: `routes_a`: in each block of 128 rows that one device holds for one layer and step, no expert is named more than 18 times, a bound that some block reaches; a row never names one expert twice. `routes_b`: as for routes_a.
All inputs are finite; a program needn't handle non-finite values.
Results may differ from a plain program's by a relative error of at most 0.0054.
Values may be sent and summed in bfloat16 or wider, within the bound.
No kernel may reach another device: no remote copies, remote signals or barrier semaphores. Data moves between devices by JAX's collectives and lax.ppermute only.
A program may use at most 128 MiB of HBM per device.

v0:
```python
import jax
import jax.numpy as jnp
from jax import lax
from jax.sharding import PartitionSpec as P

ES = 4
TOPK = 1


EPSILON = 1e-06


def from_behind(value, axis, steps):
    count = lax.axis_size(axis)
    pairs = [(source, (source + steps) % count) for source in range(count)]
    return lax.ppermute(value, axis, pairs)


def rms_norm(current, gain):
    as_float = current.astype(jnp.float32)
    inverse_rms = lax.rsqrt(jnp.mean(as_float * as_float, axis=-1, keepdims=True) + EPSILON)
    return (as_float * inverse_rms * gain).astype(jnp.bfloat16)


def routing(expert_ids, route_weights, expert_count, capacity):
    token_count, top_count = expert_ids.shape
    flat_ids = expert_ids.reshape(token_count * top_count)
    onehot = (flat_ids[:, None] == jnp.arange(expert_count, dtype=jnp.int32)[None, :]).astype(
        jnp.int32
    )
    before = jnp.cumsum(onehot, axis=0) - onehot
    slot_index = jnp.sum(before * onehot, axis=1)
    column = flat_ids * capacity + slot_index
    placed = column[:, None] == jnp.arange(expert_count * capacity, dtype=jnp.int32)[None, :]
    placed = placed.reshape(token_count, top_count, expert_count * capacity)
    picker = jnp.any(placed, axis=1).astype(jnp.bfloat16)
    mixing = jnp.sum(jnp.where(placed, route_weights[:, :, None], 0.0), axis=1)
    return (picker, mixing)


def prepare(current, expert_ids, route_weights, gain, expert_count, capacity):
    normed = rms_norm(current, gain)
    picker, mixing = routing(expert_ids, route_weights, expert_count, capacity)
    feature_width = normed.shape[1]
    slotted = jnp.einsum("ts,td->sd", picker, normed, preferred_element_type=jnp.float32).astype(
        jnp.bfloat16
    )
    slotted = slotted.reshape(expert_count, 1, capacity, feature_width)
    outgoing = jnp.broadcast_to(slotted, (expert_count, ES, capacity, feature_width))
    return (outgoing.reshape(expert_count * ES, capacity, feature_width), mixing)


def expert_pass(outgoing, gate_cols, up_cols, down_part):
    received = lax.all_to_all(outgoing, "ep", split_axis=0, concat_axis=0, tiled=True)
    source_count, slot_count, feature_width = received.shape
    row_block = received.reshape(source_count * slot_count, feature_width)
    gate_act = jnp.dot(row_block, gate_cols, preferred_element_type=jnp.float32)
    up_act = jnp.dot(row_block, up_cols, preferred_element_type=jnp.float32)
    hidden = (jax.nn.silu(gate_act) * up_act).astype(jnp.bfloat16)
    partial_value = jnp.dot(hidden, down_part, preferred_element_type=jnp.float32).astype(
        jnp.bfloat16
    )
    partial_value = partial_value.reshape(source_count, slot_count, feature_width)
    return lax.all_to_all(partial_value, "ep", split_axis=0, concat_axis=0, tiled=True)


def finish(current, returned, mixing, expert_count):
    feature_width = current.shape[1]
    slot_count = returned.shape[1]
    by_slice = returned.astype(jnp.float32).reshape(expert_count, ES, slot_count, feature_width)
    summed = jnp.sum(by_slice, axis=1).reshape(expert_count * slot_count, feature_width)
    moe_out = jnp.dot(
        mixing, summed, precision=lax.Precision.HIGHEST, preferred_element_type=jnp.float32
    )
    return (current.astype(jnp.float32) + moe_out).astype(jnp.bfloat16)


def on_device(
    flight_a, flight_b, routes_a, routes_b, scores_a, scores_b, norm_gain, w_gate, w_up, w_down
):
    ep_count = lax.axis_size("ep")
    expert_count = ep_count // ES
    tok_dev = flight_a.shape[1]
    capacity = min(tok_dev, 9 * tok_dev * TOPK * ES // (8 * ep_count))
    section_index = lax.axis_index("section")
    last_section = lax.axis_size("section") - 1
    gain = norm_gain[0]
    gate_cols = w_gate[0]
    up_cols = w_up[0]
    down_part = w_down[0]
    current_a = flight_a[0]
    current_b = flight_b[0]
    outgoing_a, mixing_a = prepare(
        current_a, routes_a[0, 0], scores_a[0, 0], gain, expert_count, capacity
    )
    outgoing_b, mixing_b = prepare(
        current_b, routes_b[0, 0], scores_b[0, 0], gain, expert_count, capacity
    )
    returned_a = expert_pass(outgoing_a, gate_cols, up_cols, down_part)
    returned_b = expert_pass(outgoing_b, gate_cols, up_cols, down_part)
    updated_a = finish(current_a, returned_a, mixing_a, expert_count)
    updated_b = finish(current_b, returned_b, mixing_b, expert_count)
    current_a = jnp.where(0 <= section_index, updated_a, current_a)
    current_b = jnp.where(section_index + 0 <= last_section, updated_b, current_b)
    current_a = from_behind(current_a, "section", 1)
    current_b = from_behind(current_b, "section", -1)
    return (current_a[None], current_b[None])


def solution(mesh):
    placed = (
        P("section", "ep", None),
        P("section", "ep", None),
        P("section", None, "ep", None),
        P("section", None, "ep", None),
        P("section", None, "ep", None),
        P("section", None, "ep", None),
        P("section", None),
        P("section", None, "ep"),
        P("section", None, "ep"),
        P("section", "ep", None),
    )
    return jax.shard_map(
        on_device,
        mesh=mesh,
        in_specs=placed,
        out_specs=(P("section", "ep", None), P("section", "ep", None)),
        check_vma=False,
    )
```

profile of v0, /device:TPU:8, one launch (start us, length us, event | category | flops | bytes accessed | tf_op | source)
XLA Modules:
  0.0 371.9 jit_solution(638930617521318947)
XLA Ops:
  0.6 0.0 copy-start
  0.6 0.9 fusion.60
  1.5 0.2 reduce_window_sum.18
  1.7 0.8 select_reduce_fusion
  2.5 0.7 multiply_add_fusion
  3.2 1.4 fusion.5
  4.6 0.8 reduce
  5.4 2.7 convolution_convert_fusion.2
  8.1 1.4 broadcast_in_dim.58
  9.5 2.8 broadcast_in_dim.59
  12.3 7.7 %all-to-all-start.2 = ((bf16[32,18,3584]{2,1,0:T(8,128)(2,1)}), bf16[32,18,3584]{2,1,0:T(8,128)(2,1)}, u32[]{:S(2)}, u32[]{:S(2)}) async-start(bf16[32,18,3584]{2,1,0:T(8,128)(2,1)} %bitcast.73), calls=%async_computation.2 | async-start | bytes 11010048 | tf_op jit(solution)/shard_map/all_to_all | solution.py:54
  20.0 0.0 copy-done.4
  20.0 0.1 fusion.61
  20.1 0.2 reduce_window_sum.17
  20.3 0.2 select_reduce_fusion.1
  20.4 0.0 copy-done.2
  20.5 0.3 fusion.4
  20.7 1.5 convolution_convert_fusion.3
  22.3 1.4 broadcast_in_dim.53
  23.7 71.5 %all-to-all-done.2 = bf16[32,18,3584]{2,1,0:T(8,128)(2,1)} async-done(((bf16[32,18,3584]{2,1,0:T(8,128)(2,1)}), bf16[32,18,3584]{2,1,0:T(8,128)(2,1)}, u32[]{:S(2)}, u32[]{:S(2)}) %all-to-all-start.2) | async-done | bytes 4128800 | tf_op jit(solution)/shard_map/all_to_all | solution.py:54
  95.2 2.9 broadcast_in_dim.54
  98.0 4.7 %all-to-all-start = ((bf16[32,18,3584]{2,1,0:T(8,128)(2,1)}), bf16[32,18,3584]{2,1,0:T(8,128)(2,1)}, u32[]{:S(2)}, u32[]{:S(2)}) async-start(bf16[32,18,3584]{2,1,0:T(8,128)(2,1)} %bitcast.74), calls=%async_computation | async-start | bytes 11010048 | tf_op jit(solution)/shard_map/all_to_all | solution.py:54
  102.7 7.3 %reshape.329 = bf16[576,3584]{1,0:T(8,128)(2,1)} reshape(bf16[32,18,3584]{2,1,0:T(8,128)(2,1)} %all-to-all-done.2) | data formatting | bytes 8257536 | tf_op jit(solution)/shard_map/reshape | solution.py:56
  110.1 4.0 %fusion.12 = f32[576,256]{1,0:T(8,128)S(1)} fusion(bf16[576,3584]{1,0:T(8,128)(2,1)} %reshape.329, bf16[1,3584,256]{2,1,0:T(8,128)(2,1)} %param.17), kind=kOutput, calls=%fused_computation.22 | convolution fusion | flops 1056964608 | bytes 6553600 | tf_op jit(solution)/shard_map/dot_general | solution.py:57
  114.0 0.0 copy-done
  114.0 9.1 %convolution_convert_fusion = bf16[576,3584]{1,0:T(8,128)(2,1)} fusion(bf16[1,256,3584]{2,1,0:T(8,128)(2,1)S(1)} %copy-done, bf16[576,3584]{1,0:T(8,128)(2,1)} %reshape.329, bf16[1,3584,256]{2,1,0:T(8,128)(2,1)} %param.18, f32[576,256]{1,0:T(8,128)S(1)} %fusion.12), kind=kOutput, calls=%fused_computation.2 | convolution fusion | flops 2116878336 | bytes 12517376 | tf_op jit(solution)/shard_map/dot_general | solution.py:60
  123.1 7.2 %reshape.330 = bf16[32,18,3584]{2,1,0:T(8,128)(2,1)} reshape(bf16[576,3584]{1,0:T(8,128)(2,1)} %convolution_convert_fusion) | data formatting | bytes 8257536 | tf_op jit(solution)/shard_map/reshape | solution.py:63
  130.3 45.7 %all-to-all-done = bf16[32,18,3584]{2,1,0:T(8,128)(2,1)} async-done(((bf16[32,18,3584]{2,1,0:T(8,128)(2,1)}), bf16[32,18,3584]{2,1,0:T(8,128)(2,1)}, u32[]{:S(2)}, u32[]{:S(2)}) %all-to-all-start) | async-done | bytes 4128800 | tf_op jit(solution)/shard_map/all_to_all | solution.py:54
  176.1 4.9 %all-to-all-start.3 = ((bf16[32,18,3584]{2,1,0:T(8,128)(2,1)}), bf16[32,18,3584]{2,1,0:T(8,128)(2,1)}, u32[]{:S(2)}, u32[]{:S(2)}) async-start(bf16[32,18,3584]{2,1,0:T(8,128)(2,1)} %reshape.330), calls=%async_computation.3 | async-start | bytes 11010048 | tf_op jit(solution)/shard_map/all_to_all | solution.py:64
  180.9 7.3 %reshape.323 = bf16[576,3584]{1,0:T(8,128)(2,1)} reshape(bf16[32,18,3584]{2,1,0:T(8,128)(2,1)} %all-to-all-done) | data formatting | bytes 8257536 | tf_op jit(solution)/shard_map/reshape | solution.py:56
  188.3 4.0 %fusion.14 = f32[576,256]{1,0:T(8,128)S(1)} fusion(bf16[576,3584]{1,0:T(8,128)(2,1)} %reshape.323, bf16[1,3584,256]{2,1,0:T(8,128)(2,1)} %param.17), kind=kOutput, calls=%fused_computation.24 | convolution fusion | flops 1056964608 | bytes 6553600 | tf_op jit(solution)/shard_map/dot_general | solution.py:57
  192.2 9.1 %convolution_convert_fusion.1 = bf16[576,3584]{1,0:T(8,128)(2,1)} fusion(bf16[1,256,3584]{2,1,0:T(8,128)(2,1)S(1)} %copy-done, bf16[576,3584]{1,0:T(8,128)(2,1)} %reshape.323, bf16[1,3584,256]{2,1,0:T(8,128)(2,1)} %param.18, f32[576,256]{1,0:T(8,128)S(1)} %fusion.14), kind=kOutput, calls=%fused_computation.3 | convolution fusion | flops 2116878336 | bytes 12517376 | tf_op jit(solution)/shard_map/dot_general | solution.py:60
  201.3 7.2 %reshape.324 = bf16[32,18,3584]{2,1,0:T(8,128)(2,1)} reshape(bf16[576,3584]{1,0:T(8,128)(2,1)} %convolution_convert_fusion.1) | data formatting | bytes 8257536 | tf_op jit(solution)/shard_map/reshape | solution.py:63
  208.6 44.4 %all-to-all-done.3 = bf16[32,18,3584]{2,1,0:T(8,128)(2,1)} async-done(((bf16[32,18,3584]{2,1,0:T(8,128)(2,1)}), bf16[32,18,3584]{2,1,0:T(8,128)(2,1)}, u32[]{:S(2)}, u32[]{:S(2)}) %all-to-all-start.3) | async-done | bytes 4128800 | tf_op jit(solution)/shard_map/all_to_all | solution.py:64
  253.0 4.7 %all-to-all-start.1 = ((bf16[32,18,3584]{2,1,0:T(8,128)(2,1)}), bf16[32,18,3584]{2,1,0:T(8,128)(2,1)}, u32[]{:S(2)}, u32[]{:S(2)}) async-start(bf16[32,18,3584]{2,1,0:T(8,128)(2,1)} %reshape.324), calls=%async_computation.1 | async-start | bytes 11010048 | tf_op jit(solution)/shard_map/all_to_all | solution.py:64
  257.6 5.3 %convert_reduce_fusion = f32[8,18,3584]{2,1,0:T(8,128)} fusion(bf16[32,18,3584]{2,1,0:T(8,128)(2,1)} %all-to-all-done.3), kind=kLoop, calls=%fused_computation | loop fusion | flops 3612672 | bytes 6193152 | tf_op jit(solution)/shard_map/reduce_sum | solution.py:71
  262.9 3.0 reshape.333
  265.9 4.4 %fusion.2 = bf16[128,3584]{1,0:T(8,128)(2,1)} fusion(f32[144,3584]{1,0:T(8,128)} %reshape.333, bf16[1,128,3584]{2,1,0:T(8,128)(2,1)S(1)} %copy-done.1, pred[]{:T(512)S(6)} %le.3, f32[128]{0:T(128)S(1)} %bitcast.80, s32[128]{0:T(128)S(1)} %multiply_add_fusion), kind=kOutput, calls=%fused_computation.10 | convolution fusion | flops 794595328 | bytes 3900417 | tf_op jit(solution)/shard_map/dot_general | solution.py:72
  270.3 5.9 %collective-permute-start.1 = (bf16[128,3584]{1,0:T(8,128)(2,1)}, bf16[128,3584]{1,0:T(8,128)(2,1)}, u32[]{:S(2)}, u32[]{:S(2)}) collective-permute-start(bf16[128,3584]{1,0:T(8,128)(2,1)} %fusion.2), channel_id=1, source_target_pairs={{0,224},{32,0},{64,32},{96,64},{128,96},{160,128},{192,160},{224,1... | collective-permute-start | bytes 2752520 | tf_op jit(solution)/shard_map/ppermute | solution.py:16
  276.1 54.9 %all-to-all-done.1 = bf16[32,18,3584]{2,1,0:T(8,128)(2,1)} async-done(((bf16[32,18,3584]{2,1,0:T(8,128)(2,1)}), bf16[32,18,3584]{2,1,0:T(8,128)(2,1)}, u32[]{:S(2)}, u32[]{:S(2)}) %all-to-all-start.1) | async-done | bytes 4128800 | tf_op jit(solution)/shard_map/all_to_all | solution.py:64
  331.0 5.3 %convert_reduce_fusion.1 = f32[8,18,3584]{2,1,0:T(8,128)} fusion(bf16[32,18,3584]{2,1,0:T(8,128)(2,1)} %all-to-all-done.1), kind=kLoop, calls=%fused_computation.1 | loop fusion | flops 3612672 | bytes 6193152 | tf_op jit(solution)/shard_map/reduce_sum | solution.py:71
  336.3 3.0 reshape.327
  339.3 3.5 fusion.3
  342.7 2.0 collective-permute-start
  344.7 0.0 collective-permute-done.1
  344.7 24.1 %collective-permute-done = bf16[128,3584]{1,0:T(8,128)(2,1)S(1)} collective-permute-done((bf16[128,3584]{1,0:T(8,128)(2,1)S(1)}, bf16[128,3584]{1,0:T(8,128)(2,1)S(1)}, u32[]{:S(2)}, u32[]{:S(2)}) %collective-permute-start) | collective-permute-done | bytes 917536 | tf_op jit(solution)/shard_map/ppermute | solution.py:16
  368.8 0.9 copy.14
  369.8 2.2 copy.15
  (13 shorter events, 0.0 us)
Async XLA Ops:
  0.6 113.4 %copy-start = (bf16[1,256,3584]{2,1,0:T(8,128)(2,1)S(1)}, bf16[1,256,3584]{2,1,0:T(8,128)(2,1)}, u32[]{:S(2)}) copy-start(bf16[1,256,3584]{2,1,0:T(8,128)(2,1)} %param.19) | copy-start | bytes 5505028
  12.3 7.7 %copy-start.4 = (s32[1,1,128,1]{2,3,1,0:T(1,128)S(1)}, s32[1,1,128,1]{2,3,1,0:T(1,128)}, u32[]{:S(2)}) copy-start(s32[1,1,128,1]{2,3,1,0:T(1,128)} %param.12) | copy-start | bytes 1540
  12.3 8.2 %copy-start.2 = (bf16[1,128,3584]{2,1,0:T(8,128)(2,1)S(1)}, bf16[1,128,3584]{2,1,0:T(8,128)(2,1)}, u32[]{:S(2)}) copy-start(bf16[1,128,3584]{2,1,0:T(8,128)(2,1)} %param.10) | copy-start | bytes 2752516
  12.3 82.9 %all-to-all-start.2 = ((bf16[32,18,3584]{2,1,0:T(8,128)(2,1)}), bf16[32,18,3584]{2,1,0:T(8,128)(2,1)}, u32[]{:S(2)}, u32[]{:S(2)}) async-start(bf16[32,18,3584]{2,1,0:T(8,128)(2,1)} %bitcast.73), calls=%async_computation.2 | async-start | bytes 11010048 | tf_op jit(solution)/shard_map/all_to_all | solution.py:54
  98.0 78.0 %all-to-all-start = ((bf16[32,18,3584]{2,1,0:T(8,128)(2,1)}), bf16[32,18,3584]{2,1,0:T(8,128)(2,1)}, u32[]{:S(2)}, u32[]{:S(2)}) async-start(bf16[32,18,3584]{2,1,0:T(8,128)(2,1)} %bitcast.74), calls=%async_computation | async-start | bytes 11010048 | tf_op jit(solution)/shard_map/all_to_all | solution.py:54
  176.1 76.9 %all-to-all-start.3 = ((bf16[32,18,3584]{2,1,0:T(8,128)(2,1)}), bf16[32,18,3584]{2,1,0:T(8,128)(2,1)}, u32[]{:S(2)}, u32[]{:S(2)}) async-start(bf16[32,18,3584]{2,1,0:T(8,128)(2,1)} %reshape.330), calls=%async_computation.3 | async-start | bytes 11010048 | tf_op jit(solution)/shard_map/all_to_all | solution.py:64
  253.0 78.0 %all-to-all-start.1 = ((bf16[32,18,3584]{2,1,0:T(8,128)(2,1)}), bf16[32,18,3584]{2,1,0:T(8,128)(2,1)}, u32[]{:S(2)}, u32[]{:S(2)}) async-start(bf16[32,18,3584]{2,1,0:T(8,128)(2,1)} %reshape.324), calls=%async_computation.1 | async-start | bytes 11010048 | tf_op jit(solution)/shard_map/all_to_all | solution.py:64
  262.9 3.0 copy-start.1
  262.9 3.0 copy-start.5
  270.3 74.5 %collective-permute-start.1 = (bf16[128,3584]{1,0:T(8,128)(2,1)}, bf16[128,3584]{1,0:T(8,128)(2,1)}, u32[]{:S(2)}, u32[]{:S(2)}) collective-permute-start(bf16[128,3584]{1,0:T(8,128)(2,1)} %fusion.2), channel_id=1, source_target_pairs={{0,224},{32,0},{64,32},{96,64},{128,96},{160,128},{192,160},{224,1... | collective-permute-start | bytes 2752520 | tf_op jit(solution)/shard_map/ppermute | solution.py:16
  336.3 3.0 copy-start.3
  336.3 3.0 copy-start.6
  342.7 26.1 %collective-permute-start = (bf16[128,3584]{1,0:T(8,128)(2,1)S(1)}, bf16[128,3584]{1,0:T(8,128)(2,1)S(1)}, u32[]{:S(2)}, u32[]{:S(2)}) collective-permute-start(bf16[128,3584]{1,0:T(8,128)(2,1)S(1)} %fusion.3), channel_id=1, source_target_pairs={{0,32},{32,64},{64,96},{96,128},{128,160},{160,192},{192,224},{224... | collective-permute-start | bytes 2752520 | tf_op jit(solution)/shard_map/ppermute | solution.py:16
where the time goes:
time: 373 us; the launch traced here: 372 us
  waiting for transfers between devices  241 us (65%)
  local copies, waits for them, and re-layouts  46.6 us (12%)
  matrix products  38.2 us (10%)
  starting transfers between devices  29.8 us (8%)
  other arithmetic  16 us (4%)
    all_to_all x2, waiting for transfers between devices, expert_pass(): lax.all_to_all(outgoing, 'ep', split_axis=0, concat_axis=0, tiled=True)  117 us
    all_to_all x2, waiting for transfers between devices, expert_pass(): lax.all_to_all(partial_value, 'ep', split_axis=0, concat_axis=0, tiled=True)  99.3 us
    ppermute x2, waiting for transfers between devices, from_behind(): return lax.ppermute(value, axis, pairs)  24.1 us
    dot_general x2, matrix products, expert_pass(): jnp.dot(hidden, down_part, preferred_element_type=jnp.float32)  18.2 us
    reshape x2, local copies, waits for them, and re-layouts, expert_pass(): row_block = received.reshape(source_count * slot_count, feature_width)  14.7 us
    reshape x2, local copies, waits for them, and re-layouts, expert_pass(): partial_value.reshape(source_count, slot_count, feature_width)  14.4 us
    all_to_all x2, starting transfers between devices, expert_pass(): lax.all_to_all(outgoing, 'ep', split_axis=0, concat_axis=0, tiled=True)  12.4 us
    reduce_sum x2, other arithmetic, finish(): jnp.sum(by_slice, axis=1).reshape(expert_count * slot_count, feature_width)  10.6 us
  transfers between devices with their start and end apart: 6, of which 5 were waited for; matrix products, arithmetic and copies ran while one was open for 22% of the time, Pallas kernels for 0%

commit v1 on v0

--- a/solution.py
+++ b/solution.py
@@ -25,11 +25,9 @@
 def routing(expert_ids, route_weights, expert_count, capacity):
     token_count, top_count = expert_ids.shape
     flat_ids = expert_ids.reshape(token_count * top_count)
-    onehot = (flat_ids[:, None] == jnp.arange(expert_count, dtype=jnp.int32)[None, :]).astype(
-        jnp.int32
-    )
-    before = jnp.cumsum(onehot, axis=0) - onehot
-    slot_index = jnp.sum(before * onehot, axis=1)
+    position = jnp.arange(token_count * top_count, dtype=jnp.int32)
+    earlier = (flat_ids[None, :] == flat_ids[:, None]) & (position[None, :] < position[:, None])
+    slot_index = jnp.sum(earlier.astype(jnp.int32), axis=1)
     column = flat_ids * capacity + slot_index
     placed = column[:, None] == jnp.arange(expert_count * capacity, dtype=jnp.int32)[None, :]
     placed = placed.reshape(token_count, top_count, expert_count * capacity)

time: 373 us -> 372 us (level)
  no operation moved by 1% of the time
where the time goes in v1:
time: 372 us; the launch traced here: 371 us
  waiting for transfers between devices  241 us (65%)
  local copies, waits for them, and re-layouts  46.6 us (13%)
  matrix products  38.2 us (10%)
  starting transfers between devices  29.7 us (8%)
  other arithmetic  14.9 us (4%)
    all_to_all x2, waiting for transfers between devices, expert_pass(): lax.all_to_all(outgoing, 'ep', split_axis=0, concat_axis=0, tiled=True)  117 us
    all_to_all x2, waiting for transfers between devices, expert_pass(): lax.all_to_all(partial_value, 'ep', split_axis=0, concat_axis=0, tiled=True)  99.3 us
    ppermute x2, waiting for transfers between devices, from_behind(): return lax.ppermute(value, axis, pairs)  24.1 us
    dot_general x2, matrix products, expert_pass(): jnp.dot(hidden, down_part, preferred_element_type=jnp.float32)  18.2 us
    reshape x2, local copies, waits for them, and re-layouts, expert_pass(): row_block = received.reshape(source_count * slot_count, feature_width)  14.7 us
    reshape x2, local copies, waits for them, and re-layouts, expert_pass(): partial_value.reshape(source_count, slot_count, feature_width)  14.4 us
    all_to_all x2, starting transfers between devices, expert_pass(): lax.all_to_all(outgoing, 'ep', split_axis=0, concat_axis=0, tiled=True)  12.4 us
    reduce_sum x2, other arithmetic, finish(): jnp.sum(by_slice, axis=1).reshape(expert_count * slot_count, feature_width)  10.6 us
  transfers between devices with their start and end apart: 6, of which 5 were waited for; matrix products, arithmetic and copies ran while one was open for 22% of the time, Pallas kernels for 0%

profile of v1, /device:TPU:8, one launch (start us, length us, event | category | flops | bytes accessed | tf_op | source)
XLA Modules:
  0.0 371.0 jit_solution(10678816585784169522)
XLA Ops:
  0.6 0.0 copy-start
  0.6 1.0 convert_reduce_fusion.2
  1.6 0.7 multiply_add_fusion
  2.3 1.4 fusion.5
  3.7 0.8 reduce
  4.5 2.7 convolution_convert_fusion.2
  7.2 1.4 broadcast_in_dim.60
  8.6 2.8 broadcast_in_dim.61
  11.4 7.7 %all-to-all-start.2 = ((bf16[32,18,3584]{2,1,0:T(8,128)(2,1)}), bf16[32,18,3584]{2,1,0:T(8,128)(2,1)}, u32[]{:S(2)}, u32[]{:S(2)}) async-start(bf16[32,18,3584]{2,1,0:T(8,128)(2,1)} %bitcast.73), calls=%async_computation.2 | async-start | bytes 11010048 | tf_op jit(solution)/shard_map/all_to_all | solution.py:52
  19.1 0.0 copy-done.6
  19.1 0.2 convert_reduce_fusion.3
  19.3 0.0 copy-done.2
  19.3 0.3 fusion.4
  19.6 1.5 convolution_convert_fusion.3
  21.1 1.4 broadcast_in_dim.55
  22.5 71.8 %all-to-all-done.2 = bf16[32,18,3584]{2,1,0:T(8,128)(2,1)} async-done(((bf16[32,18,3584]{2,1,0:T(8,128)(2,1)}), bf16[32,18,3584]{2,1,0:T(8,128)(2,1)}, u32[]{:S(2)}, u32[]{:S(2)}) %all-to-all-start.2) | async-done | bytes 4128800 | tf_op jit(solution)/shard_map/all_to_all | solution.py:52
  94.3 2.9 broadcast_in_dim.56
  97.1 4.7 %all-to-all-start = ((bf16[32,18,3584]{2,1,0:T(8,128)(2,1)}), bf16[32,18,3584]{2,1,0:T(8,128)(2,1)}, u32[]{:S(2)}, u32[]{:S(2)}) async-start(bf16[32,18,3584]{2,1,0:T(8,128)(2,1)} %bitcast.74), calls=%async_computation | async-start | bytes 11010048 | tf_op jit(solution)/shard_map/all_to_all | solution.py:52
  101.8 7.3 %reshape.331 = bf16[576,3584]{1,0:T(8,128)(2,1)} reshape(bf16[32,18,3584]{2,1,0:T(8,128)(2,1)} %all-to-all-done.2) | data formatting | bytes 8257536 | tf_op jit(solution)/shard_map/reshape | solution.py:54
  109.1 4.0 %fusion.12 = f32[576,256]{1,0:T(8,128)S(1)} fusion(bf16[576,3584]{1,0:T(8,128)(2,1)} %reshape.331, bf16[1,3584,256]{2,1,0:T(8,128)(2,1)} %param.17), kind=kOutput, calls=%fused_computation.22 | convolution fusion | flops 1056964608 | bytes 6553600 | tf_op jit(solution)/shard_map/dot_general | solution.py:55
  113.1 0.0 copy-done
  113.1 9.1 %convolution_convert_fusion = bf16[576,3584]{1,0:T(8,128)(2,1)} fusion(bf16[1,256,3584]{2,1,0:T(8,128)(2,1)S(1)} %copy-done, bf16[576,3584]{1,0:T(8,128)(2,1)} %reshape.331, bf16[1,3584,256]{2,1,0:T(8,128)(2,1)} %param.18, f32[576,256]{1,0:T(8,128)S(1)} %fusion.12), kind=kOutput, calls=%fused_computation.2 | convolution fusion | flops 2116878336 | bytes 12517376 | tf_op jit(solution)/shard_map/dot_general | solution.py:58
  122.2 7.2 %reshape.332 = bf16[32,18,3584]{2,1,0:T(8,128)(2,1)} reshape(bf16[576,3584]{1,0:T(8,128)(2,1)} %convolution_convert_fusion) | data formatting | bytes 8257536 | tf_op jit(solution)/shard_map/reshape | solution.py:61
  129.4 45.7 %all-to-all-done = bf16[32,18,3584]{2,1,0:T(8,128)(2,1)} async-done(((bf16[32,18,3584]{2,1,0:T(8,128)(2,1)}), bf16[32,18,3584]{2,1,0:T(8,128)(2,1)}, u32[]{:S(2)}, u32[]{:S(2)}) %all-to-all-start) | async-done | bytes 4128800 | tf_op jit(solution)/shard_map/all_to_all | solution.py:52
  175.2 4.9 %all-to-all-start.3 = ((bf16[32,18,3584]{2,1,0:T(8,128)(2,1)}), bf16[32,18,3584]{2,1,0:T(8,128)(2,1)}, u32[]{:S(2)}, u32[]{:S(2)}) async-start(bf16[32,18,3584]{2,1,0:T(8,128)(2,1)} %reshape.332), calls=%async_computation.3 | async-start | bytes 11010048 | tf_op jit(solution)/shard_map/all_to_all | solution.py:62
  180.0 7.3 %reshape.325 = bf16[576,3584]{1,0:T(8,128)(2,1)} reshape(bf16[32,18,3584]{2,1,0:T(8,128)(2,1)} %all-to-all-done) | data formatting | bytes 8257536 | tf_op jit(solution)/shard_map/reshape | solution.py:54
  187.4 4.0 %fusion.14 = f32[576,256]{1,0:T(8,128)S(1)} fusion(bf16[576,3584]{1,0:T(8,128)(2,1)} %reshape.325, bf16[1,3584,256]{2,1,0:T(8,128)(2,1)} %param.17), kind=kOutput, calls=%fused_computation.24 | convolution fusion | flops 1056964608 | bytes 6553600 | tf_op jit(solution)/shard_map/dot_general | solution.py:55
  191.3 9.1 %convolution_convert_fusion.1 = bf16[576,3584]{1,0:T(8,128)(2,1)} fusion(bf16[1,256,3584]{2,1,0:T(8,128)(2,1)S(1)} %copy-done, bf16[576,3584]{1,0:T(8,128)(2,1)} %reshape.325, bf16[1,3584,256]{2,1,0:T(8,128)(2,1)} %param.18, f32[576,256]{1,0:T(8,128)S(1)} %fusion.14), kind=kOutput, calls=%fused_computation.3 | convolution fusion | flops 2116878336 | bytes 12517376 | tf_op jit(solution)/shard_map/dot_general | solution.py:58
  200.4 7.2 %reshape.326 = bf16[32,18,3584]{2,1,0:T(8,128)(2,1)} reshape(bf16[576,3584]{1,0:T(8,128)(2,1)} %convolution_convert_fusion.1) | data formatting | bytes 8257536 | tf_op jit(solution)/shard_map/reshape | solution.py:61
  207.7 44.4 %all-to-all-done.3 = bf16[32,18,3584]{2,1,0:T(8,128)(2,1)} async-done(((bf16[32,18,3584]{2,1,0:T(8,128)(2,1)}), bf16[32,18,3584]{2,1,0:T(8,128)(2,1)}, u32[]{:S(2)}, u32[]{:S(2)}) %all-to-all-start.3) | async-done | bytes 4128800 | tf_op jit(solution)/shard_map/all_to_all | solution.py:62
  252.1 4.7 %all-to-all-start.1 = ((bf16[32,18,3584]{2,1,0:T(8,128)(2,1)}), bf16[32,18,3584]{2,1,0:T(8,128)(2,1)}, u32[]{:S(2)}, u32[]{:S(2)}) async-start(bf16[32,18,3584]{2,1,0:T(8,128)(2,1)} %reshape.326), calls=%async_computation.1 | async-start | bytes 11010048 | tf_op jit(solution)/shard_map/all_to_all | solution.py:62
  256.7 5.3 %convert_reduce_fusion = f32[8,18,3584]{2,1,0:T(8,128)} fusion(bf16[32,18,3584]{2,1,0:T(8,128)(2,1)} %all-to-all-done.3), kind=kLoop, calls=%fused_computation | loop fusion | flops 3612672 | bytes 6193152 | tf_op jit(solution)/shard_map/reduce_sum | solution.py:69
  262.0 3.0 reshape.335
  265.0 0.0 copy-done.1
  265.0 0.0 copy-done.4
  265.0 4.4 %fusion.2 = bf16[128,3584]{1,0:T(8,128)(2,1)} fusion(f32[144,3584]{1,0:T(8,128)} %reshape.335, bf16[1,128,3584]{2,1,0:T(8,128)(2,1)S(1)} %copy-done.1, pred[]{:T(512)S(6)} %le.3, f32[128]{0:T(128)S(1)} %bitcast.76, s32[128]{0:T(128)S(1)} %multiply_add_fusion), kind=kOutput, calls=%fused_computation.10 | convolution fusion | flops 794595328 | bytes 3900417 | tf_op jit(solution)/shard_map/dot_general | solution.py:70
  269.4 5.9 %collective-permute-start.1 = (bf16[128,3584]{1,0:T(8,128)(2,1)}, bf16[128,3584]{1,0:T(8,128)(2,1)}, u32[]{:S(2)}, u32[]{:S(2)}) collective-permute-start(bf16[128,3584]{1,0:T(8,128)(2,1)} %fusion.2), channel_id=1, source_target_pairs={{0,224},{32,0},{64,32},{96,64},{128,96},{160,128},{192,160},{224,1... | collective-permute-start | bytes 2752520 | tf_op jit(solution)/shard_map/ppermute | solution.py:16
  275.2 54.9 %all-to-all-done.1 = bf16[32,18,3584]{2,1,0:T(8,128)(2,1)} async-done(((bf16[32,18,3584]{2,1,0:T(8,128)(2,1)}), bf16[32,18,3584]{2,1,0:T(8,128)(2,1)}, u32[]{:S(2)}, u32[]{:S(2)}) %all-to-all-start.1) | async-done | bytes 4128800 | tf_op jit(solution)/shard_map/all_to_all | solution.py:62
  330.1 5.3 %convert_reduce_fusion.1 = f32[8,18,3584]{2,1,0:T(8,128)} fusion(bf16[32,18,3584]{2,1,0:T(8,128)(2,1)} %all-to-all-done.1), kind=kLoop, calls=%fused_computation.1 | loop fusion | flops 3612672 | bytes 6193152 | tf_op jit(solution)/shard_map/reduce_sum | solution.py:69
  335.4 3.0 reshape.329
  338.4 0.0 copy-done.3
  338.4 0.0 copy-done.5
  338.4 3.5 fusion.3
  341.8 2.0 collective-permute-start
  343.8 0.0 collective-permute-done.1
  343.8 24.1 %collective-permute-done = bf16[128,3584]{1,0:T(8,128)(2,1)S(1)} collective-permute-done((bf16[128,3584]{1,0:T(8,128)(2,1)S(1)}, bf16[128,3584]{1,0:T(8,128)(2,1)S(1)}, u32[]{:S(2)}, u32[]{:S(2)}) %collective-permute-start) | collective-permute-done | bytes 917536 | tf_op jit(solution)/shard_map/ppermute | solution.py:16
  367.9 0.9 copy.14
  368.9 2.2 copy.15
  (9 shorter events, 0.0 us)
Async XLA Ops:
  0.6 112.5 %copy-start = (bf16[1,256,3584]{2,1,0:T(8,128)(2,1)S(1)}, bf16[1,256,3584]{2,1,0:T(8,128)(2,1)}, u32[]{:S(2)}) copy-start(bf16[1,256,3584]{2,1,0:T(8,128)(2,1)} %param.19) | copy-start | bytes 5505028
  11.4 7.7 %copy-start.6 = (s32[1,1,128,1]{2,3,1,0:T(1,128)S(1)}, s32[1,1,128,1]{2,3,1,0:T(1,128)}, u32[]{:S(2)}) copy-start(s32[1,1,128,1]{2,3,1,0:T(1,128)} %param.12) | copy-start | bytes 1540
  11.4 7.9 %copy-start.2 = (bf16[1,128,3584]{2,1,0:T(8,128)(2,1)S(1)}, bf16[1,128,3584]{2,1,0:T(8,128)(2,1)}, u32[]{:S(2)}) copy-start(bf16[1,128,3584]{2,1,0:T(8,128)(2,1)} %param.10) | copy-start | bytes 2752516
  11.4 82.9 %all-to-all-start.2 = ((bf16[32,18,3584]{2,1,0:T(8,128)(2,1)}), bf16[32,18,3584]{2,1,0:T(8,128)(2,1)}, u32[]{:S(2)}, u32[]{:S(2)}) async-start(bf16[32,18,3584]{2,1,0:T(8,128)(2,1)} %bitcast.73), calls=%async_computation.2 | async-start | bytes 11010048 | tf_op jit(solution)/shard_map/all_to_all | solution.py:52
  97.1 78.0 %all-to-all-start = ((bf16[32,18,3584]{2,1,0:T(8,128)(2,1)}), bf16[32,18,3584]{2,1,0:T(8,128)(2,1)}, u32[]{:S(2)}, u32[]{:S(2)}) async-start(bf16[32,18,3584]{2,1,0:T(8,128)(2,1)} %bitcast.74), calls=%async_computation | async-start | bytes 11010048 | tf_op jit(solution)/shard_map/all_to_all | solution.py:52
  175.2 76.9 %all-to-all-start.3 = ((bf16[32,18,3584]{2,1,0:T(8,128)(2,1)}), bf16[32,18,3584]{2,1,0:T(8,128)(2,1)}, u32[]{:S(2)}, u32[]{:S(2)}) async-start(bf16[32,18,3584]{2,1,0:T(8,128)(2,1)} %reshape.332), calls=%async_computation.3 | async-start | bytes 11010048 | tf_op jit(solution)/shard_map/all_to_all | solution.py:62
  252.1 78.0 %all-to-all-start.1 = ((bf16[32,18,3584]{2,1,0:T(8,128)(2,1)}), bf16[32,18,3584]{2,1,0:T(8,128)(2,1)}, u32[]{:S(2)}, u32[]{:S(2)}) async-start(bf16[32,18,3584]{2,1,0:T(8,128)(2,1)} %reshape.326), calls=%async_computation.1 | async-start | bytes 11010048 | tf_op jit(solution)/shard_map/all_to_all | solution.py:62
  262.0 3.0 copy-start.1
  262.0 3.0 copy-start.4
  269.4 74.5 %collective-permute-start.1 = (bf16[128,3584]{1,0:T(8,128)(2,1)}, bf16[128,3584]{1,0:T(8,128)(2,1)}, u32[]{:S(2)}, u32[]{:S(2)}) collective-permute-start(bf16[128,3584]{1,0:T(8,128)(2,1)} %fusion.2), channel_id=1, source_target_pairs={{0,224},{32,0},{64,32},{96,64},{128,96},{160,128},{192,160},{224,1... | collective-permute-start | bytes 2752520 | tf_op jit(solution)/shard_map/ppermute | solution.py:16
  335.4 3.0 copy-start.3
  335.4 3.0 copy-start.5
  341.8 26.1 %collective-permute-start = (bf16[128,3584]{1,0:T(8,128)(2,1)S(1)}, bf16[128,3584]{1,0:T(8,128)(2,1)S(1)}, u32[]{:S(2)}, u32[]{:S(2)}) collective-permute-start(bf16[128,3584]{1,0:T(8,128)(2,1)S(1)} %fusion.3), channel_id=1, source_target_pairs={{0,32},{32,64},{64,96},{96,128},{128,160},{160,192},{192,224},{224... | collective-permute-start | bytes 2752520 | tf_op jit(solution)/shard_map/ppermute | solution.py:16

commit v2 on v1

v2 whole, which is shorter than its diff:
```python
import jax
import jax.numpy as jnp
from jax import lax
from jax.experimental import pallas as pl
from jax.experimental.pallas import tpu as pltpu
from jax.sharding import PartitionSpec as P

ES = 4
EXPERTS = 8
EP = ES * EXPERTS
CHIPS = EP // 2
MAIN = 16
LAST = 2
EPSILON = 1e-06
F32 = jnp.float32
BF16 = jnp.bfloat16
VMEM_LIMIT = 48 * 1024 * 1024


def iota(shape, axis):
    return lax.broadcasted_iota(jnp.int32, shape, axis)


def to_column(row):
    count = row.shape[1]
    eye = iota((count, count), 0) == iota((count, count), 1)
    return jnp.sum(jnp.where(eye, row, jnp.zeros_like(row)), axis=1, keepdims=True)


def dot(left, right):
    return jnp.dot(left, right, preferred_element_type=F32)


def prepare_kernel(current_ref, ids_ref, gain_ref, send_ref):
    tokens, features = current_ref.shape
    quarter = features // ES
    ids_row = ids_ref[...]
    ids_column = to_column(ids_row)
    same = ids_column == ids_row
    earlier = same & (iota((tokens, tokens), 0) < iota((tokens, tokens), 1))
    slot_row = jnp.sum(earlier.astype(jnp.int32), axis=0, keepdims=True)
    main_row = jnp.where(slot_row < MAIN, ids_row * MAIN + slot_row, -1)
    last_row = jnp.where(slot_row < MAIN, -1, ids_row * (ES * LAST) + slot_row - MAIN)
    pick_main = (iota((EXPERTS * MAIN, tokens), 0) == main_row).astype(BF16)
    as_float = current_ref[...].astype(F32)
    inverse_rms = lax.rsqrt(jnp.mean(as_float * as_float, axis=-1, keepdims=True) + EPSILON)
    last = jnp.zeros((EXPERTS * ES * LAST, quarter), F32)
    for q in range(ES):
        columns = slice(q * quarter, (q + 1) * quarter)
        normed = (current_ref[:, columns].astype(F32) * inverse_rms * gain_ref[:, columns]).astype(
            BF16
        )
        main = dot(pick_main, normed).astype(BF16)
        for expert in range(EXPERTS):
            rows = main[expert * MAIN : (expert + 1) * MAIN]
            send_ref[2 * expert, q * MAIN : (q + 1) * MAIN, :] = rows
            send_ref[2 * expert + 1, q * MAIN : (q + 1) * MAIN, :] = rows
        place = jnp.where(last_row < 0, -1, last_row + q * LAST)
        pick_last = (iota((EXPERTS * ES * LAST, tokens), 0) == place).astype(BF16)
        last = last + dot(pick_last, normed)
    for expert in range(EXPERTS):
        rows = last[expert * ES * LAST : (expert + 1) * ES * LAST].astype(BF16)
        send_ref[2 * expert, ES * MAIN :, :] = rows
        send_ref[2 * expert + 1, ES * MAIN :, :] = rows


def prepare(current, ids_row, gain):
    tokens, features = current.shape
    quarter = features // ES
    return pl.pallas_call(
        prepare_kernel,
        out_shape=jax.ShapeDtypeStruct((CHIPS, ES * (MAIN + LAST), quarter), BF16),
        compiler_params=pltpu.CompilerParams(vmem_limit_bytes=VMEM_LIMIT),
        cost_estimate=pl.CostEstimate(
            flops=3 * tokens * tokens * features, bytes_accessed=8 * tokens * features, transcendentals=0
        ),
    )(current, ids_row, gain)


def hidden_kernel(own_ref, other_ref, gate_ref, up_ref, hidden_ref):
    quarter = own_ref.shape[2]
    count = CHIPS * (MAIN + LAST)
    for half, received in enumerate((own_ref, other_ref)):
        last = received[:, ES * MAIN :, :].astype(F32).reshape(CHIPS * ES * LAST, quarter).astype(BF16)
        gate = jnp.zeros((count, gate_ref.shape[1]), F32)
        up = jnp.zeros((count, up_ref.shape[1]), F32)
        shape = (CHIPS * LAST, CHIPS * ES * LAST)
        target = iota(shape, 0)
        source = (target // LAST) * (ES * LAST) + target % LAST
        for q in range(ES):
            main = received[:, q * MAIN : (q + 1) * MAIN, :].reshape(CHIPS * MAIN, quarter)
            pick = (iota(shape, 1) == source + q * LAST).astype(BF16)
            rows = jnp.concatenate([main, dot(pick, last).astype(BF16)], axis=0)
            gate = gate + dot(rows, gate_ref[q * quarter : (q + 1) * quarter, :])
            up = up + dot(rows, up_ref[q * quarter : (q + 1) * quarter, :])
        hidden_ref[half * count : (half + 1) * count, :] = (jax.nn.silu(gate) * up).astype(BF16)


def hidden_units(own, other, gate_cols, up_cols):
    count = 2 * CHIPS * (MAIN + LAST)
    features, width = gate_cols.shape
    return pl.pallas_call(
        hidden_kernel,
        out_shape=jax.ShapeDtypeStruct((count, width), BF16),
        compiler_params=pltpu.CompilerParams(vmem_limit_bytes=VMEM_LIMIT),
        cost_estimate=pl.CostEstimate(
            flops=4 * count * features * width,
            bytes_accessed=4 * features * width + 2 * count * features,
            transcendentals=count * width,
        ),
    )(own, other, gate_cols, up_cols)


def down_kernel(core_ref, *refs):
    hidden_refs, down_refs, back_ref = refs[:ES], refs[ES : 2 * ES], refs[2 * ES]
    count = CHIPS * (MAIN + LAST)
    tiles = down_refs[0].shape[1] // 128
    core = core_ref[0]
    for half in range(2):
        total = jnp.zeros((count, tiles * 128), F32)
        for r in range(ES):
            place = half if r < 2 else 1 - half
            total = total + dot(
                hidden_refs[r][place * count : (place + 1) * count, :], down_refs[r][...]
            )
        total = total.astype(BF16)
        target = core if half == 0 else 1 - core
        last = jnp.zeros((CHIPS * MAIN, 128), F32)
        shape = (CHIPS * MAIN, CHIPS * LAST)
        row = iota(shape, 0)
        for t in range(tiles):
            lanes = slice(t * 128, (t + 1) * 128)
            inside = row % MAIN - t * LAST
            pick = (inside >= 0) & (inside < LAST)
            pick = pick & (iota(shape, 1) == (row // MAIN) * LAST + inside)
            last = last + dot(pick.astype(BF16), total[CHIPS * MAIN :, lanes])
            for chip in range(CHIPS):
                back_ref[2 * chip + target, t * MAIN : (t + 1) * MAIN, :] = total[
                    chip * MAIN : (chip + 1) * MAIN, lanes
                ]
        last = last.astype(BF16)
        for chip in range(CHIPS):
            back_ref[2 * chip + target, tiles * MAIN :, :] = last[chip * MAIN : (chip + 1) * MAIN]


def down_product(core, hidden, down):
    rows, width = hidden[0].shape
    columns = down[0].shape[1]
    tiles = columns // 128
    return pl.pallas_call(
        down_kernel,
        out_shape=jax.ShapeDtypeStruct((EP, (tiles + 1) * MAIN, 128), BF16),
        in_specs=[pl.BlockSpec(memory_space=pltpu.SMEM)]
        + [pl.BlockSpec(memory_space=pltpu.VMEM)] * (2 * ES),
        compiler_params=pltpu.CompilerParams(vmem_limit_bytes=VMEM_LIMIT),
        cost_estimate=pl.CostEstimate(
            flops=2 * ES * rows * width * columns,
            bytes_accessed=2 * (ES * (rows + columns) * width + rows * columns),
            transcendentals=0,
        ),
    )(core, *hidden, *down)


def finish_kernel(current_ref, back_ref, ids_ref, scores_ref, out_ref):
    tokens, features = current_ref.shape
    quarter = features // ES
    tiles = quarter // 128
    ids_row = ids_ref[...]
    ids_column = to_column(ids_row)
    score = to_column(scores_ref[...])
    earlier = (ids_column == ids_row) & (iota((tokens, tokens), 1) < iota((tokens, tokens), 0))
    slot = jnp.sum(earlier.astype(jnp.int32), axis=1, keepdims=True)
    main_place = ids_column * MAIN + slot
    last_place = (EXPERTS + ids_column) * MAIN + slot - MAIN
    lane = iota((tokens, 2 * EXPERTS * MAIN), 1)
    for t in range(tiles):
        place = jnp.where(slot < MAIN, main_place, last_place + t * LAST)
        pick = (lane == place).astype(BF16)
        for q in range(ES):
            blocks = [
                back_ref[expert * ES + q, t * MAIN : (t + 1) * MAIN, :] for expert in range(EXPERTS)
            ]
            blocks += [back_ref[expert * ES + q, tiles * MAIN :, :] for expert in range(EXPERTS)]
            moe = dot(pick, jnp.concatenate(blocks, axis=0)) * score
            columns = slice(q * quarter + t * 128, q * quarter + (t + 1) * 128)
            out_ref[:, columns] = (current_ref[:, columns].astype(F32) + moe).astype(BF16)


def finish(current, back, ids_row, scores_row):
    tokens, features = current.shape
    return pl.pallas_call(
        finish_kernel,
        out_shape=jax.ShapeDtypeStruct((tokens, features), BF16),
        compiler_params=pltpu.CompilerParams(vmem_limit_bytes=VMEM_LIMIT),
        cost_estimate=pl.CostEstimate(
            flops=4 * tokens * EXPERTS * MAIN * features,
            bytes_accessed=6 * tokens * features,
            transcendentals=0,
        ),
    )(current, back, ids_row, scores_row)


def from_partner(value, offset):
    return lax.ppermute(value, "ep", [(i, i ^ offset) for i in range(EP)])


def from_behind(value, steps):
    count = lax.axis_size("section")
    return lax.ppermute(value, "section", [(i, (i + steps) % count) for i in range(count)])


def dispatch(send):
    same_core = [[2 * chip + core for chip in range(CHIPS)] for core in range(2)]
    return lax.all_to_all(
        send, "ep", split_axis=0, concat_axis=0, axis_index_groups=same_core, tiled=True
    )


def give_back(back):
    return lax.all_to_all(back, "ep", split_axis=0, concat_axis=0, tiled=True)


def on_device(
    flight_a, flight_b, routes_a, routes_b, scores_a, scores_b, norm_gain, w_gate, w_up, w_down
):
    tokens = flight_a.shape[1]
    quarter = flight_a.shape[2] // ES
    index = lax.axis_index("ep")
    core = (index % 2).astype(jnp.int32)[None]
    current_a, current_b = flight_a[0], flight_b[0]
    ids_a, ids_b = routes_a.reshape(1, tokens), routes_b.reshape(1, tokens)
    marks_a, marks_b = scores_a.reshape(1, tokens), scores_b.reshape(1, tokens)
    gate_cols, up_cols, down_rows = w_gate[0], w_up[0], w_down[0]

    down_a = []
    for offset in (0, 2, 1, 3):
        start = ((index ^ offset) % ES) * quarter
        piece = lax.dynamic_slice_in_dim(down_rows, start, quarter, 1)
        down_a.append(from_partner(piece, offset) if offset else piece)

    send_a = prepare(current_a, ids_a, norm_gain)
    own_a = dispatch(send_a)
    send_b = prepare(current_b, ids_b, norm_gain)
    own_b = dispatch(send_b)

    moved_b = from_behind(current_b, -1)
    moved_ids = from_behind(ids_b, -1)
    moved_marks = from_behind(marks_b, -1)
    down_b = [from_behind(piece, -1) for piece in down_a]

    hidden_a = hidden_units(own_a, from_partner(own_a, 1), gate_cols, up_cols)
    across_a = from_partner(hidden_a, 2)
    all_a = [hidden_a, across_a, from_partner(hidden_a, 1), from_partner(across_a, 1)]
    returned_a = give_back(down_product(core, all_a, down_a))

    hidden_b = hidden_units(own_b, from_partner(own_b, 1), gate_cols, up_cols)
    here_b = from_behind(hidden_b, -1)
    sections = lax.axis_size("section")
    pairs = [
        (s * EP + i, ((s - 1) % sections) * EP + (i ^ 2)) for s in range(sections) for i in range(EP)
    ]
    across_b = lax.ppermute(hidden_b, ("section", "ep"), pairs)
    all_b = [here_b, across_b, from_partner(here_b, 1), from_partner(across_b, 1)]
    returned_b = give_back(down_product(core, all_b, down_b))

    updated_a = from_behind(finish(current_a, returned_a, ids_a, marks_a), 1)
    updated_b = finish(moved_b, returned_b, moved_ids, moved_marks)
    return (updated_a[None], updated_b[None])


def solution(mesh):
    placed = (
        P("section", "ep", None),
        P("section", "ep", None),
        P("section", None, "ep", None),
        P("section", None, "ep", None),
        P("section", None, "ep", None),
        P("section", None, "ep", None),
        P("section", None),
        P("section", None, "ep"),
        P("section", None, "ep"),
        P("section", "ep", None),
    )
    return jax.shard_map(
        on_device,
        mesh=mesh,
        in_specs=placed,
        out_specs=(P("section", "ep", None), P("section", "ep", None)),
        check_vma=False,
    )
```

time: 372 us -> 213 us (0.57)
  waiting for transfers between devices: 241 us -> 122 us
  matrix products: 38.2 us -> 0 us
  local copies, waits for them, and re-layouts: 46.6 us -> 14.7 us
  Pallas kernels: 0 us -> 22.6 us
  starting transfers between devices: 29.7 us -> 51.5 us
  other arithmetic: 14.9 us -> 0 us
    all_to_all x4, waiting for transfers between devices: 217 us -> 52.6 us  [the longest x2 52.6 us: dispatch(): lax.all_to_all(send, 'ep', split_axis=0, concat_axis=0, axis_index_groups...]
    ppermute x2 -> x20, waiting for transfers between devices: 24.1 us -> 69.8 us  [the longest x9 49.6 us: from_behind(): lax.ppermute(value, 'section', [(i, (i + steps) % count) for i in range(c...]
    dot_general x8 -> x0, matrix products: 38.2 us -> none  [the longest x2 18.2 us: expert_pass(): jnp.dot(hidden, down_part, preferred_element_type=jnp.float32)]
    reshape x6 -> x0, local copies, waits for them, and re-layouts: 35 us -> none  [the longest x2 14.7 us: expert_pass(): row_block = received.reshape(source_count * slot_count, feature_width)]
    pallas_call x0 -> x8, Pallas kernels: none -> 22.6 us  [the longest x2 10 us: hidden_units(): pl.pallas_call(hidden_kernel, out_shape=jax.ShapeDtypeStruct((count, widt...]
    ppermute x2 -> x20, starting transfers between devices: 7.85 us -> 25.5 us  [the longest x9 21 us: from_behind(): lax.ppermute(value, 'section', [(i, (i + steps) % count) for i in range(c...]
    reduce_sum x6 -> x0, other arithmetic: 13.4 us -> none  [the longest x2 10.6 us: finish(): jnp.sum(by_slice, axis=1).reshape(expert_count * slot_count, feature_width)]
    unnamed x16 -> x47, local copies, waits for them, and re-layouts: 3.11 us -> 11.9 us
  transfers between devices with their start and end apart: 6 -> 24, of which waited for: 5 -> 12; matrix products, arithmetic and copies ran while one was open for 22% -> 1% of each run, Pallas kernels for 0% -> 10%
where the time goes in v2:
time: 213 us; the launch traced here: 212 us
  waiting for transfers between devices  122 us (57%)
  starting transfers between devices  51.5 us (24%)
  Pallas kernels  22.6 us (11%)
  local copies, waits for them, and re-layouts  14.7 us (7%)
    all_to_all x2, waiting for transfers between devices, dispatch(): lax.all_to_all(send, 'ep', split_axis=0, concat_axis=0, axis_index_groups...  52.6 us
    ppermute x9, waiting for transfers between devices, from_behind(): lax.ppermute(value, 'section', [(i, (i + steps) % count) for i in range(c...  49.6 us
    ppermute x9, starting transfers between devices, from_behind(): lax.ppermute(value, 'section', [(i, (i + steps) % count) for i in range(c...  21 us
    ppermute x10, waiting for transfers between devices, from_partner(): return lax.ppermute(value, 'ep', [(i, i ^ offset) for i in range(EP)])  13.9 us
    all_to_all x2, starting transfers between devices, give_back(): return lax.all_to_all(back, 'ep', split_axis=0, concat_axis=0, tiled=True)  13.4 us
    all_to_all x2, starting transfers between devices, dispatch(): lax.all_to_all(send, 'ep', split_axis=0, concat_axis=0, axis_index_groups...  12.5 us
    unnamed x47, local copies, waits for them, and re-layouts  11.9 us
    pallas_call x2, Pallas kernels, hidden_units(): pl.pallas_call(hidden_kernel, out_shape=jax.ShapeDtypeStruct((count, widt...  10 us
  transfers between devices with their start and end apart: 24, of which 12 were waited for; matrix products, arithmetic and copies ran while one was open for 1% of the time, Pallas kernels for 10%

profile of v2, /device:TPU:8, one launch (start us, length us, event | category | flops | bytes accessed | tf_op | source)
XLA Modules:
  0.0 211.9 jit_solution(13280604028615780624)
XLA Ops:
  0.6 1.2 copy-done.7
  1.8 0.7 copy-done.16
  2.5 0.7 copy-done.18
  3.2 2.2 %shard_map.113 = bf16[16,72,896]{2,1,0:T(8,128)(2,1)} custom-call(bf16[128,3584]{1,0:T(8,128)(2,1)S(1)} %bitcast.23, s32[1,128]{1,0:T(1,128)S(1)} %bitcast.27, f32[1,3584]{1,0:T(1,128)S(1)} %copy-done.16), custom_call_target="tpu_custom_call" | custom-call | flops 176160768 | bytes 3670016 | tf_op jit(solution)/shard_map/pallas_call | solution.py:70
  5.3 7.5 %all-to-all-start = ((bf16[16,72,896]{2,1,0:T(8,128)(2,1)}), bf16[16,72,896]{2,1,0:T(8,128)(2,1)}, u32[]{:S(2)}, u32[]{:S(2)}) async-start(bf16[16,72,896]{2,1,0:T(8,128)(2,1)} %shard_map.113), calls=%async_computation | async-start | bytes 4128768 | tf_op jit(solution)/shard_map/all_to_all | solution.py:214
  12.9 0.8 shard_map.117
  13.7 1.4 copy-done
  15.1 26.4 %all-to-all-done.own_ref = bf16[16,72,896]{2,1,0:T(8,128)(2,1)} async-done(((bf16[16,72,896]{2,1,0:T(8,128)(2,1)}), bf16[16,72,896]{2,1,0:T(8,128)(2,1)}, u32[]{:S(2)}, u32[]{:S(2)}) %all-to-all-start) | async-done | bytes 2064416 | tf_op jit(solution)/shard_map/all_to_all | solution.py:214
  41.6 5.0 %all-to-all-start.2 = ((bf16[16,72,896]{2,1,0:T(8,128)(2,1)}), bf16[16,72,896]{2,1,0:T(8,128)(2,1)S(1)}, u32[]{:S(2)}, u32[]{:S(2)}) async-start(bf16[16,72,896]{2,1,0:T(8,128)(2,1)} %copy-done), calls=%async_computation.2 | async-start | bytes 4128768 | tf_op jit(solution)/shard_map/all_to_all | solution.py:214
  46.6 26.1 %all-to-all-done.2.own_ref = bf16[16,72,896]{2,1,0:T(8,128)(2,1)S(1)} async-done(((bf16[16,72,896]{2,1,0:T(8,128)(2,1)}), bf16[16,72,896]{2,1,0:T(8,128)(2,1)S(1)}, u32[]{:S(2)}, u32[]{:S(2)}) %all-to-all-start.2) | async-done | bytes 2064416 | tf_op jit(solution)/shard_map/all_to_all | solution.py:214
  72.7 2.7 %dynamic-slice_bitcast_fusion = (bf16[256,896]{1,0:T(8,128)(2,1)}, bf16[256,896]{1,0:T(8,128)(2,1)S(1)}, bf16[256,896]{1,0:T(8,128)(2,1)}, bf16[256,896]{1,0:T(8,128)(2,1)}) fusion(bf16[1,256,3584]{2,1,0:T(8,128)(2,1)} %param.19, s32[]{:T(128)S(6)} %select_n.43, s32[]{:T(128)S(6)} %select_n.39, s32[]{:T(128)S(6)} %select_n.37, s32[]{:T(128)S(6)} %select_n.41), kind=kLoop, calls=%fused_computation | loop fusion | bytes 3670032 | tf_op jit(solution)/shard_map/dynamic_slice | solution.py:238
  75.4 1.5 collective-permute-start.4
  76.9 5.3 %shard_map.114.refs_0_ = bf16[576,256]{1,0:T(8,128)(2,1)S(1)} custom-call(bf16[16,72,896]{2,1,0:T(8,128)(2,1)} %all-to-all-done.own_ref, bf16[16,72,896]{2,1,0:T(8,128)(2,1)} %collective-permute-done.other_ref, bf16[3584,256]{1,0:T(8,128)(2,1)S(1)} %bitcast.19, bf16[3584,256]{1,0:T(8,128)(2,1)S(1)} %bitcast.21), custom_call_target="tpu_custom_call" | custom-call | flops 2113929216 | bytes 7798784 | tf_op jit(solution)/shard_map/pallas_call | solution.py:102
  82.2 0.7 collective-permute-start.1
  82.8 1.6 collective-permute-start.6
  84.4 4.3 %collective-permute-done.4.refs_5_ = bf16[256,896]{1,0:T(8,128)(2,1)S(1)} collective-permute-done((bf16[256,896]{1,0:T(8,128)(2,1)S(1)}, bf16[256,896]{1,0:T(8,128)(2,1)S(1)}, u32[]{:S(2)}, u32[]{:S(2)}) %collective-permute-start.4) | collective-permute-done | bytes 458784 | tf_op jit(solution)/shard_map/ppermute | solution.py:204
  88.7 6.4 %collective-permute-done.1.refs_1_ = bf16[576,256]{1,0:T(8,128)(2,1)} collective-permute-done((bf16[576,256]{1,0:T(8,128)(2,1)S(1)}, bf16[576,256]{1,0:T(8,128)(2,1)}, u32[]{:S(2)}, u32[]{:S(2)}) %collective-permute-start.1) | collective-permute-done | bytes 294944 | tf_op jit(solution)/shard_map/ppermute | solution.py:204
  95.2 5.9 %collective-permute-start.14 = (bf16[256,896]{1,0:T(8,128)(2,1)}, bf16[256,896]{1,0:T(8,128)(2,1)}, u32[]{:S(2)}, u32[]{:S(2)}) collective-permute-start(bf16[256,896]{1,0:T(8,128)(2,1)} %get-tuple-element.4.refs_4_), channel_id=1, source_target_pairs={{0,224},{32,0},{64,32},{96,64},{128,96},{160,128},{192,160},{224,1... | collective-permute-start | bytes 1376264 | tf_op jit(solution)/shard_map/ppermute | solution.py:209
  101.1 3.1 %collective-permute-done.6.refs_7_ = bf16[256,896]{1,0:T(8,128)(2,1)} collective-permute-done((bf16[256,896]{1,0:T(8,128)(2,1)}, bf16[256,896]{1,0:T(8,128)(2,1)}, u32[]{:S(2)}, u32[]{:S(2)}) %collective-permute-start.6) | collective-permute-done | bytes 458784 | tf_op jit(solution)/shard_map/ppermute | solution.py:204
  104.2 3.3 %shard_map.115 = bf16[32,128,128]{2,1,0:T(8,128)(2,1)S(1)} custom-call(s32[1]{0:T(128)} %bitcast.1.core_ref, bf16[576,256]{1,0:T(8,128)(2,1)S(1)} %shard_map.114.refs_0_, bf16[576,256]{1,0:T(8,128)(2,1)} %collective-permute-done.1.refs_1_, bf16[576,256]{1,0:T(8,128)(2,1)} %collective-permute-done.2.refs_2_, bf16[576,256]{1,0:T(8,128)(2,1)} %collective-permute-done.3.refs_3_, ...), custom_call_target="tpu_custom_call" | custom-call | flops 1056964608 | bytes 4046848 | tf_op jit(solution)/shard_map/pallas_call | solution.py:150
  107.5 1.0 copy-done.5
  108.5 5.9 %all-to-all-start.1 = ((bf16[32,128,128]{2,1,0:T(8,128)(2,1)}), bf16[32,128,128]{2,1,0:T(8,128)(2,1)S(1)}, u32[]{:S(2)}, u32[]{:S(2)}) async-start(bf16[32,128,128]{2,1,0:T(8,128)(2,1)} %copy-done.5), calls=%async_computation.1 | async-start | bytes 2097152 | tf_op jit(solution)/shard_map/all_to_all | solution.py:220
  114.4 1.5 copy-done.2
  115.9 1.5 copy-done.4
  117.4 4.7 %shard_map.118 = bf16[576,256]{1,0:T(8,128)(2,1)S(1)} custom-call(bf16[16,72,896]{2,1,0:T(8,128)(2,1)S(1)} %all-to-all-done.2.own_ref, bf16[16,72,896]{2,1,0:T(8,128)(2,1)} %collective-permute-done.9.other_ref, bf16[3584,256]{1,0:T(8,128)(2,1)S(1)} %bitcast.20, bf16[3584,256]{1,0:T(8,128)(2,1)S(1)} %bitcast.22), custom_call_target="tpu_custom_call" | custom-call | flops 2113929216 | bytes 7798784 | tf_op jit(solution)/shard_map/pallas_call | solution.py:102
  122.2 5.9 %collective-permute-start.10 = (bf16[576,256]{1,0:T(8,128)(2,1)S(1)}, bf16[576,256]{1,0:T(8,128)(2,1)S(1)}, u32[]{:S(2)}, u32[]{:S(2)}) collective-permute-start(bf16[576,256]{1,0:T(8,128)(2,1)S(1)} %shard_map.118), channel_id=1, source_target_pairs={{0,224},{32,0},{64,32},{96,64},{128,96},{160,128},{192,160},{224,1... | collective-permute-start | bytes 884744 | tf_op jit(solution)/shard_map/ppermute | solution.py:209
  128.1 0.8 collective-permute-start.11
  128.9 1.0 collective-permute-start.15
  130.0 1.0 collective-permute-start.16
  131.0 0.2 collective-permute-start.17
  131.1 4.3 %collective-permute-done.10.refs_0_ = bf16[576,256]{1,0:T(8,128)(2,1)S(1)} collective-permute-done((bf16[576,256]{1,0:T(8,128)(2,1)S(1)}, bf16[576,256]{1,0:T(8,128)(2,1)S(1)}, u32[]{:S(2)}, u32[]{:S(2)}) %collective-permute-start.10) | collective-permute-done | bytes 294944 | tf_op jit(solution)/shard_map/ppermute | solution.py:209
  135.5 6.3 %collective-permute-done.11.refs_1_ = bf16[576,256]{1,0:T(8,128)(2,1)S(1)} collective-permute-done((bf16[576,256]{1,0:T(8,128)(2,1)S(1)}, bf16[576,256]{1,0:T(8,128)(2,1)S(1)}, u32[]{:S(2)}, u32[]{:S(2)}) %collective-permute-start.11) | collective-permute-done | bytes 294944 | tf_op jit(solution)/shard_map/ppermute | solution.py:262
  141.8 9.8 %collective-permute-done.15.refs_5_ = bf16[256,896]{1,0:T(8,128)(2,1)S(1)} collective-permute-done((bf16[256,896]{1,0:T(8,128)(2,1)S(1)}, bf16[256,896]{1,0:T(8,128)(2,1)S(1)}, u32[]{:S(2)}, u32[]{:S(2)}) %collective-permute-start.15) | collective-permute-done | bytes 458784 | tf_op jit(solution)/shard_map/ppermute | solution.py:209
  151.6 9.8 %collective-permute-done.16.refs_6_ = bf16[256,896]{1,0:T(8,128)(2,1)S(1)} collective-permute-done((bf16[256,896]{1,0:T(8,128)(2,1)S(1)}, bf16[256,896]{1,0:T(8,128)(2,1)S(1)}, u32[]{:S(2)}, u32[]{:S(2)}) %collective-permute-start.16) | collective-permute-done | bytes 458784 | tf_op jit(solution)/shard_map/ppermute | solution.py:209
  161.4 9.1 %collective-permute-done.17.refs_7_ = bf16[256,896]{1,0:T(8,128)(2,1)S(1)} collective-permute-done((bf16[256,896]{1,0:T(8,128)(2,1)}, bf16[256,896]{1,0:T(8,128)(2,1)S(1)}, u32[]{:S(2)}, u32[]{:S(2)}) %collective-permute-start.17) | collective-permute-done | bytes 458784 | tf_op jit(solution)/shard_map/ppermute | solution.py:209
  170.6 2.9 %shard_map.119 = bf16[32,128,128]{2,1,0:T(8,128)(2,1)S(1)} custom-call(s32[1]{0:T(128)} %bitcast.1.core_ref, bf16[576,256]{1,0:T(8,128)(2,1)S(1)} %collective-permute-done.10.refs_0_, bf16[576,256]{1,0:T(8,128)(2,1)S(1)} %collective-permute-done.11.refs_1_, bf16[576,256]{1,0:T(8,128)(2,1)S(1)} %collective-permute-done.12.refs_2_, ...), custom_call_target="tpu_custom_call" | custom-call | flops 1056964608 | bytes 4046848 | tf_op jit(solution)/shard_map/pallas_call | solution.py:150
  173.5 1.0 copy-done.6
  174.5 7.5 %all-to-all-start.3 = ((bf16[32,128,128]{2,1,0:T(8,128)(2,1)}), bf16[32,128,128]{2,1,0:T(8,128)(2,1)S(1)}, u32[]{:S(2)}, u32[]{:S(2)}) async-start(bf16[32,128,128]{2,1,0:T(8,128)(2,1)} %copy-done.6), calls=%async_computation.3 | async-start | bytes 2097152 | tf_op jit(solution)/shard_map/all_to_all | solution.py:220
  182.0 3.7 %collective-permute-start.8 = (bf16[128,3584]{1,0:T(8,128)(2,1)}, bf16[128,3584]{1,0:T(8,128)(2,1)S(1)}, u32[]{:S(2)}, u32[]{:S(2)}) collective-permute-start(bf16[128,3584]{1,0:T(8,128)(2,1)} %bitcast.25), channel_id=1, source_target_pairs={{0,224},{32,0},{64,32},{96,64},{128,96},{160,128},{192,160},{224,1... | collective-permute-start | bytes 2752520 | tf_op jit(solution)/shard_map/ppermute | solution.py:209
  185.7 1.7 shard_map.116
  187.4 3.2 %collective-permute-start.18 = (s32[1,128]{1,0:T(1,128)S(1)}, s32[1,128]{1,0:T(1,128)S(1)}, u32[]{:S(2)}, u32[]{:S(2)}) collective-permute-start(s32[1,128]{1,0:T(1,128)S(1)} %bitcast.31), channel_id=1, source_target_pairs={{0,224},{32,0},{64,32},{96,64},{128,96},{160,128},{192,160},{224,1... | collective-permute-start | bytes 1544 | tf_op jit(solution)/shard_map/ppermute | solution.py:209
  190.6 0.0 collective-permute-start.19
  190.7 15.3 %collective-permute-done.18.ids_ref = s32[1,128]{1,0:T(1,128)S(1)} collective-permute-done((s32[1,128]{1,0:T(1,128)S(1)}, s32[1,128]{1,0:T(1,128)S(1)}, u32[]{:S(2)}, u32[]{:S(2)}) %collective-permute-start.18) | collective-permute-done | bytes 544 | tf_op jit(solution)/shard_map/ppermute | solution.py:209
  205.9 0.9 copy-done.10
  206.9 1.2 copy-done.11
  208.0 1.7 shard_map.120
  209.7 1.2 collective-permute-done.7
  210.9 0.9 copy.13
  (56 shorter events, 0.1 us)
Async XLA Ops:
  0.6 1.2 copy-start.7
  1.8 0.7 copy-start.16
  2.5 0.7 copy-start.18
  5.3 7.5 %copy-start.9 = (bf16[1,128,3584]{2,1,0:T(8,128)(2,1)S(1)}, bf16[1,128,3584]{2,1,0:T(8,128)(2,1)}, u32[]{:S(2)}) copy-start(bf16[1,128,3584]{2,1,0:T(8,128)(2,1)} %param.11) | copy-start | bytes 2752516
  5.3 7.5 %copy-start.17 = (f32[1,3584]{1,0:T(1,128)S(1)}, f32[1,3584]{1,0:T(1,128)}, u32[]{:S(2)}) copy-start(f32[1,3584]{1,0:T(1,128)} %gain_ref.3) | copy-start | bytes 43012
  5.3 7.5 %copy-start.21 = (s32[1,1,128,1]{2,3,1,0:T(1,128)S(1)}, s32[1,1,128,1]{2,3,1,0:T(1,128)}, u32[]{:S(2)}) copy-start(s32[1,1,128,1]{2,3,1,0:T(1,128)} %param.13) | copy-start | bytes 1540
  5.3 36.2 %all-to-all-start = ((bf16[16,72,896]{2,1,0:T(8,128)(2,1)}), bf16[16,72,896]{2,1,0:T(8,128)(2,1)}, u32[]{:S(2)}, u32[]{:S(2)}) async-start(bf16[16,72,896]{2,1,0:T(8,128)(2,1)} %shard_map.113), calls=%async_computation | async-start | bytes 4128768 | tf_op jit(solution)/shard_map/all_to_all | solution.py:214
  13.7 1.4 copy-start
  41.6 31.1 %all-to-all-start.2 = ((bf16[16,72,896]{2,1,0:T(8,128)(2,1)}), bf16[16,72,896]{2,1,0:T(8,128)(2,1)S(1)}, u32[]{:S(2)}, u32[]{:S(2)}) async-start(bf16[16,72,896]{2,1,0:T(8,128)(2,1)} %copy-done), calls=%async_computation.2 | async-start | bytes 4128768 | tf_op jit(solution)/shard_map/all_to_all | solution.py:214
  46.6 30.3 %collective-permute-start = (bf16[16,72,896]{2,1,0:T(8,128)(2,1)}, bf16[16,72,896]{2,1,0:T(8,128)(2,1)}, u32[]{:S(2)}, u32[]{:S(2)}) collective-permute-start(bf16[16,72,896]{2,1,0:T(8,128)(2,1)} %all-to-all-done.own_ref), channel_id=1, source_target_pairs={{0,1},{1,0},{2,3},{3,2},{4,5},{5,4},{6,7},{7,6},{8,9},{9,8},{10,11... | collective-permute-start | bytes 6193160 | tf_op jit(solution)/shard_map/ppermute | solution.py:204
  72.7 41.7 %collective-permute-start.9 = (bf16[16,72,896]{2,1,0:T(8,128)(2,1)S(1)}, bf16[16,72,896]{2,1,0:T(8,128)(2,1)}, u32[]{:S(2)}, u32[]{:S(2)}) collective-permute-start(bf16[16,72,896]{2,1,0:T(8,128)(2,1)S(1)} %all-to-all-done.2.own_ref), channel_id=1, source_target_pairs={{0,1},{1,0},{2,3},{3,2},{4,5},{5,4},{6,7},{7,6},{8,9},{9,8},{10,11... | collective-permute-start | bytes 6193160 | tf_op jit(solution)/shard_map/ppermute | solution.py:204
  72.7 4.2 %copy-start.1 = (bf16[1,3584,256]{2,1,0:T(8,128)(2,1)S(1)}, bf16[1,3584,256]{2,1,0:T(8,128)(2,1)}, u32[]{:S(2)}) copy-start(bf16[1,3584,256]{2,1,0:T(8,128)(2,1)} %param.17) | copy-start | bytes 5505028
  72.7 4.2 %copy-start.3 = (bf16[1,3584,256]{2,1,0:T(8,128)(2,1)S(1)}, bf16[1,3584,256]{2,1,0:T(8,128)(2,1)}, u32[]{:S(2)}) copy-start(bf16[1,3584,256]{2,1,0:T(8,128)(2,1)} %param.18) | copy-start | bytes 5505028
  75.4 13.3 %collective-permute-start.4 = (bf16[256,896]{1,0:T(8,128)(2,1)S(1)}, bf16[256,896]{1,0:T(8,128)(2,1)S(1)}, u32[]{:S(2)}, u32[]{:S(2)}) collective-permute-start(bf16[256,896]{1,0:T(8,128)(2,1)S(1)} %get-tuple-element.3), channel_id=1, source_target_pairs={{0,2},{1,3},{2,0},{3,1},{4,6},{5,7},{6,4},{7,5},{8,10},{9,11},{10,... | collective-permute-start | bytes 1376264 | tf_op jit(solution)/shard_map/ppermute | solution.py:204
  82.2 13.0 %collective-permute-start.1 = (bf16[576,256]{1,0:T(8,128)(2,1)S(1)}, bf16[576,256]{1,0:T(8,128)(2,1)}, u32[]{:S(2)}, u32[]{:S(2)}) collective-permute-start(bf16[576,256]{1,0:T(8,128)(2,1)S(1)} %shard_map.114.refs_0_), channel_id=1, source_target_pairs={{0,2},{1,3},{2,0},{3,1},{4,6},{5,7},{6,4},{7,5},{8,10},{9,11},{10,... | collective-permute-start | bytes 884744 | tf_op jit(solution)/shard_map/ppermute | solution.py:204
  82.8 12.3 %collective-permute-start.5 = (bf16[256,896]{1,0:T(8,128)(2,1)}, bf16[256,896]{1,0:T(8,128)(2,1)S(1)}, u32[]{:S(2)}, u32[]{:S(2)}) collective-permute-start(bf16[256,896]{1,0:T(8,128)(2,1)} %get-tuple-element.5), channel_id=1, source_target_pairs={{0,1},{1,0},{2,3},{3,2},{4,5},{5,4},{6,7},{7,6},{8,9},{9,8},{10,11... | collective-permute-start | bytes 1376264 | tf_op jit(solution)/shard_map/ppermute | solution.py:204
  82.8 21.4 %collective-permute-start.6 = (bf16[256,896]{1,0:T(8,128)(2,1)}, bf16[256,896]{1,0:T(8,128)(2,1)}, u32[]{:S(2)}, u32[]{:S(2)}) collective-permute-start(bf16[256,896]{1,0:T(8,128)(2,1)} %get-tuple-element.2), channel_id=1, source_target_pairs={{0,3},{1,2},{2,1},{3,0},{4,7},{5,6},{6,5},{7,4},{8,11},{9,10},{10,... | collective-permute-start | bytes 1376264 | tf_op jit(solution)/shard_map/ppermute | solution.py:204
  88.7 19.7 %copy-start.12 = (bf16[256,896]{1,0:T(8,128)(2,1)}, bf16[256,896]{1,0:T(8,128)(2,1)S(1)}, u32[]{:S(2)}) copy-start(bf16[256,896]{1,0:T(8,128)(2,1)S(1)} %collective-permute-done.4.refs_5_) | copy-start | bytes 1376260
  88.7 15.5 %collective-permute-start.2 = (bf16[576,256]{1,0:T(8,128)(2,1)S(1)}, bf16[576,256]{1,0:T(8,128)(2,1)}, u32[]{:S(2)}, u32[]{:S(2)}) collective-permute-start(bf16[576,256]{1,0:T(8,128)(2,1)S(1)} %shard_map.114.refs_0_), channel_id=1, source_target_pairs={{0,1},{1,0},{2,3},{3,2},{4,5},{5,4},{6,7},{7,6},{8,9},{9,8},{10,11... | collective-permute-start | bytes 884744 | tf_op jit(solution)/shard_map/ppermute | solution.py:204
  95.2 9.1 %collective-permute-start.3 = (bf16[576,256]{1,0:T(8,128)(2,1)}, bf16[576,256]{1,0:T(8,128)(2,1)}, u32[]{:S(2)}, u32[]{:S(2)}) collective-permute-start(bf16[576,256]{1,0:T(8,128)(2,1)} %collective-permute-done.1.refs_1_), channel_id=1, source_target_pairs={{0,1},{1,0},{2,3},{3,2},{4,5},{5,4},{6,7},{7,6},{8,9},{9,8},{10,11... | collective-permute-start | bytes 884744 | tf_op jit(solution)/shard_map/ppermute | solution.py:204
  95.2 13.3 %copy-start.14 = (bf16[256,896]{1,0:T(8,128)(2,1)}, bf16[256,896]{1,0:T(8,128)(2,1)S(1)}, u32[]{:S(2)}) copy-start(bf16[256,896]{1,0:T(8,128)(2,1)S(1)} %collective-permute-done.5.refs_6_) | copy-start | bytes 1376260
  95.2 35.8 %collective-permute-start.14 = (bf16[256,896]{1,0:T(8,128)(2,1)}, bf16[256,896]{1,0:T(8,128)(2,1)}, u32[]{:S(2)}, u32[]{:S(2)}) collective-permute-start(bf16[256,896]{1,0:T(8,128)(2,1)} %get-tuple-element.4.refs_4_), channel_id=1, source_target_pairs={{0,224},{32,0},{64,32},{96,64},{128,96},{160,128},{192,160},{224,1... | collective-permute-start | bytes 1376264 | tf_op jit(solution)/shard_map/ppermute | solution.py:209
  107.5 1.0 copy-start.5
  108.5 66.0 %all-to-all-start.1 = ((bf16[32,128,128]{2,1,0:T(8,128)(2,1)}), bf16[32,128,128]{2,1,0:T(8,128)(2,1)S(1)}, u32[]{:S(2)}, u32[]{:S(2)}) async-start(bf16[32,128,128]{2,1,0:T(8,128)(2,1)} %copy-done.5), calls=%async_computation.1 | async-start | bytes 2097152 | tf_op jit(solution)/shard_map/all_to_all | solution.py:220
  114.4 1.5 copy-start.2
  115.9 1.5 copy-start.4
  117.4 11.5 %copy-start.13 = (bf16[256,896]{1,0:T(8,128)(2,1)S(1)}, bf16[256,896]{1,0:T(8,128)(2,1)}, u32[]{:S(2)}) copy-start(bf16[256,896]{1,0:T(8,128)(2,1)} %copy-done.12) | copy-start | bytes 1376260
  117.4 12.6 %copy-start.15 = (bf16[256,896]{1,0:T(8,128)(2,1)S(1)}, bf16[256,896]{1,0:T(8,128)(2,1)}, u32[]{:S(2)}) copy-start(bf16[256,896]{1,0:T(8,128)(2,1)} %copy-done.14) | copy-start | bytes 1376260
  122.2 13.3 %collective-permute-start.10 = (bf16[576,256]{1,0:T(8,128)(2,1)S(1)}, bf16[576,256]{1,0:T(8,128)(2,1)S(1)}, u32[]{:S(2)}, u32[]{:S(2)}) collective-permute-start(bf16[576,256]{1,0:T(8,128)(2,1)S(1)} %shard_map.118), channel_id=1, source_target_pairs={{0,224},{32,0},{64,32},{96,64},{128,96},{160,128},{192,160},{224,1... | collective-permute-start | bytes 884744 | tf_op jit(solution)/shard_map/ppermute | solution.py:209
  128.1 13.7 %collective-permute-start.11 = (bf16[576,256]{1,0:T(8,128)(2,1)S(1)}, bf16[576,256]{1,0:T(8,128)(2,1)S(1)}, u32[]{:S(2)}, u32[]{:S(2)}) collective-permute-start(bf16[576,256]{1,0:T(8,128)(2,1)S(1)} %shard_map.118), channel_id=1, source_target_pairs={{0,226},{1,227},{2,224},{3,225},{4,230},{5,231},{6,228},{7,229},{8... | collective-permute-start | bytes 884744 | tf_op jit(solution)/shard_map/ppermute | solution.py:262
  128.9 22.7 %collective-permute-start.15 = (bf16[256,896]{1,0:T(8,128)(2,1)S(1)}, bf16[256,896]{1,0:T(8,128)(2,1)S(1)}, u32[]{:S(2)}, u32[]{:S(2)}) collective-permute-start(bf16[256,896]{1,0:T(8,128)(2,1)S(1)} %copy-done.13), channel_id=1, source_target_pairs={{0,224},{32,0},{64,32},{96,64},{128,96},{160,128},{192,160},{224,1... | collective-permute-start | bytes 1376264 | tf_op jit(solution)/shard_map/ppermute | solution.py:209
  130.0 31.5 %collective-permute-start.16 = (bf16[256,896]{1,0:T(8,128)(2,1)S(1)}, bf16[256,896]{1,0:T(8,128)(2,1)S(1)}, u32[]{:S(2)}, u32[]{:S(2)}) collective-permute-start(bf16[256,896]{1,0:T(8,128)(2,1)S(1)} %copy-done.15), channel_id=1, source_target_pairs={{0,224},{32,0},{64,32},{96,64},{128,96},{160,128},{192,160},{224,1... | collective-permute-start | bytes 1376264 | tf_op jit(solution)/shard_map/ppermute | solution.py:209
  131.0 39.6 %collective-permute-start.17 = (bf16[256,896]{1,0:T(8,128)(2,1)}, bf16[256,896]{1,0:T(8,128)(2,1)S(1)}, u32[]{:S(2)}, u32[]{:S(2)}) collective-permute-start(bf16[256,896]{1,0:T(8,128)(2,1)} %collective-permute-done.6.refs_7_), channel_id=1, source_target_pairs={{0,224},{32,0},{64,32},{96,64},{128,96},{160,128},{192,160},{224,1... | collective-permute-start | bytes 1376264 | tf_op jit(solution)/shard_map/ppermute | solution.py:209
  135.5 35.1 %collective-permute-start.12 = (bf16[576,256]{1,0:T(8,128)(2,1)S(1)}, bf16[576,256]{1,0:T(8,128)(2,1)S(1)}, u32[]{:S(2)}, u32[]{:S(2)}) collective-permute-start(bf16[576,256]{1,0:T(8,128)(2,1)S(1)} %collective-permute-done.10.refs_0_), channel_id=1, source_target_pairs={{0,1},{1,0},{2,3},{3,2},{4,5},{5,4},{6,7},{7,6},{8,9},{9,8},{10,11... | collective-permute-start | bytes 884744 | tf_op jit(solution)/shard_map/ppermute | solution.py:204
  141.8 28.8 %collective-permute-start.13 = (bf16[576,256]{1,0:T(8,128)(2,1)S(1)}, bf16[576,256]{1,0:T(8,128)(2,1)S(1)}, u32[]{:S(2)}, u32[]{:S(2)}) collective-permute-start(bf16[576,256]{1,0:T(8,128)(2,1)S(1)} %collective-permute-done.11.refs_1_), channel_id=1, source_target_pairs={{0,1},{1,0},{2,3},{3,2},{4,5},{5,4},{6,7},{7,6},{8,9},{9,8},{10,11... | collective-permute-start | bytes 884744 | tf_op jit(solution)/shard_map/ppermute | solution.py:204
  173.5 1.0 copy-start.6
  174.5 11.2 %copy-start.8 = (bf16[1,128,3584]{2,1,0:T(8,128)(2,1)S(1)}, bf16[1,128,3584]{2,1,0:T(8,128)(2,1)}, u32[]{:S(2)}) copy-start(bf16[1,128,3584]{2,1,0:T(8,128)(2,1)} %param.10) | copy-start | bytes 2752516
  174.5 11.2 %copy-start.19 = (s32[1,1,128,1]{2,3,1,0:T(1,128)S(1)}, s32[1,1,128,1]{2,3,1,0:T(1,128)}, u32[]{:S(2)}) copy-start(s32[1,1,128,1]{2,3,1,0:T(1,128)} %param.12) | copy-start | bytes 1540
  174.5 11.2 %copy-start.20 = (f32[1,1,128,1]{2,3,1,0:T(1,128)S(1)}, f32[1,1,128,1]{2,3,1,0:T(1,128)}, u32[]{:S(2)}) copy-start(f32[1,1,128,1]{2,3,1,0:T(1,128)} %param.14) | copy-start | bytes 1540
  174.5 16.2 %copy-start.22 = (f32[1,1,128,1]{2,3,1,0:T(1,128)S(1)}, f32[1,1,128,1]{2,3,1,0:T(1,128)}, u32[]{:S(2)}) copy-start(f32[1,1,128,1]{2,3,1,0:T(1,128)} %param.15) | copy-start | bytes 1540
  174.5 32.4 %all-to-all-start.3 = ((bf16[32,128,128]{2,1,0:T(8,128)(2,1)}), bf16[32,128,128]{2,1,0:T(8,128)(2,1)S(1)}, u32[]{:S(2)}, u32[]{:S(2)}) async-start(bf16[32,128,128]{2,1,0:T(8,128)(2,1)} %copy-done.6), calls=%async_computation.3 | async-start | bytes 2097152 | tf_op jit(solution)/shard_map/all_to_all | solution.py:220
  182.0 23.9 %collective-permute-start.8 = (bf16[128,3584]{1,0:T(8,128)(2,1)}, bf16[128,3584]{1,0:T(8,128)(2,1)S(1)}, u32[]{:S(2)}, u32[]{:S(2)}) collective-permute-start(bf16[128,3584]{1,0:T(8,128)(2,1)} %bitcast.25), channel_id=1, source_target_pairs={{0,224},{32,0},{64,32},{96,64},{128,96},{160,128},{192,160},{224,1... | collective-permute-start | bytes 2752520 | tf_op jit(solution)/shard_map/ppermute | solution.py:209
  187.4 23.5 %collective-permute-start.7 = (bf16[128,3584]{1,0:T(8,128)(2,1)}, bf16[128,3584]{1,0:T(8,128)(2,1)S(1)}, u32[]{:S(2)}, u32[]{:S(2)}) collective-permute-start(bf16[128,3584]{1,0:T(8,128)(2,1)} %shard_map.116), channel_id=1, source_target_pairs={{0,32},{32,64},{64,96},{96,128},{128,160},{160,192},{192,224},{224... | collective-permute-start | bytes 2752520 | tf_op jit(solution)/shard_map/ppermute | solution.py:209
  187.4 18.5 %collective-permute-start.18 = (s32[1,128]{1,0:T(1,128)S(1)}, s32[1,128]{1,0:T(1,128)S(1)}, u32[]{:S(2)}, u32[]{:S(2)}) collective-permute-start(s32[1,128]{1,0:T(1,128)S(1)} %bitcast.31), channel_id=1, source_target_pairs={{0,224},{32,0},{64,32},{96,64},{128,96},{160,128},{192,160},{224,1... | collective-permute-start | bytes 1544 | tf_op jit(solution)/shard_map/ppermute | solution.py:209
  190.6 15.3 %collective-permute-start.19 = (f32[1,128]{1,0:T(1,128)S(1)}, f32[1,128]{1,0:T(1,128)S(1)}, u32[]{:S(2)}, u32[]{:S(2)}) collective-permute-start(f32[1,128]{1,0:T(1,128)S(1)} %bitcast.34), channel_id=1, source_target_pairs={{0,224},{32,0},{64,32},{96,64},{128,96},{160,128},{192,160},{224,1... | collective-permute-start | bytes 1544 | tf_op jit(solution)/shard_map/ppermute | solution.py:209
  205.9 0.9 copy-start.10
  206.9 1.2 copy-start.11

commit v3 on v2

--- a/solution.py
+++ b/solution.py
@@ -238,21 +238,21 @@
         piece = lax.dynamic_slice_in_dim(down_rows, start, quarter, 1)
         down_a.append(from_partner(piece, offset) if offset else piece)
 
-    send_a = prepare(current_a, ids_a, norm_gain)
-    own_a = dispatch(send_a)
+    own_a = dispatch(prepare(current_a, ids_a, norm_gain))
     send_b = prepare(current_b, ids_b, norm_gain)
+
+    moved = [from_behind(value, -1) for value in (current_b, ids_b, marks_b, down_a[0])]
+    own_a, send_b, down_a, moved = lax.optimization_barrier((own_a, send_b, down_a, moved))
     own_b = dispatch(send_b)
-
-    moved_b = from_behind(current_b, -1)
-    moved_ids = from_behind(ids_b, -1)
-    moved_marks = from_behind(marks_b, -1)
-    down_b = [from_behind(piece, -1) for piece in down_a]
+    down_b = [moved[3]] + [from_behind(piece, -1) for piece in down_a[1:]]
 
     hidden_a = hidden_units(own_a, from_partner(own_a, 1), gate_cols, up_cols)
     across_a = from_partner(hidden_a, 2)
     all_a = [hidden_a, across_a, from_partner(hidden_a, 1), from_partner(across_a, 1)]
-    returned_a = give_back(down_product(core, all_a, down_a))
-
+    back_a = down_product(core, all_a, down_a)
+
+    own_b, back_a, down_b = lax.optimization_barrier((own_b, back_a, down_b))
+    returned_a = give_back(back_a)
     hidden_b = hidden_units(own_b, from_partner(own_b, 1), gate_cols, up_cols)
     here_b = from_behind(hidden_b, -1)
     sections = lax.axis_size("section")
@@ -261,9 +261,13 @@
     ]
     across_b = lax.ppermute(hidden_b, ("section", "ep"), pairs)
     all_b = [here_b, across_b, from_partner(here_b, 1), from_partner(across_b, 1)]
-    returned_b = give_back(down_product(core, all_b, down_b))
-
-    updated_a = from_behind(finish(current_a, returned_a, ids_a, marks_a), 1)
+    back_b = down_product(core, all_b, down_b)
+
+    updated_a = finish(current_a, returned_a, ids_a, marks_a)
+    updated_a, back_b = lax.optimization_barrier((updated_a, back_b))
+    returned_b = give_back(back_b)
+    updated_a = from_behind(updated_a, 1)
+    moved_b, moved_ids, moved_marks = moved[:3]
     updated_b = finish(moved_b, returned_b, moved_ids, moved_marks)
     return (updated_a[None], updated_b[None])
 

time: 213 us -> 188 us (0.88)
  waiting for transfers between devices: 122 us -> 82.6 us
  local copies, waits for them, and re-layouts: 14.7 us -> 24.6 us
  starting transfers between devices: 51.5 us -> 55 us
    all_to_all x2, waiting for transfers between devices: 52.6 us -> 0.01 us  [dispatch(): lax.all_to_all(send, 'ep', split_axis=0, concat_axis=0, axis_index_groups...]
    ppermute x10, waiting for transfers between devices: 13.9 us -> 25.9 us  [from_partner(): return lax.ppermute(value, 'ep', [(i, i ^ offset) for i in range(EP)])]
    unnamed x47 -> x61, local copies, waits for them, and re-layouts: 11.9 us -> 23 us
    ppermute x10, starting transfers between devices: 3.7 us -> 0.58 us  [from_partner(): return lax.ppermute(value, 'ep', [(i, i ^ offset) for i in range(EP)])]
    all_to_all x2, starting transfers between devices: 12.5 us -> 15.1 us  [dispatch(): lax.all_to_all(send, 'ep', split_axis=0, concat_axis=0, axis_index_groups...]
    ppermute x9, starting transfers between devices: 21 us -> 23.4 us  [from_behind(): lax.ppermute(value, 'section', [(i, (i + steps) % count) for i in range(c...]
    all_to_all x2, starting transfers between devices: 13.4 us -> 15.8 us  [give_back(): return lax.all_to_all(back, 'ep', split_axis=0, concat_axis=0, tiled=True)]
    pallas_call x2, Pallas kernels: 6.12 us -> 8.38 us  [down_product(): pl.pallas_call(down_kernel, out_shape=jax.ShapeDtypeStruct((EP, (tiles +...]
  transfers between devices with their start and end apart: 24 -> 24, of which waited for: 12 -> 9; matrix products, arithmetic and copies ran while one was open for 1% -> 1% of each run, Pallas kernels for 10% -> 8%
where the time goes in v3:
time: 188 us; the launch traced here: 187 us
  waiting for transfers between devices  82.6 us (44%)
  starting transfers between devices  55 us (29%)
  local copies, waits for them, and re-layouts  24.6 us (13%)
  Pallas kernels  23.8 us (13%)
    ppermute x9, waiting for transfers between devices, from_behind(): lax.ppermute(value, 'section', [(i, (i + steps) % count) for i in range(c...  51.1 us
    ppermute x10, waiting for transfers between devices, from_partner(): return lax.ppermute(value, 'ep', [(i, i ^ offset) for i in range(EP)])  25.9 us
    ppermute x9, starting transfers between devices, from_behind(): lax.ppermute(value, 'section', [(i, (i + steps) % count) for i in range(c...  23.4 us
    unnamed x61, local copies, waits for them, and re-layouts  23 us
    all_to_all x2, starting transfers between devices, give_back(): return lax.all_to_all(back, 'ep', split_axis=0, concat_axis=0, tiled=True)  15.8 us
    all_to_all x2, starting transfers between devices, dispatch(): lax.all_to_all(send, 'ep', split_axis=0, concat_axis=0, axis_index_groups...  15.1 us
    pallas_call x2, Pallas kernels, hidden_units(): pl.pallas_call(hidden_kernel, out_shape=jax.ShapeDtypeStruct((count, widt...  10 us
    pallas_call x2, Pallas kernels, down_product(): pl.pallas_call(down_kernel, out_shape=jax.ShapeDtypeStruct((EP, (tiles +...  8.38 us
  transfers between devices with their start and end apart: 24, of which 9 were waited for; matrix products, arithmetic and copies ran while one was open for 1% of the time, Pallas kernels for 8%

profile of v3, /device:TPU:8, one launch (start us, length us, event | category | flops | bytes accessed | tf_op | source)
XLA Modules:
  0.0 186.7 jit_solution(3379432606162406572)
XLA Ops:
  0.6 1.2 copy-done.6
  3.2 0.8 shard_map.113
  4.0 1.3 copy-done
  5.4 7.5 %all-to-all-start = ((bf16[16,72,896]{2,1,0:T(8,128)(2,1)}), bf16[16,72,896]{2,1,0:T(8,128)(2,1)S(1)}, u32[]{:S(2)}, u32[]{:S(2)}) async-start(bf16[16,72,896]{2,1,0:T(8,128)(2,1)} %copy-done), calls=%async_computation | async-start | bytes 4128768 | tf_op jit(solution)/shard_map/all_to_all | solution.py:214
  12.9 5.9 %collective-permute-start.3 = (bf16[128,3584]{1,0:T(8,128)(2,1)S(1)}, bf16[128,3584]{1,0:T(8,128)(2,1)}, u32[]{:S(2)}, u32[]{:S(2)}) collective-permute-start(bf16[128,3584]{1,0:T(8,128)(2,1)S(1)} %bitcast.25), channel_id=1, source_target_pairs={{0,224},{32,0},{64,32},{96,64},{128,96},{160,128},{192,160},{224,1... | collective-permute-start | bytes 2752520 | tf_op jit(solution)/shard_map/ppermute | solution.py:209
  18.8 1.0 collective-permute-start.4
  19.9 1.0 collective-permute-start.5
  20.9 1.6 dynamic-slice_bitcast_fusion
  22.7 15.3 %collective-permute-done.4.ids_ref = s32[1,128]{1,0:T(1,128)S(1)} collective-permute-done((s32[1,128]{1,0:T(1,128)S(1)}, s32[1,128]{1,0:T(1,128)S(1)}, u32[]{:S(2)}, u32[]{:S(2)}) %collective-permute-start.4) | collective-permute-done | bytes 544 | tf_op jit(solution)/shard_map/ppermute | solution.py:209
  38.0 3.8 %collective-permute-start.6 = (bf16[256,896]{1,0:T(8,128)(2,1)S(1)}, bf16[256,896]{1,0:T(8,128)(2,1)S(1)}, u32[]{:S(2)}, u32[]{:S(2)}) collective-permute-start(bf16[256,896]{1,0:T(8,128)(2,1)S(1)} %get-tuple-element.22.refs_4_), channel_id=1, source_target_pairs={{0,224},{32,0},{64,32},{96,64},{128,96},{160,128},{192,160},{224,1... | collective-permute-start | bytes 1376264 | tf_op jit(solution)/shard_map/ppermute | solution.py:209
  41.7 0.8 shard_map.114
  42.6 1.3 copy-done.1
  43.9 2.0 %collective-permute-done.refs_5_ = bf16[256,896]{1,0:T(8,128)(2,1)} collective-permute-done((bf16[256,896]{1,0:T(8,128)(2,1)S(1)}, bf16[256,896]{1,0:T(8,128)(2,1)}, u32[]{:S(2)}, u32[]{:S(2)}) %collective-permute-start) | collective-permute-done | bytes 458784 | tf_op jit(solution)/shard_map/ppermute | solution.py:204
  45.9 9.8 %collective-permute-done.2.refs_7_ = bf16[256,896]{1,0:T(8,128)(2,1)} collective-permute-done((bf16[256,896]{1,0:T(8,128)(2,1)S(1)}, bf16[256,896]{1,0:T(8,128)(2,1)}, u32[]{:S(2)}, u32[]{:S(2)}) %collective-permute-start.2) | collective-permute-done | bytes 458784 | tf_op jit(solution)/shard_map/ppermute | solution.py:204
  55.7 0.8 copy-done.11
  56.6 7.6 %all-to-all-start.1 = ((bf16[16,72,896]{2,1,0:T(8,128)(2,1)}), bf16[16,72,896]{2,1,0:T(8,128)(2,1)}, u32[]{:S(2)}, u32[]{:S(2)}) async-start(bf16[16,72,896]{2,1,0:T(8,128)(2,1)} %copy-done.1), calls=%async_computation.1 | async-start | bytes 4128768 | tf_op jit(solution)/shard_map/all_to_all | solution.py:214
  64.2 1.5 copy-done.2
  65.7 1.5 copy-done.4
  67.2 4.7 %shard_map.115.refs_0_ = bf16[576,256]{1,0:T(8,128)(2,1)S(1)} custom-call(bf16[16,72,896]{2,1,0:T(8,128)(2,1)S(1)} %all-to-all-done.own_ref, bf16[16,72,896]{2,1,0:T(8,128)(2,1)} %collective-permute-done.7.other_ref, bf16[3584,256]{1,0:T(8,128)(2,1)S(1)} %bitcast.19, bf16[3584,256]{1,0:T(8,128)(2,1)S(1)} %bitcast.21), custom_call_target="tpu_custom_call" | custom-call | flops 2113929216 | bytes 7798784 | tf_op jit(solution)/shard_map/pallas_call | solution.py:102
  72.1 5.9 %collective-permute-start.11 = (bf16[256,896]{1,0:T(8,128)(2,1)}, bf16[256,896]{1,0:T(8,128)(2,1)S(1)}, u32[]{:S(2)}, u32[]{:S(2)}) collective-permute-start(bf16[256,896]{1,0:T(8,128)(2,1)} %collective-permute-done.refs_5_), channel_id=1, source_target_pairs={{0,224},{32,0},{64,32},{96,64},{128,96},{160,128},{192,160},{224,1... | collective-permute-start | bytes 1376264 | tf_op jit(solution)/shard_map/ppermute | solution.py:209
  77.9 1.0 collective-permute-start.12
  79.0 1.0 collective-permute-start.13
  80.0 14.0 %collective-permute-done.8.refs_1_ = bf16[576,256]{1,0:T(8,128)(2,1)S(1)} collective-permute-done((bf16[576,256]{1,0:T(8,128)(2,1)S(1)}, bf16[576,256]{1,0:T(8,128)(2,1)S(1)}, u32[]{:S(2)}, u32[]{:S(2)}) %collective-permute-start.8) | collective-permute-done | bytes 294944 | tf_op jit(solution)/shard_map/ppermute | solution.py:204
  94.7 0.7 copy-done.19
  95.5 0.7 copy-done.21
  96.2 1.0 copy-done.18
  97.2 1.0 copy-done.20
  98.2 1.0 copy-done.22
  99.1 4.2 %shard_map.116 = bf16[32,128,128]{2,1,0:T(8,128)(2,1)} custom-call(s32[1]{0:T(128)} %bitcast.9.core_ref, bf16[576,256]{1,0:T(8,128)(2,1)S(1)} %shard_map.115.refs_0_, bf16[576,256]{1,0:T(8,128)(2,1)S(1)} %copy-done.18, bf16[576,256]{1,0:T(8,128)(2,1)S(1)} %copy-done.20, bf16[576,256]{1,0:T(8,128)(2,1)S(1)} %copy-done.22, ...), custom_call_target="tpu_custom_call" | custom-call | flops 1056964608 | bytes 4046848 | tf_op jit(solution)/shard_map/pallas_call | solution.py:150
  103.3 0.9 copy-done.15
  104.2 3.4 %collective-permute-done.13.refs_7_ = bf16[256,896]{1,0:T(8,128)(2,1)} collective-permute-done((bf16[256,896]{1,0:T(8,128)(2,1)}, bf16[256,896]{1,0:T(8,128)(2,1)}, u32[]{:S(2)}, u32[]{:S(2)}) %collective-permute-start.13) | collective-permute-done | bytes 458784 | tf_op jit(solution)/shard_map/ppermute | solution.py:209
  107.6 8.2 %all-to-all-start.2 = ((bf16[32,128,128]{2,1,0:T(8,128)(2,1)}), bf16[32,128,128]{2,1,0:T(8,128)(2,1)S(1)}, u32[]{:S(2)}, u32[]{:S(2)}) async-start(bf16[32,128,128]{2,1,0:T(8,128)(2,1)} %shard_map.116), calls=%async_computation.2 | async-start | bytes 2097152 | tf_op jit(solution)/shard_map/all_to_all | solution.py:220
  115.9 1.5 copy-done.3
  117.4 1.5 copy-done.5
  118.9 5.3 %shard_map.118 = bf16[576,256]{1,0:T(8,128)(2,1)S(1)} custom-call(bf16[16,72,896]{2,1,0:T(8,128)(2,1)} %all-to-all-done.1.own_ref, bf16[16,72,896]{2,1,0:T(8,128)(2,1)} %collective-permute-done.14.other_ref, bf16[3584,256]{1,0:T(8,128)(2,1)S(1)} %bitcast.20, bf16[3584,256]{1,0:T(8,128)(2,1)S(1)} %bitcast.22), custom_call_target="tpu_custom_call" | custom-call | flops 2113929216 | bytes 7798784 | tf_op jit(solution)/shard_map/pallas_call | solution.py:102
  124.2 3.8 %collective-permute-start.15 = (bf16[576,256]{1,0:T(8,128)(2,1)S(1)}, bf16[576,256]{1,0:T(8,128)(2,1)S(1)}, u32[]{:S(2)}, u32[]{:S(2)}) collective-permute-start(bf16[576,256]{1,0:T(8,128)(2,1)S(1)} %shard_map.118), channel_id=1, source_target_pairs={{0,224},{32,0},{64,32},{96,64},{128,96},{160,128},{192,160},{224,1... | collective-permute-start | bytes 884744 | tf_op jit(solution)/shard_map/ppermute | solution.py:209
  128.0 7.4 %collective-permute-done.15.refs_0_ = bf16[576,256]{1,0:T(8,128)(2,1)S(1)} collective-permute-done((bf16[576,256]{1,0:T(8,128)(2,1)S(1)}, bf16[576,256]{1,0:T(8,128)(2,1)S(1)}, u32[]{:S(2)}, u32[]{:S(2)}) %collective-permute-start.15) | collective-permute-done | bytes 294944 | tf_op jit(solution)/shard_map/ppermute | solution.py:209
  135.4 5.5 %collective-permute-done.16.refs_1_ = bf16[576,256]{1,0:T(8,128)(2,1)} collective-permute-done((bf16[576,256]{1,0:T(8,128)(2,1)S(1)}, bf16[576,256]{1,0:T(8,128)(2,1)}, u32[]{:S(2)}, u32[]{:S(2)}) %collective-permute-start.16) | collective-permute-done | bytes 294944 | tf_op jit(solution)/shard_map/ppermute | solution.py:262
  140.9 1.2 copy-done.7
  142.1 0.8 shard_map.117
  142.9 0.9 copy-done.9
  143.8 1.0 copy-done.12
  144.9 1.0 copy-done.16
  145.9 4.2 %shard_map.119 = bf16[32,128,128]{2,1,0:T(8,128)(2,1)} custom-call(s32[1]{0:T(128)} %bitcast.9.core_ref, bf16[576,256]{1,0:T(8,128)(2,1)S(1)} %collective-permute-done.15.refs_0_, bf16[576,256]{1,0:T(8,128)(2,1)} %collective-permute-done.16.refs_1_, bf16[576,256]{1,0:T(8,128)(2,1)} %collective-permute-done.17.refs_2_, ...), custom_call_target="tpu_custom_call" | custom-call | flops 1056964608 | bytes 4046848 | tf_op jit(solution)/shard_map/pallas_call | solution.py:150
  150.1 7.6 %all-to-all-start.3 = ((bf16[32,128,128]{2,1,0:T(8,128)(2,1)}), bf16[32,128,128]{2,1,0:T(8,128)(2,1)S(1)}, u32[]{:S(2)}, u32[]{:S(2)}) async-start(bf16[32,128,128]{2,1,0:T(8,128)(2,1)} %shard_map.119), calls=%async_computation.3 | async-start | bytes 2097152 | tf_op jit(solution)/shard_map/all_to_all | solution.py:220
  157.8 25.1 %collective-permute-done.19 = bf16[128,3584]{1,0:T(8,128)(2,1)S(1)} collective-permute-done((bf16[128,3584]{1,0:T(8,128)(2,1)S(1)}, bf16[128,3584]{1,0:T(8,128)(2,1)S(1)}, u32[]{:S(2)}, u32[]{:S(2)}) %collective-permute-start.19) | collective-permute-done | bytes 917536 | tf_op jit(solution)/shard_map/ppermute | solution.py:209
  182.9 2.9 %shard_map.120 = bf16[128,3584]{1,0:T(8,128)(2,1)} custom-call(bf16[128,3584]{1,0:T(8,128)(2,1)} %collective-permute-done.3.current_ref, bf16[32,128,128]{2,1,0:T(8,128)(2,1)S(1)} %all-to-all-done.3.back_ref, s32[1,128]{1,0:T(1,128)S(1)} %collective-permute-done.4.ids_ref, f32[1,128]{1,0:T(1,128)S(1)} %collective-permute-done.5.scores_ref), custom_call_target="tpu_custom_call" | custom-call | flops 234881024 | bytes 2752512 | tf_op jit(solution)/shard_map/pallas_call | solution.py:191
  185.8 0.9 copy.13
  (70 shorter events, 3.0 us)
Async XLA Ops:
  0.6 1.2 copy-start.6
  4.0 1.4 copy-start
  5.4 7.5 %copy-start.8 = (bf16[1,128,3584]{2,1,0:T(8,128)(2,1)S(1)}, bf16[1,128,3584]{2,1,0:T(8,128)(2,1)}, u32[]{:S(2)}) copy-start(bf16[1,128,3584]{2,1,0:T(8,128)(2,1)} %param.11) | copy-start | bytes 2752516
  5.4 13.5 %copy-start.27 = (s32[1,1,128,1]{2,3,1,0:T(1,128)S(1)}, s32[1,1,128,1]{2,3,1,0:T(1,128)}, u32[]{:S(2)}) copy-start(s32[1,1,128,1]{2,3,1,0:T(1,128)} %param.13) | copy-start | bytes 1540
  5.4 14.5 %copy-start.29 = (f32[1,1,128,1]{2,3,1,0:T(1,128)S(1)}, f32[1,1,128,1]{2,3,1,0:T(1,128)}, u32[]{:S(2)}) copy-start(f32[1,1,128,1]{2,3,1,0:T(1,128)} %param.15) | copy-start | bytes 1540
  5.4 51.1 %all-to-all-start = ((bf16[16,72,896]{2,1,0:T(8,128)(2,1)}), bf16[16,72,896]{2,1,0:T(8,128)(2,1)S(1)}, u32[]{:S(2)}, u32[]{:S(2)}) async-start(bf16[16,72,896]{2,1,0:T(8,128)(2,1)} %copy-done), calls=%async_computation | async-start | bytes 4128768 | tf_op jit(solution)/shard_map/all_to_all | solution.py:214
  12.9 28.8 %copy-start.24 = (f32[1,3584]{1,0:T(1,128)S(1)}, f32[1,3584]{1,0:T(1,128)}, u32[]{:S(2)}) copy-start(f32[1,3584]{1,0:T(1,128)} %gain_ref.3) | copy-start | bytes 43012
  12.9 43.6 %collective-permute-start.3 = (bf16[128,3584]{1,0:T(8,128)(2,1)S(1)}, bf16[128,3584]{1,0:T(8,128)(2,1)}, u32[]{:S(2)}, u32[]{:S(2)}) collective-permute-start(bf16[128,3584]{1,0:T(8,128)(2,1)S(1)} %bitcast.25), channel_id=1, source_target_pairs={{0,224},{32,0},{64,32},{96,64},{128,96},{160,128},{192,160},{224,1... | collective-permute-start | bytes 2752520 | tf_op jit(solution)/shard_map/ppermute | solution.py:209
  18.8 19.1 %collective-permute-start.4 = (s32[1,128]{1,0:T(1,128)S(1)}, s32[1,128]{1,0:T(1,128)S(1)}, u32[]{:S(2)}, u32[]{:S(2)}) collective-permute-start(s32[1,128]{1,0:T(1,128)S(1)} %bitcast.29), channel_id=1, source_target_pairs={{0,224},{32,0},{64,32},{96,64},{128,96},{160,128},{192,160},{224,1... | collective-permute-start | bytes 1544 | tf_op jit(solution)/shard_map/ppermute | solution.py:209
  19.9 18.1 %collective-permute-start.5 = (f32[1,128]{1,0:T(1,128)S(1)}, f32[1,128]{1,0:T(1,128)S(1)}, u32[]{:S(2)}, u32[]{:S(2)}) collective-permute-start(f32[1,128]{1,0:T(1,128)S(1)} %bitcast.34), channel_id=1, source_target_pairs={{0,224},{32,0},{64,32},{96,64},{128,96},{160,128},{192,160},{224,1... | collective-permute-start | bytes 1544 | tf_op jit(solution)/shard_map/ppermute | solution.py:209
  22.5 23.4 %collective-permute-start = (bf16[256,896]{1,0:T(8,128)(2,1)S(1)}, bf16[256,896]{1,0:T(8,128)(2,1)}, u32[]{:S(2)}, u32[]{:S(2)}) collective-permute-start(bf16[256,896]{1,0:T(8,128)(2,1)S(1)} %get-tuple-element.39), channel_id=1, source_target_pairs={{0,2},{1,3},{2,0},{3,1},{4,6},{5,7},{6,4},{7,5},{8,10},{9,11},{10,... | collective-permute-start | bytes 1376264 | tf_op jit(solution)/shard_map/ppermute | solution.py:204
  22.7 23.2 %collective-permute-start.1 = (bf16[256,896]{1,0:T(8,128)(2,1)S(1)}, bf16[256,896]{1,0:T(8,128)(2,1)}, u32[]{:S(2)}, u32[]{:S(2)}) collective-permute-start(bf16[256,896]{1,0:T(8,128)(2,1)S(1)} %get-tuple-element.41), channel_id=1, source_target_pairs={{0,1},{1,0},{2,3},{3,2},{4,5},{5,4},{6,7},{7,6},{8,9},{9,8},{10,11... | collective-permute-start | bytes 1376264 | tf_op jit(solution)/shard_map/ppermute | solution.py:204
  37.9 17.8 %collective-permute-start.2 = (bf16[256,896]{1,0:T(8,128)(2,1)S(1)}, bf16[256,896]{1,0:T(8,128)(2,1)}, u32[]{:S(2)}, u32[]{:S(2)}) collective-permute-start(bf16[256,896]{1,0:T(8,128)(2,1)S(1)} %get-tuple-element.38), channel_id=1, source_target_pairs={{0,3},{1,2},{2,1},{3,0},{4,7},{5,6},{6,5},{7,4},{8,11},{9,10},{10,... | collective-permute-start | bytes 1376264 | tf_op jit(solution)/shard_map/ppermute | solution.py:204
  38.0 17.7 %collective-permute-start.6 = (bf16[256,896]{1,0:T(8,128)(2,1)S(1)}, bf16[256,896]{1,0:T(8,128)(2,1)S(1)}, u32[]{:S(2)}, u32[]{:S(2)}) collective-permute-start(bf16[256,896]{1,0:T(8,128)(2,1)S(1)} %get-tuple-element.22.refs_4_), channel_id=1, source_target_pairs={{0,224},{32,0},{64,32},{96,64},{128,96},{160,128},{192,160},{224,1... | collective-permute-start | bytes 1376264 | tf_op jit(solution)/shard_map/ppermute | solution.py:209
  42.6 1.3 copy-start.1
  56.5 7.7 %collective-permute-start.7 = (bf16[16,72,896]{2,1,0:T(8,128)(2,1)S(1)}, bf16[16,72,896]{2,1,0:T(8,128)(2,1)}, u32[]{:S(2)}, u32[]{:S(2)}) collective-permute-start(bf16[16,72,896]{2,1,0:T(8,128)(2,1)S(1)} %all-to-all-done.own_ref), channel_id=1, source_target_pairs={{0,1},{1,0},{2,3},{3,2},{4,5},{5,4},{6,7},{7,6},{8,9},{9,8},{10,11... | collective-permute-start | bytes 6193160 | tf_op jit(solution)/shard_map/ppermute | solution.py:204
  56.6 51.0 %all-to-all-start.1 = ((bf16[16,72,896]{2,1,0:T(8,128)(2,1)}), bf16[16,72,896]{2,1,0:T(8,128)(2,1)}, u32[]{:S(2)}, u32[]{:S(2)}) async-start(bf16[16,72,896]{2,1,0:T(8,128)(2,1)} %copy-done.1), calls=%async_computation.1 | async-start | bytes 4128768 | tf_op jit(solution)/shard_map/all_to_all | solution.py:214
  64.2 1.5 copy-start.2
  65.7 1.5 copy-start.4
  71.9 22.1 %collective-permute-start.8 = (bf16[576,256]{1,0:T(8,128)(2,1)S(1)}, bf16[576,256]{1,0:T(8,128)(2,1)S(1)}, u32[]{:S(2)}, u32[]{:S(2)}) collective-permute-start(bf16[576,256]{1,0:T(8,128)(2,1)S(1)} %shard_map.115.refs_0_), channel_id=1, source_target_pairs={{0,2},{1,3},{2,0},{3,1},{4,6},{5,7},{6,4},{7,5},{8,10},{9,11},{10,... | collective-permute-start | bytes 884744 | tf_op jit(solution)/shard_map/ppermute | solution.py:204
  72.1 31.2 %collective-permute-start.11 = (bf16[256,896]{1,0:T(8,128)(2,1)}, bf16[256,896]{1,0:T(8,128)(2,1)S(1)}, u32[]{:S(2)}, u32[]{:S(2)}) collective-permute-start(bf16[256,896]{1,0:T(8,128)(2,1)} %collective-permute-done.refs_5_), channel_id=1, source_target_pairs={{0,224},{32,0},{64,32},{96,64},{128,96},{160,128},{192,160},{224,1... | collective-permute-start | bytes 1376264 | tf_op jit(solution)/shard_map/ppermute | solution.py:209
  77.9 25.4 %collective-permute-start.12 = (bf16[256,896]{1,0:T(8,128)(2,1)}, bf16[256,896]{1,0:T(8,128)(2,1)S(1)}, u32[]{:S(2)}, u32[]{:S(2)}) collective-permute-start(bf16[256,896]{1,0:T(8,128)(2,1)} %collective-permute-done.1.refs_6_), channel_id=1, source_target_pairs={{0,224},{32,0},{64,32},{96,64},{128,96},{160,128},{192,160},{224,1... | collective-permute-start | bytes 1376264 | tf_op jit(solution)/shard_map/ppermute | solution.py:209
  79.0 28.6 %collective-permute-start.13 = (bf16[256,896]{1,0:T(8,128)(2,1)}, bf16[256,896]{1,0:T(8,128)(2,1)}, u32[]{:S(2)}, u32[]{:S(2)}) collective-permute-start(bf16[256,896]{1,0:T(8,128)(2,1)} %collective-permute-done.2.refs_7_), channel_id=1, source_target_pairs={{0,224},{32,0},{64,32},{96,64},{128,96},{160,128},{192,160},{224,1... | collective-permute-start | bytes 1376264 | tf_op jit(solution)/shard_map/ppermute | solution.py:209
  80.0 14.7 %collective-permute-start.9 = (bf16[576,256]{1,0:T(8,128)(2,1)S(1)}, bf16[576,256]{1,0:T(8,128)(2,1)S(1)}, u32[]{:S(2)}, u32[]{:S(2)}) collective-permute-start(bf16[576,256]{1,0:T(8,128)(2,1)S(1)} %shard_map.115.refs_0_), channel_id=1, source_target_pairs={{0,1},{1,0},{2,3},{3,2},{4,5},{5,4},{6,7},{7,6},{8,9},{9,8},{10,11... | collective-permute-start | bytes 884744 | tf_op jit(solution)/shard_map/ppermute | solution.py:204
  93.9 1.6 collective-permute-start.10
  96.2 1.0 copy-start.18
  97.2 1.0 copy-start.20
  98.2 1.0 copy-start.22
  103.3 12.5 %copy-start.13 = (bf16[256,896]{1,0:T(8,128)(2,1)}, bf16[256,896]{1,0:T(8,128)(2,1)S(1)}, u32[]{:S(2)}) copy-start(bf16[256,896]{1,0:T(8,128)(2,1)S(1)} %collective-permute-done.11.refs_5_) | copy-start | bytes 1376260
  103.3 0.9 copy-start.15
  107.6 8.2 %collective-permute-start.14 = (bf16[16,72,896]{2,1,0:T(8,128)(2,1)}, bf16[16,72,896]{2,1,0:T(8,128)(2,1)}, u32[]{:S(2)}, u32[]{:S(2)}) collective-permute-start(bf16[16,72,896]{2,1,0:T(8,128)(2,1)} %all-to-all-done.1.own_ref), channel_id=1, source_target_pairs={{0,1},{1,0},{2,3},{3,2},{4,5},{5,4},{6,7},{7,6},{8,9},{9,8},{10,11... | collective-permute-start | bytes 6193160 | tf_op jit(solution)/shard_map/ppermute | solution.py:204
  107.6 33.3 %all-to-all-start.2 = ((bf16[32,128,128]{2,1,0:T(8,128)(2,1)}), bf16[32,128,128]{2,1,0:T(8,128)(2,1)S(1)}, u32[]{:S(2)}, u32[]{:S(2)}) async-start(bf16[32,128,128]{2,1,0:T(8,128)(2,1)} %shard_map.116), calls=%async_computation.2 | async-start | bytes 2097152 | tf_op jit(solution)/shard_map/all_to_all | solution.py:220
  115.9 1.5 copy-start.3
  117.4 1.5 copy-start.5
  118.9 22.0 %copy-start.26 = (s32[1,1,128,1]{2,3,1,0:T(1,128)S(1)}, s32[1,1,128,1]{2,3,1,0:T(1,128)}, u32[]{:S(2)}) copy-start(s32[1,1,128,1]{2,3,1,0:T(1,128)} %param.12) | copy-start | bytes 1540
  118.9 22.0 %copy-start.28 = (f32[1,1,128,1]{2,3,1,0:T(1,128)S(1)}, f32[1,1,128,1]{2,3,1,0:T(1,128)}, u32[]{:S(2)}) copy-start(f32[1,1,128,1]{2,3,1,0:T(1,128)} %param.14) | copy-start | bytes 1540
  124.2 11.1 %collective-permute-start.15 = (bf16[576,256]{1,0:T(8,128)(2,1)S(1)}, bf16[576,256]{1,0:T(8,128)(2,1)S(1)}, u32[]{:S(2)}, u32[]{:S(2)}) collective-permute-start(bf16[576,256]{1,0:T(8,128)(2,1)S(1)} %shard_map.118), channel_id=1, source_target_pairs={{0,224},{32,0},{64,32},{96,64},{128,96},{160,128},{192,160},{224,1... | collective-permute-start | bytes 884744 | tf_op jit(solution)/shard_map/ppermute | solution.py:209
  128.0 12.9 %collective-permute-start.16 = (bf16[576,256]{1,0:T(8,128)(2,1)S(1)}, bf16[576,256]{1,0:T(8,128)(2,1)}, u32[]{:S(2)}, u32[]{:S(2)}) collective-permute-start(bf16[576,256]{1,0:T(8,128)(2,1)S(1)} %shard_map.118), channel_id=1, source_target_pairs={{0,226},{1,227},{2,224},{3,225},{4,230},{5,231},{6,228},{7,229},{8... | collective-permute-start | bytes 884744 | tf_op jit(solution)/shard_map/ppermute | solution.py:262
  135.4 8.5 %collective-permute-start.17 = (bf16[576,256]{1,0:T(8,128)(2,1)S(1)}, bf16[576,256]{1,0:T(8,128)(2,1)}, u32[]{:S(2)}, u32[]{:S(2)}) collective-permute-start(bf16[576,256]{1,0:T(8,128)(2,1)S(1)} %collective-permute-done.15.refs_0_), channel_id=1, source_target_pairs={{0,1},{1,0},{2,3},{3,2},{4,5},{5,4},{6,7},{7,6},{8,9},{9,8},{10,11... | collective-permute-start | bytes 884744 | tf_op jit(solution)/shard_map/ppermute | solution.py:204
  140.9 3.0 %collective-permute-start.18 = (bf16[576,256]{1,0:T(8,128)(2,1)}, bf16[576,256]{1,0:T(8,128)(2,1)}, u32[]{:S(2)}, u32[]{:S(2)}) collective-permute-start(bf16[576,256]{1,0:T(8,128)(2,1)} %collective-permute-done.16.refs_1_), channel_id=1, source_target_pairs={{0,1},{1,0},{2,3},{3,2},{4,5},{5,4},{6,7},{7,6},{8,9},{9,8},{10,11... | collective-permute-start | bytes 884744 | tf_op jit(solution)/shard_map/ppermute | solution.py:204
  140.9 1.2 copy-start.7
  142.1 1.7 copy-start.14
  142.9 0.9 copy-start.9
  143.8 1.0 copy-start.12
  144.9 1.0 copy-start.16
  150.1 7.6 %copy-start.10 = (bf16[128,3584]{1,0:T(8,128)(2,1)S(1)}, bf16[128,3584]{1,0:T(8,128)(2,1)}, u32[]{:S(2)}) copy-start(bf16[128,3584]{1,0:T(8,128)(2,1)} %copy-done.9) | copy-start | bytes 2752516
  150.1 32.8 %all-to-all-start.3 = ((bf16[32,128,128]{2,1,0:T(8,128)(2,1)}), bf16[32,128,128]{2,1,0:T(8,128)(2,1)S(1)}, u32[]{:S(2)}, u32[]{:S(2)}) async-start(bf16[32,128,128]{2,1,0:T(8,128)(2,1)} %shard_map.119), calls=%async_computation.3 | async-start | bytes 2097152 | tf_op jit(solution)/shard_map/all_to_all | solution.py:220
  157.7 25.2 %collective-permute-start.19 = (bf16[128,3584]{1,0:T(8,128)(2,1)S(1)}, bf16[128,3584]{1,0:T(8,128)(2,1)S(1)}, u32[]{:S(2)}, u32[]{:S(2)}) collective-permute-start(bf16[128,3584]{1,0:T(8,128)(2,1)S(1)} %copy-done.10), channel_id=1, source_target_pairs={{0,32},{32,64},{64,96},{96,128},{128,160},{160,192},{192,224},{224... | collective-permute-start | bytes 2752520 | tf_op jit(solution)/shard_map/ppermute | solution.py:209
  (6 other events, 4.3 us)

commit v4 on v3

--- a/solution.py
+++ b/solution.py
@@ -11,6 +11,7 @@
 CHIPS = EP // 2
 MAIN = 16
 LAST = 2
+SPARE = 2
 EPSILON = 1e-06
 F32 = jnp.float32
 BF16 = jnp.bfloat16
@@ -111,28 +112,26 @@
     )(own, other, gate_cols, up_cols)
 
 
-def down_kernel(core_ref, *refs):
-    hidden_refs, down_refs, back_ref = refs[:ES], refs[ES : 2 * ES], refs[2 * ES]
+def down_kernel(core_ref, mine_ref, theirs_ref, down_ref, other_down_ref, back_ref):
     count = CHIPS * (MAIN + LAST)
-    tiles = down_refs[0].shape[1] // 128
+    wide = back_ref.shape[1] // MAIN * 128 - SPARE * 128
+    tiles = wide // 128
     core = core_ref[0]
+    columns = pl.ds(pl.multiple_of(core * wide, 128), wide)
+    shape = (CHIPS * SPARE * MAIN, CHIPS * LAST)
+    row = iota(shape, 0)
     for half in range(2):
-        total = jnp.zeros((count, tiles * 128), F32)
-        for r in range(ES):
-            place = half if r < 2 else 1 - half
-            total = total + dot(
-                hidden_refs[r][place * count : (place + 1) * count, :], down_refs[r][...]
-            )
+        here, there = half * count, (1 - half) * count
+        total = dot(mine_ref[here : here + count, :], down_ref[:, columns])
+        total = total + dot(theirs_ref[there : there + count, :], other_down_ref[:, columns])
         total = total.astype(BF16)
         target = core if half == 0 else 1 - core
-        last = jnp.zeros((CHIPS * MAIN, 128), F32)
-        shape = (CHIPS * MAIN, CHIPS * LAST)
-        row = iota(shape, 0)
+        last = jnp.zeros((CHIPS * SPARE * MAIN, 128), F32)
         for t in range(tiles):
             lanes = slice(t * 128, (t + 1) * 128)
-            inside = row % MAIN - t * LAST
+            inside = row % (SPARE * MAIN) - t * LAST
             pick = (inside >= 0) & (inside < LAST)
-            pick = pick & (iota(shape, 1) == (row // MAIN) * LAST + inside)
+            pick = pick & (iota(shape, 1) == (row // (SPARE * MAIN)) * LAST + inside)
             last = last + dot(pick.astype(BF16), total[CHIPS * MAIN :, lanes])
             for chip in range(CHIPS):
                 back_ref[2 * chip + target, t * MAIN : (t + 1) * MAIN, :] = total[
@@ -140,50 +139,66 @@
                 ]
         last = last.astype(BF16)
         for chip in range(CHIPS):
-            back_ref[2 * chip + target, tiles * MAIN :, :] = last[chip * MAIN : (chip + 1) * MAIN]
-
-
-def down_product(core, hidden, down):
-    rows, width = hidden[0].shape
-    columns = down[0].shape[1]
+            back_ref[2 * chip + target, tiles * MAIN :, :] = last[
+                chip * SPARE * MAIN : (chip + 1) * SPARE * MAIN
+            ]
+
+
+def down_product(core, mine, theirs, down, other_down):
+    rows, width = mine.shape
+    columns = down.shape[1] // 2
     tiles = columns // 128
     return pl.pallas_call(
         down_kernel,
-        out_shape=jax.ShapeDtypeStruct((EP, (tiles + 1) * MAIN, 128), BF16),
+        out_shape=jax.ShapeDtypeStruct((EP, (tiles + SPARE) * MAIN, 128), BF16),
         in_specs=[pl.BlockSpec(memory_space=pltpu.SMEM)]
-        + [pl.BlockSpec(memory_space=pltpu.VMEM)] * (2 * ES),
-        compiler_params=pltpu.CompilerParams(vmem_limit_bytes=VMEM_LIMIT),
-        cost_estimate=pl.CostEstimate(
-            flops=2 * ES * rows * width * columns,
-            bytes_accessed=2 * (ES * (rows + columns) * width + rows * columns),
+        + [pl.BlockSpec(memory_space=pltpu.VMEM)] * 4,
+        compiler_params=pltpu.CompilerParams(vmem_limit_bytes=VMEM_LIMIT),
+        cost_estimate=pl.CostEstimate(
+            flops=4 * rows * width * columns,
+            bytes_accessed=2 * (2 * (rows + 2 * columns) * width + rows * columns),
             transcendentals=0,
         ),
-    )(core, *hidden, *down)
+    )(core, mine, theirs, down, other_down)
 
 
 def finish_kernel(current_ref, back_ref, ids_ref, scores_ref, out_ref):
     tokens, features = current_ref.shape
-    quarter = features // ES
-    tiles = quarter // 128
+    tiles = features // 256
     ids_row = ids_ref[...]
     ids_column = to_column(ids_row)
     score = to_column(scores_ref[...])
     earlier = (ids_column == ids_row) & (iota((tokens, tokens), 1) < iota((tokens, tokens), 0))
     slot = jnp.sum(earlier.astype(jnp.int32), axis=1, keepdims=True)
-    main_place = ids_column * MAIN + slot
-    last_place = (EXPERTS + ids_column) * MAIN + slot - MAIN
     lane = iota((tokens, 2 * EXPERTS * MAIN), 1)
+    pick_main = (lane // (2 * MAIN) == ids_column) & (lane % MAIN == slot)
+    pick_main = pick_main.astype(BF16)
+    lane = iota((tokens, 2 * EXPERTS * SPARE * MAIN), 1)
+    in_expert = lane // (2 * SPARE * MAIN) == ids_column
+    in_expert = in_expert & (slot >= MAIN)
+    in_block = lane % (SPARE * MAIN)
+
+    def rows(first, count):
+        sides = [
+            jnp.concatenate(
+                [back_ref[2 * source + core, first : first + count, :] for source in range(CHIPS)],
+                axis=0,
+            )
+            for core in range(2)
+        ]
+        return jnp.concatenate(sides, axis=1)
+
+    last = rows(tiles * MAIN, SPARE * MAIN)
     for t in range(tiles):
-        place = jnp.where(slot < MAIN, main_place, last_place + t * LAST)
-        pick = (lane == place).astype(BF16)
-        for q in range(ES):
-            blocks = [
-                back_ref[expert * ES + q, t * MAIN : (t + 1) * MAIN, :] for expert in range(EXPERTS)
-            ]
-            blocks += [back_ref[expert * ES + q, tiles * MAIN :, :] for expert in range(EXPERTS)]
-            moe = dot(pick, jnp.concatenate(blocks, axis=0)) * score
-            columns = slice(q * quarter + t * 128, q * quarter + (t + 1) * 128)
-            out_ref[:, columns] = (current_ref[:, columns].astype(F32) + moe).astype(BF16)
+        pick_last = in_expert & (in_block == t * LAST + slot - MAIN)
+        moe = dot(pick_main, rows(t * MAIN, MAIN)) + dot(pick_last.astype(BF16), last)
+        moe = moe * score
+        for core in range(2):
+            start = core * (features // 2) + t * 128
+            columns = slice(start, start + 128)
+            out_ref[:, columns] = (
+                current_ref[:, columns].astype(F32) + moe[:, core * 128 : (core + 1) * 128]
+            ).astype(BF16)
 
 
 def finish(current, back, ids_row, scores_row):
@@ -194,14 +209,14 @@
         compiler_params=pltpu.CompilerParams(vmem_limit_bytes=VMEM_LIMIT),
         cost_estimate=pl.CostEstimate(
             flops=4 * tokens * EXPERTS * MAIN * features,
-            bytes_accessed=6 * tokens * features,
+            bytes_accessed=8 * tokens * features,
             transcendentals=0,
         ),
     )(current, back, ids_row, scores_row)
 
 
-def from_partner(value, offset):
-    return lax.ppermute(value, "ep", [(i, i ^ offset) for i in range(EP)])
+def swap_cores(value):
+    return lax.ppermute(value, "ep", [(i, i ^ 1) for i in range(EP)])
 
 
 def from_behind(value, steps):
@@ -224,50 +239,38 @@
     flight_a, flight_b, routes_a, routes_b, scores_a, scores_b, norm_gain, w_gate, w_up, w_down
 ):
     tokens = flight_a.shape[1]
-    quarter = flight_a.shape[2] // ES
-    index = lax.axis_index("ep")
-    core = (index % 2).astype(jnp.int32)[None]
+    core = (lax.axis_index("ep") % 2).astype(jnp.int32)[None]
     current_a, current_b = flight_a[0], flight_b[0]
     ids_a, ids_b = routes_a.reshape(1, tokens), routes_b.reshape(1, tokens)
     marks_a, marks_b = scores_a.reshape(1, tokens), scores_b.reshape(1, tokens)
-    gate_cols, up_cols, down_rows = w_gate[0], w_up[0], w_down[0]
-
-    down_a = []
-    for offset in (0, 2, 1, 3):
-        start = ((index ^ offset) % ES) * quarter
-        piece = lax.dynamic_slice_in_dim(down_rows, start, quarter, 1)
-        down_a.append(from_partner(piece, offset) if offset else piece)
+    gate_cols, up_cols, down = w_gate[0], w_up[0], w_down[0]
 
     own_a = dispatch(prepare(current_a, ids_a, norm_gain))
     send_b = prepare(current_b, ids_b, norm_gain)
-
-    moved = [from_behind(value, -1) for value in (current_b, ids_b, marks_b, down_a[0])]
-    own_a, send_b, down_a, moved = lax.optimization_barrier((own_a, send_b, down_a, moved))
+    middle = down.shape[0] // 2
+    upper = from_behind(down[:middle], -1)
+    own_a, send_b, upper = lax.optimization_barrier((own_a, send_b, upper))
     own_b = dispatch(send_b)
-    down_b = [moved[3]] + [from_behind(piece, -1) for piece in down_a[1:]]
-
-    hidden_a = hidden_units(own_a, from_partner(own_a, 1), gate_cols, up_cols)
-    across_a = from_partner(hidden_a, 2)
-    all_a = [hidden_a, across_a, from_partner(hidden_a, 1), from_partner(across_a, 1)]
-    back_a = down_product(core, all_a, down_a)
-
-    own_b, back_a, down_b = lax.optimization_barrier((own_b, back_a, down_b))
+
+    lower = from_behind(down[middle:], -1)
+    hidden_a = hidden_units(own_a, swap_cores(own_a), gate_cols, up_cols)
+    hidden_a, lower = lax.optimization_barrier((hidden_a, lower))
+    back_a = down_product(core, hidden_a, swap_cores(hidden_a), down, swap_cores(down))
+    moved_down = jnp.concatenate([upper, lower], axis=0)
+    own_b, back_a, moved_down = lax.optimization_barrier((own_b, back_a, moved_down))
+
     returned_a = give_back(back_a)
-    hidden_b = hidden_units(own_b, from_partner(own_b, 1), gate_cols, up_cols)
-    here_b = from_behind(hidden_b, -1)
-    sections = lax.axis_size("section")
-    pairs = [
-        (s * EP + i, ((s - 1) % sections) * EP + (i ^ 2)) for s in range(sections) for i in range(EP)
+    hidden_b = hidden_units(own_b, swap_cores(own_b), gate_cols, up_cols)
+    hidden_b = from_behind(hidden_b, -1)
+    back_b = down_product(core, hidden_b, swap_cores(hidden_b), moved_down, swap_cores(moved_down))
+    moved_b, moved_ids, moved_marks = [
+        from_behind(value, -1) for value in (current_b, ids_b, marks_b)
     ]
-    across_b = lax.ppermute(hidden_b, ("section", "ep"), pairs)
-    all_b = [here_b, across_b, from_partner(here_b, 1), from_partner(across_b, 1)]
-    back_b = down_product(core, all_b, down_b)
-
+
+    marks_a, back_b = lax.optimization_barrier((marks_a, back_b))
+    returned_b = give_back(back_b)
     updated_a = finish(current_a, returned_a, ids_a, marks_a)
-    updated_a, back_b = lax.optimization_barrier((updated_a, back_b))
-    returned_b = give_back(back_b)
     updated_a = from_behind(updated_a, 1)
-    moved_b, moved_ids, moved_marks = moved[:3]
     updated_b = finish(moved_b, returned_b, moved_ids, moved_marks)
     return (updated_a[None], updated_b[None])
 

time: 188 us -> 158 us (0.84)
  waiting for transfers between devices: 82.6 us -> 60.8 us
  local copies, waits for them, and re-layouts: 24.6 us -> 13.5 us
  starting transfers between devices: 55 us -> 49.5 us
  Pallas kernels: 23.8 us -> 27.6 us
  other arithmetic: 0 us -> 2.58 us
    ppermute x11 -> x6, waiting for transfers between devices: 31.4 us -> 1.59 us  [swap_cores(): return lax.ppermute(value, 'ep', [(i, i ^ 1) for i in range(EP)])]
    unnamed x61 -> x37, local copies, waits for them, and re-layouts: 23 us -> 11 us
    ppermute x9 -> x7, waiting for transfers between devices: 51.1 us -> 54.8 us  [from_behind(): lax.ppermute(value, 'section', [(i, (i + steps) % count) for i in range(c...]
    all_to_all x2, waiting for transfers between devices: 0.01 us -> 3.31 us  [give_back(): return lax.all_to_all(back, 'ep', split_axis=0, concat_axis=0, tiled=True)]
    concatenate x0 -> x1, other arithmetic: none -> 2.58 us  [on_device(): moved_down = jnp.concatenate([upper, lower], axis=0)]
    slice x0 -> x1, local copies, waits for them, and re-layouts: none -> 2.57 us  [on_device(): lower = from_behind(down[middle:], -1)]
    ppermute x9 -> x7, starting transfers between devices: 23.4 us -> 21 us  [from_behind(): lax.ppermute(value, 'section', [(i, (i + steps) % count) for i in range(c...]
  transfers between devices with their start and end apart: 24 -> 17, of which waited for: 9 -> 8; matrix products, arithmetic and copies ran while one was open for 1% -> 3% of each run, Pallas kernels for 8% -> 15%
where the time goes in v4:
time: 158 us; the launch traced here: 155 us
  waiting for transfers between devices  60.8 us (38%)
  starting transfers between devices  49.5 us (31%)
  Pallas kernels  27.6 us (17%)
  local copies, waits for them, and re-layouts  13.5 us (9%)
  other arithmetic  2.58 us (2%)
    ppermute x7, waiting for transfers between devices, from_behind(): lax.ppermute(value, 'section', [(i, (i + steps) % count) for i in range(c...  54.8 us
    ppermute x7, starting transfers between devices, from_behind(): lax.ppermute(value, 'section', [(i, (i + steps) % count) for i in range(c...  21 us
    all_to_all x2, starting transfers between devices, give_back(): return lax.all_to_all(back, 'ep', split_axis=0, concat_axis=0, tiled=True)  14 us
    all_to_all x2, starting transfers between devices, dispatch(): lax.all_to_all(send, 'ep', split_axis=0, concat_axis=0, axis_index_groups...  13.5 us
    unnamed x37, local copies, waits for them, and re-layouts  11 us
    pallas_call x2, Pallas kernels, hidden_units(): pl.pallas_call(hidden_kernel, out_shape=jax.ShapeDtypeStruct((count, widt...  9.98 us
    pallas_call x2, Pallas kernels, down_product(): pl.pallas_call(down_kernel, out_shape=jax.ShapeDtypeStruct((EP, (tiles +...  9.84 us
    pallas_call x2, Pallas kernels, finish(): pl.pallas_call(finish_kernel, out_shape=jax.ShapeDtypeStruct((tokens, fea...  4.77 us
  transfers between devices with their start and end apart: 17, of which 8 were waited for; matrix products, arithmetic and copies ran while one was open for 3% of the time, Pallas kernels for 15%

profile of v4, /device:TPU:8, one launch (start us, length us, event | category | flops | bytes accessed | tf_op | source)
XLA Modules:
  0.0 154.8 jit_solution(8941169532746197369)
XLA Ops:
  0.6 0.0 copy-start.7
  0.6 1.2 copy-done.7
  1.8 0.7 copy-done.11
  2.5 0.7 copy-done.13
  3.2 0.9 shard_map.113
  4.0 1.3 copy-done
  5.4 7.4 %all-to-all-start = ((bf16[16,72,896]{2,1,0:T(8,128)(2,1)}), bf16[16,72,896]{2,1,0:T(8,128)(2,1)S(1)}, u32[]{:S(2)}, u32[]{:S(2)}) async-start(bf16[16,72,896]{2,1,0:T(8,128)(2,1)} %copy-done), calls=%async_computation | async-start | bytes 4128768 | tf_op jit(solution)/shard_map/all_to_all | solution.py:229
  12.8 0.0 copy-start.12
  12.8 0.0 copy-start.16
  12.8 2.6 %slice_bitcast_fusion = (bf16[128,3584]{1,0:T(8,128)(2,1)}, bf16[128,3584]{1,0:T(8,128)(2,1)S(1)}) fusion(bf16[1,256,3584]{2,1,0:T(8,128)(2,1)} %param.19), kind=kLoop, calls=%fused_computation.1 | loop fusion | bytes 3670016 | tf_op jit(solution)/shard_map/slice | solution.py:255
  15.4 5.9 %collective-permute-start = (bf16[128,3584]{1,0:T(8,128)(2,1)S(1)}, bf16[128,3584]{1,0:T(8,128)(2,1)S(1)}, u32[]{:S(2)}, u32[]{:S(2)}) collective-permute-start(bf16[128,3584]{1,0:T(8,128)(2,1)S(1)} %get-tuple-element.23), channel_id=1, source_target_pairs={{0,224},{32,0},{64,32},{96,64},{128,96},{160,128},{192,160},{224,1... | collective-permute-start | bytes 2752520 | tf_op jit(solution)/shard_map/ppermute | solution.py:224
  21.2 2.2 %shard_map.114 = bf16[16,72,896]{2,1,0:T(8,128)(2,1)} custom-call(bf16[128,3584]{1,0:T(8,128)(2,1)S(1)} %bitcast.24, s32[1,128]{1,0:T(1,128)S(1)} %bitcast.29, f32[1,3584]{1,0:T(1,128)S(1)} %copy-done.12), custom_call_target="tpu_custom_call" | custom-call | flops 176160768 | bytes 3670016 | tf_op jit(solution)/shard_map/pallas_call | solution.py:71
  23.4 16.9 %collective-permute-done = bf16[128,3584]{1,0:T(8,128)(2,1)S(1)} collective-permute-done((bf16[128,3584]{1,0:T(8,128)(2,1)S(1)}, bf16[128,3584]{1,0:T(8,128)(2,1)S(1)}, u32[]{:S(2)}, u32[]{:S(2)}) %collective-permute-start) | collective-permute-done | bytes 917536 | tf_op jit(solution)/shard_map/ppermute | solution.py:224
  40.3 1.1 all-to-all-done.own_ref
  41.4 6.1 %all-to-all-start.1 = ((bf16[16,72,896]{2,1,0:T(8,128)(2,1)}), bf16[16,72,896]{2,1,0:T(8,128)(2,1)}, u32[]{:S(2)}, u32[]{:S(2)}) async-start(bf16[16,72,896]{2,1,0:T(8,128)(2,1)} %shard_map.114), calls=%async_computation.1 | async-start | bytes 4128768 | tf_op jit(solution)/shard_map/all_to_all | solution.py:229
  47.5 0.0 collective-permute-start.4
  47.5 5.6 %collective-permute-start.2 = (bf16[128,3584]{1,0:T(8,128)(2,1)}, bf16[128,3584]{1,0:T(8,128)(2,1)}, u32[]{:S(2)}, u32[]{:S(2)}) collective-permute-start(bf16[128,3584]{1,0:T(8,128)(2,1)} %get-tuple-element.22), channel_id=1, source_target_pairs={{0,224},{32,0},{64,32},{96,64},{128,96},{160,128},{192,160},{224,1... | collective-permute-start | bytes 2752520 | tf_op jit(solution)/shard_map/ppermute | solution.py:224
  53.1 1.5 copy-done.3
  54.6 1.5 copy-done.5
  56.1 4.7 %shard_map.115.mine_ref = bf16[576,256]{1,0:T(8,128)(2,1)S(1)} custom-call(bf16[16,72,896]{2,1,0:T(8,128)(2,1)S(1)} %all-to-all-done.own_ref, bf16[16,72,896]{2,1,0:T(8,128)(2,1)} %collective-permute-done.1.other_ref, bf16[3584,256]{1,0:T(8,128)(2,1)S(1)} %bitcast.18, bf16[3584,256]{1,0:T(8,128)(2,1)S(1)} %bitcast.20), custom_call_target="tpu_custom_call" | custom-call | flops 2113929216 | bytes 7798784 | tf_op jit(solution)/shard_map/pallas_call | solution.py:103
  60.8 0.0 copy-start.1
  60.8 12.7 %collective-permute-done.2 = bf16[128,3584]{1,0:T(8,128)(2,1)} collective-permute-done((bf16[128,3584]{1,0:T(8,128)(2,1)}, bf16[128,3584]{1,0:T(8,128)(2,1)}, u32[]{:S(2)}, u32[]{:S(2)}) %collective-permute-start.2) | collective-permute-done | bytes 917536 | tf_op jit(solution)/shard_map/ppermute | solution.py:224
  73.5 2.6 %pad_maximum_fusion.down_ref = bf16[256,3584]{1,0:T(8,128)(2,1)} fusion(bf16[128,3584]{1,0:T(8,128)(2,1)} %collective-permute-done.2, bf16[128,3584]{1,0:T(8,128)(2,1)S(1)} %collective-permute-done), kind=kLoop, calls=%fused_computation | loop fusion | flops 3670016 | bytes 3670016 | tf_op jit(solution)/shard_map/concatenate | solution.py:259
  76.0 0.0 collective-permute-done.4.other_down_ref
  76.1 5.7 %shard_map.116 = bf16[32,256,128]{2,1,0:T(8,128)(2,1)} custom-call(s32[1]{0:T(128)} %bitcast.5.core_ref, bf16[576,256]{1,0:T(8,128)(2,1)S(1)} %shard_map.115.mine_ref, bf16[576,256]{1,0:T(8,128)(2,1)S(1)} %collective-permute-done.3.theirs_ref, bf16[256,3584]{1,0:T(8,128)(2,1)S(1)} %bitcast.17, bf16[256,3584]{1,0:T(8,128)(2,1)} %collective-permute-done.4.other_down_ref), custom_call_target="tpu_custom_call" | custom-call | flops 1056964608 | bytes 6324224 | tf_op jit(solution)/shard_map/pallas_call | solution.py:151
  81.7 0.5 collective-permute-start.5
  82.2 7.4 %all-to-all-start.2 = ((bf16[32,256,128]{2,1,0:T(8,128)(2,1)}), bf16[32,256,128]{2,1,0:T(8,128)(2,1)S(1)}, u32[]{:S(2)}, u32[]{:S(2)}) async-start(bf16[32,256,128]{2,1,0:T(8,128)(2,1)} %shard_map.116), calls=%async_computation.2 | async-start | bytes 4194304 | tf_op jit(solution)/shard_map/all_to_all | solution.py:235
  89.7 0.4 collective-permute-start.8
  90.1 1.6 %copy-done.4 = bf16[1,3584,256]{2,1,0:T(8,128)(2,1)S(1)} copy-done((bf16[1,3584,256]{2,1,0:T(8,128)(2,1)S(1)}, bf16[1,3584,256]{2,1,0:T(8,128)(2,1)}, u32[]{:S(2)}) %copy-start.4) | copy-done | bytes 1835032
  91.7 1.5 copy-done.6
  93.2 5.3 %shard_map.117 = bf16[576,256]{1,0:T(8,128)(2,1)S(1)} custom-call(bf16[16,72,896]{2,1,0:T(8,128)(2,1)} %all-to-all-done.1.own_ref, bf16[16,72,896]{2,1,0:T(8,128)(2,1)} %collective-permute-done.5.other_ref, bf16[3584,256]{1,0:T(8,128)(2,1)S(1)} %bitcast.19, bf16[3584,256]{1,0:T(8,128)(2,1)S(1)} %bitcast.21), custom_call_target="tpu_custom_call" | custom-call | flops 2113929216 | bytes 7798784 | tf_op jit(solution)/shard_map/pallas_call | solution.py:103
  98.5 3.8 %collective-permute-start.6 = (bf16[576,256]{1,0:T(8,128)(2,1)S(1)}, bf16[576,256]{1,0:T(8,128)(2,1)S(1)}, u32[]{:S(2)}, u32[]{:S(2)}) collective-permute-start(bf16[576,256]{1,0:T(8,128)(2,1)S(1)} %shard_map.117), channel_id=1, source_target_pairs={{0,224},{32,0},{64,32},{96,64},{128,96},{160,128},{192,160},{224,1... | collective-permute-start | bytes 884744 | tf_op jit(solution)/shard_map/ppermute | solution.py:224
  102.3 6.7 %collective-permute-done.6.mine_ref = bf16[576,256]{1,0:T(8,128)(2,1)S(1)} collective-permute-done((bf16[576,256]{1,0:T(8,128)(2,1)S(1)}, bf16[576,256]{1,0:T(8,128)(2,1)S(1)}, u32[]{:S(2)}, u32[]{:S(2)}) %collective-permute-start.6) | collective-permute-done | bytes 294944 | tf_op jit(solution)/shard_map/ppermute | solution.py:224
  109.0 1.6 %collective-permute-done.7.theirs_ref = bf16[576,256]{1,0:T(8,128)(2,1)S(1)} collective-permute-done((bf16[576,256]{1,0:T(8,128)(2,1)S(1)}, bf16[576,256]{1,0:T(8,128)(2,1)S(1)}, u32[]{:S(2)}, u32[]{:S(2)}) %collective-permute-start.7) | collective-permute-done | bytes 294944 | tf_op jit(solution)/shard_map/ppermute | solution.py:219
  110.6 4.2 %shard_map.118 = bf16[32,256,128]{2,1,0:T(8,128)(2,1)} custom-call(s32[1]{0:T(128)} %bitcast.5.core_ref, bf16[576,256]{1,0:T(8,128)(2,1)S(1)} %collective-permute-done.6.mine_ref, bf16[576,256]{1,0:T(8,128)(2,1)S(1)} %collective-permute-done.7.theirs_ref, bf16[256,3584]{1,0:T(8,128)(2,1)S(1)} %copy-done.2, ...), custom_call_target="tpu_custom_call" | custom-call | flops 1056964608 | bytes 6324224 | tf_op jit(solution)/shard_map/pallas_call | solution.py:151
  114.7 1.9 %all-to-all-done.2.back_ref = bf16[32,256,128]{2,1,0:T(8,128)(2,1)S(1)} async-done(((bf16[32,256,128]{2,1,0:T(8,128)(2,1)}), bf16[32,256,128]{2,1,0:T(8,128)(2,1)S(1)}, u32[]{:S(2)}, u32[]{:S(2)}) %all-to-all-start.2) | async-done | bytes 2097184 | tf_op jit(solution)/shard_map/all_to_all | solution.py:235
  116.6 6.6 %all-to-all-start.3 = ((bf16[32,256,128]{2,1,0:T(8,128)(2,1)}), bf16[32,256,128]{2,1,0:T(8,128)(2,1)}, u32[]{:S(2)}, u32[]{:S(2)}) async-start(bf16[32,256,128]{2,1,0:T(8,128)(2,1)} %shard_map.118), calls=%async_computation.3 | async-start | bytes 4194304 | tf_op jit(solution)/shard_map/all_to_all | solution.py:235
  123.2 0.0 copy-start.10
  123.2 0.0 copy-start.17
  123.2 1.2 shard_map.119
  124.4 0.1 collective-permute-start.9
  124.5 3.8 %collective-permute-start.10 = (bf16[128,3584]{1,0:T(8,128)(2,1)S(1)}, bf16[128,3584]{1,0:T(8,128)(2,1)S(1)}, u32[]{:S(2)}, u32[]{:S(2)}) collective-permute-start(bf16[128,3584]{1,0:T(8,128)(2,1)S(1)} %bitcast.25), channel_id=1, source_target_pairs={{0,224},{32,0},{64,32},{96,64},{128,96},{160,128},{192,160},{224,1... | collective-permute-start | bytes 2752520 | tf_op jit(solution)/shard_map/ppermute | solution.py:224
  128.3 1.9 %collective-permute-start.11 = (s32[1,128]{1,0:T(1,128)S(1)}, s32[1,128]{1,0:T(1,128)S(1)}, u32[]{:S(2)}, u32[]{:S(2)}) collective-permute-start(s32[1,128]{1,0:T(1,128)S(1)} %bitcast.30), channel_id=1, source_target_pairs={{0,224},{32,0},{64,32},{96,64},{128,96},{160,128},{192,160},{224,1... | collective-permute-start | bytes 1544 | tf_op jit(solution)/shard_map/ppermute | solution.py:224
  130.2 0.0 collective-permute-start.12
  130.3 18.6 %collective-permute-done.9 = bf16[128,3584]{1,0:T(8,128)(2,1)S(1)} collective-permute-done((bf16[128,3584]{1,0:T(8,128)(2,1)S(1)}, bf16[128,3584]{1,0:T(8,128)(2,1)S(1)}, u32[]{:S(2)}, u32[]{:S(2)}) %collective-permute-start.9) | collective-permute-done | bytes 917536 | tf_op jit(solution)/shard_map/ppermute | solution.py:224
  148.8 1.5 all-to-all-done.3.back_ref
  150.3 3.6 %shard_map.120 = bf16[128,3584]{1,0:T(8,128)(2,1)} custom-call(bf16[128,3584]{1,0:T(8,128)(2,1)S(1)} %collective-permute-done.10.current_ref, bf16[32,256,128]{2,1,0:T(8,128)(2,1)} %all-to-all-done.3.back_ref, s32[1,128]{1,0:T(1,128)S(1)} %collective-permute-done.11.ids_ref, f32[1,128]{1,0:T(1,128)S(1)} %collective-permute-done.12.scores_ref), custom_call_target="tpu_custom_call" | custom-call | flops 234881024 | bytes 3670016 | tf_op jit(solution)/shard_map/pallas_call | solution.py:206
  153.9 0.9 copy.13
  (33 shorter events, 0.1 us)
Async XLA Ops:
  0.6 1.2 copy-start.7
  1.8 0.7 copy-start.11
  2.5 0.7 copy-start.13
  4.0 1.3 copy-start
  5.4 36.0 %all-to-all-start = ((bf16[16,72,896]{2,1,0:T(8,128)(2,1)}), bf16[16,72,896]{2,1,0:T(8,128)(2,1)S(1)}, u32[]{:S(2)}, u32[]{:S(2)}) async-start(bf16[16,72,896]{2,1,0:T(8,128)(2,1)} %copy-done), calls=%async_computation | async-start | bytes 4128768 | tf_op jit(solution)/shard_map/all_to_all | solution.py:229
  12.8 8.5 %copy-start.9 = (bf16[1,128,3584]{2,1,0:T(8,128)(2,1)S(1)}, bf16[1,128,3584]{2,1,0:T(8,128)(2,1)}, u32[]{:S(2)}) copy-start(bf16[1,128,3584]{2,1,0:T(8,128)(2,1)} %param.11) | copy-start | bytes 2752516
  12.8 8.5 %copy-start.12 = (f32[1,3584]{1,0:T(1,128)S(1)}, f32[1,3584]{1,0:T(1,128)}, u32[]{:S(2)}) copy-start(f32[1,3584]{1,0:T(1,128)} %gain_ref.3) | copy-start | bytes 43012
  12.8 8.5 %copy-start.16 = (s32[1,1,128,1]{2,3,1,0:T(1,128)S(1)}, s32[1,1,128,1]{2,3,1,0:T(1,128)}, u32[]{:S(2)}) copy-start(s32[1,1,128,1]{2,3,1,0:T(1,128)} %param.13) | copy-start | bytes 1540
  15.4 24.9 %collective-permute-start = (bf16[128,3584]{1,0:T(8,128)(2,1)S(1)}, bf16[128,3584]{1,0:T(8,128)(2,1)S(1)}, u32[]{:S(2)}, u32[]{:S(2)}) collective-permute-start(bf16[128,3584]{1,0:T(8,128)(2,1)S(1)} %get-tuple-element.23), channel_id=1, source_target_pairs={{0,224},{32,0},{64,32},{96,64},{128,96},{160,128},{192,160},{224,1... | collective-permute-start | bytes 2752520 | tf_op jit(solution)/shard_map/ppermute | solution.py:224
  41.4 11.7 %collective-permute-start.1 = (bf16[16,72,896]{2,1,0:T(8,128)(2,1)S(1)}, bf16[16,72,896]{2,1,0:T(8,128)(2,1)}, u32[]{:S(2)}, u32[]{:S(2)}) collective-permute-start(bf16[16,72,896]{2,1,0:T(8,128)(2,1)S(1)} %all-to-all-done.own_ref), channel_id=1, source_target_pairs={{0,1},{1,0},{2,3},{3,2},{4,5},{5,4},{6,7},{7,6},{8,9},{9,8},{10,11... | collective-permute-start | bytes 6193160 | tf_op jit(solution)/shard_map/ppermute | solution.py:219
  41.4 40.4 %all-to-all-start.1 = ((bf16[16,72,896]{2,1,0:T(8,128)(2,1)}), bf16[16,72,896]{2,1,0:T(8,128)(2,1)}, u32[]{:S(2)}, u32[]{:S(2)}) async-start(bf16[16,72,896]{2,1,0:T(8,128)(2,1)} %shard_map.114), calls=%async_computation.1 | async-start | bytes 4128768 | tf_op jit(solution)/shard_map/all_to_all | solution.py:229
  47.5 28.5 %collective-permute-start.4 = (bf16[256,3584]{1,0:T(8,128)(2,1)}, bf16[256,3584]{1,0:T(8,128)(2,1)}, u32[]{:S(2)}, u32[]{:S(2)}) collective-permute-start(bf16[256,3584]{1,0:T(8,128)(2,1)} %bitcast.16), channel_id=1, source_target_pairs={{0,1},{1,0},{2,3},{3,2},{4,5},{5,4},{6,7},{7,6},{8,9},{9,8},{10,11... | collective-permute-start | bytes 5505032 | tf_op jit(solution)/shard_map/ppermute | solution.py:219
  47.5 25.9 %collective-permute-start.2 = (bf16[128,3584]{1,0:T(8,128)(2,1)}, bf16[128,3584]{1,0:T(8,128)(2,1)}, u32[]{:S(2)}, u32[]{:S(2)}) collective-permute-start(bf16[128,3584]{1,0:T(8,128)(2,1)} %get-tuple-element.22), channel_id=1, source_target_pairs={{0,224},{32,0},{64,32},{96,64},{128,96},{160,128},{192,160},{224,1... | collective-permute-start | bytes 2752520 | tf_op jit(solution)/shard_map/ppermute | solution.py:224
  53.1 1.5 copy-start.3
  54.6 1.5 copy-start.5
  60.8 15.3 %copy-start.1 = (bf16[1,256,3584]{2,1,0:T(8,128)(2,1)S(1)}, bf16[1,256,3584]{2,1,0:T(8,128)(2,1)}, u32[]{:S(2)}) copy-start(bf16[1,256,3584]{2,1,0:T(8,128)(2,1)} %param.19) | copy-start | bytes 5505028
  73.5 2.6 %collective-permute-start.3 = (bf16[576,256]{1,0:T(8,128)(2,1)S(1)}, bf16[576,256]{1,0:T(8,128)(2,1)S(1)}, u32[]{:S(2)}, u32[]{:S(2)}) collective-permute-start(bf16[576,256]{1,0:T(8,128)(2,1)S(1)} %shard_map.115.mine_ref), channel_id=1, source_target_pairs={{0,1},{1,0},{2,3},{3,2},{4,5},{5,4},{6,7},{7,6},{8,9},{9,8},{10,11... | collective-permute-start | bytes 884744 | tf_op jit(solution)/shard_map/ppermute | solution.py:219
  81.7 8.3 %collective-permute-start.5 = (bf16[16,72,896]{2,1,0:T(8,128)(2,1)}, bf16[16,72,896]{2,1,0:T(8,128)(2,1)}, u32[]{:S(2)}, u32[]{:S(2)}) collective-permute-start(bf16[16,72,896]{2,1,0:T(8,128)(2,1)} %all-to-all-done.1.own_ref), channel_id=1, source_target_pairs={{0,1},{1,0},{2,3},{3,2},{4,5},{5,4},{6,7},{7,6},{8,9},{9,8},{10,11... | collective-permute-start | bytes 6193160 | tf_op jit(solution)/shard_map/ppermute | solution.py:219
  82.2 34.3 %all-to-all-start.2 = ((bf16[32,256,128]{2,1,0:T(8,128)(2,1)}), bf16[32,256,128]{2,1,0:T(8,128)(2,1)S(1)}, u32[]{:S(2)}, u32[]{:S(2)}) async-start(bf16[32,256,128]{2,1,0:T(8,128)(2,1)} %shard_map.116), calls=%async_computation.2 | async-start | bytes 4194304 | tf_op jit(solution)/shard_map/all_to_all | solution.py:235
  89.7 20.9 %copy-start.2 = (bf16[256,3584]{1,0:T(8,128)(2,1)S(1)}, bf16[256,3584]{1,0:T(8,128)(2,1)}, u32[]{:S(2)}) copy-start(bf16[256,3584]{1,0:T(8,128)(2,1)} %pad_maximum_fusion.down_ref) | copy-start | bytes 5505028
  89.7 19.3 %collective-permute-start.8 = (bf16[256,3584]{1,0:T(8,128)(2,1)}, bf16[256,3584]{1,0:T(8,128)(2,1)S(1)}, u32[]{:S(2)}, u32[]{:S(2)}) collective-permute-start(bf16[256,3584]{1,0:T(8,128)(2,1)} %pad_maximum_fusion.down_ref), channel_id=1, source_target_pairs={{0,1},{1,0},{2,3},{3,2},{4,5},{5,4},{6,7},{7,6},{8,9},{9,8},{10,11... | collective-permute-start | bytes 5505032 | tf_op jit(solution)/shard_map/ppermute | solution.py:219
  90.1 1.6 %copy-start.4 = (bf16[1,3584,256]{2,1,0:T(8,128)(2,1)S(1)}, bf16[1,3584,256]{2,1,0:T(8,128)(2,1)}, u32[]{:S(2)}) copy-start(bf16[1,3584,256]{2,1,0:T(8,128)(2,1)} %param.17) | copy-start | bytes 5505028
  91.7 1.5 copy-start.6
  98.5 10.4 %collective-permute-start.6 = (bf16[576,256]{1,0:T(8,128)(2,1)S(1)}, bf16[576,256]{1,0:T(8,128)(2,1)S(1)}, u32[]{:S(2)}, u32[]{:S(2)}) collective-permute-start(bf16[576,256]{1,0:T(8,128)(2,1)S(1)} %shard_map.117), channel_id=1, source_target_pairs={{0,224},{32,0},{64,32},{96,64},{128,96},{160,128},{192,160},{224,1... | collective-permute-start | bytes 884744 | tf_op jit(solution)/shard_map/ppermute | solution.py:224
  109.0 1.6 %collective-permute-start.7 = (bf16[576,256]{1,0:T(8,128)(2,1)S(1)}, bf16[576,256]{1,0:T(8,128)(2,1)S(1)}, u32[]{:S(2)}, u32[]{:S(2)}) collective-permute-start(bf16[576,256]{1,0:T(8,128)(2,1)S(1)} %collective-permute-done.6.mine_ref), channel_id=1, source_target_pairs={{0,1},{1,0},{2,3},{3,2},{4,5},{5,4},{6,7},{7,6},{8,9},{9,8},{10,11... | collective-permute-start | bytes 884744 | tf_op jit(solution)/shard_map/ppermute | solution.py:219
  114.7 8.5 %copy-start.8 = (bf16[1,128,3584]{2,1,0:T(8,128)(2,1)S(1)}, bf16[1,128,3584]{2,1,0:T(8,128)(2,1)}, u32[]{:S(2)}) copy-start(bf16[1,128,3584]{2,1,0:T(8,128)(2,1)} %param.10) | copy-start | bytes 2752516
  114.7 8.5 %copy-start.14 = (s32[1,1,128,1]{2,3,1,0:T(1,128)S(1)}, s32[1,1,128,1]{2,3,1,0:T(1,128)}, u32[]{:S(2)}) copy-start(s32[1,1,128,1]{2,3,1,0:T(1,128)} %param.12) | copy-start | bytes 1540
  114.7 8.5 %copy-start.15 = (f32[1,1,128,1]{2,3,1,0:T(1,128)S(1)}, f32[1,1,128,1]{2,3,1,0:T(1,128)}, u32[]{:S(2)}) copy-start(f32[1,1,128,1]{2,3,1,0:T(1,128)} %param.14) | copy-start | bytes 1540
  116.6 33.7 %all-to-all-start.3 = ((bf16[32,256,128]{2,1,0:T(8,128)(2,1)}), bf16[32,256,128]{2,1,0:T(8,128)(2,1)}, u32[]{:S(2)}, u32[]{:S(2)}) async-start(bf16[32,256,128]{2,1,0:T(8,128)(2,1)} %shard_map.118), calls=%async_computation.3 | async-start | bytes 4194304 | tf_op jit(solution)/shard_map/all_to_all | solution.py:235
  123.2 1.3 copy-start.10
  123.2 7.0 %copy-start.17 = (f32[1,1,128,1]{2,3,1,0:T(1,128)S(1)}, f32[1,1,128,1]{2,3,1,0:T(1,128)}, u32[]{:S(2)}) copy-start(f32[1,1,128,1]{2,3,1,0:T(1,128)} %param.15) | copy-start | bytes 1540
  124.4 24.4 %collective-permute-start.9 = (bf16[128,3584]{1,0:T(8,128)(2,1)S(1)}, bf16[128,3584]{1,0:T(8,128)(2,1)S(1)}, u32[]{:S(2)}, u32[]{:S(2)}) collective-permute-start(bf16[128,3584]{1,0:T(8,128)(2,1)S(1)} %shard_map.119), channel_id=1, source_target_pairs={{0,32},{32,64},{64,96},{96,128},{128,160},{160,192},{192,224},{224... | collective-permute-start | bytes 2752520 | tf_op jit(solution)/shard_map/ppermute | solution.py:224
  124.5 24.3 %collective-permute-start.10 = (bf16[128,3584]{1,0:T(8,128)(2,1)S(1)}, bf16[128,3584]{1,0:T(8,128)(2,1)S(1)}, u32[]{:S(2)}, u32[]{:S(2)}) collective-permute-start(bf16[128,3584]{1,0:T(8,128)(2,1)S(1)} %bitcast.25), channel_id=1, source_target_pairs={{0,224},{32,0},{64,32},{96,64},{128,96},{160,128},{192,160},{224,1... | collective-permute-start | bytes 2752520 | tf_op jit(solution)/shard_map/ppermute | solution.py:224
  128.3 20.6 %collective-permute-start.11 = (s32[1,128]{1,0:T(1,128)S(1)}, s32[1,128]{1,0:T(1,128)S(1)}, u32[]{:S(2)}, u32[]{:S(2)}) collective-permute-start(s32[1,128]{1,0:T(1,128)S(1)} %bitcast.30), channel_id=1, source_target_pairs={{0,224},{32,0},{64,32},{96,64},{128,96},{160,128},{192,160},{224,1... | collective-permute-start | bytes 1544 | tf_op jit(solution)/shard_map/ppermute | solution.py:224
  130.2 18.6 %collective-permute-start.12 = (f32[1,128]{1,0:T(1,128)S(1)}, f32[1,128]{1,0:T(1,128)S(1)}, u32[]{:S(2)}, u32[]{:S(2)}) collective-permute-start(f32[1,128]{1,0:T(1,128)S(1)} %bitcast.33), channel_id=1, source_target_pairs={{0,224},{32,0},{64,32},{96,64},{128,96},{160,128},{192,160},{224,1... | collective-permute-start | bytes 1544 | tf_op jit(solution)/shard_map/ppermute | solution.py:224

commit v5 on v4

v5 whole, which is shorter than its diff:
```python
import functools

import jax
import jax.numpy as jnp
from jax import lax
from jax.experimental import pallas as pl
from jax.experimental.pallas import tpu as pltpu
from jax.sharding import PartitionSpec as P

ES = 4
EXPERTS = 8
EP = ES * EXPERTS
CHIPS = EP // 2
MAIN = 16
LAST = 2
ORDER = (2, 10, 0, 14, 6, 5, 3, 8, 7, 11, 15, 1, 12, 13, 9, 4)
EPSILON = 1e-06
F32 = jnp.float32
BF16 = jnp.bfloat16
VMEM_LIMIT = 48 * 1024 * 1024


def iota(shape, axis):
    return lax.broadcasted_iota(jnp.int32, shape, axis)


def to_column(row):
    count = row.shape[1]
    eye = iota((count, count), 0) == iota((count, count), 1)
    return jnp.sum(jnp.where(eye, row, jnp.zeros_like(row)), axis=1, keepdims=True)


def dot(left, right):
    return jnp.dot(left, right, preferred_element_type=F32)


def prepare_kernel(current_ref, ids_ref, gain_ref, send_ref):
    tokens, features = current_ref.shape
    quarter = features // ES
    ids_row = ids_ref[...]
    ids_column = to_column(ids_row)
    same = ids_column == ids_row
    earlier = same & (iota((tokens, tokens), 0) < iota((tokens, tokens), 1))
    slot_row = jnp.sum(earlier.astype(jnp.int32), axis=0, keepdims=True)
    main_row = jnp.where(slot_row < MAIN, ids_row * MAIN + slot_row, -1)
    last_row = jnp.where(slot_row < MAIN, -1, ids_row * (ES * LAST) + slot_row - MAIN)
    pick_main = (iota((EXPERTS * MAIN, tokens), 0) == main_row).astype(BF16)
    as_float = current_ref[...].astype(F32)
    inverse_rms = lax.rsqrt(jnp.mean(as_float * as_float, axis=-1, keepdims=True) + EPSILON)
    last = jnp.zeros((EXPERTS * ES * LAST, quarter), F32)
    for q in range(ES):
        columns = slice(q * quarter, (q + 1) * quarter)
        normed = (current_ref[:, columns].astype(F32) * inverse_rms * gain_ref[:, columns]).astype(
            BF16
        )
        main = dot(pick_main, normed).astype(BF16)
        for expert in range(EXPERTS):
            rows = main[expert * MAIN : (expert + 1) * MAIN]
            for chip in (2 * expert, 2 * expert + 1):
                send_ref[ORDER.index(chip), q * MAIN : (q + 1) * MAIN, :] = rows
        place = jnp.where(last_row < 0, -1, last_row + q * LAST)
        pick_last = (iota((EXPERTS * ES * LAST, tokens), 0) == place).astype(BF16)
        last = last + dot(pick_last, normed)
    for expert in range(EXPERTS):
        rows = last[expert * ES * LAST : (expert + 1) * ES * LAST].astype(BF16)
        for chip in (2 * expert, 2 * expert + 1):
            send_ref[ORDER.index(chip), ES * MAIN :, :] = rows


def prepare(current, ids_row, gain):
    tokens, features = current.shape
    quarter = features // ES
    return pl.pallas_call(
        prepare_kernel,
        out_shape=jax.ShapeDtypeStruct((CHIPS, ES * (MAIN + LAST), quarter), BF16),
        compiler_params=pltpu.CompilerParams(vmem_limit_bytes=VMEM_LIMIT),
        cost_estimate=pl.CostEstimate(
            flops=3 * tokens * tokens * features, bytes_accessed=8 * tokens * features, transcendentals=0
        ),
    )(current, ids_row, gain)


def hidden_kernel(own_ref, other_ref, gate_ref, up_ref, mine_ref, give_ref):
    quarter = own_ref.shape[2]
    count = CHIPS * (MAIN + LAST)
    for received, hidden_ref in ((own_ref, mine_ref), (other_ref, give_ref)):
        last = received[:, ES * MAIN :, :].astype(F32).reshape(CHIPS * ES * LAST, quarter).astype(BF16)
        gate = jnp.zeros((count, gate_ref.shape[1]), F32)
        up = jnp.zeros((count, up_ref.shape[1]), F32)
        shape = (CHIPS * LAST, CHIPS * ES * LAST)
        target = iota(shape, 0)
        source = (target // LAST) * (ES * LAST) + target % LAST
        for q in range(ES):
            main = received[:, q * MAIN : (q + 1) * MAIN, :].reshape(CHIPS * MAIN, quarter)
            pick = (iota(shape, 1) == source + q * LAST).astype(BF16)
            rows = jnp.concatenate([main, dot(pick, last).astype(BF16)], axis=0)
            gate = gate + dot(rows, gate_ref[q * quarter : (q + 1) * quarter, :])
            up = up + dot(rows, up_ref[q * quarter : (q + 1) * quarter, :])
        hidden_ref[...] = (jax.nn.silu(gate) * up).astype(BF16)


def hidden_units(own, other, gate_cols, up_cols):
    count = CHIPS * (MAIN + LAST)
    features, width = gate_cols.shape
    return pl.pallas_call(
        hidden_kernel,
        out_shape=[jax.ShapeDtypeStruct((count, width), BF16)] * 2,
        compiler_params=pltpu.CompilerParams(vmem_limit_bytes=VMEM_LIMIT),
        cost_estimate=pl.CostEstimate(
            flops=8 * count * features * width,
            bytes_accessed=4 * features * width + 4 * count * features,
            transcendentals=2 * count * width,
        ),
    )(own, other, gate_cols, up_cols)


def down_kernel(pieces, mine_ref, theirs_ref, *refs):
    down_refs, other_refs, back_ref = refs[:pieces], refs[pieces : 2 * pieces], refs[2 * pieces]
    quarter = back_ref.shape[2]
    shape = (CHIPS * ES * LAST, CHIPS * LAST)
    row = iota(shape, 0)
    source = iota(shape, 1)
    last = jnp.zeros((CHIPS * ES * LAST, quarter), F32)
    for q in range(ES):
        columns = slice(q * quarter, (q + 1) * quarter)
        total = jnp.zeros((mine_ref.shape[0], quarter), F32)
        for hidden_ref, weights in ((mine_ref, down_refs), (theirs_ref, other_refs)):
            block = jnp.concatenate([ref[:, columns] for ref in weights], axis=0)
            total = total + dot(hidden_ref[...], block)
        total = total.astype(BF16)
        for chip in range(CHIPS):
            back_ref[chip, q * MAIN : (q + 1) * MAIN, :] = total[chip * MAIN : (chip + 1) * MAIN]
        inside = row % (ES * LAST) - q * LAST
        pick = (inside >= 0) & (inside < LAST)
        pick = pick & (source == (row // (ES * LAST)) * LAST + inside)
        last = last + dot(pick.astype(BF16), total[CHIPS * MAIN :])
    for chip in range(CHIPS):
        rows = last[chip * ES * LAST : (chip + 1) * ES * LAST]
        back_ref[chip, ES * MAIN :, :] = rows.astype(BF16)


def down_product(mine, theirs, down, other_down):
    count, width = mine.shape
    features = down[0].shape[1]
    return pl.pallas_call(
        functools.partial(down_kernel, len(down)),
        out_shape=jax.ShapeDtypeStruct((CHIPS, ES * (MAIN + LAST), features // ES), BF16),
        compiler_params=pltpu.CompilerParams(vmem_limit_bytes=VMEM_LIMIT),
        cost_estimate=pl.CostEstimate(
            flops=4 * count * width * features,
            bytes_accessed=4 * width * features + 2 * count * features,
            transcendentals=0,
        ),
    )(mine, theirs, *down, *other_down)


def finish_kernel(current_ref, back_ref, ids_ref, scores_ref, out_ref):
    tokens, features = current_ref.shape
    quarter = features // ES
    ids_row = ids_ref[...]
    ids_column = to_column(ids_row)
    score = to_column(scores_ref[...])
    earlier = (ids_column == ids_row) & (iota((tokens, tokens), 1) < iota((tokens, tokens), 0))
    slot = jnp.sum(earlier.astype(jnp.int32), axis=1, keepdims=True)
    lane = iota((tokens, CHIPS * MAIN), 1)
    pick_main = (lane // (2 * MAIN) == ids_column) & (lane % MAIN == slot)
    pick_main = pick_main.astype(BF16)
    lane = iota((tokens, CHIPS * ES * LAST), 1)
    in_expert = (lane // (2 * ES * LAST) == ids_column) & (slot >= MAIN)
    in_block = lane % (ES * LAST)
    last = jnp.concatenate(
        [back_ref[ORDER.index(chip), ES * MAIN :, :].astype(F32) for chip in range(CHIPS)], axis=0
    ).astype(BF16)
    for q in range(ES):
        main = jnp.concatenate(
            [
                back_ref[ORDER.index(chip), q * MAIN : (q + 1) * MAIN, :]
                for chip in range(CHIPS)
            ],
            axis=0,
        )
        pick_last = in_expert & (in_block == q * LAST + slot - MAIN)
        moe = (dot(pick_main, main) + dot(pick_last.astype(BF16), last)) * score
        columns = slice(q * quarter, (q + 1) * quarter)
        out_ref[:, columns] = (current_ref[:, columns].astype(F32) + moe).astype(BF16)


def finish(current, back, ids_row, scores_row):
    tokens, features = current.shape
    return pl.pallas_call(
        finish_kernel,
        out_shape=jax.ShapeDtypeStruct((tokens, features), BF16),
        compiler_params=pltpu.CompilerParams(vmem_limit_bytes=VMEM_LIMIT),
        cost_estimate=pl.CostEstimate(
            flops=6 * tokens * EXPERTS * MAIN * features,
            bytes_accessed=8 * tokens * features,
            transcendentals=0,
        ),
    )(current, back, ids_row, scores_row)


def swap_cores(value):
    return lax.ppermute(value, "ep", [(i, i ^ 1) for i in range(EP)])


def from_behind(value, steps):
    count = lax.axis_size("section")
    return lax.ppermute(value, "section", [(i, (i + steps) % count) for i in range(count)])


def behind_other_core(value, steps):
    count = lax.axis_size("section")
    pairs = [
        (s * EP + i, ((s + steps) % count) * EP + (i ^ 1)) for s in range(count) for i in range(EP)
    ]
    return lax.ppermute(value, ("section", "ep"), pairs)


def exchange(blocks):
    same_core = [[2 * chip + core for chip in ORDER] for core in range(2)]
    return lax.all_to_all(
        blocks, "ep", split_axis=0, concat_axis=0, axis_index_groups=same_core, tiled=True
    )


def on_device(
    flight_a, flight_b, routes_a, routes_b, scores_a, scores_b, norm_gain, w_gate, w_up, w_down
):
    tokens = flight_a.shape[1]
    current_a, current_b = flight_a[0], flight_b[0]
    ids_a, ids_b = routes_a.reshape(1, tokens), routes_b.reshape(1, tokens)
    marks_a, marks_b = scores_a.reshape(1, tokens), scores_b.reshape(1, tokens)
    gate_cols, up_cols, down = w_gate[0], w_up[0], w_down[0]

    own_a = exchange(prepare(current_a, ids_a, norm_gain))
    send_b = prepare(current_b, ids_b, norm_gain)
    middle = down.shape[0] // 2
    upper = from_behind(down[:middle], -1)
    own_a, send_b, upper = lax.optimization_barrier((own_a, send_b, upper))
    own_b = exchange(send_b)

    lower = from_behind(down[middle:], -1)
    mine_a, give_a = hidden_units(own_a, swap_cores(own_a), gate_cols, up_cols)
    back_a = down_product(mine_a, swap_cores(give_a), [down], [swap_cores(down)])
    own_b, back_a, lower = lax.optimization_barrier((own_b, back_a, lower))

    returned_a = exchange(back_a)
    mine_b, give_b = hidden_units(own_b, swap_cores(own_b), gate_cols, up_cols)
    back_b = down_product(
        from_behind(mine_b, -1),
        behind_other_core(give_b, -1),
        [upper, lower],
        [swap_cores(upper), swap_cores(lower)],
    )
    moved_b, moved_ids, moved_marks = [
        from_behind(value, -1) for value in (current_b, ids_b, marks_b)
    ]

    marks_a, back_b = lax.optimization_barrier((marks_a, back_b))
    returned_b = exchange(back_b)
    updated_a = from_behind(finish(current_a, returned_a, ids_a, marks_a), 1)
    updated_b = finish(moved_b, returned_b, moved_ids, moved_marks)
    return (updated_a[None], updated_b[None])


def solution(mesh):
    placed = (
        P("section", "ep", None),
        P("section", "ep", None),
        P("section", None, "ep", None),
        P("section", None, "ep", None),
        P("section", None, "ep", None),
        P("section", None, "ep", None),
        P("section", None),
        P("section", None, "ep"),
        P("section", None, "ep"),
        P("section", "ep", None),
    )
    return jax.shard_map(
        on_device,
        mesh=mesh,
        in_specs=placed,
        out_specs=(P("section", "ep", None), P("section", "ep", None)),
        check_vma=False,
    )
```

time: 158 us -> 159 us (level)
  the two profiles are of different devices: /device:TPU:8 before, /device:TPU:1 now
where the time goes in v5:
time: 159 us
  waiting for transfers between devices  66.2 us (42%)
  starting transfers between devices  54.1 us (34%)
  Pallas kernels  27 us (17%)
  local copies, waits for them, and re-layouts  10.5 us (7%)
    ppermute x7, waiting for transfers between devices, from_behind(): lax.ppermute(value, 'section', [(i, (i + steps) % count) for i in range(c...  42.1 us
    all_to_all x4, starting transfers between devices, exchange(): lax.all_to_all(blocks, 'ep', split_axis=0, concat_axis=0, axis_index_grou...  24.8 us
    ppermute x7, starting transfers between devices, from_behind(): lax.ppermute(value, 'section', [(i, (i + steps) % count) for i in range(c...  24.5 us
    all_to_all x4, waiting for transfers between devices, exchange(): lax.all_to_all(blocks, 'ep', split_axis=0, concat_axis=0, axis_index_grou...  20 us
    pallas_call x2, Pallas kernels, hidden_units(): pl.pallas_call(hidden_kernel, out_shape=[jax.ShapeDtypeStruct((count, wid...  10.6 us
    unnamed x33, local copies, waits for them, and re-layouts  9.51 us
    pallas_call x2, Pallas kernels, down_product(): pl.pallas_call(functools.partial(down_kernel, len(down)), out_shape=jax.S...  7.84 us
    pallas_call x2, Pallas kernels, prepare(): pl.pallas_call(prepare_kernel, out_shape=jax.ShapeDtypeStruct((CHIPS, ES...  4.34 us
  transfers between devices with their start and end apart: 18, of which 10 were waited for; matrix products, arithmetic and copies ran while one was open for 1% of the time, Pallas kernels for 14%

profile of v5, /device:TPU:1, one launch (start us, length us, event | category | flops | bytes accessed | tf_op | source)
XLA Modules:
  0.0 158.6 jit_solution(11997068442866541294)
XLA Ops:
  0.6 0.0 copy-start.1
  0.6 1.2 copy-done.1
  1.8 0.7 copy-done.5
  2.5 0.7 copy-done.7
  3.2 2.1 %shard_map.113 = bf16[16,72,896]{2,1,0:T(8,128)(2,1)} custom-call(bf16[128,3584]{1,0:T(8,128)(2,1)S(1)} %bitcast.17, s32[1,128]{1,0:T(1,128)S(1)} %bitcast.21, f32[1,3584]{1,0:T(1,128)S(1)} %copy-done.5), custom_call_target="tpu_custom_call" | custom-call | flops 176160768 | bytes 3670016 | tf_op jit(solution)/shard_map/pallas_call | solution.py:73
  5.3 8.6 %all-to-all-start = ((bf16[16,72,896]{2,1,0:T(8,128)(2,1)}), bf16[16,72,896]{2,1,0:T(8,128)(2,1)}, u32[]{:S(2)}, u32[]{:S(2)}) async-start(bf16[16,72,896]{2,1,0:T(8,128)(2,1)} %shard_map.113), calls=%async_computation | async-start | bytes 4128768 | tf_op jit(solution)/shard_map/all_to_all | solution.py:221
  14.0 0.0 copy-start.6
  14.0 0.0 copy-start.10
  14.0 1.0 slice_bitcast_fusion
  15.0 5.6 %collective-permute-start = (bf16[128,3584]{1,0:T(8,128)(2,1)S(1)}, bf16[128,3584]{1,0:T(8,128)(2,1)S(1)}, u32[]{:S(2)}, u32[]{:S(2)}) collective-permute-start(bf16[128,3584]{1,0:T(8,128)(2,1)S(1)} %get-tuple-element.27), channel_id=1, source_target_pairs={{0,224},{32,0},{64,32},{96,64},{128,96},{160,128},{192,160},{224,1... | collective-permute-start | bytes 2752520 | tf_op jit(solution)/shard_map/ppermute | solution.py:208
  20.6 2.2 %shard_map.114 = bf16[16,72,896]{2,1,0:T(8,128)(2,1)} custom-call(bf16[128,3584]{1,0:T(8,128)(2,1)S(1)} %bitcast.19, s32[1,128]{1,0:T(1,128)S(1)} %bitcast.24, f32[1,3584]{1,0:T(1,128)S(1)} %copy-done.6), custom_call_target="tpu_custom_call" | custom-call | flops 176160768 | bytes 3670016 | tf_op jit(solution)/shard_map/pallas_call | solution.py:73
  22.8 16.2 %collective-permute-done.refs_0_ = bf16[128,3584]{1,0:T(8,128)(2,1)S(1)} collective-permute-done((bf16[128,3584]{1,0:T(8,128)(2,1)S(1)}, bf16[128,3584]{1,0:T(8,128)(2,1)S(1)}, u32[]{:S(2)}, u32[]{:S(2)}) %collective-permute-start) | collective-permute-done | bytes 917536 | tf_op jit(solution)/shard_map/ppermute | solution.py:208
  39.0 5.2 %all-to-all-done.own_ref = bf16[16,72,896]{2,1,0:T(8,128)(2,1)} async-done(((bf16[16,72,896]{2,1,0:T(8,128)(2,1)}), bf16[16,72,896]{2,1,0:T(8,128)(2,1)}, u32[]{:S(2)}, u32[]{:S(2)}) %all-to-all-start) | async-done | bytes 2064416 | tf_op jit(solution)/shard_map/all_to_all | solution.py:221
  44.2 0.8 collective-permute-start.1
  45.1 5.1 %all-to-all-start.1 = ((bf16[16,72,896]{2,1,0:T(8,128)(2,1)}), bf16[16,72,896]{2,1,0:T(8,128)(2,1)}, u32[]{:S(2)}, u32[]{:S(2)}) async-start(bf16[16,72,896]{2,1,0:T(8,128)(2,1)} %shard_map.114), calls=%async_computation.1 | async-start | bytes 4128768 | tf_op jit(solution)/shard_map/all_to_all | solution.py:221
  50.2 0.6 collective-permute-start.3
  50.7 5.6 %collective-permute-start.4 = (bf16[128,3584]{1,0:T(8,128)(2,1)}, bf16[128,3584]{1,0:T(8,128)(2,1)}, u32[]{:S(2)}, u32[]{:S(2)}) collective-permute-start(bf16[128,3584]{1,0:T(8,128)(2,1)} %get-tuple-element.26), channel_id=1, source_target_pairs={{0,224},{32,0},{64,32},{96,64},{128,96},{160,128},{192,160},{224,1... | collective-permute-start | bytes 2752520 | tf_op jit(solution)/shard_map/ppermute | solution.py:208
  56.3 1.5 copy-done.11
  57.8 1.5 copy-done.13
  59.3 5.3 %shard_map.115 = (bf16[288,256]{1,0:T(8,128)(2,1)S(1)}, bf16[288,256]{1,0:T(8,128)(2,1)S(1)}) custom-call(bf16[16,72,896]{2,1,0:T(8,128)(2,1)} %all-to-all-done.own_ref, bf16[16,72,896]{2,1,0:T(8,128)(2,1)} %collective-permute-done.1.other_ref, bf16[3584,256]{1,0:T(8,128)(2,1)S(1)} %bitcast.26, bf16[3584,256]{1,0:T(8,128)(2,1)S(1)} %bitcast.28), custom_call_target="tpu_custom_call" | custom-call | flops 2113929216 | bytes 7798784 | tf_op jit(solution)/shard_map/pallas_call | solution.py:105
  64.6 0.4 collective-permute-start.2
  65.0 1.0 collective-permute-done.2.theirs_ref
  66.0 3.3 %shard_map.116 = bf16[16,72,896]{2,1,0:T(8,128)(2,1)} custom-call(bf16[288,256]{1,0:T(8,128)(2,1)S(1)} %get-tuple-element.16.mine_ref, bf16[288,256]{1,0:T(8,128)(2,1)S(1)} %collective-permute-done.2.theirs_ref, bf16[256,3584]{1,0:T(8,128)(2,1)S(1)} %bitcast.16, bf16[256,3584]{1,0:T(8,128)(2,1)S(1)} %collective-permute-done.3.refs_1_), custom_call_target="tpu_custom_call" | custom-call | flops 1056964608 | bytes 5734400 | tf_op jit(solution)/shard_map/pallas_call | solution.py:145
  69.4 6.9 %collective-permute-done.4.refs_1_ = bf16[128,3584]{1,0:T(8,128)(2,1)} collective-permute-done((bf16[128,3584]{1,0:T(8,128)(2,1)}, bf16[128,3584]{1,0:T(8,128)(2,1)}, u32[]{:S(2)}, u32[]{:S(2)}) %collective-permute-start.4) | collective-permute-done | bytes 917536 | tf_op jit(solution)/shard_map/ppermute | solution.py:208
  76.3 5.2 %all-to-all-done.1.own_ref = bf16[16,72,896]{2,1,0:T(8,128)(2,1)} async-done(((bf16[16,72,896]{2,1,0:T(8,128)(2,1)}), bf16[16,72,896]{2,1,0:T(8,128)(2,1)}, u32[]{:S(2)}, u32[]{:S(2)}) %all-to-all-start.1) | async-done | bytes 2064416 | tf_op jit(solution)/shard_map/all_to_all | solution.py:221
  81.5 1.0 collective-permute-start.5
  82.5 5.8 %all-to-all-start.2 = ((bf16[16,72,896]{2,1,0:T(8,128)(2,1)}), bf16[16,72,896]{2,1,0:T(8,128)(2,1)S(1)}, u32[]{:S(2)}, u32[]{:S(2)}) async-start(bf16[16,72,896]{2,1,0:T(8,128)(2,1)} %shard_map.116), calls=%async_computation.2 | async-start | bytes 4128768 | tf_op jit(solution)/shard_map/all_to_all | solution.py:221
  88.3 0.6 collective-permute-start.8
  88.9 0.3 collective-permute-start.9
  89.2 1.5 copy-done.12
  90.7 1.5 copy-done.14
  92.1 5.3 %shard_map.117 = (bf16[288,256]{1,0:T(8,128)(2,1)S(1)}, bf16[288,256]{1,0:T(8,128)(2,1)S(1)}) custom-call(bf16[16,72,896]{2,1,0:T(8,128)(2,1)} %all-to-all-done.1.own_ref, bf16[16,72,896]{2,1,0:T(8,128)(2,1)} %collective-permute-done.5.other_ref, bf16[3584,256]{1,0:T(8,128)(2,1)S(1)} %bitcast.27, bf16[3584,256]{1,0:T(8,128)(2,1)S(1)} %bitcast.29), custom_call_target="tpu_custom_call" | custom-call | flops 2113929216 | bytes 7798784 | tf_op jit(solution)/shard_map/pallas_call | solution.py:105
  97.4 5.6 %collective-permute-start.6 = (bf16[288,256]{1,0:T(8,128)(2,1)S(1)}, bf16[288,256]{1,0:T(8,128)(2,1)S(1)}, u32[]{:S(2)}, u32[]{:S(2)}) collective-permute-start(bf16[288,256]{1,0:T(8,128)(2,1)S(1)} %get-tuple-element.20), channel_id=1, source_target_pairs={{0,224},{32,0},{64,32},{96,64},{128,96},{160,128},{192,160},{224,1... | collective-permute-start | bytes 442376 | tf_op jit(solution)/shard_map/ppermute | solution.py:208
  103.0 1.1 collective-permute-start.7
  104.1 1.9 %collective-permute-done.6.mine_ref = bf16[288,256]{1,0:T(8,128)(2,1)S(1)} collective-permute-done((bf16[288,256]{1,0:T(8,128)(2,1)S(1)}, bf16[288,256]{1,0:T(8,128)(2,1)S(1)}, u32[]{:S(2)}, u32[]{:S(2)}) %collective-permute-start.6) | collective-permute-done | bytes 147488 | tf_op jit(solution)/shard_map/ppermute | solution.py:208
  106.1 3.2 %collective-permute-done.7.theirs_ref = bf16[288,256]{1,0:T(8,128)(2,1)S(1)} collective-permute-done((bf16[288,256]{1,0:T(8,128)(2,1)S(1)}, bf16[288,256]{1,0:T(8,128)(2,1)S(1)}, u32[]{:S(2)}, u32[]{:S(2)}) %collective-permute-start.7) | collective-permute-done | bytes 147488 | tf_op jit(solution)/shard_map/ppermute | solution.py:216
  109.2 4.5 %shard_map.118 = bf16[16,72,896]{2,1,0:T(8,128)(2,1)} custom-call(bf16[288,256]{1,0:T(8,128)(2,1)S(1)} %collective-permute-done.6.mine_ref, bf16[288,256]{1,0:T(8,128)(2,1)S(1)} %collective-permute-done.7.theirs_ref, bf16[128,3584]{1,0:T(8,128)(2,1)S(1)} %collective-permute-done.refs_0_, bf16[128,3584]{1,0:T(8,128)(2,1)} %collective-permute-done.4.refs_1_, ...), custom_call_target="tpu_custom_call" | custom-call | flops 1056964608 | bytes 5734400 | tf_op jit(solution)/shard_map/pallas_call | solution.py:145
  113.7 6.0 %all-to-all-done.2.back_ref = bf16[16,72,896]{2,1,0:T(8,128)(2,1)S(1)} async-done(((bf16[16,72,896]{2,1,0:T(8,128)(2,1)}), bf16[16,72,896]{2,1,0:T(8,128)(2,1)S(1)}, u32[]{:S(2)}, u32[]{:S(2)}) %all-to-all-start.2) | async-done | bytes 2064416 | tf_op jit(solution)/shard_map/all_to_all | solution.py:221
  119.7 5.3 %all-to-all-start.3 = ((bf16[16,72,896]{2,1,0:T(8,128)(2,1)}), bf16[16,72,896]{2,1,0:T(8,128)(2,1)}, u32[]{:S(2)}, u32[]{:S(2)}) async-start(bf16[16,72,896]{2,1,0:T(8,128)(2,1)} %shard_map.118), calls=%async_computation.3 | async-start | bytes 4128768 | tf_op jit(solution)/shard_map/all_to_all | solution.py:221
  125.0 0.9 shard_map.119
  125.9 1.6 %collective-permute-start.10 = (bf16[128,3584]{1,0:T(8,128)(2,1)S(1)}, bf16[128,3584]{1,0:T(8,128)(2,1)S(1)}, u32[]{:S(2)}, u32[]{:S(2)}) collective-permute-start(bf16[128,3584]{1,0:T(8,128)(2,1)S(1)} %shard_map.119), channel_id=1, source_target_pairs={{0,32},{32,64},{64,96},{96,128},{128,160},{160,192},{192,224},{224... | collective-permute-start | bytes 2752520 | tf_op jit(solution)/shard_map/ppermute | solution.py:208
  127.5 4.1 %collective-permute-start.11 = (bf16[128,3584]{1,0:T(8,128)(2,1)S(1)}, bf16[128,3584]{1,0:T(8,128)(2,1)S(1)}, u32[]{:S(2)}, u32[]{:S(2)}) collective-permute-start(bf16[128,3584]{1,0:T(8,128)(2,1)S(1)} %bitcast.20), channel_id=1, source_target_pairs={{0,224},{32,0},{64,32},{96,64},{128,96},{160,128},{192,160},{224,1... | collective-permute-start | bytes 2752520 | tf_op jit(solution)/shard_map/ppermute | solution.py:208
  131.7 1.3 collective-permute-start.12
  132.9 0.7 collective-permute-start.13
  133.6 17.0 %collective-permute-done.10 = bf16[128,3584]{1,0:T(8,128)(2,1)S(1)} collective-permute-done((bf16[128,3584]{1,0:T(8,128)(2,1)S(1)}, bf16[128,3584]{1,0:T(8,128)(2,1)S(1)}, u32[]{:S(2)}, u32[]{:S(2)}) %collective-permute-start.10) | collective-permute-done | bytes 917536 | tf_op jit(solution)/shard_map/ppermute | solution.py:208
  150.6 3.7 %all-to-all-done.3.back_ref = bf16[16,72,896]{2,1,0:T(8,128)(2,1)} async-done(((bf16[16,72,896]{2,1,0:T(8,128)(2,1)}), bf16[16,72,896]{2,1,0:T(8,128)(2,1)}, u32[]{:S(2)}, u32[]{:S(2)}) %all-to-all-start.3) | async-done | bytes 2064416 | tf_op jit(solution)/shard_map/all_to_all | solution.py:221
  154.3 3.4 %shard_map.120 = bf16[128,3584]{1,0:T(8,128)(2,1)} custom-call(bf16[128,3584]{1,0:T(8,128)(2,1)S(1)} %collective-permute-done.11.current_ref, bf16[16,72,896]{2,1,0:T(8,128)(2,1)} %all-to-all-done.3.back_ref, s32[1,128]{1,0:T(1,128)S(1)} %collective-permute-done.12.ids_ref, f32[1,128]{1,0:T(1,128)S(1)} %collective-permute-done.13.scores_ref), custom_call_target="tpu_custom_call" | custom-call | flops 352321536 | bytes 3670016 | tf_op jit(solution)/shard_map/pallas_call | solution.py:190
  157.7 0.9 copy.13
  (30 shorter events, 0.1 us)
Async XLA Ops:
  0.6 1.2 copy-start.1
  1.8 0.7 copy-start.5
  2.5 0.7 copy-start.7
  5.3 8.6 %copy-start = (bf16[1,256,3584]{2,1,0:T(8,128)(2,1)S(1)}, bf16[1,256,3584]{2,1,0:T(8,128)(2,1)}, u32[]{:S(2)}) copy-start(bf16[1,256,3584]{2,1,0:T(8,128)(2,1)} %param.19) | copy-start | bytes 5505028
  5.3 38.9 %all-to-all-start = ((bf16[16,72,896]{2,1,0:T(8,128)(2,1)}), bf16[16,72,896]{2,1,0:T(8,128)(2,1)}, u32[]{:S(2)}, u32[]{:S(2)}) async-start(bf16[16,72,896]{2,1,0:T(8,128)(2,1)} %shard_map.113), calls=%async_computation | async-start | bytes 4128768 | tf_op jit(solution)/shard_map/all_to_all | solution.py:221
  14.0 6.7 %copy-start.3 = (bf16[1,128,3584]{2,1,0:T(8,128)(2,1)S(1)}, bf16[1,128,3584]{2,1,0:T(8,128)(2,1)}, u32[]{:S(2)}) copy-start(bf16[1,128,3584]{2,1,0:T(8,128)(2,1)} %param.11) | copy-start | bytes 2752516
  14.0 6.7 %copy-start.6 = (f32[1,3584]{1,0:T(1,128)S(1)}, f32[1,3584]{1,0:T(1,128)}, u32[]{:S(2)}) copy-start(f32[1,3584]{1,0:T(1,128)} %gain_ref.3) | copy-start | bytes 43012
  14.0 6.6 %copy-start.10 = (s32[1,1,128,1]{2,3,1,0:T(1,128)S(1)}, s32[1,1,128,1]{2,3,1,0:T(1,128)}, u32[]{:S(2)}) copy-start(s32[1,1,128,1]{2,3,1,0:T(1,128)} %param.13) | copy-start | bytes 1540
  15.0 24.0 %collective-permute-start = (bf16[128,3584]{1,0:T(8,128)(2,1)S(1)}, bf16[128,3584]{1,0:T(8,128)(2,1)S(1)}, u32[]{:S(2)}, u32[]{:S(2)}) collective-permute-start(bf16[128,3584]{1,0:T(8,128)(2,1)S(1)} %get-tuple-element.27), channel_id=1, source_target_pairs={{0,224},{32,0},{64,32},{96,64},{128,96},{160,128},{192,160},{224,1... | collective-permute-start | bytes 2752520 | tf_op jit(solution)/shard_map/ppermute | solution.py:208
  44.2 12.1 %collective-permute-start.1 = (bf16[16,72,896]{2,1,0:T(8,128)(2,1)}, bf16[16,72,896]{2,1,0:T(8,128)(2,1)}, u32[]{:S(2)}, u32[]{:S(2)}) collective-permute-start(bf16[16,72,896]{2,1,0:T(8,128)(2,1)} %all-to-all-done.own_ref), channel_id=1, source_target_pairs={{0,1},{1,0},{2,3},{3,2},{4,5},{5,4},{6,7},{7,6},{8,9},{9,8},{10,11... | collective-permute-start | bytes 6193160 | tf_op jit(solution)/shard_map/ppermute | solution.py:203
  45.1 36.4 %all-to-all-start.1 = ((bf16[16,72,896]{2,1,0:T(8,128)(2,1)}), bf16[16,72,896]{2,1,0:T(8,128)(2,1)}, u32[]{:S(2)}, u32[]{:S(2)}) async-start(bf16[16,72,896]{2,1,0:T(8,128)(2,1)} %shard_map.114), calls=%async_computation.1 | async-start | bytes 4128768 | tf_op jit(solution)/shard_map/all_to_all | solution.py:221
  50.2 14.9 %collective-permute-start.3 = (bf16[256,3584]{1,0:T(8,128)(2,1)S(1)}, bf16[256,3584]{1,0:T(8,128)(2,1)S(1)}, u32[]{:S(2)}, u32[]{:S(2)}) collective-permute-start(bf16[256,3584]{1,0:T(8,128)(2,1)S(1)} %bitcast.15), channel_id=1, source_target_pairs={{0,1},{1,0},{2,3},{3,2},{4,5},{5,4},{6,7},{7,6},{8,9},{9,8},{10,11... | collective-permute-start | bytes 5505032 | tf_op jit(solution)/shard_map/ppermute | solution.py:203
  50.7 25.6 %collective-permute-start.4 = (bf16[128,3584]{1,0:T(8,128)(2,1)}, bf16[128,3584]{1,0:T(8,128)(2,1)}, u32[]{:S(2)}, u32[]{:S(2)}) collective-permute-start(bf16[128,3584]{1,0:T(8,128)(2,1)} %get-tuple-element.26), channel_id=1, source_target_pairs={{0,224},{32,0},{64,32},{96,64},{128,96},{160,128},{192,160},{224,1... | collective-permute-start | bytes 2752520 | tf_op jit(solution)/shard_map/ppermute | solution.py:208
  56.3 1.5 copy-start.11
  57.8 1.5 copy-start.13
  64.6 1.5 collective-permute-start.2
  81.5 7.7 %collective-permute-start.5 = (bf16[16,72,896]{2,1,0:T(8,128)(2,1)}, bf16[16,72,896]{2,1,0:T(8,128)(2,1)}, u32[]{:S(2)}, u32[]{:S(2)}) collective-permute-start(bf16[16,72,896]{2,1,0:T(8,128)(2,1)} %all-to-all-done.1.own_ref), channel_id=1, source_target_pairs={{0,1},{1,0},{2,3},{3,2},{4,5},{5,4},{6,7},{7,6},{8,9},{9,8},{10,11... | collective-permute-start | bytes 6193160 | tf_op jit(solution)/shard_map/ppermute | solution.py:203
  82.5 37.1 %all-to-all-start.2 = ((bf16[16,72,896]{2,1,0:T(8,128)(2,1)}), bf16[16,72,896]{2,1,0:T(8,128)(2,1)S(1)}, u32[]{:S(2)}, u32[]{:S(2)}) async-start(bf16[16,72,896]{2,1,0:T(8,128)(2,1)} %shard_map.116), calls=%async_computation.2 | async-start | bytes 4128768 | tf_op jit(solution)/shard_map/all_to_all | solution.py:221
  88.3 15.8 %collective-permute-start.8 = (bf16[128,3584]{1,0:T(8,128)(2,1)S(1)}, bf16[128,3584]{1,0:T(8,128)(2,1)S(1)}, u32[]{:S(2)}, u32[]{:S(2)}) collective-permute-start(bf16[128,3584]{1,0:T(8,128)(2,1)S(1)} %collective-permute-done.refs_0_), channel_id=1, source_target_pairs={{0,1},{1,0},{2,3},{3,2},{4,5},{5,4},{6,7},{7,6},{8,9},{9,8},{10,11... | collective-permute-start | bytes 2752520 | tf_op jit(solution)/shard_map/ppermute | solution.py:203
  88.9 15.3 %collective-permute-start.9 = (bf16[128,3584]{1,0:T(8,128)(2,1)}, bf16[128,3584]{1,0:T(8,128)(2,1)S(1)}, u32[]{:S(2)}, u32[]{:S(2)}) collective-permute-start(bf16[128,3584]{1,0:T(8,128)(2,1)} %collective-permute-done.4.refs_1_), channel_id=1, source_target_pairs={{0,1},{1,0},{2,3},{3,2},{4,5},{5,4},{6,7},{7,6},{8,9},{9,8},{10,11... | collective-permute-start | bytes 2752520 | tf_op jit(solution)/shard_map/ppermute | solution.py:203
  89.1 1.5 copy-start.12
  90.6 1.5 copy-start.14
  97.4 8.6 %collective-permute-start.6 = (bf16[288,256]{1,0:T(8,128)(2,1)S(1)}, bf16[288,256]{1,0:T(8,128)(2,1)S(1)}, u32[]{:S(2)}, u32[]{:S(2)}) collective-permute-start(bf16[288,256]{1,0:T(8,128)(2,1)S(1)} %get-tuple-element.20), channel_id=1, source_target_pairs={{0,224},{32,0},{64,32},{96,64},{128,96},{160,128},{192,160},{224,1... | collective-permute-start | bytes 442376 | tf_op jit(solution)/shard_map/ppermute | solution.py:208
  103.0 6.2 %collective-permute-start.7 = (bf16[288,256]{1,0:T(8,128)(2,1)S(1)}, bf16[288,256]{1,0:T(8,128)(2,1)S(1)}, u32[]{:S(2)}, u32[]{:S(2)}) collective-permute-start(bf16[288,256]{1,0:T(8,128)(2,1)S(1)} %get-tuple-element.21), channel_id=1, source_target_pairs={{0,225},{1,224},{2,227},{3,226},{4,229},{5,228},{6,231},{7,230},{8... | collective-permute-start | bytes 442376 | tf_op jit(solution)/shard_map/ppermute | solution.py:216
  113.7 11.2 %copy-start.2 = (bf16[1,128,3584]{2,1,0:T(8,128)(2,1)S(1)}, bf16[1,128,3584]{2,1,0:T(8,128)(2,1)}, u32[]{:S(2)}) copy-start(bf16[1,128,3584]{2,1,0:T(8,128)(2,1)} %param.10) | copy-start | bytes 2752516
  113.7 11.2 %copy-start.8 = (s32[1,1,128,1]{2,3,1,0:T(1,128)S(1)}, s32[1,1,128,1]{2,3,1,0:T(1,128)}, u32[]{:S(2)}) copy-start(s32[1,1,128,1]{2,3,1,0:T(1,128)} %param.12) | copy-start | bytes 1540
  113.7 11.2 %copy-start.9 = (f32[1,1,128,1]{2,3,1,0:T(1,128)S(1)}, f32[1,1,128,1]{2,3,1,0:T(1,128)}, u32[]{:S(2)}) copy-start(f32[1,1,128,1]{2,3,1,0:T(1,128)} %param.14) | copy-start | bytes 1540
  119.7 34.6 %all-to-all-start.3 = ((bf16[16,72,896]{2,1,0:T(8,128)(2,1)}), bf16[16,72,896]{2,1,0:T(8,128)(2,1)}, u32[]{:S(2)}, u32[]{:S(2)}) async-start(bf16[16,72,896]{2,1,0:T(8,128)(2,1)} %shard_map.118), calls=%async_computation.3 | async-start | bytes 4128768 | tf_op jit(solution)/shard_map/all_to_all | solution.py:221
  125.0 2.6 %copy-start.4 = (bf16[1,128,3584]{2,1,0:T(8,128)(2,1)S(1)}, bf16[1,128,3584]{2,1,0:T(8,128)(2,1)}, u32[]{:S(2)}) copy-start(bf16[1,128,3584]{2,1,0:T(8,128)(2,1)} %param.11) | copy-start | bytes 2752516
  125.0 8.0 %copy-start.15 = (f32[1,1,128,1]{2,3,1,0:T(1,128)S(1)}, f32[1,1,128,1]{2,3,1,0:T(1,128)}, u32[]{:S(2)}) copy-start(f32[1,1,128,1]{2,3,1,0:T(1,128)} %param.15) | copy-start | bytes 1540
  125.9 24.8 %collective-permute-start.10 = (bf16[128,3584]{1,0:T(8,128)(2,1)S(1)}, bf16[128,3584]{1,0:T(8,128)(2,1)S(1)}, u32[]{:S(2)}, u32[]{:S(2)}) collective-permute-start(bf16[128,3584]{1,0:T(8,128)(2,1)S(1)} %shard_map.119), channel_id=1, source_target_pairs={{0,32},{32,64},{64,96},{96,128},{128,160},{160,192},{192,224},{224... | collective-permute-start | bytes 2752520 | tf_op jit(solution)/shard_map/ppermute | solution.py:208
  127.5 23.1 %collective-permute-start.11 = (bf16[128,3584]{1,0:T(8,128)(2,1)S(1)}, bf16[128,3584]{1,0:T(8,128)(2,1)S(1)}, u32[]{:S(2)}, u32[]{:S(2)}) collective-permute-start(bf16[128,3584]{1,0:T(8,128)(2,1)S(1)} %bitcast.20), channel_id=1, source_target_pairs={{0,224},{32,0},{64,32},{96,64},{128,96},{160,128},{192,160},{224,1... | collective-permute-start | bytes 2752520 | tf_op jit(solution)/shard_map/ppermute | solution.py:208
  131.7 19.0 %collective-permute-start.12 = (s32[1,128]{1,0:T(1,128)S(1)}, s32[1,128]{1,0:T(1,128)S(1)}, u32[]{:S(2)}, u32[]{:S(2)}) collective-permute-start(s32[1,128]{1,0:T(1,128)S(1)} %bitcast.25), channel_id=1, source_target_pairs={{0,224},{32,0},{64,32},{96,64},{128,96},{160,128},{192,160},{224,1... | collective-permute-start | bytes 1544 | tf_op jit(solution)/shard_map/ppermute | solution.py:208
  132.9 17.7 %collective-permute-start.13 = (f32[1,128]{1,0:T(1,128)S(1)}, f32[1,128]{1,0:T(1,128)S(1)}, u32[]{:S(2)}, u32[]{:S(2)}) collective-permute-start(f32[1,128]{1,0:T(1,128)S(1)} %bitcast.32), channel_id=1, source_target_pairs={{0,224},{32,0},{64,32},{96,64},{128,96},{160,128},{192,160},{224,1... | collective-permute-start | bytes 1544 | tf_op jit(solution)/shard_map/ppermute | solution.py:208

commit v6 on v5

--- a/solution.py
+++ b/solution.py
@@ -13,7 +13,6 @@
 CHIPS = EP // 2
 MAIN = 16
 LAST = 2
-ORDER = (2, 10, 0, 14, 6, 5, 3, 8, 7, 11, 15, 1, 12, 13, 9, 4)
 EPSILON = 1e-06
 F32 = jnp.float32
 BF16 = jnp.bfloat16
@@ -57,14 +56,14 @@
         for expert in range(EXPERTS):
             rows = main[expert * MAIN : (expert + 1) * MAIN]
             for chip in (2 * expert, 2 * expert + 1):
-                send_ref[ORDER.index(chip), q * MAIN : (q + 1) * MAIN, :] = rows
+                send_ref[chip, q * MAIN : (q + 1) * MAIN, :] = rows
         place = jnp.where(last_row < 0, -1, last_row + q * LAST)
         pick_last = (iota((EXPERTS * ES * LAST, tokens), 0) == place).astype(BF16)
         last = last + dot(pick_last, normed)
     for expert in range(EXPERTS):
         rows = last[expert * ES * LAST : (expert + 1) * ES * LAST].astype(BF16)
         for chip in (2 * expert, 2 * expert + 1):
-            send_ref[ORDER.index(chip), ES * MAIN :, :] = rows
+            send_ref[chip, ES * MAIN :, :] = rows
 
 
 def prepare(current, ids_row, gain):
@@ -169,15 +168,11 @@
     in_expert = (lane // (2 * ES * LAST) == ids_column) & (slot >= MAIN)
     in_block = lane % (ES * LAST)
     last = jnp.concatenate(
-        [back_ref[ORDER.index(chip), ES * MAIN :, :].astype(F32) for chip in range(CHIPS)], axis=0
+        [back_ref[chip, ES * MAIN :, :].astype(F32) for chip in range(CHIPS)], axis=0
     ).astype(BF16)
     for q in range(ES):
         main = jnp.concatenate(
-            [
-                back_ref[ORDER.index(chip), q * MAIN : (q + 1) * MAIN, :]
-                for chip in range(CHIPS)
-            ],
-            axis=0,
+            [back_ref[chip, q * MAIN : (q + 1) * MAIN, :] for chip in range(CHIPS)], axis=0
         )
         pick_last = in_expert & (in_block == q * LAST + slot - MAIN)
         moe = (dot(pick_main, main) + dot(pick_last.astype(BF16), last)) * score
@@ -217,7 +212,7 @@
 
 
 def exchange(blocks):
-    same_core = [[2 * chip + core for chip in ORDER] for core in range(2)]
+    same_core = [[2 * chip + core for chip in range(CHIPS)] for core in range(2)]
     return lax.all_to_all(
         blocks, "ep", split_axis=0, concat_axis=0, axis_index_groups=same_core, tiled=True
     )
@@ -236,12 +231,13 @@
     send_b = prepare(current_b, ids_b, norm_gain)
     middle = down.shape[0] // 2
     upper = from_behind(down[:middle], -1)
-    own_a, send_b, upper = lax.optimization_barrier((own_a, send_b, upper))
+    other_down = swap_cores(down)
+    own_a, send_b, upper, other_down = lax.optimization_barrier((own_a, send_b, upper, other_down))
     own_b = exchange(send_b)
 
     lower = from_behind(down[middle:], -1)
     mine_a, give_a = hidden_units(own_a, swap_cores(own_a), gate_cols, up_cols)
-    back_a = down_product(mine_a, swap_cores(give_a), [down], [swap_cores(down)])
+    back_a = down_product(mine_a, swap_cores(give_a), [down], [other_down])
     own_b, back_a, lower = lax.optimization_barrier((own_b, back_a, lower))
 
     returned_a = exchange(back_a)

time: 159 us -> 153 us (0.962)
  the two profiles are of different devices: /device:TPU:1 before, /device:TPU:8 now
where the time goes in v6:
time: 153 us; the launch traced here: 152 us
  waiting for transfers between devices  58.9 us (38%)
  starting transfers between devices  53.4 us (35%)
  Pallas kernels  27.1 us (18%)
  local copies, waits for them, and re-layouts  11.8 us (8%)
    ppermute x7, waiting for transfers between devices, from_behind(): lax.ppermute(value, 'section', [(i, (i + steps) % count) for i in range(c...  45 us
    all_to_all x4, starting transfers between devices, exchange(): lax.all_to_all(blocks, 'ep', split_axis=0, concat_axis=0, axis_index_grou...  27.9 us
    ppermute x7, starting transfers between devices, from_behind(): lax.ppermute(value, 'section', [(i, (i + steps) % count) for i in range(c...  24.2 us
    unnamed x37, local copies, waits for them, and re-layouts  10.8 us
    pallas_call x2, Pallas kernels, hidden_units(): pl.pallas_call(hidden_kernel, out_shape=[jax.ShapeDtypeStruct((count, wid...  10.7 us
    all_to_all x4, waiting for transfers between devices, exchange(): lax.all_to_all(blocks, 'ep', split_axis=0, concat_axis=0, axis_index_grou...  9.97 us
    pallas_call x2, Pallas kernels, down_product(): pl.pallas_call(functools.partial(down_kernel, len(down)), out_shape=jax.S...  7.84 us
    pallas_call x2, Pallas kernels, prepare(): pl.pallas_call(prepare_kernel, out_shape=jax.ShapeDtypeStruct((CHIPS, ES...  4.33 us
  transfers between devices with their start and end apart: 18, of which 10 were waited for; matrix products, arithmetic and copies ran while one was open for 1% of the time, Pallas kernels for 14%

profile of v6, /device:TPU:8, one launch (start us, length us, event | category | flops | bytes accessed | tf_op | source)
XLA Modules:
  0.0 151.9 jit_solution(4776758802016780842)
XLA Ops:
  0.6 0.0 copy-start.1
  0.6 1.2 copy-done.1
  1.8 0.7 copy-done.7
  2.5 0.7 copy-done.9
  3.2 2.2 %shard_map.113 = bf16[16,72,896]{2,1,0:T(8,128)(2,1)} custom-call(bf16[128,3584]{1,0:T(8,128)(2,1)S(1)} %bitcast.17, s32[1,128]{1,0:T(1,128)S(1)} %bitcast.21, f32[1,3584]{1,0:T(1,128)S(1)} %copy-done.7), custom_call_target="tpu_custom_call" | custom-call | flops 176160768 | bytes 3670016 | tf_op jit(solution)/shard_map/pallas_call | solution.py:72
  5.3 7.5 %all-to-all-start = ((bf16[16,72,896]{2,1,0:T(8,128)(2,1)}), bf16[16,72,896]{2,1,0:T(8,128)(2,1)}, u32[]{:S(2)}, u32[]{:S(2)}) async-start(bf16[16,72,896]{2,1,0:T(8,128)(2,1)} %shard_map.113), calls=%async_computation | async-start | bytes 4128768 | tf_op jit(solution)/shard_map/all_to_all | solution.py:216
  12.9 0.0 copy-start.8
  12.9 0.0 copy-start.12
  12.9 0.1 collective-permute-start.1
  13.0 1.0 slice_bitcast_fusion
  14.0 5.9 %collective-permute-start = (bf16[128,3584]{1,0:T(8,128)(2,1)S(1)}, bf16[128,3584]{1,0:T(8,128)(2,1)S(1)}, u32[]{:S(2)}, u32[]{:S(2)}) collective-permute-start(bf16[128,3584]{1,0:T(8,128)(2,1)S(1)} %get-tuple-element.29), channel_id=1, source_target_pairs={{0,224},{32,0},{64,32},{96,64},{128,96},{160,128},{192,160},{224,1... | collective-permute-start | bytes 2752520 | tf_op jit(solution)/shard_map/ppermute | solution.py:203
  19.9 2.2 %shard_map.114 = bf16[16,72,896]{2,1,0:T(8,128)(2,1)} custom-call(bf16[128,3584]{1,0:T(8,128)(2,1)S(1)} %bitcast.19, s32[1,128]{1,0:T(1,128)S(1)} %bitcast.24, f32[1,3584]{1,0:T(1,128)S(1)} %copy-done.8), custom_call_target="tpu_custom_call" | custom-call | flops 176160768 | bytes 3670016 | tf_op jit(solution)/shard_map/pallas_call | solution.py:72
  22.1 18.1 %collective-permute-done.refs_0_ = bf16[128,3584]{1,0:T(8,128)(2,1)S(1)} collective-permute-done((bf16[128,3584]{1,0:T(8,128)(2,1)S(1)}, bf16[128,3584]{1,0:T(8,128)(2,1)S(1)}, u32[]{:S(2)}, u32[]{:S(2)}) %collective-permute-start) | collective-permute-done | bytes 917536 | tf_op jit(solution)/shard_map/ppermute | solution.py:203
  40.2 1.3 copy-done.3
  41.5 0.1 all-to-all-done.own_ref
  41.6 7.1 %all-to-all-start.1 = ((bf16[16,72,896]{2,1,0:T(8,128)(2,1)}), bf16[16,72,896]{2,1,0:T(8,128)(2,1)}, u32[]{:S(2)}, u32[]{:S(2)}) async-start(bf16[16,72,896]{2,1,0:T(8,128)(2,1)} %shard_map.114), calls=%async_computation.1 | async-start | bytes 4128768 | tf_op jit(solution)/shard_map/all_to_all | solution.py:216
  48.7 4.4 %collective-permute-start.4 = (bf16[128,3584]{1,0:T(8,128)(2,1)}, bf16[128,3584]{1,0:T(8,128)(2,1)}, u32[]{:S(2)}, u32[]{:S(2)}) collective-permute-start(bf16[128,3584]{1,0:T(8,128)(2,1)} %get-tuple-element.28), channel_id=1, source_target_pairs={{0,224},{32,0},{64,32},{96,64},{128,96},{160,128},{192,160},{224,1... | collective-permute-start | bytes 2752520 | tf_op jit(solution)/shard_map/ppermute | solution.py:203
  53.1 1.5 copy-done.13
  54.6 1.5 copy-done.15
  56.1 5.4 %shard_map.115 = (bf16[288,256]{1,0:T(8,128)(2,1)S(1)}, bf16[288,256]{1,0:T(8,128)(2,1)S(1)}) custom-call(bf16[16,72,896]{2,1,0:T(8,128)(2,1)} %all-to-all-done.own_ref, bf16[16,72,896]{2,1,0:T(8,128)(2,1)} %collective-permute-done.2.other_ref, bf16[3584,256]{1,0:T(8,128)(2,1)S(1)} %bitcast.26, bf16[3584,256]{1,0:T(8,128)(2,1)S(1)} %bitcast.28), custom_call_target="tpu_custom_call" | custom-call | flops 2113929216 | bytes 7798784 | tf_op jit(solution)/shard_map/pallas_call | solution.py:104
  61.5 0.1 collective-permute-start.3
  61.6 1.4 collective-permute-done.3.theirs_ref
  62.9 3.3 %shard_map.116 = bf16[16,72,896]{2,1,0:T(8,128)(2,1)} custom-call(bf16[288,256]{1,0:T(8,128)(2,1)S(1)} %get-tuple-element.17.mine_ref, bf16[288,256]{1,0:T(8,128)(2,1)S(1)} %collective-permute-done.3.theirs_ref, bf16[256,3584]{1,0:T(8,128)(2,1)S(1)} %bitcast.16, bf16[256,3584]{1,0:T(8,128)(2,1)S(1)} %copy-done.4), custom_call_target="tpu_custom_call" | custom-call | flops 1056964608 | bytes 5734400 | tf_op jit(solution)/shard_map/pallas_call | solution.py:144
  66.3 7.1 %collective-permute-done.4.refs_1_ = bf16[128,3584]{1,0:T(8,128)(2,1)} collective-permute-done((bf16[128,3584]{1,0:T(8,128)(2,1)}, bf16[128,3584]{1,0:T(8,128)(2,1)}, u32[]{:S(2)}, u32[]{:S(2)}) %collective-permute-start.4) | collective-permute-done | bytes 917536 | tf_op jit(solution)/shard_map/ppermute | solution.py:203
  73.4 4.4 %all-to-all-done.1.own_ref = bf16[16,72,896]{2,1,0:T(8,128)(2,1)} async-done(((bf16[16,72,896]{2,1,0:T(8,128)(2,1)}), bf16[16,72,896]{2,1,0:T(8,128)(2,1)}, u32[]{:S(2)}, u32[]{:S(2)}) %all-to-all-start.1) | async-done | bytes 2064416 | tf_op jit(solution)/shard_map/all_to_all | solution.py:216
  77.7 6.6 %all-to-all-start.2 = ((bf16[16,72,896]{2,1,0:T(8,128)(2,1)}), bf16[16,72,896]{2,1,0:T(8,128)(2,1)S(1)}, u32[]{:S(2)}, u32[]{:S(2)}) async-start(bf16[16,72,896]{2,1,0:T(8,128)(2,1)} %shard_map.116), calls=%async_computation.2 | async-start | bytes 4128768 | tf_op jit(solution)/shard_map/all_to_all | solution.py:216
  84.4 0.5 collective-permute-start.9
  84.9 1.5 copy-done.14
  86.4 1.5 copy-done.16
  87.9 5.3 %shard_map.117 = (bf16[288,256]{1,0:T(8,128)(2,1)S(1)}, bf16[288,256]{1,0:T(8,128)(2,1)S(1)}) custom-call(bf16[16,72,896]{2,1,0:T(8,128)(2,1)} %all-to-all-done.1.own_ref, bf16[16,72,896]{2,1,0:T(8,128)(2,1)} %collective-permute-done.5.other_ref, bf16[3584,256]{1,0:T(8,128)(2,1)S(1)} %bitcast.27, bf16[3584,256]{1,0:T(8,128)(2,1)S(1)} %bitcast.29), custom_call_target="tpu_custom_call" | custom-call | flops 2113929216 | bytes 7798784 | tf_op jit(solution)/shard_map/pallas_call | solution.py:104
  93.2 5.5 %collective-permute-start.6 = (bf16[288,256]{1,0:T(8,128)(2,1)S(1)}, bf16[288,256]{1,0:T(8,128)(2,1)S(1)}, u32[]{:S(2)}, u32[]{:S(2)}) collective-permute-start(bf16[288,256]{1,0:T(8,128)(2,1)S(1)} %get-tuple-element.22), channel_id=1, source_target_pairs={{0,224},{32,0},{64,32},{96,64},{128,96},{160,128},{192,160},{224,1... | collective-permute-start | bytes 442376 | tf_op jit(solution)/shard_map/ppermute | solution.py:203
  98.6 0.6 collective-permute-start.7
  99.2 3.6 %collective-permute-done.6.mine_ref = bf16[288,256]{1,0:T(8,128)(2,1)S(1)} collective-permute-done((bf16[288,256]{1,0:T(8,128)(2,1)S(1)}, bf16[288,256]{1,0:T(8,128)(2,1)S(1)}, u32[]{:S(2)}, u32[]{:S(2)}) %collective-permute-start.6) | collective-permute-done | bytes 147488 | tf_op jit(solution)/shard_map/ppermute | solution.py:203
  102.8 2.5 %collective-permute-done.7.theirs_ref = bf16[288,256]{1,0:T(8,128)(2,1)S(1)} collective-permute-done((bf16[288,256]{1,0:T(8,128)(2,1)S(1)}, bf16[288,256]{1,0:T(8,128)(2,1)S(1)}, u32[]{:S(2)}, u32[]{:S(2)}) %collective-permute-start.7) | collective-permute-done | bytes 147488 | tf_op jit(solution)/shard_map/ppermute | solution.py:211
  105.3 4.5 %shard_map.118 = bf16[16,72,896]{2,1,0:T(8,128)(2,1)} custom-call(bf16[288,256]{1,0:T(8,128)(2,1)S(1)} %collective-permute-done.6.mine_ref, bf16[288,256]{1,0:T(8,128)(2,1)S(1)} %collective-permute-done.7.theirs_ref, bf16[128,3584]{1,0:T(8,128)(2,1)S(1)} %collective-permute-done.refs_0_, bf16[128,3584]{1,0:T(8,128)(2,1)} %collective-permute-done.4.refs_1_, ...), custom_call_target="tpu_custom_call" | custom-call | flops 1056964608 | bytes 5734400 | tf_op jit(solution)/shard_map/pallas_call | solution.py:144
  109.8 3.5 %all-to-all-done.2.back_ref = bf16[16,72,896]{2,1,0:T(8,128)(2,1)S(1)} async-done(((bf16[16,72,896]{2,1,0:T(8,128)(2,1)}), bf16[16,72,896]{2,1,0:T(8,128)(2,1)S(1)}, u32[]{:S(2)}, u32[]{:S(2)}) %all-to-all-start.2) | async-done | bytes 2064416 | tf_op jit(solution)/shard_map/all_to_all | solution.py:216
  113.3 6.6 %all-to-all-start.3 = ((bf16[16,72,896]{2,1,0:T(8,128)(2,1)}), bf16[16,72,896]{2,1,0:T(8,128)(2,1)}, u32[]{:S(2)}, u32[]{:S(2)}) async-start(bf16[16,72,896]{2,1,0:T(8,128)(2,1)} %shard_map.118), calls=%async_computation.3 | async-start | bytes 4128768 | tf_op jit(solution)/shard_map/all_to_all | solution.py:216
  119.9 0.0 copy-start.6
  120.0 0.0 copy-start.17
  120.0 0.9 shard_map.119
  120.8 1.5 %collective-permute-start.10 = (bf16[128,3584]{1,0:T(8,128)(2,1)S(1)}, bf16[128,3584]{1,0:T(8,128)(2,1)S(1)}, u32[]{:S(2)}, u32[]{:S(2)}) collective-permute-start(bf16[128,3584]{1,0:T(8,128)(2,1)S(1)} %shard_map.119), channel_id=1, source_target_pairs={{0,32},{32,64},{64,96},{96,128},{128,160},{160,192},{192,224},{224... | collective-permute-start | bytes 2752520 | tf_op jit(solution)/shard_map/ppermute | solution.py:203
  122.4 4.1 %collective-permute-start.11 = (bf16[128,3584]{1,0:T(8,128)(2,1)S(1)}, bf16[128,3584]{1,0:T(8,128)(2,1)S(1)}, u32[]{:S(2)}, u32[]{:S(2)}) collective-permute-start(bf16[128,3584]{1,0:T(8,128)(2,1)S(1)} %bitcast.20), channel_id=1, source_target_pairs={{0,224},{32,0},{64,32},{96,64},{128,96},{160,128},{192,160},{224,1... | collective-permute-start | bytes 2752520 | tf_op jit(solution)/shard_map/ppermute | solution.py:203
  126.5 1.8 %collective-permute-start.12 = (s32[1,128]{1,0:T(1,128)S(1)}, s32[1,128]{1,0:T(1,128)S(1)}, u32[]{:S(2)}, u32[]{:S(2)}) collective-permute-start(s32[1,128]{1,0:T(1,128)S(1)} %bitcast.25), channel_id=1, source_target_pairs={{0,224},{32,0},{64,32},{96,64},{128,96},{160,128},{192,160},{224,1... | collective-permute-start | bytes 1544 | tf_op jit(solution)/shard_map/ppermute | solution.py:203
  128.3 1.0 collective-permute-start.13
  129.4 16.3 %collective-permute-done.10 = bf16[128,3584]{1,0:T(8,128)(2,1)S(1)} collective-permute-done((bf16[128,3584]{1,0:T(8,128)(2,1)S(1)}, bf16[128,3584]{1,0:T(8,128)(2,1)S(1)}, u32[]{:S(2)}, u32[]{:S(2)}) %collective-permute-start.10) | collective-permute-done | bytes 917536 | tf_op jit(solution)/shard_map/ppermute | solution.py:203
  145.6 2.0 %all-to-all-done.3.back_ref = bf16[16,72,896]{2,1,0:T(8,128)(2,1)} async-done(((bf16[16,72,896]{2,1,0:T(8,128)(2,1)}), bf16[16,72,896]{2,1,0:T(8,128)(2,1)}, u32[]{:S(2)}, u32[]{:S(2)}) %all-to-all-start.3) | async-done | bytes 2064416 | tf_op jit(solution)/shard_map/all_to_all | solution.py:216
  147.6 3.4 %shard_map.120 = bf16[128,3584]{1,0:T(8,128)(2,1)} custom-call(bf16[128,3584]{1,0:T(8,128)(2,1)S(1)} %collective-permute-done.11.current_ref, bf16[16,72,896]{2,1,0:T(8,128)(2,1)} %all-to-all-done.3.back_ref, s32[1,128]{1,0:T(1,128)S(1)} %collective-permute-done.12.ids_ref, f32[1,128]{1,0:T(1,128)S(1)} %collective-permute-done.13.scores_ref), custom_call_target="tpu_custom_call" | custom-call | flops 352321536 | bytes 3670016 | tf_op jit(solution)/shard_map/pallas_call | solution.py:185
  151.0 0.9 copy.13
  (34 shorter events, 0.1 us)
Async XLA Ops:
  0.6 1.2 copy-start.1
  1.8 0.7 copy-start.7
  2.5 0.7 copy-start.9
  5.3 7.6 %copy-start = (bf16[1,256,3584]{2,1,0:T(8,128)(2,1)S(1)}, bf16[1,256,3584]{2,1,0:T(8,128)(2,1)}, u32[]{:S(2)}) copy-start(bf16[1,256,3584]{2,1,0:T(8,128)(2,1)} %param.19) | copy-start | bytes 5505028
  5.3 36.2 %all-to-all-start = ((bf16[16,72,896]{2,1,0:T(8,128)(2,1)}), bf16[16,72,896]{2,1,0:T(8,128)(2,1)}, u32[]{:S(2)}, u32[]{:S(2)}) async-start(bf16[16,72,896]{2,1,0:T(8,128)(2,1)} %shard_map.113), calls=%async_computation | async-start | bytes 4128768 | tf_op jit(solution)/shard_map/all_to_all | solution.py:216
  12.9 7.0 %copy-start.5 = (bf16[1,128,3584]{2,1,0:T(8,128)(2,1)S(1)}, bf16[1,128,3584]{2,1,0:T(8,128)(2,1)}, u32[]{:S(2)}) copy-start(bf16[1,128,3584]{2,1,0:T(8,128)(2,1)} %param.11) | copy-start | bytes 2752516
  12.9 7.0 %copy-start.8 = (f32[1,3584]{1,0:T(1,128)S(1)}, f32[1,3584]{1,0:T(1,128)}, u32[]{:S(2)}) copy-start(f32[1,3584]{1,0:T(1,128)} %gain_ref.3) | copy-start | bytes 43012
  12.9 7.0 %copy-start.12 = (s32[1,1,128,1]{2,3,1,0:T(1,128)S(1)}, s32[1,1,128,1]{2,3,1,0:T(1,128)}, u32[]{:S(2)}) copy-start(s32[1,1,128,1]{2,3,1,0:T(1,128)} %param.13) | copy-start | bytes 1540
  12.9 27.3 %collective-permute-start.1 = (bf16[256,3584]{1,0:T(8,128)(2,1)S(1)}, bf16[256,3584]{1,0:T(8,128)(2,1)S(1)}, u32[]{:S(2)}, u32[]{:S(2)}) collective-permute-start(bf16[256,3584]{1,0:T(8,128)(2,1)S(1)} %bitcast.15), channel_id=1, source_target_pairs={{0,1},{1,0},{2,3},{3,2},{4,5},{5,4},{6,7},{7,6},{8,9},{9,8},{10,11... | collective-permute-start | bytes 5505032 | tf_op jit(solution)/shard_map/ppermute | solution.py:198
  14.0 26.1 %collective-permute-start = (bf16[128,3584]{1,0:T(8,128)(2,1)S(1)}, bf16[128,3584]{1,0:T(8,128)(2,1)S(1)}, u32[]{:S(2)}, u32[]{:S(2)}) collective-permute-start(bf16[128,3584]{1,0:T(8,128)(2,1)S(1)} %get-tuple-element.29), channel_id=1, source_target_pairs={{0,224},{32,0},{64,32},{96,64},{128,96},{160,128},{192,160},{224,1... | collective-permute-start | bytes 2752520 | tf_op jit(solution)/shard_map/ppermute | solution.py:203
  40.2 1.3 copy-start.3
  41.6 11.5 %collective-permute-start.2 = (bf16[16,72,896]{2,1,0:T(8,128)(2,1)}, bf16[16,72,896]{2,1,0:T(8,128)(2,1)}, u32[]{:S(2)}, u32[]{:S(2)}) collective-permute-start(bf16[16,72,896]{2,1,0:T(8,128)(2,1)} %all-to-all-done.own_ref), channel_id=1, source_target_pairs={{0,1},{1,0},{2,3},{3,2},{4,5},{5,4},{6,7},{7,6},{8,9},{9,8},{10,11... | collective-permute-start | bytes 6193160 | tf_op jit(solution)/shard_map/ppermute | solution.py:198
  41.6 36.2 %all-to-all-start.1 = ((bf16[16,72,896]{2,1,0:T(8,128)(2,1)}), bf16[16,72,896]{2,1,0:T(8,128)(2,1)}, u32[]{:S(2)}, u32[]{:S(2)}) async-start(bf16[16,72,896]{2,1,0:T(8,128)(2,1)} %shard_map.114), calls=%async_computation.1 | async-start | bytes 4128768 | tf_op jit(solution)/shard_map/all_to_all | solution.py:216
  48.7 24.7 %collective-permute-start.4 = (bf16[128,3584]{1,0:T(8,128)(2,1)}, bf16[128,3584]{1,0:T(8,128)(2,1)}, u32[]{:S(2)}, u32[]{:S(2)}) collective-permute-start(bf16[128,3584]{1,0:T(8,128)(2,1)} %get-tuple-element.28), channel_id=1, source_target_pairs={{0,224},{32,0},{64,32},{96,64},{128,96},{160,128},{192,160},{224,1... | collective-permute-start | bytes 2752520 | tf_op jit(solution)/shard_map/ppermute | solution.py:203
  53.1 1.5 copy-start.13
  54.6 1.5 copy-start.15
  56.1 6.9 %copy-start.4 = (bf16[256,3584]{1,0:T(8,128)(2,1)S(1)}, bf16[256,3584]{1,0:T(8,128)(2,1)}, u32[]{:S(2)}) copy-start(bf16[256,3584]{1,0:T(8,128)(2,1)} %copy-done.3) | copy-start | bytes 5505028
  61.5 1.5 collective-permute-start.3
  77.7 7.1 %collective-permute-start.5 = (bf16[16,72,896]{2,1,0:T(8,128)(2,1)}, bf16[16,72,896]{2,1,0:T(8,128)(2,1)}, u32[]{:S(2)}, u32[]{:S(2)}) collective-permute-start(bf16[16,72,896]{2,1,0:T(8,128)(2,1)} %all-to-all-done.1.own_ref), channel_id=1, source_target_pairs={{0,1},{1,0},{2,3},{3,2},{4,5},{5,4},{6,7},{7,6},{8,9},{9,8},{10,11... | collective-permute-start | bytes 6193160 | tf_op jit(solution)/shard_map/ppermute | solution.py:198
  77.7 35.6 %all-to-all-start.2 = ((bf16[16,72,896]{2,1,0:T(8,128)(2,1)}), bf16[16,72,896]{2,1,0:T(8,128)(2,1)S(1)}, u32[]{:S(2)}, u32[]{:S(2)}) async-start(bf16[16,72,896]{2,1,0:T(8,128)(2,1)} %shard_map.116), calls=%async_computation.2 | async-start | bytes 4128768 | tf_op jit(solution)/shard_map/all_to_all | solution.py:216
  84.4 14.9 %collective-permute-start.8 = (bf16[128,3584]{1,0:T(8,128)(2,1)S(1)}, bf16[128,3584]{1,0:T(8,128)(2,1)S(1)}, u32[]{:S(2)}, u32[]{:S(2)}) collective-permute-start(bf16[128,3584]{1,0:T(8,128)(2,1)S(1)} %collective-permute-done.refs_0_), channel_id=1, source_target_pairs={{0,1},{1,0},{2,3},{3,2},{4,5},{5,4},{6,7},{7,6},{8,9},{9,8},{10,11... | collective-permute-start | bytes 2752520 | tf_op jit(solution)/shard_map/ppermute | solution.py:198
  84.4 14.9 %collective-permute-start.9 = (bf16[128,3584]{1,0:T(8,128)(2,1)}, bf16[128,3584]{1,0:T(8,128)(2,1)S(1)}, u32[]{:S(2)}, u32[]{:S(2)}) collective-permute-start(bf16[128,3584]{1,0:T(8,128)(2,1)} %collective-permute-done.4.refs_1_), channel_id=1, source_target_pairs={{0,1},{1,0},{2,3},{3,2},{4,5},{5,4},{6,7},{7,6},{8,9},{9,8},{10,11... | collective-permute-start | bytes 2752520 | tf_op jit(solution)/shard_map/ppermute | solution.py:198
  84.9 1.5 copy-start.14
  86.4 1.5 copy-start.16
  93.2 9.7 %collective-permute-start.6 = (bf16[288,256]{1,0:T(8,128)(2,1)S(1)}, bf16[288,256]{1,0:T(8,128)(2,1)S(1)}, u32[]{:S(2)}, u32[]{:S(2)}) collective-permute-start(bf16[288,256]{1,0:T(8,128)(2,1)S(1)} %get-tuple-element.22), channel_id=1, source_target_pairs={{0,224},{32,0},{64,32},{96,64},{128,96},{160,128},{192,160},{224,1... | collective-permute-start | bytes 442376 | tf_op jit(solution)/shard_map/ppermute | solution.py:203
  98.6 6.7 %collective-permute-start.7 = (bf16[288,256]{1,0:T(8,128)(2,1)S(1)}, bf16[288,256]{1,0:T(8,128)(2,1)S(1)}, u32[]{:S(2)}, u32[]{:S(2)}) collective-permute-start(bf16[288,256]{1,0:T(8,128)(2,1)S(1)} %get-tuple-element.23), channel_id=1, source_target_pairs={{0,225},{1,224},{2,227},{3,226},{4,229},{5,228},{6,231},{7,230},{8... | collective-permute-start | bytes 442376 | tf_op jit(solution)/shard_map/ppermute | solution.py:211
  109.8 10.1 %copy-start.2 = (bf16[1,128,3584]{2,1,0:T(8,128)(2,1)S(1)}, bf16[1,128,3584]{2,1,0:T(8,128)(2,1)}, u32[]{:S(2)}) copy-start(bf16[1,128,3584]{2,1,0:T(8,128)(2,1)} %param.10) | copy-start | bytes 2752516
  109.8 10.1 %copy-start.10 = (s32[1,1,128,1]{2,3,1,0:T(1,128)S(1)}, s32[1,1,128,1]{2,3,1,0:T(1,128)}, u32[]{:S(2)}) copy-start(s32[1,1,128,1]{2,3,1,0:T(1,128)} %param.12) | copy-start | bytes 1540
  109.8 10.1 %copy-start.11 = (f32[1,1,128,1]{2,3,1,0:T(1,128)S(1)}, f32[1,1,128,1]{2,3,1,0:T(1,128)}, u32[]{:S(2)}) copy-start(f32[1,1,128,1]{2,3,1,0:T(1,128)} %param.14) | copy-start | bytes 1540
  113.3 34.3 %all-to-all-start.3 = ((bf16[16,72,896]{2,1,0:T(8,128)(2,1)}), bf16[16,72,896]{2,1,0:T(8,128)(2,1)}, u32[]{:S(2)}, u32[]{:S(2)}) async-start(bf16[16,72,896]{2,1,0:T(8,128)(2,1)} %shard_map.118), calls=%async_computation.3 | async-start | bytes 4128768 | tf_op jit(solution)/shard_map/all_to_all | solution.py:216
  119.9 2.4 %copy-start.6 = (bf16[1,128,3584]{2,1,0:T(8,128)(2,1)S(1)}, bf16[1,128,3584]{2,1,0:T(8,128)(2,1)}, u32[]{:S(2)}) copy-start(bf16[1,128,3584]{2,1,0:T(8,128)(2,1)} %param.11) | copy-start | bytes 2752516
  120.0 8.4 %copy-start.17 = (f32[1,1,128,1]{2,3,1,0:T(1,128)S(1)}, f32[1,1,128,1]{2,3,1,0:T(1,128)}, u32[]{:S(2)}) copy-start(f32[1,1,128,1]{2,3,1,0:T(1,128)} %param.15) | copy-start | bytes 1540
  120.8 24.8 %collective-permute-start.10 = (bf16[128,3584]{1,0:T(8,128)(2,1)S(1)}, bf16[128,3584]{1,0:T(8,128)(2,1)S(1)}, u32[]{:S(2)}, u32[]{:S(2)}) collective-permute-start(bf16[128,3584]{1,0:T(8,128)(2,1)S(1)} %shard_map.119), channel_id=1, source_target_pairs={{0,32},{32,64},{64,96},{96,128},{128,160},{160,192},{192,224},{224... | collective-permute-start | bytes 2752520 | tf_op jit(solution)/shard_map/ppermute | solution.py:203
  122.4 23.3 %collective-permute-start.11 = (bf16[128,3584]{1,0:T(8,128)(2,1)S(1)}, bf16[128,3584]{1,0:T(8,128)(2,1)S(1)}, u32[]{:S(2)}, u32[]{:S(2)}) collective-permute-start(bf16[128,3584]{1,0:T(8,128)(2,1)S(1)} %bitcast.20), channel_id=1, source_target_pairs={{0,224},{32,0},{64,32},{96,64},{128,96},{160,128},{192,160},{224,1... | collective-permute-start | bytes 2752520 | tf_op jit(solution)/shard_map/ppermute | solution.py:203
  126.5 19.1 %collective-permute-start.12 = (s32[1,128]{1,0:T(1,128)S(1)}, s32[1,128]{1,0:T(1,128)S(1)}, u32[]{:S(2)}, u32[]{:S(2)}) collective-permute-start(s32[1,128]{1,0:T(1,128)S(1)} %bitcast.25), channel_id=1, source_target_pairs={{0,224},{32,0},{64,32},{96,64},{128,96},{160,128},{192,160},{224,1... | collective-permute-start | bytes 1544 | tf_op jit(solution)/shard_map/ppermute | solution.py:203
  128.3 17.3 %collective-permute-start.13 = (f32[1,128]{1,0:T(1,128)S(1)}, f32[1,128]{1,0:T(1,128)S(1)}, u32[]{:S(2)}, u32[]{:S(2)}) collective-permute-start(f32[1,128]{1,0:T(1,128)S(1)} %bitcast.32), channel_id=1, source_target_pairs={{0,224},{32,0},{64,32},{96,64},{128,96},{160,128},{192,160},{224,1... | collective-permute-start | bytes 1544 | tf_op jit(solution)/shard_map/ppermute | solution.py:203

commit v7 on v6

--- a/solution.py
+++ b/solution.py
@@ -17,6 +17,7 @@
 F32 = jnp.float32
 BF16 = jnp.bfloat16
 VMEM_LIMIT = 48 * 1024 * 1024
+VMEM_WHOLE = 64 * 1024 * 1024 - 512 * 1024
 
 
 def iota(shape, axis):
@@ -33,9 +34,18 @@
     return jnp.dot(left, right, preferred_element_type=F32)
 
 
-def prepare_kernel(current_ref, ids_ref, gain_ref, send_ref):
+def prepare_kernel(current_hbm, ids_hbm, gain_hbm, send_ref, current_ref, ids_ref, gain_ref, ready):
+    loads = [
+        pltpu.make_async_copy(source, target, ready.at[place])
+        for place, (source, target) in enumerate(
+            ((ids_hbm, ids_ref), (current_hbm, current_ref), (gain_hbm, gain_ref))
+        )
+    ]
+    for load in loads:
+        load.start()
     tokens, features = current_ref.shape
     quarter = features // ES
+    loads[0].wait()
     ids_row = ids_ref[...]
     ids_column = to_column(ids_row)
     same = ids_column == ids_row
@@ -44,6 +54,8 @@
     main_row = jnp.where(slot_row < MAIN, ids_row * MAIN + slot_row, -1)
     last_row = jnp.where(slot_row < MAIN, -1, ids_row * (ES * LAST) + slot_row - MAIN)
     pick_main = (iota((EXPERTS * MAIN, tokens), 0) == main_row).astype(BF16)
+    loads[1].wait()
+    loads[2].wait()
     as_float = current_ref[...].astype(F32)
     inverse_rms = lax.rsqrt(jnp.mean(as_float * as_float, axis=-1, keepdims=True) + EPSILON)
     last = jnp.zeros((EXPERTS * ES * LAST, quarter), F32)
@@ -72,7 +84,14 @@
     return pl.pallas_call(
         prepare_kernel,
         out_shape=jax.ShapeDtypeStruct((CHIPS, ES * (MAIN + LAST), quarter), BF16),
-        compiler_params=pltpu.CompilerParams(vmem_limit_bytes=VMEM_LIMIT),
+        in_specs=[pl.BlockSpec(memory_space=pltpu.HBM)] * 3,
+        scratch_shapes=[
+            pltpu.VMEM(current.shape, current.dtype),
+            pltpu.VMEM(ids_row.shape, ids_row.dtype),
+            pltpu.VMEM(gain.shape, gain.dtype),
+            pltpu.SemaphoreType.DMA((3,)),
+        ],
+        compiler_params=pltpu.CompilerParams(vmem_limit_bytes=VMEM_WHOLE),
         cost_estimate=pl.CostEstimate(
             flops=3 * tokens * tokens * features, bytes_accessed=8 * tokens * features, transcendentals=0
         ),
@@ -194,6 +213,19 @@
     )(current, back, ids_row, scores_row)
 
 
+def settle_kernel(value_ref, out_ref):
+    out_ref[...] = value_ref[...]
+
+
+def settle(value):
+    return pl.pallas_call(
+        settle_kernel,
+        out_shape=jax.ShapeDtypeStruct(value.shape, value.dtype),
+        compiler_params=pltpu.CompilerParams(vmem_limit_bytes=VMEM_LIMIT),
+        cost_estimate=pl.CostEstimate(flops=0, bytes_accessed=4 * value.size, transcendentals=0),
+    )(value)
+
+
 def swap_cores(value):
     return lax.ppermute(value, "ep", [(i, i ^ 1) for i in range(EP)])
 
@@ -228,25 +260,28 @@
     gate_cols, up_cols, down = w_gate[0], w_up[0], w_down[0]
 
     own_a = exchange(prepare(current_a, ids_a, norm_gain))
-    send_b = prepare(current_b, ids_b, norm_gain)
-    middle = down.shape[0] // 2
-    upper = from_behind(down[:middle], -1)
     other_down = swap_cores(down)
-    own_a, send_b, upper, other_down = lax.optimization_barrier((own_a, send_b, upper, other_down))
+    staged_b, other_down = lax.optimization_barrier((current_b, other_down))
+    send_b = prepare(staged_b, ids_b, norm_gain)
+    upper = from_behind(down[:96], -1)
+    own_a, send_b, upper = lax.optimization_barrier((own_a, send_b, upper))
     own_b = exchange(send_b)
 
-    lower = from_behind(down[middle:], -1)
+    middle = from_behind(down[96:208], -1)
     mine_a, give_a = hidden_units(own_a, swap_cores(own_a), gate_cols, up_cols)
     back_a = down_product(mine_a, swap_cores(give_a), [down], [other_down])
-    own_b, back_a, lower = lax.optimization_barrier((own_b, back_a, lower))
+    own_b, back_a, middle = lax.optimization_barrier((own_b, back_a, middle))
 
     returned_a = exchange(back_a)
+    lower = from_behind(down[208:], -1)
     mine_b, give_b = hidden_units(own_b, swap_cores(own_b), gate_cols, up_cols)
+    mine_b, give_b, lower = lax.optimization_barrier((mine_b, give_b, lower))
+    moved_down = [upper, middle, lower]
     back_b = down_product(
         from_behind(mine_b, -1),
         behind_other_core(give_b, -1),
-        [upper, lower],
-        [swap_cores(upper), swap_cores(lower)],
+        moved_down,
+        [swap_cores(piece) for piece in moved_down],
     )
     moved_b, moved_ids, moved_marks = [
         from_behind(value, -1) for value in (current_b, ids_b, marks_b)
@@ -254,7 +289,7 @@
 
     marks_a, back_b = lax.optimization_barrier((marks_a, back_b))
     returned_b = exchange(back_b)
-    updated_a = from_behind(finish(current_a, returned_a, ids_a, marks_a), 1)
+    updated_a = settle(from_behind(finish(current_a, returned_a, ids_a, marks_a), 1))
     updated_b = finish(moved_b, returned_b, moved_ids, moved_marks)
     return (updated_a[None], updated_b[None])
 

time: 153 us -> 152 us (level)
  waiting for transfers between devices: 58.9 us -> 54.9 us
  Pallas kernels: 27.1 us -> 30.4 us
  starting transfers between devices: 53.4 us -> 56.4 us
  local copies, waits for them, and re-layouts: 11.8 us -> 9.34 us
    ppermute x7 -> x8, waiting for transfers between devices: 45 us -> 36.1 us  [from_behind(): lax.ppermute(value, 'section', [(i, (i + steps) % count) for i in range(c...]
    all_to_all x4, waiting for transfers between devices: 9.97 us -> 14.6 us  [exchange(): lax.all_to_all(blocks, 'ep', split_axis=0, concat_axis=0, axis_index_grou...]
    unnamed x37 -> x28, local copies, waits for them, and re-layouts: 10.8 us -> 7.38 us
    ppermute x7 -> x8, starting transfers between devices: 24.2 us -> 27.6 us  [from_behind(): lax.ppermute(value, 'section', [(i, (i + steps) % count) for i in range(c...]
    pallas_call x2, Pallas kernels: 4.33 us -> 6.76 us  [prepare(): pl.pallas_call(prepare_kernel, out_shape=jax.ShapeDtypeStruct((CHIPS, ES...]
  transfers between devices with their start and end apart: 18 -> 20, of which waited for: 10 -> 9; matrix products, arithmetic and copies ran while one was open for 1% -> 1% of each run, Pallas kernels for 14% -> 16%
where the time goes in v7:
time: 152 us
  starting transfers between devices  56.4 us (37%)
  waiting for transfers between devices  54.9 us (36%)
  Pallas kernels  30.4 us (20%)
  local copies, waits for them, and re-layouts  9.34 us (6%)
    ppermute x8, waiting for transfers between devices, from_behind(): lax.ppermute(value, 'section', [(i, (i + steps) % count) for i in range(c...  36.1 us
    all_to_all x4, starting transfers between devices, exchange(): lax.all_to_all(blocks, 'ep', split_axis=0, concat_axis=0, axis_index_grou...  27.9 us
    ppermute x8, starting transfers between devices, from_behind(): lax.ppermute(value, 'section', [(i, (i + steps) % count) for i in range(c...  27.6 us
    all_to_all x4, waiting for transfers between devices, exchange(): lax.all_to_all(blocks, 'ep', split_axis=0, concat_axis=0, axis_index_grou...  14.6 us
    pallas_call x2, Pallas kernels, hidden_units(): pl.pallas_call(hidden_kernel, out_shape=[jax.ShapeDtypeStruct((count, wid...  10.7 us
    pallas_call x2, Pallas kernels, down_product(): pl.pallas_call(functools.partial(down_kernel, len(down)), out_shape=jax.S...  7.7 us
    unnamed x28, local copies, waits for them, and re-layouts  7.38 us
    pallas_call x2, Pallas kernels, prepare(): pl.pallas_call(prepare_kernel, out_shape=jax.ShapeDtypeStruct((CHIPS, ES...  6.76 us
  transfers between devices with their start and end apart: 20, of which 9 were waited for; matrix products, arithmetic and copies ran while one was open for 1% of the time, Pallas kernels for 16%

profile of v7, /device:TPU:8, one launch (start us, length us, event | category | flops | bytes accessed | tf_op | source)
XLA Modules:
  0.0 151.8 jit_solution(8654898013056120123)
XLA Ops:
  0.6 3.4 %shard_map.113 = bf16[16,72,896]{2,1,0:T(8,128)(2,1)} custom-call(bf16[128,3584]{1,0:T(8,128)(2,1)} %bitcast.19, s32[1,128]{1,0:T(1,128)} %bitcast.21, f32[1,3584]{1,0:T(1,128)} %gain_hbm.3), custom_call_target="tpu_custom_call" | custom-call | flops 176160768 | bytes 3670016 | tf_op jit(solution)/shard_map/pallas_call | solution.py:84
  4.0 0.0 copy-start
  4.0 7.5 %all-to-all-start = ((bf16[16,72,896]{2,1,0:T(8,128)(2,1)}), bf16[16,72,896]{2,1,0:T(8,128)(2,1)}, u32[]{:S(2)}, u32[]{:S(2)}) async-start(bf16[16,72,896]{2,1,0:T(8,128)(2,1)} %shard_map.113), calls=%async_computation | async-start | bytes 4128768 | tf_op jit(solution)/shard_map/all_to_all | solution.py:248
  11.6 0.1 collective-permute-start
  11.7 0.9 slice_bitcast_fusion.1
  12.6 5.9 %collective-permute-start.1 = (bf16[96,3584]{1,0:T(8,128)(2,1)}, bf16[96,3584]{1,0:T(8,128)(2,1)}, u32[]{:S(2)}, u32[]{:S(2)}) collective-permute-start(bf16[96,3584]{1,0:T(8,128)(2,1)} %slice_bitcast_fusion.1), channel_id=1, source_target_pairs={{0,224},{32,0},{64,32},{96,64},{128,96},{160,128},{192,160},{224,1... | collective-permute-start | bytes 2064392 | tf_op jit(solution)/shard_map/ppermute | solution.py:235
  18.4 1.3 copy-done.3
  19.7 3.4 %shard_map.114 = bf16[16,72,896]{2,1,0:T(8,128)(2,1)} custom-call(bf16[128,3584]{1,0:T(8,128)(2,1)} %bitcast.29, s32[1,128]{1,0:T(1,128)} %bitcast.32, f32[1,3584]{1,0:T(1,128)} %gain_hbm.3), custom_call_target="tpu_custom_call" | custom-call | flops 176160768 | bytes 3670016 | tf_op jit(solution)/shard_map/pallas_call | solution.py:84
  23.1 0.0 copy-start.1
  23.1 11.0 %collective-permute-done.1.refs_0_ = bf16[96,3584]{1,0:T(8,128)(2,1)} collective-permute-done((bf16[96,3584]{1,0:T(8,128)(2,1)}, bf16[96,3584]{1,0:T(8,128)(2,1)}, u32[]{:S(2)}, u32[]{:S(2)}) %collective-permute-start.1) | collective-permute-done | bytes 688160 | tf_op jit(solution)/shard_map/ppermute | solution.py:235
  34.1 6.2 %all-to-all-done.own_ref = bf16[16,72,896]{2,1,0:T(8,128)(2,1)} async-done(((bf16[16,72,896]{2,1,0:T(8,128)(2,1)}), bf16[16,72,896]{2,1,0:T(8,128)(2,1)}, u32[]{:S(2)}, u32[]{:S(2)}) %all-to-all-start) | async-done | bytes 2064416 | tf_op jit(solution)/shard_map/all_to_all | solution.py:248
  40.3 5.6 %all-to-all-start.1 = ((bf16[16,72,896]{2,1,0:T(8,128)(2,1)}), bf16[16,72,896]{2,1,0:T(8,128)(2,1)}, u32[]{:S(2)}, u32[]{:S(2)}) async-start(bf16[16,72,896]{2,1,0:T(8,128)(2,1)} %shard_map.114), calls=%async_computation.1 | async-start | bytes 4128768 | tf_op jit(solution)/shard_map/all_to_all | solution.py:248
  45.9 0.1 slice_bitcast_fusion
  46.0 5.9 %collective-permute-start.4 = (bf16[112,3584]{1,0:T(8,128)(2,1)S(1)}, bf16[112,3584]{1,0:T(8,128)(2,1)S(1)}, u32[]{:S(2)}, u32[]{:S(2)}) collective-permute-start(bf16[112,3584]{1,0:T(8,128)(2,1)S(1)} %slice_bitcast_fusion), channel_id=1, source_target_pairs={{0,224},{32,0},{64,32},{96,64},{128,96},{160,128},{192,160},{224,1... | collective-permute-start | bytes 2408456 | tf_op jit(solution)/shard_map/ppermute | solution.py:235
  51.9 1.5 copy-done.7
  53.4 1.5 copy-done.9
  54.9 5.4 %shard_map.115 = (bf16[288,256]{1,0:T(8,128)(2,1)S(1)}, bf16[288,256]{1,0:T(8,128)(2,1)S(1)}) custom-call(bf16[16,72,896]{2,1,0:T(8,128)(2,1)} %all-to-all-done.own_ref, bf16[16,72,896]{2,1,0:T(8,128)(2,1)} %collective-permute-done.2.other_ref, bf16[3584,256]{1,0:T(8,128)(2,1)S(1)} %bitcast.24, bf16[3584,256]{1,0:T(8,128)(2,1)S(1)} %bitcast.26), custom_call_target="tpu_custom_call" | custom-call | flops 2113929216 | bytes 7798784 | tf_op jit(solution)/shard_map/pallas_call | solution.py:123
  60.3 0.1 collective-permute-start.3
  60.4 1.4 collective-permute-done.3.theirs_ref
  61.8 3.3 %shard_map.116 = bf16[16,72,896]{2,1,0:T(8,128)(2,1)} custom-call(bf16[288,256]{1,0:T(8,128)(2,1)S(1)} %get-tuple-element.22.mine_ref, bf16[288,256]{1,0:T(8,128)(2,1)S(1)} %collective-permute-done.3.theirs_ref, bf16[256,3584]{1,0:T(8,128)(2,1)S(1)} %bitcast.18, bf16[256,3584]{1,0:T(8,128)(2,1)S(1)} %copy-done.4), custom_call_target="tpu_custom_call" | custom-call | flops 1056964608 | bytes 5734400 | tf_op jit(solution)/shard_map/pallas_call | solution.py:163
  65.1 4.4 %collective-permute-done.4.refs_1_ = bf16[112,3584]{1,0:T(8,128)(2,1)S(1)} collective-permute-done((bf16[112,3584]{1,0:T(8,128)(2,1)S(1)}, bf16[112,3584]{1,0:T(8,128)(2,1)S(1)}, u32[]{:S(2)}, u32[]{:S(2)}) %collective-permute-start.4) | collective-permute-done | bytes 802848 | tf_op jit(solution)/shard_map/ppermute | solution.py:235
  69.4 5.7 %all-to-all-done.1.own_ref = bf16[16,72,896]{2,1,0:T(8,128)(2,1)} async-done(((bf16[16,72,896]{2,1,0:T(8,128)(2,1)}), bf16[16,72,896]{2,1,0:T(8,128)(2,1)}, u32[]{:S(2)}, u32[]{:S(2)}) %all-to-all-start.1) | async-done | bytes 2064416 | tf_op jit(solution)/shard_map/all_to_all | solution.py:248
  75.2 7.4 %all-to-all-start.2 = ((bf16[16,72,896]{2,1,0:T(8,128)(2,1)}), bf16[16,72,896]{2,1,0:T(8,128)(2,1)S(1)}, u32[]{:S(2)}, u32[]{:S(2)}) async-start(bf16[16,72,896]{2,1,0:T(8,128)(2,1)} %shard_map.116), calls=%async_computation.2 | async-start | bytes 4128768 | tf_op jit(solution)/shard_map/all_to_all | solution.py:248
  82.6 1.0 slice_bitcast_fusion.2
  83.6 5.9 %collective-permute-start.6 = (bf16[48,3584]{1,0:T(8,128)(2,1)S(1)}, bf16[48,3584]{1,0:T(8,128)(2,1)S(1)}, u32[]{:S(2)}, u32[]{:S(2)}) collective-permute-start(bf16[48,3584]{1,0:T(8,128)(2,1)S(1)} %slice_bitcast_fusion.2), channel_id=1, source_target_pairs={{0,224},{32,0},{64,32},{96,64},{128,96},{160,128},{192,160},{224,1... | collective-permute-start | bytes 1032200 | tf_op jit(solution)/shard_map/ppermute | solution.py:235
  89.6 0.2 collective-permute-start.9
  89.8 1.5 copy-done.8
  91.3 1.5 copy-done.10
  92.8 5.3 %shard_map.117 = (bf16[288,256]{1,0:T(8,128)(2,1)S(1)}, bf16[288,256]{1,0:T(8,128)(2,1)S(1)}) custom-call(bf16[16,72,896]{2,1,0:T(8,128)(2,1)} %all-to-all-done.1.own_ref, bf16[16,72,896]{2,1,0:T(8,128)(2,1)} %collective-permute-done.5.other_ref, bf16[3584,256]{1,0:T(8,128)(2,1)S(1)} %bitcast.25, bf16[3584,256]{1,0:T(8,128)(2,1)S(1)} %bitcast.27), custom_call_target="tpu_custom_call" | custom-call | flops 2113929216 | bytes 7798784 | tf_op jit(solution)/shard_map/pallas_call | solution.py:123
  98.1 0.4 collective-permute-start.11
  98.5 2.8 %collective-permute-start.7 = (bf16[288,256]{1,0:T(8,128)(2,1)S(1)}, bf16[288,256]{1,0:T(8,128)(2,1)S(1)}, u32[]{:S(2)}, u32[]{:S(2)}) collective-permute-start(bf16[288,256]{1,0:T(8,128)(2,1)S(1)} %get-tuple-element.29), channel_id=1, source_target_pairs={{0,224},{32,0},{64,32},{96,64},{128,96},{160,128},{192,160},{224,1... | collective-permute-start | bytes 442376 | tf_op jit(solution)/shard_map/ppermute | solution.py:235
  101.2 0.1 collective-permute-start.8
  101.4 4.0 %collective-permute-done.7.mine_ref = bf16[288,256]{1,0:T(8,128)(2,1)S(1)} collective-permute-done((bf16[288,256]{1,0:T(8,128)(2,1)S(1)}, bf16[288,256]{1,0:T(8,128)(2,1)S(1)}, u32[]{:S(2)}, u32[]{:S(2)}) %collective-permute-start.7) | collective-permute-done | bytes 147488 | tf_op jit(solution)/shard_map/ppermute | solution.py:235
  105.4 2.8 %collective-permute-done.8.theirs_ref = bf16[288,256]{1,0:T(8,128)(2,1)S(1)} collective-permute-done((bf16[288,256]{1,0:T(8,128)(2,1)S(1)}, bf16[288,256]{1,0:T(8,128)(2,1)S(1)}, u32[]{:S(2)}, u32[]{:S(2)}) %collective-permute-start.8) | collective-permute-done | bytes 147488 | tf_op jit(solution)/shard_map/ppermute | solution.py:243
  108.2 4.4 %shard_map.118 = bf16[16,72,896]{2,1,0:T(8,128)(2,1)} custom-call(bf16[288,256]{1,0:T(8,128)(2,1)S(1)} %collective-permute-done.7.mine_ref, bf16[288,256]{1,0:T(8,128)(2,1)S(1)} %collective-permute-done.8.theirs_ref, bf16[96,3584]{1,0:T(8,128)(2,1)} %collective-permute-done.1.refs_0_, bf16[112,3584]{1,0:T(8,128)(2,1)S(1)} %collective-permute-done.4.refs_1_, ...), custom_call_target="tpu_custom_call" | custom-call | flops 1056964608 | bytes 5734400 | tf_op jit(solution)/shard_map/pallas_call | solution.py:163
  112.6 7.4 %all-to-all-start.3 = ((bf16[16,72,896]{2,1,0:T(8,128)(2,1)}), bf16[16,72,896]{2,1,0:T(8,128)(2,1)}, u32[]{:S(2)}, u32[]{:S(2)}) async-start(bf16[16,72,896]{2,1,0:T(8,128)(2,1)} %shard_map.118), calls=%async_computation.3 | async-start | bytes 4128768 | tf_op jit(solution)/shard_map/all_to_all | solution.py:248
  120.0 0.0 copy-start.11
  120.0 0.0 copy-start.12
  120.0 0.9 shard_map.119
  120.9 0.2 collective-permute-start.12
  121.1 0.1 copy-done.11
  121.2 4.0 %collective-permute-start.13 = (bf16[128,3584]{1,0:T(8,128)(2,1)S(1)}, bf16[128,3584]{1,0:T(8,128)(2,1)S(1)}, u32[]{:S(2)}, u32[]{:S(2)}) collective-permute-start(bf16[128,3584]{1,0:T(8,128)(2,1)S(1)} %bitcast.30), channel_id=1, source_target_pairs={{0,224},{32,0},{64,32},{96,64},{128,96},{160,128},{192,160},{224,1... | collective-permute-start | bytes 2752520 | tf_op jit(solution)/shard_map/ppermute | solution.py:235
  125.2 1.8 %collective-permute-start.14 = (s32[1,128]{1,0:T(1,128)S(1)}, s32[1,128]{1,0:T(1,128)S(1)}, u32[]{:S(2)}, u32[]{:S(2)}) collective-permute-start(s32[1,128]{1,0:T(1,128)S(1)} %bitcast.33), channel_id=1, source_target_pairs={{0,224},{32,0},{64,32},{96,64},{128,96},{160,128},{192,160},{224,1... | collective-permute-start | bytes 1544 | tf_op jit(solution)/shard_map/ppermute | solution.py:235
  127.1 1.0 collective-permute-start.15
  128.1 16.7 %collective-permute-done.12.value_ref = bf16[128,3584]{1,0:T(8,128)(2,1)S(1)} collective-permute-done((bf16[128,3584]{1,0:T(8,128)(2,1)S(1)}, bf16[128,3584]{1,0:T(8,128)(2,1)S(1)}, u32[]{:S(2)}, u32[]{:S(2)}) %collective-permute-start.12) | collective-permute-done | bytes 917536 | tf_op jit(solution)/shard_map/ppermute | solution.py:235
  144.8 1.0 shard_map.120
  145.8 2.7 %all-to-all-done.3.back_ref = bf16[16,72,896]{2,1,0:T(8,128)(2,1)} async-done(((bf16[16,72,896]{2,1,0:T(8,128)(2,1)}), bf16[16,72,896]{2,1,0:T(8,128)(2,1)}, u32[]{:S(2)}, u32[]{:S(2)}) %all-to-all-start.3) | async-done | bytes 2064416 | tf_op jit(solution)/shard_map/all_to_all | solution.py:248
  148.5 3.4 %shard_map.121 = bf16[128,3584]{1,0:T(8,128)(2,1)} custom-call(bf16[128,3584]{1,0:T(8,128)(2,1)S(1)} %collective-permute-done.13.current_ref, bf16[16,72,896]{2,1,0:T(8,128)(2,1)} %all-to-all-done.3.back_ref, s32[1,128]{1,0:T(1,128)S(1)} %collective-permute-done.14.ids_ref, f32[1,128]{1,0:T(1,128)S(1)} %collective-permute-done.15.scores_ref), custom_call_target="tpu_custom_call" | custom-call | flops 352321536 | bytes 3670016 | tf_op jit(solution)/shard_map/pallas_call | solution.py:204
  (32 shorter events, 0.1 us)
Async XLA Ops:
  4.0 7.5 %copy-start = (bf16[1,256,3584]{2,1,0:T(8,128)(2,1)S(1)}, bf16[1,256,3584]{2,1,0:T(8,128)(2,1)}, u32[]{:S(2)}) copy-start(bf16[1,256,3584]{2,1,0:T(8,128)(2,1)} %param.19) | copy-start | bytes 5505028
  4.0 36.2 %all-to-all-start = ((bf16[16,72,896]{2,1,0:T(8,128)(2,1)}), bf16[16,72,896]{2,1,0:T(8,128)(2,1)}, u32[]{:S(2)}, u32[]{:S(2)}) async-start(bf16[16,72,896]{2,1,0:T(8,128)(2,1)} %shard_map.113), calls=%async_computation | async-start | bytes 4128768 | tf_op jit(solution)/shard_map/all_to_all | solution.py:248
  11.6 6.9 %collective-permute-start = (bf16[256,3584]{1,0:T(8,128)(2,1)S(1)}, bf16[256,3584]{1,0:T(8,128)(2,1)S(1)}, u32[]{:S(2)}, u32[]{:S(2)}) collective-permute-start(bf16[256,3584]{1,0:T(8,128)(2,1)S(1)} %bitcast.17), channel_id=1, source_target_pairs={{0,1},{1,0},{2,3},{3,2},{4,5},{5,4},{6,7},{7,6},{8,9},{9,8},{10,11... | collective-permute-start | bytes 5505032 | tf_op jit(solution)/shard_map/ppermute | solution.py:230
  12.6 21.5 %collective-permute-start.1 = (bf16[96,3584]{1,0:T(8,128)(2,1)}, bf16[96,3584]{1,0:T(8,128)(2,1)}, u32[]{:S(2)}, u32[]{:S(2)}) collective-permute-start(bf16[96,3584]{1,0:T(8,128)(2,1)} %slice_bitcast_fusion.1), channel_id=1, source_target_pairs={{0,224},{32,0},{64,32},{96,64},{128,96},{160,128},{192,160},{224,1... | collective-permute-start | bytes 2064392 | tf_op jit(solution)/shard_map/ppermute | solution.py:235
  18.4 1.3 copy-start.3
  23.1 22.8 %copy-start.1 = (bf16[1,256,3584]{2,1,0:T(8,128)(2,1)S(1)}, bf16[1,256,3584]{2,1,0:T(8,128)(2,1)}, u32[]{:S(2)}) copy-start(bf16[1,256,3584]{2,1,0:T(8,128)(2,1)} %param.19) | copy-start | bytes 5505028
  40.3 11.6 %collective-permute-start.2 = (bf16[16,72,896]{2,1,0:T(8,128)(2,1)}, bf16[16,72,896]{2,1,0:T(8,128)(2,1)}, u32[]{:S(2)}, u32[]{:S(2)}) collective-permute-start(bf16[16,72,896]{2,1,0:T(8,128)(2,1)} %all-to-all-done.own_ref), channel_id=1, source_target_pairs={{0,1},{1,0},{2,3},{3,2},{4,5},{5,4},{6,7},{7,6},{8,9},{9,8},{10,11... | collective-permute-start | bytes 6193160 | tf_op jit(solution)/shard_map/ppermute | solution.py:230
  40.3 34.9 %all-to-all-start.1 = ((bf16[16,72,896]{2,1,0:T(8,128)(2,1)}), bf16[16,72,896]{2,1,0:T(8,128)(2,1)}, u32[]{:S(2)}, u32[]{:S(2)}) async-start(bf16[16,72,896]{2,1,0:T(8,128)(2,1)} %shard_map.114), calls=%async_computation.1 | async-start | bytes 4128768 | tf_op jit(solution)/shard_map/all_to_all | solution.py:248
  46.0 23.5 %collective-permute-start.4 = (bf16[112,3584]{1,0:T(8,128)(2,1)S(1)}, bf16[112,3584]{1,0:T(8,128)(2,1)S(1)}, u32[]{:S(2)}, u32[]{:S(2)}) collective-permute-start(bf16[112,3584]{1,0:T(8,128)(2,1)S(1)} %slice_bitcast_fusion), channel_id=1, source_target_pairs={{0,224},{32,0},{64,32},{96,64},{128,96},{160,128},{192,160},{224,1... | collective-permute-start | bytes 2408456 | tf_op jit(solution)/shard_map/ppermute | solution.py:235
  51.9 1.5 copy-start.7
  53.4 1.5 copy-start.9
  54.9 6.9 %copy-start.4 = (bf16[256,3584]{1,0:T(8,128)(2,1)S(1)}, bf16[256,3584]{1,0:T(8,128)(2,1)}, u32[]{:S(2)}) copy-start(bf16[256,3584]{1,0:T(8,128)(2,1)} %copy-done.3) | copy-start | bytes 5505028
  60.3 1.5 collective-permute-start.3
  75.2 14.6 %collective-permute-start.5 = (bf16[16,72,896]{2,1,0:T(8,128)(2,1)}, bf16[16,72,896]{2,1,0:T(8,128)(2,1)}, u32[]{:S(2)}, u32[]{:S(2)}) collective-permute-start(bf16[16,72,896]{2,1,0:T(8,128)(2,1)} %all-to-all-done.1.own_ref), channel_id=1, source_target_pairs={{0,1},{1,0},{2,3},{3,2},{4,5},{5,4},{6,7},{7,6},{8,9},{9,8},{10,11... | collective-permute-start | bytes 6193160 | tf_op jit(solution)/shard_map/ppermute | solution.py:230
  75.2 37.4 %all-to-all-start.2 = ((bf16[16,72,896]{2,1,0:T(8,128)(2,1)}), bf16[16,72,896]{2,1,0:T(8,128)(2,1)S(1)}, u32[]{:S(2)}, u32[]{:S(2)}) async-start(bf16[16,72,896]{2,1,0:T(8,128)(2,1)} %shard_map.116), calls=%async_computation.2 | async-start | bytes 4128768 | tf_op jit(solution)/shard_map/all_to_all | solution.py:248
  82.6 18.8 %collective-permute-start.10 = (bf16[112,3584]{1,0:T(8,128)(2,1)S(1)}, bf16[112,3584]{1,0:T(8,128)(2,1)S(1)}, u32[]{:S(2)}, u32[]{:S(2)}) collective-permute-start(bf16[112,3584]{1,0:T(8,128)(2,1)S(1)} %collective-permute-done.4.refs_1_), channel_id=1, source_target_pairs={{0,1},{1,0},{2,3},{3,2},{4,5},{5,4},{6,7},{7,6},{8,9},{9,8},{10,11... | collective-permute-start | bytes 2408456 | tf_op jit(solution)/shard_map/ppermute | solution.py:230
  83.6 14.4 %collective-permute-start.6 = (bf16[48,3584]{1,0:T(8,128)(2,1)S(1)}, bf16[48,3584]{1,0:T(8,128)(2,1)S(1)}, u32[]{:S(2)}, u32[]{:S(2)}) collective-permute-start(bf16[48,3584]{1,0:T(8,128)(2,1)S(1)} %slice_bitcast_fusion.2), channel_id=1, source_target_pairs={{0,224},{32,0},{64,32},{96,64},{128,96},{160,128},{192,160},{224,1... | collective-permute-start | bytes 1032200 | tf_op jit(solution)/shard_map/ppermute | solution.py:235
  89.6 11.8 %collective-permute-start.9 = (bf16[96,3584]{1,0:T(8,128)(2,1)}, bf16[96,3584]{1,0:T(8,128)(2,1)S(1)}, u32[]{:S(2)}, u32[]{:S(2)}) collective-permute-start(bf16[96,3584]{1,0:T(8,128)(2,1)} %collective-permute-done.1.refs_0_), channel_id=1, source_target_pairs={{0,1},{1,0},{2,3},{3,2},{4,5},{5,4},{6,7},{7,6},{8,9},{9,8},{10,11... | collective-permute-start | bytes 2064392 | tf_op jit(solution)/shard_map/ppermute | solution.py:230
  89.8 1.5 copy-start.8
  91.3 1.5 copy-start.10
  98.1 10.1 %collective-permute-start.11 = (bf16[48,3584]{1,0:T(8,128)(2,1)S(1)}, bf16[48,3584]{1,0:T(8,128)(2,1)S(1)}, u32[]{:S(2)}, u32[]{:S(2)}) collective-permute-start(bf16[48,3584]{1,0:T(8,128)(2,1)S(1)} %collective-permute-done.6.refs_2_), channel_id=1, source_target_pairs={{0,1},{1,0},{2,3},{3,2},{4,5},{5,4},{6,7},{7,6},{8,9},{9,8},{10,11... | collective-permute-start | bytes 1032200 | tf_op jit(solution)/shard_map/ppermute | solution.py:230
  98.5 6.9 %collective-permute-start.7 = (bf16[288,256]{1,0:T(8,128)(2,1)S(1)}, bf16[288,256]{1,0:T(8,128)(2,1)S(1)}, u32[]{:S(2)}, u32[]{:S(2)}) collective-permute-start(bf16[288,256]{1,0:T(8,128)(2,1)S(1)} %get-tuple-element.29), channel_id=1, source_target_pairs={{0,224},{32,0},{64,32},{96,64},{128,96},{160,128},{192,160},{224,1... | collective-permute-start | bytes 442376 | tf_op jit(solution)/shard_map/ppermute | solution.py:235
  101.2 6.9 %collective-permute-start.8 = (bf16[288,256]{1,0:T(8,128)(2,1)S(1)}, bf16[288,256]{1,0:T(8,128)(2,1)S(1)}, u32[]{:S(2)}, u32[]{:S(2)}) collective-permute-start(bf16[288,256]{1,0:T(8,128)(2,1)S(1)} %get-tuple-element.30), channel_id=1, source_target_pairs={{0,225},{1,224},{2,227},{3,226},{4,229},{5,228},{6,231},{7,230},{8... | collective-permute-start | bytes 442376 | tf_op jit(solution)/shard_map/ppermute | solution.py:243
  112.6 7.4 %copy-start.2 = (bf16[1,128,3584]{2,1,0:T(8,128)(2,1)S(1)}, bf16[1,128,3584]{2,1,0:T(8,128)(2,1)}, u32[]{:S(2)}) copy-start(bf16[1,128,3584]{2,1,0:T(8,128)(2,1)} %param.10) | copy-start | bytes 2752516
  112.6 7.4 %copy-start.5 = (s32[1,1,128,1]{2,3,1,0:T(1,128)S(1)}, s32[1,1,128,1]{2,3,1,0:T(1,128)}, u32[]{:S(2)}) copy-start(s32[1,1,128,1]{2,3,1,0:T(1,128)} %param.12) | copy-start | bytes 1540
  112.6 7.4 %copy-start.6 = (f32[1,1,128,1]{2,3,1,0:T(1,128)S(1)}, f32[1,1,128,1]{2,3,1,0:T(1,128)}, u32[]{:S(2)}) copy-start(f32[1,1,128,1]{2,3,1,0:T(1,128)} %param.14) | copy-start | bytes 1540
  112.6 35.9 %all-to-all-start.3 = ((bf16[16,72,896]{2,1,0:T(8,128)(2,1)}), bf16[16,72,896]{2,1,0:T(8,128)(2,1)}, u32[]{:S(2)}, u32[]{:S(2)}) async-start(bf16[16,72,896]{2,1,0:T(8,128)(2,1)} %shard_map.118), calls=%async_computation.3 | async-start | bytes 4128768 | tf_op jit(solution)/shard_map/all_to_all | solution.py:248
  120.0 1.2 copy-start.11
  120.0 5.2 %copy-start.12 = (s32[1,1,128,1]{2,3,1,0:T(1,128)S(1)}, s32[1,1,128,1]{2,3,1,0:T(1,128)}, u32[]{:S(2)}) copy-start(s32[1,1,128,1]{2,3,1,0:T(1,128)} %param.13) | copy-start | bytes 1540
  120.0 7.1 %copy-start.13 = (f32[1,1,128,1]{2,3,1,0:T(1,128)S(1)}, f32[1,1,128,1]{2,3,1,0:T(1,128)}, u32[]{:S(2)}) copy-start(f32[1,1,128,1]{2,3,1,0:T(1,128)} %param.15) | copy-start | bytes 1540
  120.9 23.8 %collective-permute-start.12 = (bf16[128,3584]{1,0:T(8,128)(2,1)S(1)}, bf16[128,3584]{1,0:T(8,128)(2,1)S(1)}, u32[]{:S(2)}, u32[]{:S(2)}) collective-permute-start(bf16[128,3584]{1,0:T(8,128)(2,1)S(1)} %shard_map.119), channel_id=1, source_target_pairs={{0,32},{32,64},{64,96},{96,128},{128,160},{160,192},{192,224},{224... | collective-permute-start | bytes 2752520 | tf_op jit(solution)/shard_map/ppermute | solution.py:235
  121.2 24.6 %collective-permute-start.13 = (bf16[128,3584]{1,0:T(8,128)(2,1)S(1)}, bf16[128,3584]{1,0:T(8,128)(2,1)S(1)}, u32[]{:S(2)}, u32[]{:S(2)}) collective-permute-start(bf16[128,3584]{1,0:T(8,128)(2,1)S(1)} %bitcast.30), channel_id=1, source_target_pairs={{0,224},{32,0},{64,32},{96,64},{128,96},{160,128},{192,160},{224,1... | collective-permute-start | bytes 2752520 | tf_op jit(solution)/shard_map/ppermute | solution.py:235
  125.2 20.5 %collective-permute-start.14 = (s32[1,128]{1,0:T(1,128)S(1)}, s32[1,128]{1,0:T(1,128)S(1)}, u32[]{:S(2)}, u32[]{:S(2)}) collective-permute-start(s32[1,128]{1,0:T(1,128)S(1)} %bitcast.33), channel_id=1, source_target_pairs={{0,224},{32,0},{64,32},{96,64},{128,96},{160,128},{192,160},{224,1... | collective-permute-start | bytes 1544 | tf_op jit(solution)/shard_map/ppermute | solution.py:235
  127.1 18.7 %collective-permute-start.15 = (f32[1,128]{1,0:T(1,128)S(1)}, f32[1,128]{1,0:T(1,128)S(1)}, u32[]{:S(2)}, u32[]{:S(2)}) collective-permute-start(f32[1,128]{1,0:T(1,128)S(1)} %bitcast.34), channel_id=1, source_target_pairs={{0,224},{32,0},{64,32},{96,64},{128,96},{160,128},{192,160},{224,1... | collective-permute-start | bytes 1544 | tf_op jit(solution)/shard_map/ppermute | solution.py:235

commit v8 on v7

--- a/solution.py
+++ b/solution.py
@@ -98,38 +98,59 @@
     )(current, ids_row, gain)
 
 
-def hidden_kernel(own_ref, other_ref, gate_ref, up_ref, mine_ref, give_ref):
-    quarter = own_ref.shape[2]
+def hidden_kernel(
+    received_hbm, gate_hbm, up_hbm, hidden_ref, received_ref, gate_ref, up_ref, ready
+):
+    quarter = received_ref.shape[2]
     count = CHIPS * (MAIN + LAST)
-    for received, hidden_ref in ((own_ref, mine_ref), (other_ref, give_ref)):
-        last = received[:, ES * MAIN :, :].astype(F32).reshape(CHIPS * ES * LAST, quarter).astype(BF16)
-        gate = jnp.zeros((count, gate_ref.shape[1]), F32)
-        up = jnp.zeros((count, up_ref.shape[1]), F32)
-        shape = (CHIPS * LAST, CHIPS * ES * LAST)
-        target = iota(shape, 0)
-        source = (target // LAST) * (ES * LAST) + target % LAST
-        for q in range(ES):
-            main = received[:, q * MAIN : (q + 1) * MAIN, :].reshape(CHIPS * MAIN, quarter)
-            pick = (iota(shape, 1) == source + q * LAST).astype(BF16)
-            rows = jnp.concatenate([main, dot(pick, last).astype(BF16)], axis=0)
-            gate = gate + dot(rows, gate_ref[q * quarter : (q + 1) * quarter, :])
-            up = up + dot(rows, up_ref[q * quarter : (q + 1) * quarter, :])
-        hidden_ref[...] = (jax.nn.silu(gate) * up).astype(BF16)
-
-
-def hidden_units(own, other, gate_cols, up_cols):
+    loads = [pltpu.make_async_copy(received_hbm, received_ref, ready.at[2 * ES])]
+    for q in range(ES):
+        part = pl.ds(q * quarter, quarter)
+        for side, (source, target) in enumerate(((gate_hbm, gate_ref), (up_hbm, up_ref))):
+            loads.append(
+                pltpu.make_async_copy(source.at[part, :], target.at[part, :], ready.at[2 * q + side])
+            )
+    for load in loads:
+        load.start()
+    gate = jnp.zeros((count, gate_ref.shape[1]), F32)
+    up = jnp.zeros((count, up_ref.shape[1]), F32)
+    shape = (CHIPS * LAST, CHIPS * ES * LAST)
+    target = iota(shape, 0)
+    source = (target // LAST) * (ES * LAST) + target % LAST
+    loads[0].wait()
+    last = received_ref[:, ES * MAIN :, :].astype(F32)
+    last = last.reshape(CHIPS * ES * LAST, quarter).astype(BF16)
+    for q in range(ES):
+        main = received_ref[:, q * MAIN : (q + 1) * MAIN, :].reshape(CHIPS * MAIN, quarter)
+        pick = (iota(shape, 1) == source + q * LAST).astype(BF16)
+        rows = jnp.concatenate([main, dot(pick, last).astype(BF16)], axis=0)
+        loads[1 + 2 * q].wait()
+        gate = gate + dot(rows, gate_ref[q * quarter : (q + 1) * quarter, :])
+        loads[2 + 2 * q].wait()
+        up = up + dot(rows, up_ref[q * quarter : (q + 1) * quarter, :])
+    hidden_ref[...] = (jax.nn.silu(gate) * up).astype(BF16)
+
+
+def hidden_units(received, gate_cols, up_cols):
     count = CHIPS * (MAIN + LAST)
     features, width = gate_cols.shape
     return pl.pallas_call(
         hidden_kernel,
-        out_shape=[jax.ShapeDtypeStruct((count, width), BF16)] * 2,
-        compiler_params=pltpu.CompilerParams(vmem_limit_bytes=VMEM_LIMIT),
+        out_shape=jax.ShapeDtypeStruct((count, width), BF16),
+        in_specs=[pl.BlockSpec(memory_space=pltpu.HBM)] * 3,
+        scratch_shapes=[
+            pltpu.VMEM(received.shape, received.dtype),
+            pltpu.VMEM(gate_cols.shape, gate_cols.dtype),
+            pltpu.VMEM(up_cols.shape, up_cols.dtype),
+            pltpu.SemaphoreType.DMA((2 * ES + 1,)),
+        ],
+        compiler_params=pltpu.CompilerParams(vmem_limit_bytes=VMEM_WHOLE),
         cost_estimate=pl.CostEstimate(
-            flops=8 * count * features * width,
-            bytes_accessed=4 * features * width + 4 * count * features,
-            transcendentals=2 * count * width,
+            flops=4 * count * features * width,
+            bytes_accessed=4 * features * width + 2 * count * features,
+            transcendentals=count * width,
         ),
-    )(own, other, gate_cols, up_cols)
+    )(received, gate_cols, up_cols)
 
 
 def down_kernel(pieces, mine_ref, theirs_ref, *refs):
@@ -172,7 +193,15 @@
     )(mine, theirs, *down, *other_down)
 
 
-def finish_kernel(current_ref, back_ref, ids_ref, scores_ref, out_ref):
+def finish_kernel(
+    current_hbm, back_hbm, ids_ref, scores_ref, out_hbm, current_ref, back_ref, out_ref, ready, done
+):
+    loads = [
+        pltpu.make_async_copy(back_hbm, back_ref, ready.at[0]),
+        pltpu.make_async_copy(current_hbm, current_ref, ready.at[1]),
+    ]
+    for load in loads:
+        load.start()
     tokens, features = current_ref.shape
     quarter = features // ES
     ids_row = ids_ref[...]
@@ -186,9 +215,12 @@
     lane = iota((tokens, CHIPS * ES * LAST), 1)
     in_expert = (lane // (2 * ES * LAST) == ids_column) & (slot >= MAIN)
     in_block = lane % (ES * LAST)
+    loads[0].wait()
     last = jnp.concatenate(
         [back_ref[chip, ES * MAIN :, :].astype(F32) for chip in range(CHIPS)], axis=0
     ).astype(BF16)
+    loads[1].wait()
+    stores = []
     for q in range(ES):
         main = jnp.concatenate(
             [back_ref[chip, q * MAIN : (q + 1) * MAIN, :] for chip in range(CHIPS)], axis=0
@@ -197,6 +229,11 @@
         moe = (dot(pick_main, main) + dot(pick_last.astype(BF16), last)) * score
         columns = slice(q * quarter, (q + 1) * quarter)
         out_ref[:, columns] = (current_ref[:, columns].astype(F32) + moe).astype(BF16)
+        part = pl.ds(q * quarter, quarter)
+        stores.append(pltpu.make_async_copy(out_ref.at[:, part], out_hbm.at[:, part], done.at[q]))
+        stores[q].start()
+    for store in stores:
+        store.wait()
 
 
 def finish(current, back, ids_row, scores_row):
@@ -204,7 +241,17 @@
     return pl.pallas_call(
         finish_kernel,
         out_shape=jax.ShapeDtypeStruct((tokens, features), BF16),
-        compiler_params=pltpu.CompilerParams(vmem_limit_bytes=VMEM_LIMIT),
+        in_specs=[pl.BlockSpec(memory_space=pltpu.HBM)] * 2
+        + [pl.BlockSpec(memory_space=pltpu.VMEM)] * 2,
+        out_specs=pl.BlockSpec(memory_space=pltpu.HBM),
+        scratch_shapes=[
+            pltpu.VMEM(current.shape, BF16),
+            pltpu.VMEM(back.shape, BF16),
+            pltpu.VMEM(current.shape, BF16),
+            pltpu.SemaphoreType.DMA((2,)),
+            pltpu.SemaphoreType.DMA((ES,)),
+        ],
+        compiler_params=pltpu.CompilerParams(vmem_limit_bytes=VMEM_WHOLE),
         cost_estimate=pl.CostEstimate(
             flops=6 * tokens * EXPERTS * MAIN * features,
             bytes_accessed=8 * tokens * features,
@@ -263,20 +310,21 @@
     other_down = swap_cores(down)
     staged_b, other_down = lax.optimization_barrier((current_b, other_down))
     send_b = prepare(staged_b, ids_b, norm_gain)
-    upper = from_behind(down[:96], -1)
+    middle = down.shape[0] // 2
+    upper = from_behind(down[:middle], -1)
     own_a, send_b, upper = lax.optimization_barrier((own_a, send_b, upper))
     own_b = exchange(send_b)
 
-    middle = from_behind(down[96:208], -1)
-    mine_a, give_a = hidden_units(own_a, swap_cores(own_a), gate_cols, up_cols)
+    lower = from_behind(down[middle:], -1)
+    mine_a = hidden_units(own_a, gate_cols, up_cols)
+    give_a = hidden_units(swap_cores(own_a), gate_cols, up_cols)
     back_a = down_product(mine_a, swap_cores(give_a), [down], [other_down])
-    own_b, back_a, middle = lax.optimization_barrier((own_b, back_a, middle))
+    own_b, back_a, lower = lax.optimization_barrier((own_b, back_a, lower))
 
     returned_a = exchange(back_a)
-    lower = from_behind(down[208:], -1)
-    mine_b, give_b = hidden_units(own_b, swap_cores(own_b), gate_cols, up_cols)
-    mine_b, give_b, lower = lax.optimization_barrier((mine_b, give_b, lower))
-    moved_down = [upper, middle, lower]
+    mine_b = hidden_units(own_b, gate_cols, up_cols)
+    give_b = hidden_units(swap_cores(own_b), gate_cols, up_cols)
+    moved_down = [upper, lower]
     back_b = down_product(
         from_behind(mine_b, -1),
         behind_other_core(give_b, -1),

time: 152 us -> 154 us (1.013)
  Pallas kernels: 30.4 us -> 47.8 us
  waiting for transfers between devices: 54.9 us -> 43.9 us
  starting transfers between devices: 56.4 us -> 53.8 us
  local copies, waits for them, and re-layouts: 9.34 us -> 6.89 us
    pallas_call x2 -> x4, Pallas kernels: 10.7 us -> 23.7 us  [hidden_units(): pl.pallas_call(hidden_kernel, out_shape=jax.ShapeDtypeStruct((count, widt...]
    all_to_all x4, waiting for transfers between devices: 14.6 us -> 4.7 us  [exchange(): lax.all_to_all(blocks, 'ep', split_axis=0, concat_axis=0, axis_index_grou...]
    pallas_call x2, Pallas kernels: 4.25 us -> 7.85 us  [finish(): pl.pallas_call(finish_kernel, out_shape=jax.ShapeDtypeStruct((tokens, fea...]
    ppermute x8 -> x7, starting transfers between devices: 27.6 us -> 24.6 us  [from_behind(): lax.ppermute(value, 'section', [(i, (i + steps) % count) for i in range(c...]
    ppermute x1, waiting for transfers between devices: 2.78 us -> 5.56 us  [behind_other_core(): return lax.ppermute(value, ('section', 'ep'), pairs)]
    ppermute x8 -> x7, waiting for transfers between devices: 36.1 us -> 33.6 us  [from_behind(): lax.ppermute(value, 'section', [(i, (i + steps) % count) for i in range(c...]
    unnamed x28 -> x18, local copies, waits for them, and re-layouts: 7.38 us -> 5.54 us
  transfers between devices with their start and end apart: 20 -> 18, of which waited for: 9 -> 7; matrix products, arithmetic and copies ran while one was open for 1% -> 1% of each run, Pallas kernels for 16% -> 26%
where the time goes in v8:
time: 154 us; the launch traced here: 153 us
  starting transfers between devices  53.8 us (35%)
  Pallas kernels  47.8 us (31%)
  waiting for transfers between devices  43.9 us (29%)
  local copies, waits for them, and re-layouts  6.89 us (4%)
    ppermute x7, waiting for transfers between devices, from_behind(): lax.ppermute(value, 'section', [(i, (i + steps) % count) for i in range(c...  33.6 us
    all_to_all x4, starting transfers between devices, exchange(): lax.all_to_all(blocks, 'ep', split_axis=0, concat_axis=0, axis_index_grou...  27.8 us
    ppermute x7, starting transfers between devices, from_behind(): lax.ppermute(value, 'section', [(i, (i + steps) % count) for i in range(c...  24.6 us
    pallas_call x4, Pallas kernels, hidden_units(): pl.pallas_call(hidden_kernel, out_shape=jax.ShapeDtypeStruct((count, widt...  23.7 us
    pallas_call x2, Pallas kernels, down_product(): pl.pallas_call(functools.partial(down_kernel, len(down)), out_shape=jax.S...  8.55 us
    pallas_call x2, Pallas kernels, finish(): pl.pallas_call(finish_kernel, out_shape=jax.ShapeDtypeStruct((tokens, fea...  7.85 us
    pallas_call x2, Pallas kernels, prepare(): pl.pallas_call(prepare_kernel, out_shape=jax.ShapeDtypeStruct((CHIPS, ES...  6.72 us
    ppermute x1, waiting for transfers between devices, behind_other_core(): return lax.ppermute(value, ('section', 'ep'), pairs)  5.56 us
  transfers between devices with their start and end apart: 18, of which 7 were waited for; matrix products, arithmetic and copies ran while one was open for 1% of the time, Pallas kernels for 26%

profile of v8, /device:TPU:8, one launch (start us, length us, event | category | flops | bytes accessed | tf_op | source)
XLA Modules:
  0.0 153.3 jit_solution(9845769155197633612)
XLA Ops:
  0.6 3.4 %shard_map.113 = bf16[16,72,896]{2,1,0:T(8,128)(2,1)} custom-call(bf16[128,3584]{1,0:T(8,128)(2,1)} %bitcast.25, s32[1,128]{1,0:T(1,128)} %bitcast.31, f32[1,3584]{1,0:T(1,128)} %gain_hbm.3), custom_call_target="tpu_custom_call" | custom-call | flops 176160768 | bytes 3670016 | tf_op jit(solution)/shard_map/pallas_call | solution.py:84
  4.0 0.0 copy-start
  4.0 7.5 %all-to-all-start = ((bf16[16,72,896]{2,1,0:T(8,128)(2,1)}), bf16[16,72,896]{2,1,0:T(8,128)(2,1)}, u32[]{:S(2)}, u32[]{:S(2)}) async-start(bf16[16,72,896]{2,1,0:T(8,128)(2,1)} %shard_map.113), calls=%async_computation | async-start | bytes 4128768 | tf_op jit(solution)/shard_map/all_to_all | solution.py:295
  11.5 0.1 collective-permute-start
  11.6 1.3 slice_bitcast_fusion
  13.0 5.9 %collective-permute-start.1 = (bf16[128,3584]{1,0:T(8,128)(2,1)}, bf16[128,3584]{1,0:T(8,128)(2,1)}, u32[]{:S(2)}, u32[]{:S(2)}) collective-permute-start(bf16[128,3584]{1,0:T(8,128)(2,1)} %get-tuple-element.23), channel_id=1, source_target_pairs={{0,224},{32,0},{64,32},{96,64},{128,96},{160,128},{192,160},{224,1... | collective-permute-start | bytes 2752520 | tf_op jit(solution)/shard_map/ppermute | solution.py:282
  18.9 1.3 copy-done.2
  20.1 3.4 %shard_map.114 = bf16[16,72,896]{2,1,0:T(8,128)(2,1)} custom-call(bf16[128,3584]{1,0:T(8,128)(2,1)} %bitcast.28, s32[1,128]{1,0:T(1,128)} %bitcast.34, f32[1,3584]{1,0:T(1,128)} %gain_hbm.3), custom_call_target="tpu_custom_call" | custom-call | flops 176160768 | bytes 3670016 | tf_op jit(solution)/shard_map/pallas_call | solution.py:84
  23.5 15.9 %collective-permute-done.1.refs_0_ = bf16[128,3584]{1,0:T(8,128)(2,1)} collective-permute-done((bf16[128,3584]{1,0:T(8,128)(2,1)}, bf16[128,3584]{1,0:T(8,128)(2,1)}, u32[]{:S(2)}, u32[]{:S(2)}) %collective-permute-start.1) | collective-permute-done | bytes 917536 | tf_op jit(solution)/shard_map/ppermute | solution.py:282
  39.4 0.8 all-to-all-done.received_hbm
  40.2 0.0 collective-permute-start.2
  40.2 6.4 %all-to-all-start.1 = ((bf16[16,72,896]{2,1,0:T(8,128)(2,1)}), bf16[16,72,896]{2,1,0:T(8,128)(2,1)}, u32[]{:S(2)}, u32[]{:S(2)}) async-start(bf16[16,72,896]{2,1,0:T(8,128)(2,1)} %shard_map.114), calls=%async_computation.1 | async-start | bytes 4128768 | tf_op jit(solution)/shard_map/all_to_all | solution.py:295
  46.7 5.1 %collective-permute-start.4 = (bf16[128,3584]{1,0:T(8,128)(2,1)}, bf16[128,3584]{1,0:T(8,128)(2,1)}, u32[]{:S(2)}, u32[]{:S(2)}) collective-permute-start(bf16[128,3584]{1,0:T(8,128)(2,1)} %get-tuple-element.22), channel_id=1, source_target_pairs={{0,224},{32,0},{64,32},{96,64},{128,96},{160,128},{192,160},{224,1... | collective-permute-start | bytes 2752520 | tf_op jit(solution)/shard_map/ppermute | solution.py:282
  51.7 0.0 collective-permute-done.2.received_hbm
  51.7 5.9 %shard_map.116 = bf16[288,256]{1,0:T(8,128)(2,1)} custom-call(bf16[16,72,896]{2,1,0:T(8,128)(2,1)} %collective-permute-done.2.received_hbm, bf16[3584,256]{1,0:T(8,128)(2,1)} %bitcast.17, bf16[3584,256]{1,0:T(8,128)(2,1)} %bitcast.21), custom_call_target="tpu_custom_call" | custom-call | flops 1056964608 | bytes 5734400 | tf_op jit(solution)/shard_map/pallas_call | solution.py:137
  57.7 0.1 collective-permute-start.3
  57.8 5.9 %shard_map.115.mine_ref = bf16[288,256]{1,0:T(8,128)(2,1)} custom-call(bf16[16,72,896]{2,1,0:T(8,128)(2,1)} %all-to-all-done.received_hbm, bf16[3584,256]{1,0:T(8,128)(2,1)} %bitcast.18, bf16[3584,256]{1,0:T(8,128)(2,1)} %bitcast.22), custom_call_target="tpu_custom_call" | custom-call | flops 1056964608 | bytes 5734400 | tf_op jit(solution)/shard_map/pallas_call | solution.py:137
  63.7 0.0 copy-start.1
  63.7 1.5 copy-done.1
  65.2 1.5 copy-done.3
  66.7 0.9 copy-done.4
  67.6 3.2 %shard_map.117 = bf16[16,72,896]{2,1,0:T(8,128)(2,1)} custom-call(bf16[288,256]{1,0:T(8,128)(2,1)S(1)} %copy-done.4, bf16[288,256]{1,0:T(8,128)(2,1)S(1)} %collective-permute-done.3.theirs_ref, bf16[256,3584]{1,0:T(8,128)(2,1)S(1)} %bitcast.16, bf16[256,3584]{1,0:T(8,128)(2,1)S(1)} %copy-done.3), custom_call_target="tpu_custom_call" | custom-call | flops 1056964608 | bytes 5734400 | tf_op jit(solution)/shard_map/pallas_call | solution.py:184
  70.9 1.2 collective-permute-done.4.refs_1_
  72.0 3.7 %all-to-all-done.1.received_hbm = bf16[16,72,896]{2,1,0:T(8,128)(2,1)} async-done(((bf16[16,72,896]{2,1,0:T(8,128)(2,1)}), bf16[16,72,896]{2,1,0:T(8,128)(2,1)}, u32[]{:S(2)}, u32[]{:S(2)}) %all-to-all-start.1) | async-done | bytes 2064416 | tf_op jit(solution)/shard_map/all_to_all | solution.py:295
  75.7 0.0 collective-permute-start.6
  75.7 6.6 %all-to-all-start.2 = ((bf16[16,72,896]{2,1,0:T(8,128)(2,1)}), bf16[16,72,896]{2,1,0:T(8,128)(2,1)}, u32[]{:S(2)}, u32[]{:S(2)}) async-start(bf16[16,72,896]{2,1,0:T(8,128)(2,1)} %shard_map.117), calls=%async_computation.2 | async-start | bytes 4128768 | tf_op jit(solution)/shard_map/all_to_all | solution.py:295
  82.3 0.0 collective-permute-start.8
  82.3 0.5 collective-permute-start.9
  82.8 5.9 %shard_map.118 = bf16[288,256]{1,0:T(8,128)(2,1)} custom-call(bf16[16,72,896]{2,1,0:T(8,128)(2,1)} %all-to-all-done.1.received_hbm, bf16[3584,256]{1,0:T(8,128)(2,1)} %bitcast.19, bf16[3584,256]{1,0:T(8,128)(2,1)} %bitcast.23), custom_call_target="tpu_custom_call" | custom-call | flops 1056964608 | bytes 5734400 | tf_op jit(solution)/shard_map/pallas_call | solution.py:137
  88.8 6.2 %collective-permute-start.5 = (bf16[288,256]{1,0:T(8,128)(2,1)}, bf16[288,256]{1,0:T(8,128)(2,1)S(1)}, u32[]{:S(2)}, u32[]{:S(2)}) collective-permute-start(bf16[288,256]{1,0:T(8,128)(2,1)} %shard_map.118), channel_id=1, source_target_pairs={{0,224},{32,0},{64,32},{96,64},{128,96},{160,128},{192,160},{224,1... | collective-permute-start | bytes 442376 | tf_op jit(solution)/shard_map/ppermute | solution.py:282
  95.0 0.0 collective-permute-done.6.received_hbm
  95.0 5.9 %shard_map.119 = bf16[288,256]{1,0:T(8,128)(2,1)} custom-call(bf16[16,72,896]{2,1,0:T(8,128)(2,1)} %collective-permute-done.6.received_hbm, bf16[3584,256]{1,0:T(8,128)(2,1)} %bitcast.20, bf16[3584,256]{1,0:T(8,128)(2,1)} %bitcast.24), custom_call_target="tpu_custom_call" | custom-call | flops 1056964608 | bytes 5734400 | tf_op jit(solution)/shard_map/pallas_call | solution.py:137
  100.9 0.7 collective-permute-start.7
  101.6 0.0 collective-permute-done.8.refs_2_
  101.6 5.6 %collective-permute-done.7.theirs_ref = bf16[288,256]{1,0:T(8,128)(2,1)S(1)} collective-permute-done((bf16[288,256]{1,0:T(8,128)(2,1)}, bf16[288,256]{1,0:T(8,128)(2,1)S(1)}, u32[]{:S(2)}, u32[]{:S(2)}) %collective-permute-start.7) | collective-permute-done | bytes 147488 | tf_op jit(solution)/shard_map/ppermute | solution.py:290
  107.1 5.3 %shard_map.120 = bf16[16,72,896]{2,1,0:T(8,128)(2,1)} custom-call(bf16[288,256]{1,0:T(8,128)(2,1)S(1)} %collective-permute-done.5.mine_ref, bf16[288,256]{1,0:T(8,128)(2,1)S(1)} %collective-permute-done.7.theirs_ref, bf16[128,3584]{1,0:T(8,128)(2,1)} %collective-permute-done.1.refs_0_, bf16[128,3584]{1,0:T(8,128)(2,1)} %collective-permute-done.4.refs_1_, ...), custom_call_target="tpu_custom_call" | custom-call | flops 1056964608 | bytes 5734400 | tf_op jit(solution)/shard_map/pallas_call | solution.py:184
  112.4 7.2 %all-to-all-start.3 = ((bf16[16,72,896]{2,1,0:T(8,128)(2,1)}), bf16[16,72,896]{2,1,0:T(8,128)(2,1)}, u32[]{:S(2)}, u32[]{:S(2)}) async-start(bf16[16,72,896]{2,1,0:T(8,128)(2,1)} %shard_map.120), calls=%async_computation.3 | async-start | bytes 4128768 | tf_op jit(solution)/shard_map/all_to_all | solution.py:295
  119.7 0.0 copy-start.8
  119.7 3.9 %shard_map.121 = bf16[128,3584]{1,0:T(8,128)(2,1)} custom-call(bf16[128,3584]{1,0:T(8,128)(2,1)} %bitcast.26, bf16[16,72,896]{2,1,0:T(8,128)(2,1)} %all-to-all-done.2.back_hbm, s32[1,128]{1,0:T(1,128)} %bitcast.32, f32[1,128]{1,0:T(1,128)} %bitcast.33), custom_call_target="tpu_custom_call" | custom-call | flops 352321536 | bytes 3670016 | tf_op jit(solution)/shard_map/pallas_call | solution.py:241
  123.6 0.6 collective-permute-start.10
  124.2 4.0 %collective-permute-start.11 = (bf16[128,3584]{1,0:T(8,128)(2,1)}, bf16[128,3584]{1,0:T(8,128)(2,1)}, u32[]{:S(2)}, u32[]{:S(2)}) collective-permute-start(bf16[128,3584]{1,0:T(8,128)(2,1)} %bitcast.29), channel_id=1, source_target_pairs={{0,224},{32,0},{64,32},{96,64},{128,96},{160,128},{192,160},{224,1... | collective-permute-start | bytes 2752520 | tf_op jit(solution)/shard_map/ppermute | solution.py:282
  128.2 1.9 %collective-permute-start.12 = (s32[1,128]{1,0:T(1,128)S(1)}, s32[1,128]{1,0:T(1,128)S(1)}, u32[]{:S(2)}, u32[]{:S(2)}) collective-permute-start(s32[1,128]{1,0:T(1,128)S(1)} %bitcast.35), channel_id=1, source_target_pairs={{0,224},{32,0},{64,32},{96,64},{128,96},{160,128},{192,160},{224,1... | collective-permute-start | bytes 1544 | tf_op jit(solution)/shard_map/ppermute | solution.py:282
  130.2 1.0 collective-permute-start.13
  131.2 16.5 %collective-permute-done.10.value_ref = bf16[128,3584]{1,0:T(8,128)(2,1)S(1)} collective-permute-done((bf16[128,3584]{1,0:T(8,128)(2,1)}, bf16[128,3584]{1,0:T(8,128)(2,1)S(1)}, u32[]{:S(2)}, u32[]{:S(2)}) %collective-permute-start.10) | collective-permute-done | bytes 917536 | tf_op jit(solution)/shard_map/ppermute | solution.py:282
  147.6 1.0 shard_map.122
  148.7 0.2 all-to-all-done.3.back_hbm
  148.9 0.3 copy-done.5
  149.2 3.9 %shard_map.123 = bf16[128,3584]{1,0:T(8,128)(2,1)} custom-call(bf16[128,3584]{1,0:T(8,128)(2,1)} %collective-permute-done.11.current_hbm, bf16[16,72,896]{2,1,0:T(8,128)(2,1)} %all-to-all-done.3.back_hbm, s32[1,128]{1,0:T(1,128)} %copy-done.5, f32[1,128]{1,0:T(1,128)} %copy-done.6), custom_call_target="tpu_custom_call" | custom-call | flops 352321536 | bytes 3670016 | tf_op jit(solution)/shard_map/pallas_call | solution.py:241
  (18 shorter events, 0.0 us)
Async XLA Ops:
  4.0 7.5 %copy-start = (bf16[1,256,3584]{2,1,0:T(8,128)(2,1)S(1)}, bf16[1,256,3584]{2,1,0:T(8,128)(2,1)}, u32[]{:S(2)}) copy-start(bf16[1,256,3584]{2,1,0:T(8,128)(2,1)} %param.19) | copy-start | bytes 5505028
  4.0 36.2 %all-to-all-start = ((bf16[16,72,896]{2,1,0:T(8,128)(2,1)}), bf16[16,72,896]{2,1,0:T(8,128)(2,1)}, u32[]{:S(2)}, u32[]{:S(2)}) async-start(bf16[16,72,896]{2,1,0:T(8,128)(2,1)} %shard_map.113), calls=%async_computation | async-start | bytes 4128768 | tf_op jit(solution)/shard_map/all_to_all | solution.py:295
  11.5 7.3 %collective-permute-start = (bf16[256,3584]{1,0:T(8,128)(2,1)S(1)}, bf16[256,3584]{1,0:T(8,128)(2,1)S(1)}, u32[]{:S(2)}, u32[]{:S(2)}) collective-permute-start(bf16[256,3584]{1,0:T(8,128)(2,1)S(1)} %bitcast.15), channel_id=1, source_target_pairs={{0,1},{1,0},{2,3},{3,2},{4,5},{5,4},{6,7},{7,6},{8,9},{9,8},{10,11... | collective-permute-start | bytes 5505032 | tf_op jit(solution)/shard_map/ppermute | solution.py:277
  13.0 26.4 %collective-permute-start.1 = (bf16[128,3584]{1,0:T(8,128)(2,1)}, bf16[128,3584]{1,0:T(8,128)(2,1)}, u32[]{:S(2)}, u32[]{:S(2)}) collective-permute-start(bf16[128,3584]{1,0:T(8,128)(2,1)} %get-tuple-element.23), channel_id=1, source_target_pairs={{0,224},{32,0},{64,32},{96,64},{128,96},{160,128},{192,160},{224,1... | collective-permute-start | bytes 2752520 | tf_op jit(solution)/shard_map/ppermute | solution.py:282
  18.8 1.3 copy-start.2
  40.2 11.5 %collective-permute-start.2 = (bf16[16,72,896]{2,1,0:T(8,128)(2,1)}, bf16[16,72,896]{2,1,0:T(8,128)(2,1)}, u32[]{:S(2)}, u32[]{:S(2)}) collective-permute-start(bf16[16,72,896]{2,1,0:T(8,128)(2,1)} %all-to-all-done.received_hbm), channel_id=1, source_target_pairs={{0,1},{1,0},{2,3},{3,2},{4,5},{5,4},{6,7},{7,6},{8,9},{9,8},{10,11... | collective-permute-start | bytes 6193160 | tf_op jit(solution)/shard_map/ppermute | solution.py:277
  40.2 35.5 %all-to-all-start.1 = ((bf16[16,72,896]{2,1,0:T(8,128)(2,1)}), bf16[16,72,896]{2,1,0:T(8,128)(2,1)}, u32[]{:S(2)}, u32[]{:S(2)}) async-start(bf16[16,72,896]{2,1,0:T(8,128)(2,1)} %shard_map.114), calls=%async_computation.1 | async-start | bytes 4128768 | tf_op jit(solution)/shard_map/all_to_all | solution.py:295
  46.7 25.4 %collective-permute-start.4 = (bf16[128,3584]{1,0:T(8,128)(2,1)}, bf16[128,3584]{1,0:T(8,128)(2,1)}, u32[]{:S(2)}, u32[]{:S(2)}) collective-permute-start(bf16[128,3584]{1,0:T(8,128)(2,1)} %get-tuple-element.22), channel_id=1, source_target_pairs={{0,224},{32,0},{64,32},{96,64},{128,96},{160,128},{192,160},{224,1... | collective-permute-start | bytes 2752520 | tf_op jit(solution)/shard_map/ppermute | solution.py:282
  57.7 6.0 %collective-permute-start.3 = (bf16[288,256]{1,0:T(8,128)(2,1)}, bf16[288,256]{1,0:T(8,128)(2,1)S(1)}, u32[]{:S(2)}, u32[]{:S(2)}) collective-permute-start(bf16[288,256]{1,0:T(8,128)(2,1)} %shard_map.116), channel_id=1, source_target_pairs={{0,1},{1,0},{2,3},{3,2},{4,5},{5,4},{6,7},{7,6},{8,9},{9,8},{10,11... | collective-permute-start | bytes 442376 | tf_op jit(solution)/shard_map/ppermute | solution.py:277
  63.7 1.5 copy-start.1
  65.2 1.5 copy-start.3
  66.7 0.9 copy-start.4
  75.7 19.2 %collective-permute-start.6 = (bf16[16,72,896]{2,1,0:T(8,128)(2,1)}, bf16[16,72,896]{2,1,0:T(8,128)(2,1)}, u32[]{:S(2)}, u32[]{:S(2)}) collective-permute-start(bf16[16,72,896]{2,1,0:T(8,128)(2,1)} %all-to-all-done.1.received_hbm), channel_id=1, source_target_pairs={{0,1},{1,0},{2,3},{3,2},{4,5},{5,4},{6,7},{7,6},{8,9},{9,8},{10,11... | collective-permute-start | bytes 6193160 | tf_op jit(solution)/shard_map/ppermute | solution.py:277
  75.7 36.7 %all-to-all-start.2 = ((bf16[16,72,896]{2,1,0:T(8,128)(2,1)}), bf16[16,72,896]{2,1,0:T(8,128)(2,1)}, u32[]{:S(2)}, u32[]{:S(2)}) async-start(bf16[16,72,896]{2,1,0:T(8,128)(2,1)} %shard_map.117), calls=%async_computation.2 | async-start | bytes 4128768 | tf_op jit(solution)/shard_map/all_to_all | solution.py:295
  82.3 19.2 %collective-permute-start.8 = (bf16[128,3584]{1,0:T(8,128)(2,1)}, bf16[128,3584]{1,0:T(8,128)(2,1)}, u32[]{:S(2)}, u32[]{:S(2)}) collective-permute-start(bf16[128,3584]{1,0:T(8,128)(2,1)} %collective-permute-done.1.refs_0_), channel_id=1, source_target_pairs={{0,1},{1,0},{2,3},{3,2},{4,5},{5,4},{6,7},{7,6},{8,9},{9,8},{10,11... | collective-permute-start | bytes 2752520 | tf_op jit(solution)/shard_map/ppermute | solution.py:277
  82.3 19.2 %collective-permute-start.9 = (bf16[128,3584]{1,0:T(8,128)(2,1)}, bf16[128,3584]{1,0:T(8,128)(2,1)}, u32[]{:S(2)}, u32[]{:S(2)}) collective-permute-start(bf16[128,3584]{1,0:T(8,128)(2,1)} %collective-permute-done.4.refs_1_), channel_id=1, source_target_pairs={{0,1},{1,0},{2,3},{3,2},{4,5},{5,4},{6,7},{7,6},{8,9},{9,8},{10,11... | collective-permute-start | bytes 2752520 | tf_op jit(solution)/shard_map/ppermute | solution.py:277
  88.8 12.8 %collective-permute-start.5 = (bf16[288,256]{1,0:T(8,128)(2,1)}, bf16[288,256]{1,0:T(8,128)(2,1)S(1)}, u32[]{:S(2)}, u32[]{:S(2)}) collective-permute-start(bf16[288,256]{1,0:T(8,128)(2,1)} %shard_map.118), channel_id=1, source_target_pairs={{0,224},{32,0},{64,32},{96,64},{128,96},{160,128},{192,160},{224,1... | collective-permute-start | bytes 442376 | tf_op jit(solution)/shard_map/ppermute | solution.py:282
  100.9 6.3 %collective-permute-start.7 = (bf16[288,256]{1,0:T(8,128)(2,1)}, bf16[288,256]{1,0:T(8,128)(2,1)S(1)}, u32[]{:S(2)}, u32[]{:S(2)}) collective-permute-start(bf16[288,256]{1,0:T(8,128)(2,1)} %shard_map.119), channel_id=1, source_target_pairs={{0,225},{1,224},{2,227},{3,226},{4,229},{5,228},{6,231},{7,230},{8... | collective-permute-start | bytes 442376 | tf_op jit(solution)/shard_map/ppermute | solution.py:290
  112.4 36.4 %all-to-all-start.3 = ((bf16[16,72,896]{2,1,0:T(8,128)(2,1)}), bf16[16,72,896]{2,1,0:T(8,128)(2,1)}, u32[]{:S(2)}, u32[]{:S(2)}) async-start(bf16[16,72,896]{2,1,0:T(8,128)(2,1)} %shard_map.120), calls=%async_computation.3 | async-start | bytes 4128768 | tf_op jit(solution)/shard_map/all_to_all | solution.py:295
  119.7 8.5 %copy-start.7 = (s32[1,1,128,1]{2,3,1,0:T(1,128)S(1)}, s32[1,1,128,1]{2,3,1,0:T(1,128)}, u32[]{:S(2)}) copy-start(s32[1,1,128,1]{2,3,1,0:T(1,128)} %param.13) | copy-start | bytes 1540
  119.7 10.5 %copy-start.8 = (f32[1,1,128,1]{2,3,1,0:T(1,128)S(1)}, f32[1,1,128,1]{2,3,1,0:T(1,128)}, u32[]{:S(2)}) copy-start(f32[1,1,128,1]{2,3,1,0:T(1,128)} %param.15) | copy-start | bytes 1540
  123.6 24.0 %collective-permute-start.10 = (bf16[128,3584]{1,0:T(8,128)(2,1)}, bf16[128,3584]{1,0:T(8,128)(2,1)S(1)}, u32[]{:S(2)}, u32[]{:S(2)}) collective-permute-start(bf16[128,3584]{1,0:T(8,128)(2,1)} %shard_map.121), channel_id=1, source_target_pairs={{0,32},{32,64},{64,96},{96,128},{128,160},{160,192},{192,224},{224... | collective-permute-start | bytes 2752520 | tf_op jit(solution)/shard_map/ppermute | solution.py:282
  124.2 24.4 %collective-permute-start.11 = (bf16[128,3584]{1,0:T(8,128)(2,1)}, bf16[128,3584]{1,0:T(8,128)(2,1)}, u32[]{:S(2)}, u32[]{:S(2)}) collective-permute-start(bf16[128,3584]{1,0:T(8,128)(2,1)} %bitcast.29), channel_id=1, source_target_pairs={{0,224},{32,0},{64,32},{96,64},{128,96},{160,128},{192,160},{224,1... | collective-permute-start | bytes 2752520 | tf_op jit(solution)/shard_map/ppermute | solution.py:282
  128.2 20.4 %collective-permute-start.12 = (s32[1,128]{1,0:T(1,128)S(1)}, s32[1,128]{1,0:T(1,128)S(1)}, u32[]{:S(2)}, u32[]{:S(2)}) collective-permute-start(s32[1,128]{1,0:T(1,128)S(1)} %bitcast.35), channel_id=1, source_target_pairs={{0,224},{32,0},{64,32},{96,64},{128,96},{160,128},{192,160},{224,1... | collective-permute-start | bytes 1544 | tf_op jit(solution)/shard_map/ppermute | solution.py:282
  130.2 18.5 %collective-permute-start.13 = (f32[1,128]{1,0:T(1,128)S(1)}, f32[1,128]{1,0:T(1,128)S(1)}, u32[]{:S(2)}, u32[]{:S(2)}) collective-permute-start(f32[1,128]{1,0:T(1,128)S(1)} %bitcast.36), channel_id=1, source_target_pairs={{0,224},{32,0},{64,32},{96,64},{128,96},{160,128},{192,160},{224,1... | collective-permute-start | bytes 1544 | tf_op jit(solution)/shard_map/ppermute | solution.py:282
  148.6 0.6 copy-start.5
  148.6 0.6 copy-start.6

commit v9 on v8

--- a/solution.py
+++ b/solution.py
@@ -16,7 +16,7 @@
 EPSILON = 1e-06
 F32 = jnp.float32
 BF16 = jnp.bfloat16
-VMEM_LIMIT = 48 * 1024 * 1024
+VMEM_LIMIT = 20 * 1024 * 1024
 VMEM_WHOLE = 64 * 1024 * 1024 - 512 * 1024
 
 
@@ -78,7 +78,7 @@
             send_ref[chip, ES * MAIN :, :] = rows
 
 
-def prepare(current, ids_row, gain):
+def prepare(current, ids_row, gain, vmem):
     tokens, features = current.shape
     quarter = features // ES
     return pl.pallas_call(
@@ -91,42 +91,28 @@
             pltpu.VMEM(gain.shape, gain.dtype),
             pltpu.SemaphoreType.DMA((3,)),
         ],
-        compiler_params=pltpu.CompilerParams(vmem_limit_bytes=VMEM_WHOLE),
+        compiler_params=pltpu.CompilerParams(vmem_limit_bytes=vmem),
         cost_estimate=pl.CostEstimate(
             flops=3 * tokens * tokens * features, bytes_accessed=8 * tokens * features, transcendentals=0
         ),
     )(current, ids_row, gain)
 
 
-def hidden_kernel(
-    received_hbm, gate_hbm, up_hbm, hidden_ref, received_ref, gate_ref, up_ref, ready
-):
+def hidden_kernel(received_ref, gate_ref, up_ref, hidden_ref):
     quarter = received_ref.shape[2]
     count = CHIPS * (MAIN + LAST)
-    loads = [pltpu.make_async_copy(received_hbm, received_ref, ready.at[2 * ES])]
-    for q in range(ES):
-        part = pl.ds(q * quarter, quarter)
-        for side, (source, target) in enumerate(((gate_hbm, gate_ref), (up_hbm, up_ref))):
-            loads.append(
-                pltpu.make_async_copy(source.at[part, :], target.at[part, :], ready.at[2 * q + side])
-            )
-    for load in loads:
-        load.start()
     gate = jnp.zeros((count, gate_ref.shape[1]), F32)
     up = jnp.zeros((count, up_ref.shape[1]), F32)
     shape = (CHIPS * LAST, CHIPS * ES * LAST)
     target = iota(shape, 0)
     source = (target // LAST) * (ES * LAST) + target % LAST
-    loads[0].wait()
     last = received_ref[:, ES * MAIN :, :].astype(F32)
     last = last.reshape(CHIPS * ES * LAST, quarter).astype(BF16)
     for q in range(ES):
         main = received_ref[:, q * MAIN : (q + 1) * MAIN, :].reshape(CHIPS * MAIN, quarter)
         pick = (iota(shape, 1) == source + q * LAST).astype(BF16)
         rows = jnp.concatenate([main, dot(pick, last).astype(BF16)], axis=0)
-        loads[1 + 2 * q].wait()
         gate = gate + dot(rows, gate_ref[q * quarter : (q + 1) * quarter, :])
-        loads[2 + 2 * q].wait()
         up = up + dot(rows, up_ref[q * quarter : (q + 1) * quarter, :])
     hidden_ref[...] = (jax.nn.silu(gate) * up).astype(BF16)
 
@@ -137,14 +123,7 @@
     return pl.pallas_call(
         hidden_kernel,
         out_shape=jax.ShapeDtypeStruct((count, width), BF16),
-        in_specs=[pl.BlockSpec(memory_space=pltpu.HBM)] * 3,
-        scratch_shapes=[
-            pltpu.VMEM(received.shape, received.dtype),
-            pltpu.VMEM(gate_cols.shape, gate_cols.dtype),
-            pltpu.VMEM(up_cols.shape, up_cols.dtype),
-            pltpu.SemaphoreType.DMA((2 * ES + 1,)),
-        ],
-        compiler_params=pltpu.CompilerParams(vmem_limit_bytes=VMEM_WHOLE),
+        compiler_params=pltpu.CompilerParams(vmem_limit_bytes=VMEM_LIMIT),
         cost_estimate=pl.CostEstimate(
             flops=4 * count * features * width,
             bytes_accessed=4 * features * width + 2 * count * features,
@@ -193,15 +172,7 @@
     )(mine, theirs, *down, *other_down)
 
 
-def finish_kernel(
-    current_hbm, back_hbm, ids_ref, scores_ref, out_hbm, current_ref, back_ref, out_ref, ready, done
-):
-    loads = [
-        pltpu.make_async_copy(back_hbm, back_ref, ready.at[0]),
-        pltpu.make_async_copy(current_hbm, current_ref, ready.at[1]),
-    ]
-    for load in loads:
-        load.start()
+def finish_kernel(current_ref, back_ref, ids_ref, scores_ref, out_ref):
     tokens, features = current_ref.shape
     quarter = features // ES
     ids_row = ids_ref[...]
@@ -215,12 +186,9 @@
     lane = iota((tokens, CHIPS * ES * LAST), 1)
     in_expert = (lane // (2 * ES * LAST) == ids_column) & (slot >= MAIN)
     in_block = lane % (ES * LAST)
-    loads[0].wait()
     last = jnp.concatenate(
         [back_ref[chip, ES * MAIN :, :].astype(F32) for chip in range(CHIPS)], axis=0
     ).astype(BF16)
-    loads[1].wait()
-    stores = []
     for q in range(ES):
         main = jnp.concatenate(
             [back_ref[chip, q * MAIN : (q + 1) * MAIN, :] for chip in range(CHIPS)], axis=0
@@ -229,11 +197,6 @@
         moe = (dot(pick_main, main) + dot(pick_last.astype(BF16), last)) * score
         columns = slice(q * quarter, (q + 1) * quarter)
         out_ref[:, columns] = (current_ref[:, columns].astype(F32) + moe).astype(BF16)
-        part = pl.ds(q * quarter, quarter)
-        stores.append(pltpu.make_async_copy(out_ref.at[:, part], out_hbm.at[:, part], done.at[q]))
-        stores[q].start()
-    for store in stores:
-        store.wait()
 
 
 def finish(current, back, ids_row, scores_row):
@@ -241,17 +204,7 @@
     return pl.pallas_call(
         finish_kernel,
         out_shape=jax.ShapeDtypeStruct((tokens, features), BF16),
-        in_specs=[pl.BlockSpec(memory_space=pltpu.HBM)] * 2
-        + [pl.BlockSpec(memory_space=pltpu.VMEM)] * 2,
-        out_specs=pl.BlockSpec(memory_space=pltpu.HBM),
-        scratch_shapes=[
-            pltpu.VMEM(current.shape, BF16),
-            pltpu.VMEM(back.shape, BF16),
-            pltpu.VMEM(current.shape, BF16),
-            pltpu.SemaphoreType.DMA((2,)),
-            pltpu.SemaphoreType.DMA((ES,)),
-        ],
-        compiler_params=pltpu.CompilerParams(vmem_limit_bytes=VMEM_WHOLE),
+        compiler_params=pltpu.CompilerParams(vmem_limit_bytes=VMEM_LIMIT),
         cost_estimate=pl.CostEstimate(
             flops=6 * tokens * EXPERTS * MAIN * features,
             bytes_accessed=8 * tokens * features,
@@ -306,10 +259,10 @@
     marks_a, marks_b = scores_a.reshape(1, tokens), scores_b.reshape(1, tokens)
     gate_cols, up_cols, down = w_gate[0], w_up[0], w_down[0]
 
-    own_a = exchange(prepare(current_a, ids_a, norm_gain))
+    own_a = exchange(prepare(current_a, ids_a, norm_gain, VMEM_WHOLE))
     other_down = swap_cores(down)
     staged_b, other_down = lax.optimization_barrier((current_b, other_down))
-    send_b = prepare(staged_b, ids_b, norm_gain)
+    send_b = prepare(staged_b, ids_b, norm_gain, VMEM_LIMIT)
     middle = down.shape[0] // 2
     upper = from_behind(down[:middle], -1)
     own_a, send_b, upper = lax.optimization_barrier((own_a, send_b, upper))

time: 154 us -> 150 us (0.974)
  Pallas kernels: 47.8 us -> 29.4 us
  waiting for transfers between devices: 43.9 us -> 55 us
  starting transfers between devices: 53.8 us -> 55.6 us
    pallas_call x4, Pallas kernels: 23.7 us -> 13.1 us  [hidden_units(): pl.pallas_call(hidden_kernel, out_shape=jax.ShapeDtypeStruct((count, widt...]
    ppermute x7, waiting for transfers between devices: 33.6 us -> 41.4 us  [from_behind(): lax.ppermute(value, 'section', [(i, (i + steps) % count) for i in range(c...]
    pallas_call x2, Pallas kernels: 7.85 us -> 4.34 us  [finish(): pl.pallas_call(finish_kernel, out_shape=jax.ShapeDtypeStruct((tokens, fea...]
    all_to_all x4, waiting for transfers between devices: 4.7 us -> 7.89 us  [exchange(): lax.all_to_all(blocks, 'ep', split_axis=0, concat_axis=0, axis_index_grou...]
    ppermute x7, starting transfers between devices: 24.6 us -> 27.6 us  [from_behind(): lax.ppermute(value, 'section', [(i, (i + steps) % count) for i in range(c...]
    pallas_call x2, Pallas kernels: 6.72 us -> 4.58 us  [prepare(): pl.pallas_call(prepare_kernel, out_shape=jax.ShapeDtypeStruct((CHIPS, ES...]
    pallas_call x2, Pallas kernels: 8.55 us -> 6.47 us  [down_product(): pl.pallas_call(functools.partial(down_kernel, len(down)), out_shape=jax.S...]
    unnamed x18 -> x36, local copies, waits for them, and re-layouts: 5.54 us -> 7 us
  transfers between devices with their start and end apart: 18 -> 18, of which waited for: 7 -> 7; matrix products, arithmetic and copies ran while one was open for 1% -> 1% of each run, Pallas kernels for 26% -> 16%
where the time goes in v9:
time: 150 us; the launch traced here: 149 us
  starting transfers between devices  55.6 us (37%)
  waiting for transfers between devices  55 us (37%)
  Pallas kernels  29.4 us (20%)
  local copies, waits for them, and re-layouts  8.04 us (5%)
    ppermute x7, waiting for transfers between devices, from_behind(): lax.ppermute(value, 'section', [(i, (i + steps) % count) for i in range(c...  41.4 us
    ppermute x7, starting transfers between devices, from_behind(): lax.ppermute(value, 'section', [(i, (i + steps) % count) for i in range(c...  27.6 us
    all_to_all x4, starting transfers between devices, exchange(): lax.all_to_all(blocks, 'ep', split_axis=0, concat_axis=0, axis_index_grou...  26.8 us
    pallas_call x4, Pallas kernels, hidden_units(): pl.pallas_call(hidden_kernel, out_shape=jax.ShapeDtypeStruct((count, widt...  13.1 us
    all_to_all x4, waiting for transfers between devices, exchange(): lax.all_to_all(blocks, 'ep', split_axis=0, concat_axis=0, axis_index_grou...  7.89 us
    unnamed x36, local copies, waits for them, and re-layouts  7 us
    pallas_call x2, Pallas kernels, down_product(): pl.pallas_call(functools.partial(down_kernel, len(down)), out_shape=jax.S...  6.47 us
    ppermute x1, waiting for transfers between devices, behind_other_core(): return lax.ppermute(value, ('section', 'ep'), pairs)  5.7 us
  transfers between devices with their start and end apart: 18, of which 7 were waited for; matrix products, arithmetic and copies ran while one was open for 1% of the time, Pallas kernels for 16%

profile of v9, /device:TPU:8, one launch (start us, length us, event | category | flops | bytes accessed | tf_op | source)
XLA Modules:
  0.0 148.9 jit_solution(11886883845052638260)
XLA Ops:
  0.6 3.4 %shard_map.113 = bf16[16,72,896]{2,1,0:T(8,128)(2,1)} custom-call(bf16[128,3584]{1,0:T(8,128)(2,1)} %bitcast.25, s32[1,128]{1,0:T(1,128)} %bitcast.29, f32[1,3584]{1,0:T(1,128)} %gain_hbm.3), custom_call_target="tpu_custom_call" | custom-call | flops 176160768 | bytes 3670016 | tf_op jit(solution)/shard_map/pallas_call | solution.py:84
  4.0 0.0 copy-start.6
  4.0 7.5 %all-to-all-start = ((bf16[16,72,896]{2,1,0:T(8,128)(2,1)}), bf16[16,72,896]{2,1,0:T(8,128)(2,1)}, u32[]{:S(2)}, u32[]{:S(2)}) async-start(bf16[16,72,896]{2,1,0:T(8,128)(2,1)} %shard_map.113), calls=%async_computation | async-start | bytes 4128768 | tf_op jit(solution)/shard_map/all_to_all | solution.py:248
  11.6 0.0 copy-start.13
  11.6 0.0 copy-start.16
  11.6 0.1 collective-permute-start
  11.7 1.0 slice_bitcast_fusion
  12.8 5.9 %collective-permute-start.1 = (bf16[128,3584]{1,0:T(8,128)(2,1)S(1)}, bf16[128,3584]{1,0:T(8,128)(2,1)S(1)}, u32[]{:S(2)}, u32[]{:S(2)}) collective-permute-start(bf16[128,3584]{1,0:T(8,128)(2,1)S(1)} %get-tuple-element.23), channel_id=1, source_target_pairs={{0,224},{32,0},{64,32},{96,64},{128,96},{160,128},{192,160},{224,1... | collective-permute-start | bytes 2752520 | tf_op jit(solution)/shard_map/ppermute | solution.py:235
  18.6 0.0 collective-permute-done.refs_1_
  18.6 1.3 copy-done.9
  19.9 1.2 shard_map.114
  21.1 1.3 copy-done.5
  22.4 16.5 %collective-permute-done.1.refs_0_ = bf16[128,3584]{1,0:T(8,128)(2,1)S(1)} collective-permute-done((bf16[128,3584]{1,0:T(8,128)(2,1)S(1)}, bf16[128,3584]{1,0:T(8,128)(2,1)S(1)}, u32[]{:S(2)}, u32[]{:S(2)}) %collective-permute-start.1) | collective-permute-done | bytes 917536 | tf_op jit(solution)/shard_map/ppermute | solution.py:235
  38.9 1.4 all-to-all-done.received_ref
  40.3 5.8 %all-to-all-start.1 = ((bf16[16,72,896]{2,1,0:T(8,128)(2,1)}), bf16[16,72,896]{2,1,0:T(8,128)(2,1)}, u32[]{:S(2)}, u32[]{:S(2)}) async-start(bf16[16,72,896]{2,1,0:T(8,128)(2,1)} %copy-done.5), calls=%async_computation.1 | async-start | bytes 4128768 | tf_op jit(solution)/shard_map/all_to_all | solution.py:248
  46.1 5.6 %collective-permute-start.4 = (bf16[128,3584]{1,0:T(8,128)(2,1)}, bf16[128,3584]{1,0:T(8,128)(2,1)}, u32[]{:S(2)}, u32[]{:S(2)}) collective-permute-start(bf16[128,3584]{1,0:T(8,128)(2,1)} %get-tuple-element.22), channel_id=1, source_target_pairs={{0,224},{32,0},{64,32},{96,64},{128,96},{160,128},{192,160},{224,1... | collective-permute-start | bytes 2752520 | tf_op jit(solution)/shard_map/ppermute | solution.py:235
  51.8 1.5 %copy-done.1 = bf16[1,3584,256]{2,1,0:T(8,128)(2,1)S(1)} copy-done((bf16[1,3584,256]{2,1,0:T(8,128)(2,1)S(1)}, bf16[1,3584,256]{2,1,0:T(8,128)(2,1)}, u32[]{:S(2)}) %copy-start.1) | copy-done | bytes 1835032
  53.3 3.3 %shard_map.116 = bf16[288,256]{1,0:T(8,128)(2,1)S(1)} custom-call(bf16[16,72,896]{2,1,0:T(8,128)(2,1)} %collective-permute-done.2.received_ref, bf16[3584,256]{1,0:T(8,128)(2,1)S(1)} %bitcast.15, bf16[3584,256]{1,0:T(8,128)(2,1)S(1)} %bitcast.19), custom_call_target="tpu_custom_call" | custom-call | flops 1056964608 | bytes 5734400 | tf_op jit(solution)/shard_map/pallas_call | solution.py:123
  56.6 0.0 copy-start.7
  56.6 0.1 collective-permute-start.3
  56.7 3.3 %shard_map.115.mine_ref = bf16[288,256]{1,0:T(8,128)(2,1)S(1)} custom-call(bf16[16,72,896]{2,1,0:T(8,128)(2,1)} %all-to-all-done.received_ref, bf16[3584,256]{1,0:T(8,128)(2,1)S(1)} %bitcast.16, bf16[3584,256]{1,0:T(8,128)(2,1)S(1)} %bitcast.20), custom_call_target="tpu_custom_call" | custom-call | flops 1056964608 | bytes 5734400 | tf_op jit(solution)/shard_map/pallas_call | solution.py:123
  60.1 0.0 collective-permute-done.3.theirs_ref
  60.1 2.0 %shard_map.117 = bf16[16,72,896]{2,1,0:T(8,128)(2,1)S(1)} custom-call(bf16[288,256]{1,0:T(8,128)(2,1)S(1)} %shard_map.115.mine_ref, bf16[288,256]{1,0:T(8,128)(2,1)S(1)} %collective-permute-done.3.theirs_ref, bf16[256,3584]{1,0:T(8,128)(2,1)S(1)} %bitcast.24, bf16[256,3584]{1,0:T(8,128)(2,1)S(1)} %copy-done.10), custom_call_target="tpu_custom_call" | custom-call | flops 1056964608 | bytes 5734400 | tf_op jit(solution)/shard_map/pallas_call | solution.py:163
  62.1 1.4 copy-done.4
  63.5 8.6 %collective-permute-done.4.refs_1_ = bf16[128,3584]{1,0:T(8,128)(2,1)} collective-permute-done((bf16[128,3584]{1,0:T(8,128)(2,1)}, bf16[128,3584]{1,0:T(8,128)(2,1)}, u32[]{:S(2)}, u32[]{:S(2)}) %collective-permute-start.4) | collective-permute-done | bytes 917536 | tf_op jit(solution)/shard_map/ppermute | solution.py:235
  72.1 3.2 %all-to-all-done.1.received_ref = bf16[16,72,896]{2,1,0:T(8,128)(2,1)} async-done(((bf16[16,72,896]{2,1,0:T(8,128)(2,1)}), bf16[16,72,896]{2,1,0:T(8,128)(2,1)}, u32[]{:S(2)}, u32[]{:S(2)}) %all-to-all-start.1) | async-done | bytes 2064416 | tf_op jit(solution)/shard_map/all_to_all | solution.py:248
  75.3 0.0 collective-permute-start.6
  75.3 6.8 %all-to-all-start.2 = ((bf16[16,72,896]{2,1,0:T(8,128)(2,1)}), bf16[16,72,896]{2,1,0:T(8,128)(2,1)}, u32[]{:S(2)}, u32[]{:S(2)}) async-start(bf16[16,72,896]{2,1,0:T(8,128)(2,1)} %copy-done.4), calls=%async_computation.2 | async-start | bytes 4128768 | tf_op jit(solution)/shard_map/all_to_all | solution.py:248
  82.1 0.5 collective-permute-start.9
  82.6 1.5 %copy-done.3 = bf16[1,3584,256]{2,1,0:T(8,128)(2,1)S(1)} copy-done((bf16[1,3584,256]{2,1,0:T(8,128)(2,1)S(1)}, bf16[1,3584,256]{2,1,0:T(8,128)(2,1)}, u32[]{:S(2)}) %copy-start.3) | copy-done | bytes 1835032
  84.1 3.2 %shard_map.118 = bf16[288,256]{1,0:T(8,128)(2,1)S(1)} custom-call(bf16[16,72,896]{2,1,0:T(8,128)(2,1)} %all-to-all-done.1.received_ref, bf16[3584,256]{1,0:T(8,128)(2,1)S(1)} %bitcast.17, bf16[3584,256]{1,0:T(8,128)(2,1)S(1)} %bitcast.21), custom_call_target="tpu_custom_call" | custom-call | flops 1056964608 | bytes 5734400 | tf_op jit(solution)/shard_map/pallas_call | solution.py:123
  87.3 6.6 %collective-permute-start.5 = (bf16[288,256]{1,0:T(8,128)(2,1)S(1)}, bf16[288,256]{1,0:T(8,128)(2,1)S(1)}, u32[]{:S(2)}, u32[]{:S(2)}) collective-permute-start(bf16[288,256]{1,0:T(8,128)(2,1)S(1)} %shard_map.118), channel_id=1, source_target_pairs={{0,224},{32,0},{64,32},{96,64},{128,96},{160,128},{192,160},{224,1... | collective-permute-start | bytes 442376 | tf_op jit(solution)/shard_map/ppermute | solution.py:235
  93.9 3.2 %shard_map.119 = bf16[288,256]{1,0:T(8,128)(2,1)S(1)} custom-call(bf16[16,72,896]{2,1,0:T(8,128)(2,1)} %collective-permute-done.6.received_ref, bf16[3584,256]{1,0:T(8,128)(2,1)S(1)} %bitcast.18, bf16[3584,256]{1,0:T(8,128)(2,1)S(1)} %bitcast.22), custom_call_target="tpu_custom_call" | custom-call | flops 1056964608 | bytes 5734400 | tf_op jit(solution)/shard_map/pallas_call | solution.py:123
  97.1 0.5 collective-permute-start.7
  97.7 5.7 %collective-permute-done.7.theirs_ref = bf16[288,256]{1,0:T(8,128)(2,1)S(1)} collective-permute-done((bf16[288,256]{1,0:T(8,128)(2,1)S(1)}, bf16[288,256]{1,0:T(8,128)(2,1)S(1)}, u32[]{:S(2)}, u32[]{:S(2)}) %collective-permute-start.7) | collective-permute-done | bytes 147488 | tf_op jit(solution)/shard_map/ppermute | solution.py:243
  103.4 4.5 %shard_map.120 = bf16[16,72,896]{2,1,0:T(8,128)(2,1)} custom-call(bf16[288,256]{1,0:T(8,128)(2,1)S(1)} %collective-permute-done.5.mine_ref, bf16[288,256]{1,0:T(8,128)(2,1)S(1)} %collective-permute-done.7.theirs_ref, bf16[128,3584]{1,0:T(8,128)(2,1)S(1)} %collective-permute-done.1.refs_0_, bf16[128,3584]{1,0:T(8,128)(2,1)} %collective-permute-done.4.refs_1_, ...), custom_call_target="tpu_custom_call" | custom-call | flops 1056964608 | bytes 5734400 | tf_op jit(solution)/shard_map/pallas_call | solution.py:163
  107.9 3.3 %all-to-all-done.2.back_ref = bf16[16,72,896]{2,1,0:T(8,128)(2,1)} async-done(((bf16[16,72,896]{2,1,0:T(8,128)(2,1)}), bf16[16,72,896]{2,1,0:T(8,128)(2,1)}, u32[]{:S(2)}, u32[]{:S(2)}) %all-to-all-start.2) | async-done | bytes 2064416 | tf_op jit(solution)/shard_map/all_to_all | solution.py:248
  111.1 6.6 %all-to-all-start.3 = ((bf16[16,72,896]{2,1,0:T(8,128)(2,1)}), bf16[16,72,896]{2,1,0:T(8,128)(2,1)S(1)}, u32[]{:S(2)}, u32[]{:S(2)}) async-start(bf16[16,72,896]{2,1,0:T(8,128)(2,1)} %shard_map.120), calls=%async_computation.3 | async-start | bytes 4128768 | tf_op jit(solution)/shard_map/all_to_all | solution.py:248
  117.8 0.0 copy-start.12
  117.8 0.0 copy-start.17
  117.8 2.5 %shard_map.121 = bf16[128,3584]{1,0:T(8,128)(2,1)S(1)} custom-call(bf16[128,3584]{1,0:T(8,128)(2,1)S(1)} %bitcast.26, bf16[16,72,896]{2,1,0:T(8,128)(2,1)} %all-to-all-done.2.back_ref, s32[1,128]{1,0:T(1,128)S(1)} %bitcast.30, f32[1,128]{1,0:T(1,128)S(1)} %bitcast.31), custom_call_target="tpu_custom_call" | custom-call | flops 352321536 | bytes 3670016 | tf_op jit(solution)/shard_map/pallas_call | solution.py:204
  120.3 2.5 %collective-permute-start.10 = (bf16[128,3584]{1,0:T(8,128)(2,1)S(1)}, bf16[128,3584]{1,0:T(8,128)(2,1)S(1)}, u32[]{:S(2)}, u32[]{:S(2)}) collective-permute-start(bf16[128,3584]{1,0:T(8,128)(2,1)S(1)} %shard_map.121), channel_id=1, source_target_pairs={{0,32},{32,64},{64,96},{96,128},{128,160},{160,192},{192,224},{224... | collective-permute-start | bytes 2752520 | tf_op jit(solution)/shard_map/ppermute | solution.py:235
  122.9 4.0 %collective-permute-start.11 = (bf16[128,3584]{1,0:T(8,128)(2,1)S(1)}, bf16[128,3584]{1,0:T(8,128)(2,1)S(1)}, u32[]{:S(2)}, u32[]{:S(2)}) collective-permute-start(bf16[128,3584]{1,0:T(8,128)(2,1)S(1)} %bitcast.28), channel_id=1, source_target_pairs={{0,224},{32,0},{64,32},{96,64},{128,96},{160,128},{192,160},{224,1... | collective-permute-start | bytes 2752520 | tf_op jit(solution)/shard_map/ppermute | solution.py:235
  126.9 1.9 %collective-permute-start.12 = (s32[1,128]{1,0:T(1,128)S(1)}, s32[1,128]{1,0:T(1,128)S(1)}, u32[]{:S(2)}, u32[]{:S(2)}) collective-permute-start(s32[1,128]{1,0:T(1,128)S(1)} %bitcast.33), channel_id=1, source_target_pairs={{0,224},{32,0},{64,32},{96,64},{128,96},{160,128},{192,160},{224,1... | collective-permute-start | bytes 1544 | tf_op jit(solution)/shard_map/ppermute | solution.py:235
  128.8 1.0 collective-permute-start.13
  129.8 16.3 %collective-permute-done.10.value_ref = bf16[128,3584]{1,0:T(8,128)(2,1)S(1)} collective-permute-done((bf16[128,3584]{1,0:T(8,128)(2,1)S(1)}, bf16[128,3584]{1,0:T(8,128)(2,1)S(1)}, u32[]{:S(2)}, u32[]{:S(2)}) %collective-permute-start.10) | collective-permute-done | bytes 917536 | tf_op jit(solution)/shard_map/ppermute | solution.py:235
  146.1 1.0 shard_map.122
  147.1 1.8 %shard_map.123 = bf16[128,3584]{1,0:T(8,128)(2,1)} custom-call(bf16[128,3584]{1,0:T(8,128)(2,1)S(1)} %collective-permute-done.11.current_ref, bf16[16,72,896]{2,1,0:T(8,128)(2,1)S(1)} %all-to-all-done.3.back_ref, s32[1,128]{1,0:T(1,128)S(1)} %collective-permute-done.12.ids_ref, f32[1,128]{1,0:T(1,128)S(1)} %collective-permute-done.13.scores_ref), custom_call_target="tpu_custom_call" | custom-call | flops 352321536 | bytes 3670016 | tf_op jit(solution)/shard_map/pallas_call | solution.py:204
  (36 shorter events, 0.1 us)
Async XLA Ops:
  4.0 7.6 %copy-start.6 = (bf16[1,256,3584]{2,1,0:T(8,128)(2,1)S(1)}, bf16[1,256,3584]{2,1,0:T(8,128)(2,1)}, u32[]{:S(2)}) copy-start(bf16[1,256,3584]{2,1,0:T(8,128)(2,1)} %param.19) | copy-start | bytes 5505028
  4.0 36.2 %all-to-all-start = ((bf16[16,72,896]{2,1,0:T(8,128)(2,1)}), bf16[16,72,896]{2,1,0:T(8,128)(2,1)}, u32[]{:S(2)}, u32[]{:S(2)}) async-start(bf16[16,72,896]{2,1,0:T(8,128)(2,1)} %shard_map.113), calls=%async_computation | async-start | bytes 4128768 | tf_op jit(solution)/shard_map/all_to_all | solution.py:248
  11.6 8.3 %copy-start.11 = (bf16[1,128,3584]{2,1,0:T(8,128)(2,1)S(1)}, bf16[1,128,3584]{2,1,0:T(8,128)(2,1)}, u32[]{:S(2)}) copy-start(bf16[1,128,3584]{2,1,0:T(8,128)(2,1)} %param.11) | copy-start | bytes 2752516
  11.6 8.3 %copy-start.13 = (f32[1,3584]{1,0:T(1,128)S(1)}, f32[1,3584]{1,0:T(1,128)}, u32[]{:S(2)}) copy-start(f32[1,3584]{1,0:T(1,128)} %gain_hbm.3) | copy-start | bytes 43012
  11.6 8.3 %copy-start.16 = (s32[1,1,128,1]{2,3,1,0:T(1,128)S(1)}, s32[1,1,128,1]{2,3,1,0:T(1,128)}, u32[]{:S(2)}) copy-start(s32[1,1,128,1]{2,3,1,0:T(1,128)} %param.13) | copy-start | bytes 1540
  11.6 7.0 %collective-permute-start = (bf16[256,3584]{1,0:T(8,128)(2,1)S(1)}, bf16[256,3584]{1,0:T(8,128)(2,1)S(1)}, u32[]{:S(2)}, u32[]{:S(2)}) collective-permute-start(bf16[256,3584]{1,0:T(8,128)(2,1)S(1)} %bitcast.23), channel_id=1, source_target_pairs={{0,1},{1,0},{2,3},{3,2},{4,5},{5,4},{6,7},{7,6},{8,9},{9,8},{10,11... | collective-permute-start | bytes 5505032 | tf_op jit(solution)/shard_map/ppermute | solution.py:230
  12.8 26.1 %collective-permute-start.1 = (bf16[128,3584]{1,0:T(8,128)(2,1)S(1)}, bf16[128,3584]{1,0:T(8,128)(2,1)S(1)}, u32[]{:S(2)}, u32[]{:S(2)}) collective-permute-start(bf16[128,3584]{1,0:T(8,128)(2,1)S(1)} %get-tuple-element.23), channel_id=1, source_target_pairs={{0,224},{32,0},{64,32},{96,64},{128,96},{160,128},{192,160},{224,1... | collective-permute-start | bytes 2752520 | tf_op jit(solution)/shard_map/ppermute | solution.py:235
  18.6 1.3 copy-start.9
  21.1 1.3 copy-start.5
  22.4 29.4 %copy-start = (bf16[1,3584,256]{2,1,0:T(8,128)(2,1)S(1)}, bf16[1,3584,256]{2,1,0:T(8,128)(2,1)}, u32[]{:S(2)}) copy-start(bf16[1,3584,256]{2,1,0:T(8,128)(2,1)} %param.17) | copy-start | bytes 5505028
  40.3 11.5 %collective-permute-start.2 = (bf16[16,72,896]{2,1,0:T(8,128)(2,1)}, bf16[16,72,896]{2,1,0:T(8,128)(2,1)}, u32[]{:S(2)}, u32[]{:S(2)}) collective-permute-start(bf16[16,72,896]{2,1,0:T(8,128)(2,1)} %all-to-all-done.received_ref), channel_id=1, source_target_pairs={{0,1},{1,0},{2,3},{3,2},{4,5},{5,4},{6,7},{7,6},{8,9},{9,8},{10,11... | collective-permute-start | bytes 6193160 | tf_op jit(solution)/shard_map/ppermute | solution.py:230
  40.3 35.0 %all-to-all-start.1 = ((bf16[16,72,896]{2,1,0:T(8,128)(2,1)}), bf16[16,72,896]{2,1,0:T(8,128)(2,1)}, u32[]{:S(2)}, u32[]{:S(2)}) async-start(bf16[16,72,896]{2,1,0:T(8,128)(2,1)} %copy-done.5), calls=%async_computation.1 | async-start | bytes 4128768 | tf_op jit(solution)/shard_map/all_to_all | solution.py:248
  46.1 26.0 %collective-permute-start.4 = (bf16[128,3584]{1,0:T(8,128)(2,1)}, bf16[128,3584]{1,0:T(8,128)(2,1)}, u32[]{:S(2)}, u32[]{:S(2)}) collective-permute-start(bf16[128,3584]{1,0:T(8,128)(2,1)} %get-tuple-element.22), channel_id=1, source_target_pairs={{0,224},{32,0},{64,32},{96,64},{128,96},{160,128},{192,160},{224,1... | collective-permute-start | bytes 2752520 | tf_op jit(solution)/shard_map/ppermute | solution.py:235
  51.8 1.5 %copy-start.1 = (bf16[1,3584,256]{2,1,0:T(8,128)(2,1)S(1)}, bf16[1,3584,256]{2,1,0:T(8,128)(2,1)}, u32[]{:S(2)}) copy-start(bf16[1,3584,256]{2,1,0:T(8,128)(2,1)} %param.18) | copy-start | bytes 5505028
  53.3 3.5 %copy-start.2 = (bf16[1,3584,256]{2,1,0:T(8,128)(2,1)S(1)}, bf16[1,3584,256]{2,1,0:T(8,128)(2,1)}, u32[]{:S(2)}) copy-start(bf16[1,3584,256]{2,1,0:T(8,128)(2,1)} %param.18) | copy-start | bytes 5505028
  56.6 3.5 %copy-start.7 = (bf16[1,256,3584]{2,1,0:T(8,128)(2,1)S(1)}, bf16[1,256,3584]{2,1,0:T(8,128)(2,1)}, u32[]{:S(2)}) copy-start(bf16[1,256,3584]{2,1,0:T(8,128)(2,1)} %param.19) | copy-start | bytes 5505028
  56.6 3.5 %copy-start.10 = (bf16[256,3584]{1,0:T(8,128)(2,1)S(1)}, bf16[256,3584]{1,0:T(8,128)(2,1)}, u32[]{:S(2)}) copy-start(bf16[256,3584]{1,0:T(8,128)(2,1)} %copy-done.9) | copy-start | bytes 5505028
  56.6 3.5 %collective-permute-start.3 = (bf16[288,256]{1,0:T(8,128)(2,1)S(1)}, bf16[288,256]{1,0:T(8,128)(2,1)S(1)}, u32[]{:S(2)}, u32[]{:S(2)}) collective-permute-start(bf16[288,256]{1,0:T(8,128)(2,1)S(1)} %shard_map.116), channel_id=1, source_target_pairs={{0,1},{1,0},{2,3},{3,2},{4,5},{5,4},{6,7},{7,6},{8,9},{9,8},{10,11... | collective-permute-start | bytes 442376 | tf_op jit(solution)/shard_map/ppermute | solution.py:230
  62.1 1.4 copy-start.4
  75.3 18.6 %collective-permute-start.6 = (bf16[16,72,896]{2,1,0:T(8,128)(2,1)}, bf16[16,72,896]{2,1,0:T(8,128)(2,1)}, u32[]{:S(2)}, u32[]{:S(2)}) collective-permute-start(bf16[16,72,896]{2,1,0:T(8,128)(2,1)} %all-to-all-done.1.received_ref), channel_id=1, source_target_pairs={{0,1},{1,0},{2,3},{3,2},{4,5},{5,4},{6,7},{7,6},{8,9},{9,8},{10,11... | collective-permute-start | bytes 6193160 | tf_op jit(solution)/shard_map/ppermute | solution.py:230
  75.3 35.9 %all-to-all-start.2 = ((bf16[16,72,896]{2,1,0:T(8,128)(2,1)}), bf16[16,72,896]{2,1,0:T(8,128)(2,1)}, u32[]{:S(2)}, u32[]{:S(2)}) async-start(bf16[16,72,896]{2,1,0:T(8,128)(2,1)} %copy-done.4), calls=%async_computation.2 | async-start | bytes 4128768 | tf_op jit(solution)/shard_map/all_to_all | solution.py:248
  82.1 15.6 %collective-permute-start.8 = (bf16[128,3584]{1,0:T(8,128)(2,1)S(1)}, bf16[128,3584]{1,0:T(8,128)(2,1)S(1)}, u32[]{:S(2)}, u32[]{:S(2)}) collective-permute-start(bf16[128,3584]{1,0:T(8,128)(2,1)S(1)} %collective-permute-done.1.refs_0_), channel_id=1, source_target_pairs={{0,1},{1,0},{2,3},{3,2},{4,5},{5,4},{6,7},{7,6},{8,9},{9,8},{10,11... | collective-permute-start | bytes 2752520 | tf_op jit(solution)/shard_map/ppermute | solution.py:230
  82.1 15.6 %collective-permute-start.9 = (bf16[128,3584]{1,0:T(8,128)(2,1)}, bf16[128,3584]{1,0:T(8,128)(2,1)S(1)}, u32[]{:S(2)}, u32[]{:S(2)}) collective-permute-start(bf16[128,3584]{1,0:T(8,128)(2,1)} %collective-permute-done.4.refs_1_), channel_id=1, source_target_pairs={{0,1},{1,0},{2,3},{3,2},{4,5},{5,4},{6,7},{7,6},{8,9},{9,8},{10,11... | collective-permute-start | bytes 2752520 | tf_op jit(solution)/shard_map/ppermute | solution.py:230
  82.6 1.5 %copy-start.3 = (bf16[1,3584,256]{2,1,0:T(8,128)(2,1)S(1)}, bf16[1,3584,256]{2,1,0:T(8,128)(2,1)}, u32[]{:S(2)}) copy-start(bf16[1,3584,256]{2,1,0:T(8,128)(2,1)} %param.18) | copy-start | bytes 5505028
  87.3 10.3 %collective-permute-start.5 = (bf16[288,256]{1,0:T(8,128)(2,1)S(1)}, bf16[288,256]{1,0:T(8,128)(2,1)S(1)}, u32[]{:S(2)}, u32[]{:S(2)}) collective-permute-start(bf16[288,256]{1,0:T(8,128)(2,1)S(1)} %shard_map.118), channel_id=1, source_target_pairs={{0,224},{32,0},{64,32},{96,64},{128,96},{160,128},{192,160},{224,1... | collective-permute-start | bytes 442376 | tf_op jit(solution)/shard_map/ppermute | solution.py:235
  97.1 6.2 %collective-permute-start.7 = (bf16[288,256]{1,0:T(8,128)(2,1)S(1)}, bf16[288,256]{1,0:T(8,128)(2,1)S(1)}, u32[]{:S(2)}, u32[]{:S(2)}) collective-permute-start(bf16[288,256]{1,0:T(8,128)(2,1)S(1)} %shard_map.119), channel_id=1, source_target_pairs={{0,225},{1,224},{2,227},{3,226},{4,229},{5,228},{6,231},{7,230},{8... | collective-permute-start | bytes 442376 | tf_op jit(solution)/shard_map/ppermute | solution.py:243
  107.9 9.9 %copy-start.8 = (bf16[1,128,3584]{2,1,0:T(8,128)(2,1)S(1)}, bf16[1,128,3584]{2,1,0:T(8,128)(2,1)}, u32[]{:S(2)}) copy-start(bf16[1,128,3584]{2,1,0:T(8,128)(2,1)} %param.10) | copy-start | bytes 2752516
  107.9 9.9 %copy-start.14 = (s32[1,1,128,1]{2,3,1,0:T(1,128)S(1)}, s32[1,1,128,1]{2,3,1,0:T(1,128)}, u32[]{:S(2)}) copy-start(s32[1,1,128,1]{2,3,1,0:T(1,128)} %param.12) | copy-start | bytes 1540
  107.9 9.9 %copy-start.15 = (f32[1,1,128,1]{2,3,1,0:T(1,128)S(1)}, f32[1,1,128,1]{2,3,1,0:T(1,128)}, u32[]{:S(2)}) copy-start(f32[1,1,128,1]{2,3,1,0:T(1,128)} %param.14) | copy-start | bytes 1540
  111.1 35.9 %all-to-all-start.3 = ((bf16[16,72,896]{2,1,0:T(8,128)(2,1)}), bf16[16,72,896]{2,1,0:T(8,128)(2,1)S(1)}, u32[]{:S(2)}, u32[]{:S(2)}) async-start(bf16[16,72,896]{2,1,0:T(8,128)(2,1)} %shard_map.120), calls=%async_computation.3 | async-start | bytes 4128768 | tf_op jit(solution)/shard_map/all_to_all | solution.py:248
  117.8 5.1 %copy-start.12 = (bf16[1,128,3584]{2,1,0:T(8,128)(2,1)S(1)}, bf16[1,128,3584]{2,1,0:T(8,128)(2,1)}, u32[]{:S(2)}) copy-start(bf16[1,128,3584]{2,1,0:T(8,128)(2,1)} %param.11) | copy-start | bytes 2752516
  117.8 11.0 %copy-start.17 = (f32[1,1,128,1]{2,3,1,0:T(1,128)S(1)}, f32[1,1,128,1]{2,3,1,0:T(1,128)}, u32[]{:S(2)}) copy-start(f32[1,1,128,1]{2,3,1,0:T(1,128)} %param.15) | copy-start | bytes 1540
  120.3 25.8 %collective-permute-start.10 = (bf16[128,3584]{1,0:T(8,128)(2,1)S(1)}, bf16[128,3584]{1,0:T(8,128)(2,1)S(1)}, u32[]{:S(2)}, u32[]{:S(2)}) collective-permute-start(bf16[128,3584]{1,0:T(8,128)(2,1)S(1)} %shard_map.121), channel_id=1, source_target_pairs={{0,32},{32,64},{64,96},{96,128},{128,160},{160,192},{192,224},{224... | collective-permute-start | bytes 2752520 | tf_op jit(solution)/shard_map/ppermute | solution.py:235
  122.9 24.2 %collective-permute-start.11 = (bf16[128,3584]{1,0:T(8,128)(2,1)S(1)}, bf16[128,3584]{1,0:T(8,128)(2,1)S(1)}, u32[]{:S(2)}, u32[]{:S(2)}) collective-permute-start(bf16[128,3584]{1,0:T(8,128)(2,1)S(1)} %bitcast.28), channel_id=1, source_target_pairs={{0,224},{32,0},{64,32},{96,64},{128,96},{160,128},{192,160},{224,1... | collective-permute-start | bytes 2752520 | tf_op jit(solution)/shard_map/ppermute | solution.py:235
  126.9 20.2 %collective-permute-start.12 = (s32[1,128]{1,0:T(1,128)S(1)}, s32[1,128]{1,0:T(1,128)S(1)}, u32[]{:S(2)}, u32[]{:S(2)}) collective-permute-start(s32[1,128]{1,0:T(1,128)S(1)} %bitcast.33), channel_id=1, source_target_pairs={{0,224},{32,0},{64,32},{96,64},{128,96},{160,128},{192,160},{224,1... | collective-permute-start | bytes 1544 | tf_op jit(solution)/shard_map/ppermute | solution.py:235
  128.8 18.3 %collective-permute-start.13 = (f32[1,128]{1,0:T(1,128)S(1)}, f32[1,128]{1,0:T(1,128)S(1)}, u32[]{:S(2)}, u32[]{:S(2)}) collective-permute-start(f32[1,128]{1,0:T(1,128)S(1)} %bitcast.36), channel_id=1, source_target_pairs={{0,224},{32,0},{64,32},{96,64},{128,96},{160,128},{192,160},{224,1... | collective-permute-start | bytes 1544 | tf_op jit(solution)/shard_map/ppermute | solution.py:235

commit v10 on v9

--- a/solution.py
+++ b/solution.py
@@ -34,7 +34,10 @@
     return jnp.dot(left, right, preferred_element_type=F32)
 
 
-def prepare_kernel(current_hbm, ids_hbm, gain_hbm, send_ref, current_ref, ids_ref, gain_ref, ready):
+def prepare_kernel(
+    current_hbm, ids_hbm, gain_hbm, send_hbm,
+    current_ref, ids_ref, gain_ref, normed_ref, send_ref, ready, done,
+):
     loads = [
         pltpu.make_async_copy(source, target, ready.at[place])
         for place, (source, target) in enumerate(
@@ -53,29 +56,40 @@
     slot_row = jnp.sum(earlier.astype(jnp.int32), axis=0, keepdims=True)
     main_row = jnp.where(slot_row < MAIN, ids_row * MAIN + slot_row, -1)
     last_row = jnp.where(slot_row < MAIN, -1, ids_row * (ES * LAST) + slot_row - MAIN)
-    pick_main = (iota((EXPERTS * MAIN, tokens), 0) == main_row).astype(BF16)
     loads[1].wait()
     loads[2].wait()
     as_float = current_ref[...].astype(F32)
     inverse_rms = lax.rsqrt(jnp.mean(as_float * as_float, axis=-1, keepdims=True) + EPSILON)
-    last = jnp.zeros((EXPERTS * ES * LAST, quarter), F32)
-    for q in range(ES):
-        columns = slice(q * quarter, (q + 1) * quarter)
-        normed = (current_ref[:, columns].astype(F32) * inverse_rms * gain_ref[:, columns]).astype(
-            BF16
-        )
-        main = dot(pick_main, normed).astype(BF16)
-        for expert in range(EXPERTS):
-            rows = main[expert * MAIN : (expert + 1) * MAIN]
-            for chip in (2 * expert, 2 * expert + 1):
-                send_ref[chip, q * MAIN : (q + 1) * MAIN, :] = rows
-        place = jnp.where(last_row < 0, -1, last_row + q * LAST)
-        pick_last = (iota((EXPERTS * ES * LAST, tokens), 0) == place).astype(BF16)
-        last = last + dot(pick_last, normed)
-    for expert in range(EXPERTS):
-        rows = last[expert * ES * LAST : (expert + 1) * ES * LAST].astype(BF16)
-        for chip in (2 * expert, 2 * expert + 1):
-            send_ref[chip, ES * MAIN :, :] = rows
+    group = EXPERTS // 2
+    stores = []
+    for half in range(2):
+        first = half * group
+        pick_main = iota((group * MAIN, tokens), 0) + first * MAIN == main_row
+        pick_main = pick_main.astype(BF16)
+        last = jnp.zeros((group * ES * LAST, quarter), F32)
+        for q in range(ES):
+            columns = slice(q * quarter, (q + 1) * quarter)
+            if half == 0:
+                normed = current_ref[:, columns].astype(F32) * inverse_rms * gain_ref[:, columns]
+                normed_ref[:, columns] = normed.astype(BF16)
+            normed = normed_ref[:, columns]
+            main = dot(pick_main, normed).astype(BF16)
+            for expert in range(group):
+                rows = main[expert * MAIN : (expert + 1) * MAIN]
+                for chip in (2 * (first + expert), 2 * (first + expert) + 1):
+                    send_ref[chip, q * MAIN : (q + 1) * MAIN, :] = rows
+            place = jnp.where(last_row < 0, -1, last_row + q * LAST)
+            pick_last = iota((group * ES * LAST, tokens), 0) + first * ES * LAST == place
+            last = last + dot(pick_last.astype(BF16), normed)
+        for expert in range(group):
+            rows = last[expert * ES * LAST : (expert + 1) * ES * LAST].astype(BF16)
+            for chip in (2 * (first + expert), 2 * (first + expert) + 1):
+                send_ref[chip, ES * MAIN :, :] = rows
+        part = pl.ds(2 * first, 2 * group)
+        stores.append(pltpu.make_async_copy(send_ref.at[part], send_hbm.at[part], done.at[half]))
+        stores[half].start()
+    for store in stores:
+        store.wait()
 
 
 def prepare(current, ids_row, gain, vmem):
@@ -85,11 +99,15 @@
         prepare_kernel,
         out_shape=jax.ShapeDtypeStruct((CHIPS, ES * (MAIN + LAST), quarter), BF16),
         in_specs=[pl.BlockSpec(memory_space=pltpu.HBM)] * 3,
+        out_specs=pl.BlockSpec(memory_space=pltpu.HBM),
         scratch_shapes=[
             pltpu.VMEM(current.shape, current.dtype),
             pltpu.VMEM(ids_row.shape, ids_row.dtype),
             pltpu.VMEM(gain.shape, gain.dtype),
+            pltpu.VMEM(current.shape, BF16),
+            pltpu.VMEM((CHIPS, ES * (MAIN + LAST), quarter), BF16),
             pltpu.SemaphoreType.DMA((3,)),
+            pltpu.SemaphoreType.DMA((2,)),
         ],
         compiler_params=pltpu.CompilerParams(vmem_limit_bytes=vmem),
         cost_estimate=pl.CostEstimate(
@@ -213,17 +231,31 @@
     )(current, back, ids_row, scores_row)
 
 
-def settle_kernel(value_ref, out_ref):
-    out_ref[...] = value_ref[...]
-
-
-def settle(value):
-    return pl.pallas_call(
-        settle_kernel,
-        out_shape=jax.ShapeDtypeStruct(value.shape, value.dtype),
+def finish_both_kernel(
+    moved_hbm, current_ref, back_ref, ids_ref, scores_ref, settled_hbm, out_ref, done
+):
+    copy = pltpu.make_async_copy(moved_hbm, settled_hbm, done)
+    copy.start()
+    finish_kernel(current_ref, back_ref, ids_ref, scores_ref, out_ref)
+    copy.wait()
+
+
+def finish_both(moved, current, back, ids_row, scores_row):
+    tokens, features = current.shape
+    return pl.pallas_call(
+        finish_both_kernel,
+        out_shape=[jax.ShapeDtypeStruct((tokens, features), BF16)] * 2,
+        in_specs=[pl.BlockSpec(memory_space=pltpu.HBM)]
+        + [pl.BlockSpec(memory_space=pltpu.VMEM)] * 4,
+        out_specs=[pl.BlockSpec(memory_space=pltpu.HBM), pl.BlockSpec(memory_space=pltpu.VMEM)],
+        scratch_shapes=[pltpu.SemaphoreType.DMA],
         compiler_params=pltpu.CompilerParams(vmem_limit_bytes=VMEM_LIMIT),
-        cost_estimate=pl.CostEstimate(flops=0, bytes_accessed=4 * value.size, transcendentals=0),
-    )(value)
+        cost_estimate=pl.CostEstimate(
+            flops=6 * tokens * EXPERTS * MAIN * features,
+            bytes_accessed=12 * tokens * features,
+            transcendentals=0,
+        ),
+    )(moved, current, back, ids_row, scores_row)
 
 
 def swap_cores(value):
@@ -290,8 +322,8 @@
 
     marks_a, back_b = lax.optimization_barrier((marks_a, back_b))
     returned_b = exchange(back_b)
-    updated_a = settle(from_behind(finish(current_a, returned_a, ids_a, marks_a), 1))
-    updated_b = finish(moved_b, returned_b, moved_ids, moved_marks)
+    updated_a = from_behind(finish(current_a, returned_a, ids_a, marks_a), 1)
+    updated_a, updated_b = finish_both(updated_a, moved_b, returned_b, moved_ids, moved_marks)
     return (updated_a[None], updated_b[None])
 
 

time: 150 us -> 153 us (1.020)
  local copies, waits for them, and re-layouts: 8.04 us -> 10.2 us
    unnamed x36 -> x38, local copies, waits for them, and re-layouts: 7 us -> 9.12 us
    pallas_call x2 -> x1, Pallas kernels: 4.34 us -> 2.45 us  [finish(): pl.pallas_call(finish_kernel, out_shape=jax.ShapeDtypeStruct((tokens, fea...]
  transfers between devices with their start and end apart: 18 -> 18, of which waited for: 7 -> 8; matrix products, arithmetic and copies ran while one was open for 1% -> 1% of each run, Pallas kernels for 16% -> 16%
where the time goes in v10:
time: 153 us; the launch traced here: 152 us
  starting transfers between devices  55.9 us (37%)
  waiting for transfers between devices  55.3 us (36%)
  Pallas kernels  29.6 us (19%)
  local copies, waits for them, and re-layouts  10.2 us (7%)
    ppermute x7, waiting for transfers between devices, from_behind(): lax.ppermute(value, 'section', [(i, (i + steps) % count) for i in range(c...  41.7 us
    ppermute x7, starting transfers between devices, from_behind(): lax.ppermute(value, 'section', [(i, (i + steps) % count) for i in range(c...  27.8 us
    all_to_all x4, starting transfers between devices, exchange(): lax.all_to_all(blocks, 'ep', split_axis=0, concat_axis=0, axis_index_grou...  26.8 us
    pallas_call x4, Pallas kernels, hidden_units(): pl.pallas_call(hidden_kernel, out_shape=jax.ShapeDtypeStruct((count, widt...  13.1 us
    unnamed x38, local copies, waits for them, and re-layouts  9.12 us
    all_to_all x4, waiting for transfers between devices, exchange(): lax.all_to_all(blocks, 'ep', split_axis=0, concat_axis=0, axis_index_grou...  8.23 us
    pallas_call x2, Pallas kernels, down_product(): pl.pallas_call(functools.partial(down_kernel, len(down)), out_shape=jax.S...  6.46 us
    pallas_call x2, Pallas kernels, prepare(): pl.pallas_call(prepare_kernel, out_shape=jax.ShapeDtypeStruct((CHIPS, ES...  5.62 us
  transfers between devices with their start and end apart: 18, of which 8 were waited for; matrix products, arithmetic and copies ran while one was open for 1% of the time, Pallas kernels for 16%

profile of v10, /device:TPU:8, one launch (start us, length us, event | category | flops | bytes accessed | tf_op | source)
XLA Modules:
  0.0 152.0 jit_solution(1343243773485904621)
XLA Ops:
  0.6 3.3 %shard_map.113 = bf16[16,72,896]{2,1,0:T(8,128)(2,1)} custom-call(bf16[128,3584]{1,0:T(8,128)(2,1)} %bitcast.25, s32[1,128]{1,0:T(1,128)} %bitcast.29, f32[1,3584]{1,0:T(1,128)} %gain_hbm.3), custom_call_target="tpu_custom_call" | custom-call | flops 176160768 | bytes 3670016 | tf_op jit(solution)/shard_map/pallas_call | solution.py:98
  4.0 0.0 copy-start.6
  4.0 7.5 %all-to-all-start = ((bf16[16,72,896]{2,1,0:T(8,128)(2,1)}), bf16[16,72,896]{2,1,0:T(8,128)(2,1)}, u32[]{:S(2)}, u32[]{:S(2)}) async-start(bf16[16,72,896]{2,1,0:T(8,128)(2,1)} %shard_map.113), calls=%async_computation | async-start | bytes 4128768 | tf_op jit(solution)/shard_map/all_to_all | solution.py:280
  11.5 0.0 copy-start.14
  11.5 0.0 copy-start.17
  11.5 0.1 collective-permute-start
  11.6 1.0 slice_bitcast_fusion
  12.7 5.9 %collective-permute-start.1 = (bf16[128,3584]{1,0:T(8,128)(2,1)S(1)}, bf16[128,3584]{1,0:T(8,128)(2,1)S(1)}, u32[]{:S(2)}, u32[]{:S(2)}) collective-permute-start(bf16[128,3584]{1,0:T(8,128)(2,1)S(1)} %get-tuple-element.27), channel_id=1, source_target_pairs={{0,224},{32,0},{64,32},{96,64},{128,96},{160,128},{192,160},{224,1... | collective-permute-start | bytes 2752520 | tf_op jit(solution)/shard_map/ppermute | solution.py:267
  18.5 0.0 collective-permute-done.refs_1_
  18.6 1.3 copy-done.9
  19.8 2.3 %shard_map.114 = bf16[16,72,896]{2,1,0:T(8,128)(2,1)S(1)} custom-call(bf16[128,3584]{1,0:T(8,128)(2,1)S(1)} %bitcast.28, s32[1,128]{1,0:T(1,128)S(1)} %bitcast.32, f32[1,3584]{1,0:T(1,128)S(1)} %copy-done.14), custom_call_target="tpu_custom_call" | custom-call | flops 176160768 | bytes 3670016 | tf_op jit(solution)/shard_map/pallas_call | solution.py:98
  22.2 1.3 copy-done.5
  23.5 15.3 %collective-permute-done.1.refs_0_ = bf16[128,3584]{1,0:T(8,128)(2,1)S(1)} collective-permute-done((bf16[128,3584]{1,0:T(8,128)(2,1)S(1)}, bf16[128,3584]{1,0:T(8,128)(2,1)S(1)}, u32[]{:S(2)}, u32[]{:S(2)}) %collective-permute-start.1) | collective-permute-done | bytes 917536 | tf_op jit(solution)/shard_map/ppermute | solution.py:267
  38.8 1.4 all-to-all-done.received_ref
  40.2 5.8 %all-to-all-start.1 = ((bf16[16,72,896]{2,1,0:T(8,128)(2,1)}), bf16[16,72,896]{2,1,0:T(8,128)(2,1)}, u32[]{:S(2)}, u32[]{:S(2)}) async-start(bf16[16,72,896]{2,1,0:T(8,128)(2,1)} %copy-done.5), calls=%async_computation.1 | async-start | bytes 4128768 | tf_op jit(solution)/shard_map/all_to_all | solution.py:280
  46.0 5.6 %collective-permute-start.4 = (bf16[128,3584]{1,0:T(8,128)(2,1)}, bf16[128,3584]{1,0:T(8,128)(2,1)}, u32[]{:S(2)}, u32[]{:S(2)}) collective-permute-start(bf16[128,3584]{1,0:T(8,128)(2,1)} %get-tuple-element.26), channel_id=1, source_target_pairs={{0,224},{32,0},{64,32},{96,64},{128,96},{160,128},{192,160},{224,1... | collective-permute-start | bytes 2752520 | tf_op jit(solution)/shard_map/ppermute | solution.py:267
  51.7 0.0 collective-permute-done.2.received_ref
  51.7 1.5 copy-done.1
  53.2 3.3 %shard_map.116 = bf16[288,256]{1,0:T(8,128)(2,1)S(1)} custom-call(bf16[16,72,896]{2,1,0:T(8,128)(2,1)} %collective-permute-done.2.received_ref, bf16[3584,256]{1,0:T(8,128)(2,1)S(1)} %bitcast.15, bf16[3584,256]{1,0:T(8,128)(2,1)S(1)} %bitcast.19), custom_call_target="tpu_custom_call" | custom-call | flops 1056964608 | bytes 5734400 | tf_op jit(solution)/shard_map/pallas_call | solution.py:141
  56.5 0.0 copy-start.7
  56.6 0.1 collective-permute-start.3
  56.7 3.3 %shard_map.115.mine_ref = bf16[288,256]{1,0:T(8,128)(2,1)S(1)} custom-call(bf16[16,72,896]{2,1,0:T(8,128)(2,1)} %all-to-all-done.received_ref, bf16[3584,256]{1,0:T(8,128)(2,1)S(1)} %bitcast.16, bf16[3584,256]{1,0:T(8,128)(2,1)S(1)} %bitcast.20), custom_call_target="tpu_custom_call" | custom-call | flops 1056964608 | bytes 5734400 | tf_op jit(solution)/shard_map/pallas_call | solution.py:141
  60.1 2.0 %shard_map.117 = bf16[16,72,896]{2,1,0:T(8,128)(2,1)S(1)} custom-call(bf16[288,256]{1,0:T(8,128)(2,1)S(1)} %shard_map.115.mine_ref, bf16[288,256]{1,0:T(8,128)(2,1)S(1)} %collective-permute-done.3.theirs_ref, bf16[256,3584]{1,0:T(8,128)(2,1)S(1)} %bitcast.24, bf16[256,3584]{1,0:T(8,128)(2,1)S(1)} %copy-done.10), custom_call_target="tpu_custom_call" | custom-call | flops 1056964608 | bytes 5734400 | tf_op jit(solution)/shard_map/pallas_call | solution.py:181
  62.0 1.4 copy-done.4
  63.4 8.6 %collective-permute-done.4.refs_1_ = bf16[128,3584]{1,0:T(8,128)(2,1)} collective-permute-done((bf16[128,3584]{1,0:T(8,128)(2,1)}, bf16[128,3584]{1,0:T(8,128)(2,1)}, u32[]{:S(2)}, u32[]{:S(2)}) %collective-permute-start.4) | collective-permute-done | bytes 917536 | tf_op jit(solution)/shard_map/ppermute | solution.py:267
  72.0 3.2 %all-to-all-done.1.received_ref = bf16[16,72,896]{2,1,0:T(8,128)(2,1)} async-done(((bf16[16,72,896]{2,1,0:T(8,128)(2,1)}), bf16[16,72,896]{2,1,0:T(8,128)(2,1)}, u32[]{:S(2)}, u32[]{:S(2)}) %all-to-all-start.1) | async-done | bytes 2064416 | tf_op jit(solution)/shard_map/all_to_all | solution.py:280
  75.2 0.0 collective-permute-start.6
  75.2 6.8 %all-to-all-start.2 = ((bf16[16,72,896]{2,1,0:T(8,128)(2,1)}), bf16[16,72,896]{2,1,0:T(8,128)(2,1)}, u32[]{:S(2)}, u32[]{:S(2)}) async-start(bf16[16,72,896]{2,1,0:T(8,128)(2,1)} %copy-done.4), calls=%async_computation.2 | async-start | bytes 4128768 | tf_op jit(solution)/shard_map/all_to_all | solution.py:280
  82.0 0.5 collective-permute-start.9
  82.5 1.5 copy-done.3
  84.0 3.2 %shard_map.118 = bf16[288,256]{1,0:T(8,128)(2,1)S(1)} custom-call(bf16[16,72,896]{2,1,0:T(8,128)(2,1)} %all-to-all-done.1.received_ref, bf16[3584,256]{1,0:T(8,128)(2,1)S(1)} %bitcast.17, bf16[3584,256]{1,0:T(8,128)(2,1)S(1)} %bitcast.21), custom_call_target="tpu_custom_call" | custom-call | flops 1056964608 | bytes 5734400 | tf_op jit(solution)/shard_map/pallas_call | solution.py:141
  87.2 6.5 %collective-permute-start.5 = (bf16[288,256]{1,0:T(8,128)(2,1)S(1)}, bf16[288,256]{1,0:T(8,128)(2,1)S(1)}, u32[]{:S(2)}, u32[]{:S(2)}) collective-permute-start(bf16[288,256]{1,0:T(8,128)(2,1)S(1)} %shard_map.118), channel_id=1, source_target_pairs={{0,224},{32,0},{64,32},{96,64},{128,96},{160,128},{192,160},{224,1... | collective-permute-start | bytes 442376 | tf_op jit(solution)/shard_map/ppermute | solution.py:267
  93.7 3.2 %shard_map.119 = bf16[288,256]{1,0:T(8,128)(2,1)S(1)} custom-call(bf16[16,72,896]{2,1,0:T(8,128)(2,1)} %collective-permute-done.6.received_ref, bf16[3584,256]{1,0:T(8,128)(2,1)S(1)} %bitcast.18, bf16[3584,256]{1,0:T(8,128)(2,1)S(1)} %bitcast.22), custom_call_target="tpu_custom_call" | custom-call | flops 1056964608 | bytes 5734400 | tf_op jit(solution)/shard_map/pallas_call | solution.py:141
  96.9 0.7 collective-permute-start.7
  97.6 5.4 %collective-permute-done.7.theirs_ref = bf16[288,256]{1,0:T(8,128)(2,1)S(1)} collective-permute-done((bf16[288,256]{1,0:T(8,128)(2,1)S(1)}, bf16[288,256]{1,0:T(8,128)(2,1)S(1)}, u32[]{:S(2)}, u32[]{:S(2)}) %collective-permute-start.7) | collective-permute-done | bytes 147488 | tf_op jit(solution)/shard_map/ppermute | solution.py:275
  102.9 4.5 %shard_map.120 = bf16[16,72,896]{2,1,0:T(8,128)(2,1)} custom-call(bf16[288,256]{1,0:T(8,128)(2,1)S(1)} %collective-permute-done.5.mine_ref, bf16[288,256]{1,0:T(8,128)(2,1)S(1)} %collective-permute-done.7.theirs_ref, bf16[128,3584]{1,0:T(8,128)(2,1)S(1)} %collective-permute-done.1.refs_0_, bf16[128,3584]{1,0:T(8,128)(2,1)} %collective-permute-done.4.refs_1_, ...), custom_call_target="tpu_custom_call" | custom-call | flops 1056964608 | bytes 5734400 | tf_op jit(solution)/shard_map/pallas_call | solution.py:181
  107.4 3.6 %all-to-all-done.2.back_ref = bf16[16,72,896]{2,1,0:T(8,128)(2,1)} async-done(((bf16[16,72,896]{2,1,0:T(8,128)(2,1)}), bf16[16,72,896]{2,1,0:T(8,128)(2,1)}, u32[]{:S(2)}, u32[]{:S(2)}) %all-to-all-start.2) | async-done | bytes 2064416 | tf_op jit(solution)/shard_map/all_to_all | solution.py:280
  111.1 6.6 %all-to-all-start.3 = ((bf16[16,72,896]{2,1,0:T(8,128)(2,1)}), bf16[16,72,896]{2,1,0:T(8,128)(2,1)S(1)}, u32[]{:S(2)}, u32[]{:S(2)}) async-start(bf16[16,72,896]{2,1,0:T(8,128)(2,1)} %shard_map.120), calls=%async_computation.3 | async-start | bytes 4128768 | tf_op jit(solution)/shard_map/all_to_all | solution.py:280
  117.7 6.5 %collective-permute-start.11 = (bf16[128,3584]{1,0:T(8,128)(2,1)}, bf16[128,3584]{1,0:T(8,128)(2,1)S(1)}, u32[]{:S(2)}, u32[]{:S(2)}) collective-permute-start(bf16[128,3584]{1,0:T(8,128)(2,1)} %bitcast.27), channel_id=1, source_target_pairs={{0,224},{32,0},{64,32},{96,64},{128,96},{160,128},{192,160},{224,1... | collective-permute-start | bytes 2752520 | tf_op jit(solution)/shard_map/ppermute | solution.py:267
  124.1 2.5 %shard_map.121 = bf16[128,3584]{1,0:T(8,128)(2,1)S(1)} custom-call(bf16[128,3584]{1,0:T(8,128)(2,1)S(1)} %bitcast.26, bf16[16,72,896]{2,1,0:T(8,128)(2,1)} %all-to-all-done.2.back_ref, s32[1,128]{1,0:T(1,128)S(1)} %bitcast.30, f32[1,128]{1,0:T(1,128)S(1)} %bitcast.31), custom_call_target="tpu_custom_call" | custom-call | flops 352321536 | bytes 3670016 | tf_op jit(solution)/shard_map/pallas_call | solution.py:222
  126.6 0.1 collective-permute-start.10
  126.7 3.2 %collective-permute-start.12 = (s32[1,128]{1,0:T(1,128)S(1)}, s32[1,128]{1,0:T(1,128)S(1)}, u32[]{:S(2)}, u32[]{:S(2)}) collective-permute-start(s32[1,128]{1,0:T(1,128)S(1)} %bitcast.33), channel_id=1, source_target_pairs={{0,224},{32,0},{64,32},{96,64},{128,96},{160,128},{192,160},{224,1... | collective-permute-start | bytes 1544 | tf_op jit(solution)/shard_map/ppermute | solution.py:267
  129.9 0.0 collective-permute-start.13
  130.0 13.1 %collective-permute-done.12.ids_ref = s32[1,128]{1,0:T(1,128)S(1)} collective-permute-done((s32[1,128]{1,0:T(1,128)S(1)}, s32[1,128]{1,0:T(1,128)S(1)}, u32[]{:S(2)}, u32[]{:S(2)}) %collective-permute-start.12) | collective-permute-done | bytes 544 | tf_op jit(solution)/shard_map/ppermute | solution.py:267
  143.0 0.9 copy-done.12
  144.0 4.7 %collective-permute-done.10.moved_hbm = bf16[128,3584]{1,0:T(8,128)(2,1)S(1)} collective-permute-done((bf16[128,3584]{1,0:T(8,128)(2,1)S(1)}, bf16[128,3584]{1,0:T(8,128)(2,1)S(1)}, u32[]{:S(2)}, u32[]{:S(2)}) %collective-permute-start.10) | collective-permute-done | bytes 917536 | tf_op jit(solution)/shard_map/ppermute | solution.py:267
  148.7 1.2 copy-done.13
  149.8 2.0 %shard_map.122 = (bf16[128,3584]{1,0:T(8,128)(2,1)}, bf16[128,3584]{1,0:T(8,128)(2,1)}) custom-call(bf16[128,3584]{1,0:T(8,128)(2,1)S(1)} %collective-permute-done.10.moved_hbm, bf16[128,3584]{1,0:T(8,128)(2,1)S(1)} %copy-done.13, bf16[16,72,896]{2,1,0:T(8,128)(2,1)S(1)} %all-to-all-done.3.back_ref, s32[1,128]{1,0:T(1,128)S(1)} %collective-permute-done.12.ids_ref, ...), custom_call_target="tpu_custom_call" | custom-call | flops 352321536 | bytes 5505024 | tf_op jit(solution)/shard_map/pallas_call | solution.py:245
  (37 shorter events, 0.1 us)
Async XLA Ops:
  4.0 7.6 %copy-start.6 = (bf16[1,256,3584]{2,1,0:T(8,128)(2,1)S(1)}, bf16[1,256,3584]{2,1,0:T(8,128)(2,1)}, u32[]{:S(2)}) copy-start(bf16[1,256,3584]{2,1,0:T(8,128)(2,1)} %param.19) | copy-start | bytes 5505028
  4.0 36.2 %all-to-all-start = ((bf16[16,72,896]{2,1,0:T(8,128)(2,1)}), bf16[16,72,896]{2,1,0:T(8,128)(2,1)}, u32[]{:S(2)}, u32[]{:S(2)}) async-start(bf16[16,72,896]{2,1,0:T(8,128)(2,1)} %shard_map.113), calls=%async_computation | async-start | bytes 4128768 | tf_op jit(solution)/shard_map/all_to_all | solution.py:280
  11.5 8.3 %copy-start.11 = (bf16[1,128,3584]{2,1,0:T(8,128)(2,1)S(1)}, bf16[1,128,3584]{2,1,0:T(8,128)(2,1)}, u32[]{:S(2)}) copy-start(bf16[1,128,3584]{2,1,0:T(8,128)(2,1)} %param.11) | copy-start | bytes 2752516
  11.5 8.3 %copy-start.14 = (f32[1,3584]{1,0:T(1,128)S(1)}, f32[1,3584]{1,0:T(1,128)}, u32[]{:S(2)}) copy-start(f32[1,3584]{1,0:T(1,128)} %gain_hbm.3) | copy-start | bytes 43012
  11.5 8.3 %copy-start.17 = (s32[1,1,128,1]{2,3,1,0:T(1,128)S(1)}, s32[1,1,128,1]{2,3,1,0:T(1,128)}, u32[]{:S(2)}) copy-start(s32[1,1,128,1]{2,3,1,0:T(1,128)} %param.13) | copy-start | bytes 1540
  11.5 7.0 %collective-permute-start = (bf16[256,3584]{1,0:T(8,128)(2,1)S(1)}, bf16[256,3584]{1,0:T(8,128)(2,1)S(1)}, u32[]{:S(2)}, u32[]{:S(2)}) collective-permute-start(bf16[256,3584]{1,0:T(8,128)(2,1)S(1)} %bitcast.23), channel_id=1, source_target_pairs={{0,1},{1,0},{2,3},{3,2},{4,5},{5,4},{6,7},{7,6},{8,9},{9,8},{10,11... | collective-permute-start | bytes 5505032 | tf_op jit(solution)/shard_map/ppermute | solution.py:262
  12.7 26.1 %collective-permute-start.1 = (bf16[128,3584]{1,0:T(8,128)(2,1)S(1)}, bf16[128,3584]{1,0:T(8,128)(2,1)S(1)}, u32[]{:S(2)}, u32[]{:S(2)}) collective-permute-start(bf16[128,3584]{1,0:T(8,128)(2,1)S(1)} %get-tuple-element.27), channel_id=1, source_target_pairs={{0,224},{32,0},{64,32},{96,64},{128,96},{160,128},{192,160},{224,1... | collective-permute-start | bytes 2752520 | tf_op jit(solution)/shard_map/ppermute | solution.py:267
  18.5 1.3 copy-start.9
  22.1 1.3 copy-start.5
  23.5 28.2 %copy-start = (bf16[1,3584,256]{2,1,0:T(8,128)(2,1)S(1)}, bf16[1,3584,256]{2,1,0:T(8,128)(2,1)}, u32[]{:S(2)}) copy-start(bf16[1,3584,256]{2,1,0:T(8,128)(2,1)} %param.17) | copy-start | bytes 5505028
  40.2 11.5 %collective-permute-start.2 = (bf16[16,72,896]{2,1,0:T(8,128)(2,1)}, bf16[16,72,896]{2,1,0:T(8,128)(2,1)}, u32[]{:S(2)}, u32[]{:S(2)}) collective-permute-start(bf16[16,72,896]{2,1,0:T(8,128)(2,1)} %all-to-all-done.received_ref), channel_id=1, source_target_pairs={{0,1},{1,0},{2,3},{3,2},{4,5},{5,4},{6,7},{7,6},{8,9},{9,8},{10,11... | collective-permute-start | bytes 6193160 | tf_op jit(solution)/shard_map/ppermute | solution.py:262
  40.2 35.0 %all-to-all-start.1 = ((bf16[16,72,896]{2,1,0:T(8,128)(2,1)}), bf16[16,72,896]{2,1,0:T(8,128)(2,1)}, u32[]{:S(2)}, u32[]{:S(2)}) async-start(bf16[16,72,896]{2,1,0:T(8,128)(2,1)} %copy-done.5), calls=%async_computation.1 | async-start | bytes 4128768 | tf_op jit(solution)/shard_map/all_to_all | solution.py:280
  46.0 26.0 %collective-permute-start.4 = (bf16[128,3584]{1,0:T(8,128)(2,1)}, bf16[128,3584]{1,0:T(8,128)(2,1)}, u32[]{:S(2)}, u32[]{:S(2)}) collective-permute-start(bf16[128,3584]{1,0:T(8,128)(2,1)} %get-tuple-element.26), channel_id=1, source_target_pairs={{0,224},{32,0},{64,32},{96,64},{128,96},{160,128},{192,160},{224,1... | collective-permute-start | bytes 2752520 | tf_op jit(solution)/shard_map/ppermute | solution.py:267
  51.7 1.5 copy-start.1
  53.2 3.5 %copy-start.2 = (bf16[1,3584,256]{2,1,0:T(8,128)(2,1)S(1)}, bf16[1,3584,256]{2,1,0:T(8,128)(2,1)}, u32[]{:S(2)}) copy-start(bf16[1,3584,256]{2,1,0:T(8,128)(2,1)} %param.18) | copy-start | bytes 5505028
  56.5 3.5 %copy-start.7 = (bf16[1,256,3584]{2,1,0:T(8,128)(2,1)S(1)}, bf16[1,256,3584]{2,1,0:T(8,128)(2,1)}, u32[]{:S(2)}) copy-start(bf16[1,256,3584]{2,1,0:T(8,128)(2,1)} %param.19) | copy-start | bytes 5505028
  56.5 3.5 %copy-start.10 = (bf16[256,3584]{1,0:T(8,128)(2,1)S(1)}, bf16[256,3584]{1,0:T(8,128)(2,1)}, u32[]{:S(2)}) copy-start(bf16[256,3584]{1,0:T(8,128)(2,1)} %copy-done.9) | copy-start | bytes 5505028
  56.6 3.5 %collective-permute-start.3 = (bf16[288,256]{1,0:T(8,128)(2,1)S(1)}, bf16[288,256]{1,0:T(8,128)(2,1)S(1)}, u32[]{:S(2)}, u32[]{:S(2)}) collective-permute-start(bf16[288,256]{1,0:T(8,128)(2,1)S(1)} %shard_map.116), channel_id=1, source_target_pairs={{0,1},{1,0},{2,3},{3,2},{4,5},{5,4},{6,7},{7,6},{8,9},{9,8},{10,11... | collective-permute-start | bytes 442376 | tf_op jit(solution)/shard_map/ppermute | solution.py:262
  62.0 1.4 copy-start.4
  75.2 18.5 %collective-permute-start.6 = (bf16[16,72,896]{2,1,0:T(8,128)(2,1)}, bf16[16,72,896]{2,1,0:T(8,128)(2,1)}, u32[]{:S(2)}, u32[]{:S(2)}) collective-permute-start(bf16[16,72,896]{2,1,0:T(8,128)(2,1)} %all-to-all-done.1.received_ref), channel_id=1, source_target_pairs={{0,1},{1,0},{2,3},{3,2},{4,5},{5,4},{6,7},{7,6},{8,9},{9,8},{10,11... | collective-permute-start | bytes 6193160 | tf_op jit(solution)/shard_map/ppermute | solution.py:262
  75.2 35.8 %all-to-all-start.2 = ((bf16[16,72,896]{2,1,0:T(8,128)(2,1)}), bf16[16,72,896]{2,1,0:T(8,128)(2,1)}, u32[]{:S(2)}, u32[]{:S(2)}) async-start(bf16[16,72,896]{2,1,0:T(8,128)(2,1)} %copy-done.4), calls=%async_computation.2 | async-start | bytes 4128768 | tf_op jit(solution)/shard_map/all_to_all | solution.py:280
  82.0 15.6 %collective-permute-start.8 = (bf16[128,3584]{1,0:T(8,128)(2,1)S(1)}, bf16[128,3584]{1,0:T(8,128)(2,1)S(1)}, u32[]{:S(2)}, u32[]{:S(2)}) collective-permute-start(bf16[128,3584]{1,0:T(8,128)(2,1)S(1)} %collective-permute-done.1.refs_0_), channel_id=1, source_target_pairs={{0,1},{1,0},{2,3},{3,2},{4,5},{5,4},{6,7},{7,6},{8,9},{9,8},{10,11... | collective-permute-start | bytes 2752520 | tf_op jit(solution)/shard_map/ppermute | solution.py:262
  82.0 15.6 %collective-permute-start.9 = (bf16[128,3584]{1,0:T(8,128)(2,1)}, bf16[128,3584]{1,0:T(8,128)(2,1)S(1)}, u32[]{:S(2)}, u32[]{:S(2)}) collective-permute-start(bf16[128,3584]{1,0:T(8,128)(2,1)} %collective-permute-done.4.refs_1_), channel_id=1, source_target_pairs={{0,1},{1,0},{2,3},{3,2},{4,5},{5,4},{6,7},{7,6},{8,9},{9,8},{10,11... | collective-permute-start | bytes 2752520 | tf_op jit(solution)/shard_map/ppermute | solution.py:262
  82.5 1.5 copy-start.3
  87.2 10.4 %collective-permute-start.5 = (bf16[288,256]{1,0:T(8,128)(2,1)S(1)}, bf16[288,256]{1,0:T(8,128)(2,1)S(1)}, u32[]{:S(2)}, u32[]{:S(2)}) collective-permute-start(bf16[288,256]{1,0:T(8,128)(2,1)S(1)} %shard_map.118), channel_id=1, source_target_pairs={{0,224},{32,0},{64,32},{96,64},{128,96},{160,128},{192,160},{224,1... | collective-permute-start | bytes 442376 | tf_op jit(solution)/shard_map/ppermute | solution.py:267
  96.9 6.1 %collective-permute-start.7 = (bf16[288,256]{1,0:T(8,128)(2,1)S(1)}, bf16[288,256]{1,0:T(8,128)(2,1)S(1)}, u32[]{:S(2)}, u32[]{:S(2)}) collective-permute-start(bf16[288,256]{1,0:T(8,128)(2,1)S(1)} %shard_map.119), channel_id=1, source_target_pairs={{0,225},{1,224},{2,227},{3,226},{4,229},{5,228},{6,231},{7,230},{8... | collective-permute-start | bytes 442376 | tf_op jit(solution)/shard_map/ppermute | solution.py:275
  107.4 16.7 %copy-start.8 = (bf16[1,128,3584]{2,1,0:T(8,128)(2,1)S(1)}, bf16[1,128,3584]{2,1,0:T(8,128)(2,1)}, u32[]{:S(2)}) copy-start(bf16[1,128,3584]{2,1,0:T(8,128)(2,1)} %param.10) | copy-start | bytes 2752516
  107.4 16.7 %copy-start.15 = (s32[1,1,128,1]{2,3,1,0:T(1,128)S(1)}, s32[1,1,128,1]{2,3,1,0:T(1,128)}, u32[]{:S(2)}) copy-start(s32[1,1,128,1]{2,3,1,0:T(1,128)} %param.12) | copy-start | bytes 1540
  107.4 16.7 %copy-start.16 = (f32[1,1,128,1]{2,3,1,0:T(1,128)S(1)}, f32[1,1,128,1]{2,3,1,0:T(1,128)}, u32[]{:S(2)}) copy-start(f32[1,1,128,1]{2,3,1,0:T(1,128)} %param.14) | copy-start | bytes 1540
  111.1 37.6 %all-to-all-start.3 = ((bf16[16,72,896]{2,1,0:T(8,128)(2,1)}), bf16[16,72,896]{2,1,0:T(8,128)(2,1)S(1)}, u32[]{:S(2)}, u32[]{:S(2)}) async-start(bf16[16,72,896]{2,1,0:T(8,128)(2,1)} %shard_map.120), calls=%async_computation.3 | async-start | bytes 4128768 | tf_op jit(solution)/shard_map/all_to_all | solution.py:280
  117.7 12.3 %copy-start.18 = (f32[1,1,128,1]{2,3,1,0:T(1,128)S(1)}, f32[1,1,128,1]{2,3,1,0:T(1,128)}, u32[]{:S(2)}) copy-start(f32[1,1,128,1]{2,3,1,0:T(1,128)} %param.15) | copy-start | bytes 1540
  117.7 25.4 %collective-permute-start.11 = (bf16[128,3584]{1,0:T(8,128)(2,1)}, bf16[128,3584]{1,0:T(8,128)(2,1)S(1)}, u32[]{:S(2)}, u32[]{:S(2)}) collective-permute-start(bf16[128,3584]{1,0:T(8,128)(2,1)} %bitcast.27), channel_id=1, source_target_pairs={{0,224},{32,0},{64,32},{96,64},{128,96},{160,128},{192,160},{224,1... | collective-permute-start | bytes 2752520 | tf_op jit(solution)/shard_map/ppermute | solution.py:267
  126.6 22.1 %collective-permute-start.10 = (bf16[128,3584]{1,0:T(8,128)(2,1)S(1)}, bf16[128,3584]{1,0:T(8,128)(2,1)S(1)}, u32[]{:S(2)}, u32[]{:S(2)}) collective-permute-start(bf16[128,3584]{1,0:T(8,128)(2,1)S(1)} %shard_map.121), channel_id=1, source_target_pairs={{0,32},{32,64},{64,96},{96,128},{128,160},{160,192},{192,224},{224... | collective-permute-start | bytes 2752520 | tf_op jit(solution)/shard_map/ppermute | solution.py:267
  126.7 16.3 %collective-permute-start.12 = (s32[1,128]{1,0:T(1,128)S(1)}, s32[1,128]{1,0:T(1,128)S(1)}, u32[]{:S(2)}, u32[]{:S(2)}) collective-permute-start(s32[1,128]{1,0:T(1,128)S(1)} %bitcast.33), channel_id=1, source_target_pairs={{0,224},{32,0},{64,32},{96,64},{128,96},{160,128},{192,160},{224,1... | collective-permute-start | bytes 1544 | tf_op jit(solution)/shard_map/ppermute | solution.py:267
  129.9 13.1 %collective-permute-start.13 = (f32[1,128]{1,0:T(1,128)S(1)}, f32[1,128]{1,0:T(1,128)S(1)}, u32[]{:S(2)}, u32[]{:S(2)}) collective-permute-start(f32[1,128]{1,0:T(1,128)S(1)} %bitcast.36), channel_id=1, source_target_pairs={{0,224},{32,0},{64,32},{96,64},{128,96},{160,128},{192,160},{224,1... | collective-permute-start | bytes 1544 | tf_op jit(solution)/shard_map/ppermute | solution.py:267
  143.0 0.9 copy-start.12
  148.7 1.2 copy-start.13

commit v11 on v9

--- a/solution.py
+++ b/solution.py
@@ -13,6 +13,7 @@
 CHIPS = EP // 2
 MAIN = 16
 LAST = 2
+ORDER = (0, 1, 2, 3, 5, 6, 7, 4, 10, 11, 8, 9, 15, 12, 13, 14)
 EPSILON = 1e-06
 F32 = jnp.float32
 BF16 = jnp.bfloat16
@@ -68,14 +69,14 @@
         for expert in range(EXPERTS):
             rows = main[expert * MAIN : (expert + 1) * MAIN]
             for chip in (2 * expert, 2 * expert + 1):
-                send_ref[chip, q * MAIN : (q + 1) * MAIN, :] = rows
+                send_ref[ORDER.index(chip), q * MAIN : (q + 1) * MAIN, :] = rows
         place = jnp.where(last_row < 0, -1, last_row + q * LAST)
         pick_last = (iota((EXPERTS * ES * LAST, tokens), 0) == place).astype(BF16)
         last = last + dot(pick_last, normed)
     for expert in range(EXPERTS):
         rows = last[expert * ES * LAST : (expert + 1) * ES * LAST].astype(BF16)
         for chip in (2 * expert, 2 * expert + 1):
-            send_ref[chip, ES * MAIN :, :] = rows
+            send_ref[ORDER.index(chip), ES * MAIN :, :] = rows
 
 
 def prepare(current, ids_row, gain, vmem):
@@ -187,11 +188,11 @@
     in_expert = (lane // (2 * ES * LAST) == ids_column) & (slot >= MAIN)
     in_block = lane % (ES * LAST)
     last = jnp.concatenate(
-        [back_ref[chip, ES * MAIN :, :].astype(F32) for chip in range(CHIPS)], axis=0
+        [back_ref[ORDER.index(chip), ES * MAIN :, :].astype(F32) for chip in range(CHIPS)], axis=0
     ).astype(BF16)
     for q in range(ES):
         main = jnp.concatenate(
-            [back_ref[chip, q * MAIN : (q + 1) * MAIN, :] for chip in range(CHIPS)], axis=0
+            [back_ref[ORDER.index(chip), q * MAIN : (q + 1) * MAIN, :] for chip in range(CHIPS)], axis=0
         )
         pick_last = in_expert & (in_block == q * LAST + slot - MAIN)
         moe = (dot(pick_main, main) + dot(pick_last.astype(BF16), last)) * score
@@ -244,7 +245,7 @@
 
 
 def exchange(blocks):
-    same_core = [[2 * chip + core for chip in range(CHIPS)] for core in range(2)]
+    same_core = [[2 * chip + core for chip in ORDER] for core in range(2)]
     return lax.all_to_all(
         blocks, "ep", split_axis=0, concat_axis=0, axis_index_groups=same_core, tiled=True
     )

time: 150 us -> 149 us (level)
  starting transfers between devices: 55.6 us -> 50.9 us
  waiting for transfers between devices: 55 us -> 58.9 us
    ppermute x7, starting transfers between devices: 27.6 us -> 20.6 us  [from_behind(): lax.ppermute(value, 'section', [(i, (i + steps) % count) for i in range(c...]
    all_to_all x4, waiting for transfers between devices: 7.89 us -> 11.9 us  [exchange(): lax.all_to_all(blocks, 'ep', split_axis=0, concat_axis=0, axis_index_grou...]
    all_to_all x4, starting transfers between devices: 26.8 us -> 29 us  [exchange(): lax.all_to_all(blocks, 'ep', split_axis=0, concat_axis=0, axis_index_grou...]
  transfers between devices with their start and end apart: 18 -> 18, of which waited for: 7 -> 6; matrix products, arithmetic and copies ran while one was open for 1% -> 1% of each run, Pallas kernels for 16% -> 16%
where the time goes in v11:
time: 149 us; the launch traced here: 148 us
  waiting for transfers between devices  58.9 us (40%)
  starting transfers between devices  50.9 us (34%)
  Pallas kernels  29.4 us (20%)
  local copies, waits for them, and re-layouts  8.04 us (5%)
    ppermute x7, waiting for transfers between devices, from_behind(): lax.ppermute(value, 'section', [(i, (i + steps) % count) for i in range(c...  41.4 us
    all_to_all x4, starting transfers between devices, exchange(): lax.all_to_all(blocks, 'ep', split_axis=0, concat_axis=0, axis_index_grou...  29 us
    ppermute x7, starting transfers between devices, from_behind(): lax.ppermute(value, 'section', [(i, (i + steps) % count) for i in range(c...  20.6 us
    pallas_call x4, Pallas kernels, hidden_units(): pl.pallas_call(hidden_kernel, out_shape=jax.ShapeDtypeStruct((count, widt...  13.1 us
    all_to_all x4, waiting for transfers between devices, exchange(): lax.all_to_all(blocks, 'ep', split_axis=0, concat_axis=0, axis_index_grou...  11.9 us
    unnamed x36, local copies, waits for them, and re-layouts  7 us
    pallas_call x2, Pallas kernels, down_product(): pl.pallas_call(functools.partial(down_kernel, len(down)), out_shape=jax.S...  6.46 us
    ppermute x1, waiting for transfers between devices, behind_other_core(): return lax.ppermute(value, ('section', 'ep'), pairs)  5.6 us
  transfers between devices with their start and end apart: 18, of which 6 were waited for; matrix products, arithmetic and copies ran while one was open for 1% of the time, Pallas kernels for 16%

profile of v11, /device:TPU:8, one launch (start us, length us, event | category | flops | bytes accessed | tf_op | source)
XLA Modules:
  0.0 148.2 jit_solution(9466595495041353064)
XLA Ops:
  0.6 3.4 %shard_map.113 = bf16[16,72,896]{2,1,0:T(8,128)(2,1)} custom-call(bf16[128,3584]{1,0:T(8,128)(2,1)} %bitcast.25, s32[1,128]{1,0:T(1,128)} %bitcast.29, f32[1,3584]{1,0:T(1,128)} %gain_hbm.3), custom_call_target="tpu_custom_call" | custom-call | flops 176160768 | bytes 3670016 | tf_op jit(solution)/shard_map/pallas_call | solution.py:85
  4.0 0.0 copy-start.6
  4.0 7.5 %all-to-all-start = ((bf16[16,72,896]{2,1,0:T(8,128)(2,1)}), bf16[16,72,896]{2,1,0:T(8,128)(2,1)}, u32[]{:S(2)}, u32[]{:S(2)}) async-start(bf16[16,72,896]{2,1,0:T(8,128)(2,1)} %shard_map.113), calls=%async_computation | async-start | bytes 4128768 | tf_op jit(solution)/shard_map/all_to_all | solution.py:249
  11.6 0.0 copy-start.13
  11.6 0.0 copy-start.16
  11.6 0.1 collective-permute-start
  11.7 1.0 slice_bitcast_fusion
  12.8 5.9 %collective-permute-start.1 = (bf16[128,3584]{1,0:T(8,128)(2,1)S(1)}, bf16[128,3584]{1,0:T(8,128)(2,1)S(1)}, u32[]{:S(2)}, u32[]{:S(2)}) collective-permute-start(bf16[128,3584]{1,0:T(8,128)(2,1)S(1)} %get-tuple-element.23), channel_id=1, source_target_pairs={{0,224},{32,0},{64,32},{96,64},{128,96},{160,128},{192,160},{224,1... | collective-permute-start | bytes 2752520 | tf_op jit(solution)/shard_map/ppermute | solution.py:236
  18.6 0.0 collective-permute-done.refs_1_
  18.6 1.3 copy-done.9
  19.9 1.2 shard_map.114
  21.1 1.3 copy-done.5
  22.4 16.5 %collective-permute-done.1.refs_0_ = bf16[128,3584]{1,0:T(8,128)(2,1)S(1)} collective-permute-done((bf16[128,3584]{1,0:T(8,128)(2,1)S(1)}, bf16[128,3584]{1,0:T(8,128)(2,1)S(1)}, u32[]{:S(2)}, u32[]{:S(2)}) %collective-permute-start.1) | collective-permute-done | bytes 917536 | tf_op jit(solution)/shard_map/ppermute | solution.py:236
  38.9 7.2 %all-to-all-start.1 = ((bf16[16,72,896]{2,1,0:T(8,128)(2,1)}), bf16[16,72,896]{2,1,0:T(8,128)(2,1)}, u32[]{:S(2)}, u32[]{:S(2)}) async-start(bf16[16,72,896]{2,1,0:T(8,128)(2,1)} %copy-done.5), calls=%async_computation.1 | async-start | bytes 4128768 | tf_op jit(solution)/shard_map/all_to_all | solution.py:249
  46.1 3.8 %collective-permute-start.4 = (bf16[128,3584]{1,0:T(8,128)(2,1)}, bf16[128,3584]{1,0:T(8,128)(2,1)}, u32[]{:S(2)}, u32[]{:S(2)}) collective-permute-start(bf16[128,3584]{1,0:T(8,128)(2,1)} %get-tuple-element.22), channel_id=1, source_target_pairs={{0,224},{32,0},{64,32},{96,64},{128,96},{160,128},{192,160},{224,1... | collective-permute-start | bytes 2752520 | tf_op jit(solution)/shard_map/ppermute | solution.py:236
  49.9 1.5 %copy-done.1 = bf16[1,3584,256]{2,1,0:T(8,128)(2,1)S(1)} copy-done((bf16[1,3584,256]{2,1,0:T(8,128)(2,1)S(1)}, bf16[1,3584,256]{2,1,0:T(8,128)(2,1)}, u32[]{:S(2)}) %copy-start.1) | copy-done | bytes 1835032
  51.4 3.3 %shard_map.116 = bf16[288,256]{1,0:T(8,128)(2,1)S(1)} custom-call(bf16[16,72,896]{2,1,0:T(8,128)(2,1)} %collective-permute-done.2.received_ref, bf16[3584,256]{1,0:T(8,128)(2,1)S(1)} %bitcast.15, bf16[3584,256]{1,0:T(8,128)(2,1)S(1)} %bitcast.19), custom_call_target="tpu_custom_call" | custom-call | flops 1056964608 | bytes 5734400 | tf_op jit(solution)/shard_map/pallas_call | solution.py:124
  54.8 0.0 copy-start.7
  54.8 0.1 collective-permute-start.3
  54.9 3.3 %shard_map.115.mine_ref = bf16[288,256]{1,0:T(8,128)(2,1)S(1)} custom-call(bf16[16,72,896]{2,1,0:T(8,128)(2,1)} %all-to-all-done.received_ref, bf16[3584,256]{1,0:T(8,128)(2,1)S(1)} %bitcast.16, bf16[3584,256]{1,0:T(8,128)(2,1)S(1)} %bitcast.20), custom_call_target="tpu_custom_call" | custom-call | flops 1056964608 | bytes 5734400 | tf_op jit(solution)/shard_map/pallas_call | solution.py:124
  58.3 2.0 %shard_map.117 = bf16[16,72,896]{2,1,0:T(8,128)(2,1)S(1)} custom-call(bf16[288,256]{1,0:T(8,128)(2,1)S(1)} %shard_map.115.mine_ref, bf16[288,256]{1,0:T(8,128)(2,1)S(1)} %collective-permute-done.3.theirs_ref, bf16[256,3584]{1,0:T(8,128)(2,1)S(1)} %bitcast.24, bf16[256,3584]{1,0:T(8,128)(2,1)S(1)} %copy-done.10), custom_call_target="tpu_custom_call" | custom-call | flops 1056964608 | bytes 5734400 | tf_op jit(solution)/shard_map/pallas_call | solution.py:164
  60.3 1.4 copy-done.4
  61.6 8.3 %collective-permute-done.4.refs_1_ = bf16[128,3584]{1,0:T(8,128)(2,1)} collective-permute-done((bf16[128,3584]{1,0:T(8,128)(2,1)}, bf16[128,3584]{1,0:T(8,128)(2,1)}, u32[]{:S(2)}, u32[]{:S(2)}) %collective-permute-start.4) | collective-permute-done | bytes 917536 | tf_op jit(solution)/shard_map/ppermute | solution.py:236
  70.0 5.1 %all-to-all-done.1.received_ref = bf16[16,72,896]{2,1,0:T(8,128)(2,1)} async-done(((bf16[16,72,896]{2,1,0:T(8,128)(2,1)}), bf16[16,72,896]{2,1,0:T(8,128)(2,1)}, u32[]{:S(2)}, u32[]{:S(2)}) %all-to-all-start.1) | async-done | bytes 2064416 | tf_op jit(solution)/shard_map/all_to_all | solution.py:249
  75.0 6.3 %all-to-all-start.2 = ((bf16[16,72,896]{2,1,0:T(8,128)(2,1)}), bf16[16,72,896]{2,1,0:T(8,128)(2,1)}, u32[]{:S(2)}, u32[]{:S(2)}) async-start(bf16[16,72,896]{2,1,0:T(8,128)(2,1)} %copy-done.4), calls=%async_computation.2 | async-start | bytes 4128768 | tf_op jit(solution)/shard_map/all_to_all | solution.py:249
  81.3 0.2 collective-permute-start.8
  81.4 0.4 collective-permute-start.9
  81.8 1.5 %copy-done.3 = bf16[1,3584,256]{2,1,0:T(8,128)(2,1)S(1)} copy-done((bf16[1,3584,256]{2,1,0:T(8,128)(2,1)S(1)}, bf16[1,3584,256]{2,1,0:T(8,128)(2,1)}, u32[]{:S(2)}) %copy-start.3) | copy-done | bytes 1835032
  83.3 3.2 %shard_map.118 = bf16[288,256]{1,0:T(8,128)(2,1)S(1)} custom-call(bf16[16,72,896]{2,1,0:T(8,128)(2,1)} %all-to-all-done.1.received_ref, bf16[3584,256]{1,0:T(8,128)(2,1)S(1)} %bitcast.17, bf16[3584,256]{1,0:T(8,128)(2,1)S(1)} %bitcast.21), custom_call_target="tpu_custom_call" | custom-call | flops 1056964608 | bytes 5734400 | tf_op jit(solution)/shard_map/pallas_call | solution.py:124
  86.5 4.1 %collective-permute-start.5 = (bf16[288,256]{1,0:T(8,128)(2,1)S(1)}, bf16[288,256]{1,0:T(8,128)(2,1)S(1)}, u32[]{:S(2)}, u32[]{:S(2)}) collective-permute-start(bf16[288,256]{1,0:T(8,128)(2,1)S(1)} %shard_map.118), channel_id=1, source_target_pairs={{0,224},{32,0},{64,32},{96,64},{128,96},{160,128},{192,160},{224,1... | collective-permute-start | bytes 442376 | tf_op jit(solution)/shard_map/ppermute | solution.py:236
  90.6 0.0 collective-permute-done.6.received_ref
  90.6 3.2 %shard_map.119 = bf16[288,256]{1,0:T(8,128)(2,1)S(1)} custom-call(bf16[16,72,896]{2,1,0:T(8,128)(2,1)} %collective-permute-done.6.received_ref, bf16[3584,256]{1,0:T(8,128)(2,1)S(1)} %bitcast.18, bf16[3584,256]{1,0:T(8,128)(2,1)S(1)} %bitcast.22), custom_call_target="tpu_custom_call" | custom-call | flops 1056964608 | bytes 5734400 | tf_op jit(solution)/shard_map/pallas_call | solution.py:124
  93.8 0.6 collective-permute-start.7
  94.3 0.0 collective-permute-done.8.refs_2_
  94.3 5.6 %collective-permute-done.7.theirs_ref = bf16[288,256]{1,0:T(8,128)(2,1)S(1)} collective-permute-done((bf16[288,256]{1,0:T(8,128)(2,1)S(1)}, bf16[288,256]{1,0:T(8,128)(2,1)S(1)}, u32[]{:S(2)}, u32[]{:S(2)}) %collective-permute-start.7) | collective-permute-done | bytes 147488 | tf_op jit(solution)/shard_map/ppermute | solution.py:244
  99.9 4.5 %shard_map.120 = bf16[16,72,896]{2,1,0:T(8,128)(2,1)} custom-call(bf16[288,256]{1,0:T(8,128)(2,1)S(1)} %collective-permute-done.5.mine_ref, bf16[288,256]{1,0:T(8,128)(2,1)S(1)} %collective-permute-done.7.theirs_ref, bf16[128,3584]{1,0:T(8,128)(2,1)S(1)} %collective-permute-done.1.refs_0_, bf16[128,3584]{1,0:T(8,128)(2,1)} %collective-permute-done.4.refs_1_, ...), custom_call_target="tpu_custom_call" | custom-call | flops 1056964608 | bytes 5734400 | tf_op jit(solution)/shard_map/pallas_call | solution.py:164
  104.4 6.8 %all-to-all-done.2.back_ref = bf16[16,72,896]{2,1,0:T(8,128)(2,1)} async-done(((bf16[16,72,896]{2,1,0:T(8,128)(2,1)}), bf16[16,72,896]{2,1,0:T(8,128)(2,1)}, u32[]{:S(2)}, u32[]{:S(2)}) %all-to-all-start.2) | async-done | bytes 2064416 | tf_op jit(solution)/shard_map/all_to_all | solution.py:249
  111.3 8.0 %all-to-all-start.3 = ((bf16[16,72,896]{2,1,0:T(8,128)(2,1)}), bf16[16,72,896]{2,1,0:T(8,128)(2,1)S(1)}, u32[]{:S(2)}, u32[]{:S(2)}) async-start(bf16[16,72,896]{2,1,0:T(8,128)(2,1)} %shard_map.120), calls=%async_computation.3 | async-start | bytes 4128768 | tf_op jit(solution)/shard_map/all_to_all | solution.py:249
  119.3 0.0 copy-start.12
  119.3 0.0 copy-start.17
  119.3 2.5 %shard_map.121 = bf16[128,3584]{1,0:T(8,128)(2,1)S(1)} custom-call(bf16[128,3584]{1,0:T(8,128)(2,1)S(1)} %bitcast.26, bf16[16,72,896]{2,1,0:T(8,128)(2,1)} %all-to-all-done.2.back_ref, s32[1,128]{1,0:T(1,128)S(1)} %bitcast.30, f32[1,128]{1,0:T(1,128)S(1)} %bitcast.31), custom_call_target="tpu_custom_call" | custom-call | flops 352321536 | bytes 3670016 | tf_op jit(solution)/shard_map/pallas_call | solution.py:205
  121.9 0.1 collective-permute-start.10
  122.0 3.9 %collective-permute-start.11 = (bf16[128,3584]{1,0:T(8,128)(2,1)S(1)}, bf16[128,3584]{1,0:T(8,128)(2,1)S(1)}, u32[]{:S(2)}, u32[]{:S(2)}) collective-permute-start(bf16[128,3584]{1,0:T(8,128)(2,1)S(1)} %bitcast.28), channel_id=1, source_target_pairs={{0,224},{32,0},{64,32},{96,64},{128,96},{160,128},{192,160},{224,1... | collective-permute-start | bytes 2752520 | tf_op jit(solution)/shard_map/ppermute | solution.py:236
  125.8 1.9 %collective-permute-start.12 = (s32[1,128]{1,0:T(1,128)S(1)}, s32[1,128]{1,0:T(1,128)S(1)}, u32[]{:S(2)}, u32[]{:S(2)}) collective-permute-start(s32[1,128]{1,0:T(1,128)S(1)} %bitcast.33), channel_id=1, source_target_pairs={{0,224},{32,0},{64,32},{96,64},{128,96},{160,128},{192,160},{224,1... | collective-permute-start | bytes 1544 | tf_op jit(solution)/shard_map/ppermute | solution.py:236
  127.8 1.0 collective-permute-start.13
  128.8 16.6 %collective-permute-done.10.value_ref = bf16[128,3584]{1,0:T(8,128)(2,1)S(1)} collective-permute-done((bf16[128,3584]{1,0:T(8,128)(2,1)S(1)}, bf16[128,3584]{1,0:T(8,128)(2,1)S(1)}, u32[]{:S(2)}, u32[]{:S(2)}) %collective-permute-start.10) | collective-permute-done | bytes 917536 | tf_op jit(solution)/shard_map/ppermute | solution.py:236
  145.4 1.0 shard_map.122
  146.4 1.8 %shard_map.123 = bf16[128,3584]{1,0:T(8,128)(2,1)} custom-call(bf16[128,3584]{1,0:T(8,128)(2,1)S(1)} %collective-permute-done.11.current_ref, bf16[16,72,896]{2,1,0:T(8,128)(2,1)S(1)} %all-to-all-done.3.back_ref, s32[1,128]{1,0:T(1,128)S(1)} %collective-permute-done.12.ids_ref, f32[1,128]{1,0:T(1,128)S(1)} %collective-permute-done.13.scores_ref), custom_call_target="tpu_custom_call" | custom-call | flops 352321536 | bytes 3670016 | tf_op jit(solution)/shard_map/pallas_call | solution.py:205
  (36 shorter events, 0.1 us)
Async XLA Ops:
  4.0 7.6 %copy-start.6 = (bf16[1,256,3584]{2,1,0:T(8,128)(2,1)S(1)}, bf16[1,256,3584]{2,1,0:T(8,128)(2,1)}, u32[]{:S(2)}) copy-start(bf16[1,256,3584]{2,1,0:T(8,128)(2,1)} %param.19) | copy-start | bytes 5505028
  4.0 34.8 %all-to-all-start = ((bf16[16,72,896]{2,1,0:T(8,128)(2,1)}), bf16[16,72,896]{2,1,0:T(8,128)(2,1)}, u32[]{:S(2)}, u32[]{:S(2)}) async-start(bf16[16,72,896]{2,1,0:T(8,128)(2,1)} %shard_map.113), calls=%async_computation | async-start | bytes 4128768 | tf_op jit(solution)/shard_map/all_to_all | solution.py:249
  11.6 8.3 %copy-start.11 = (bf16[1,128,3584]{2,1,0:T(8,128)(2,1)S(1)}, bf16[1,128,3584]{2,1,0:T(8,128)(2,1)}, u32[]{:S(2)}) copy-start(bf16[1,128,3584]{2,1,0:T(8,128)(2,1)} %param.11) | copy-start | bytes 2752516
  11.6 8.3 %copy-start.13 = (f32[1,3584]{1,0:T(1,128)S(1)}, f32[1,3584]{1,0:T(1,128)}, u32[]{:S(2)}) copy-start(f32[1,3584]{1,0:T(1,128)} %gain_hbm.3) | copy-start | bytes 43012
  11.6 8.3 %copy-start.16 = (s32[1,1,128,1]{2,3,1,0:T(1,128)S(1)}, s32[1,1,128,1]{2,3,1,0:T(1,128)}, u32[]{:S(2)}) copy-start(s32[1,1,128,1]{2,3,1,0:T(1,128)} %param.13) | copy-start | bytes 1540
  11.6 7.0 %collective-permute-start = (bf16[256,3584]{1,0:T(8,128)(2,1)S(1)}, bf16[256,3584]{1,0:T(8,128)(2,1)S(1)}, u32[]{:S(2)}, u32[]{:S(2)}) collective-permute-start(bf16[256,3584]{1,0:T(8,128)(2,1)S(1)} %bitcast.23), channel_id=1, source_target_pairs={{0,1},{1,0},{2,3},{3,2},{4,5},{5,4},{6,7},{7,6},{8,9},{9,8},{10,11... | collective-permute-start | bytes 5505032 | tf_op jit(solution)/shard_map/ppermute | solution.py:231
  12.8 26.1 %collective-permute-start.1 = (bf16[128,3584]{1,0:T(8,128)(2,1)S(1)}, bf16[128,3584]{1,0:T(8,128)(2,1)S(1)}, u32[]{:S(2)}, u32[]{:S(2)}) collective-permute-start(bf16[128,3584]{1,0:T(8,128)(2,1)S(1)} %get-tuple-element.23), channel_id=1, source_target_pairs={{0,224},{32,0},{64,32},{96,64},{128,96},{160,128},{192,160},{224,1... | collective-permute-start | bytes 2752520 | tf_op jit(solution)/shard_map/ppermute | solution.py:236
  18.6 1.3 copy-start.9
  21.1 1.3 copy-start.5
  22.4 27.5 %copy-start = (bf16[1,3584,256]{2,1,0:T(8,128)(2,1)S(1)}, bf16[1,3584,256]{2,1,0:T(8,128)(2,1)}, u32[]{:S(2)}) copy-start(bf16[1,3584,256]{2,1,0:T(8,128)(2,1)} %param.17) | copy-start | bytes 5505028
  38.9 11.0 %collective-permute-start.2 = (bf16[16,72,896]{2,1,0:T(8,128)(2,1)}, bf16[16,72,896]{2,1,0:T(8,128)(2,1)}, u32[]{:S(2)}, u32[]{:S(2)}) collective-permute-start(bf16[16,72,896]{2,1,0:T(8,128)(2,1)} %all-to-all-done.received_ref), channel_id=1, source_target_pairs={{0,1},{1,0},{2,3},{3,2},{4,5},{5,4},{6,7},{7,6},{8,9},{9,8},{10,11... | collective-permute-start | bytes 6193160 | tf_op jit(solution)/shard_map/ppermute | solution.py:231
  38.9 36.1 %all-to-all-start.1 = ((bf16[16,72,896]{2,1,0:T(8,128)(2,1)}), bf16[16,72,896]{2,1,0:T(8,128)(2,1)}, u32[]{:S(2)}, u32[]{:S(2)}) async-start(bf16[16,72,896]{2,1,0:T(8,128)(2,1)} %copy-done.5), calls=%async_computation.1 | async-start | bytes 4128768 | tf_op jit(solution)/shard_map/all_to_all | solution.py:249
  46.1 23.8 %collective-permute-start.4 = (bf16[128,3584]{1,0:T(8,128)(2,1)}, bf16[128,3584]{1,0:T(8,128)(2,1)}, u32[]{:S(2)}, u32[]{:S(2)}) collective-permute-start(bf16[128,3584]{1,0:T(8,128)(2,1)} %get-tuple-element.22), channel_id=1, source_target_pairs={{0,224},{32,0},{64,32},{96,64},{128,96},{160,128},{192,160},{224,1... | collective-permute-start | bytes 2752520 | tf_op jit(solution)/shard_map/ppermute | solution.py:236
  49.9 1.5 %copy-start.1 = (bf16[1,3584,256]{2,1,0:T(8,128)(2,1)S(1)}, bf16[1,3584,256]{2,1,0:T(8,128)(2,1)}, u32[]{:S(2)}) copy-start(bf16[1,3584,256]{2,1,0:T(8,128)(2,1)} %param.18) | copy-start | bytes 5505028
  51.4 3.5 %copy-start.2 = (bf16[1,3584,256]{2,1,0:T(8,128)(2,1)S(1)}, bf16[1,3584,256]{2,1,0:T(8,128)(2,1)}, u32[]{:S(2)}) copy-start(bf16[1,3584,256]{2,1,0:T(8,128)(2,1)} %param.18) | copy-start | bytes 5505028
  54.8 3.5 %copy-start.7 = (bf16[1,256,3584]{2,1,0:T(8,128)(2,1)S(1)}, bf16[1,256,3584]{2,1,0:T(8,128)(2,1)}, u32[]{:S(2)}) copy-start(bf16[1,256,3584]{2,1,0:T(8,128)(2,1)} %param.19) | copy-start | bytes 5505028
  54.8 3.5 %copy-start.10 = (bf16[256,3584]{1,0:T(8,128)(2,1)S(1)}, bf16[256,3584]{1,0:T(8,128)(2,1)}, u32[]{:S(2)}) copy-start(bf16[256,3584]{1,0:T(8,128)(2,1)} %copy-done.9) | copy-start | bytes 5505028
  54.8 3.5 %collective-permute-start.3 = (bf16[288,256]{1,0:T(8,128)(2,1)S(1)}, bf16[288,256]{1,0:T(8,128)(2,1)S(1)}, u32[]{:S(2)}, u32[]{:S(2)}) collective-permute-start(bf16[288,256]{1,0:T(8,128)(2,1)S(1)} %shard_map.116), channel_id=1, source_target_pairs={{0,1},{1,0},{2,3},{3,2},{4,5},{5,4},{6,7},{7,6},{8,9},{9,8},{10,11... | collective-permute-start | bytes 442376 | tf_op jit(solution)/shard_map/ppermute | solution.py:231
  60.2 1.4 copy-start.4
  75.0 15.6 %collective-permute-start.6 = (bf16[16,72,896]{2,1,0:T(8,128)(2,1)}, bf16[16,72,896]{2,1,0:T(8,128)(2,1)}, u32[]{:S(2)}, u32[]{:S(2)}) collective-permute-start(bf16[16,72,896]{2,1,0:T(8,128)(2,1)} %all-to-all-done.1.received_ref), channel_id=1, source_target_pairs={{0,1},{1,0},{2,3},{3,2},{4,5},{5,4},{6,7},{7,6},{8,9},{9,8},{10,11... | collective-permute-start | bytes 6193160 | tf_op jit(solution)/shard_map/ppermute | solution.py:231
  75.0 36.2 %all-to-all-start.2 = ((bf16[16,72,896]{2,1,0:T(8,128)(2,1)}), bf16[16,72,896]{2,1,0:T(8,128)(2,1)}, u32[]{:S(2)}, u32[]{:S(2)}) async-start(bf16[16,72,896]{2,1,0:T(8,128)(2,1)} %copy-done.4), calls=%async_computation.2 | async-start | bytes 4128768 | tf_op jit(solution)/shard_map/all_to_all | solution.py:249
  81.3 13.0 %collective-permute-start.8 = (bf16[128,3584]{1,0:T(8,128)(2,1)S(1)}, bf16[128,3584]{1,0:T(8,128)(2,1)S(1)}, u32[]{:S(2)}, u32[]{:S(2)}) collective-permute-start(bf16[128,3584]{1,0:T(8,128)(2,1)S(1)} %collective-permute-done.1.refs_0_), channel_id=1, source_target_pairs={{0,1},{1,0},{2,3},{3,2},{4,5},{5,4},{6,7},{7,6},{8,9},{9,8},{10,11... | collective-permute-start | bytes 2752520 | tf_op jit(solution)/shard_map/ppermute | solution.py:231
  81.4 12.9 %collective-permute-start.9 = (bf16[128,3584]{1,0:T(8,128)(2,1)}, bf16[128,3584]{1,0:T(8,128)(2,1)S(1)}, u32[]{:S(2)}, u32[]{:S(2)}) collective-permute-start(bf16[128,3584]{1,0:T(8,128)(2,1)} %collective-permute-done.4.refs_1_), channel_id=1, source_target_pairs={{0,1},{1,0},{2,3},{3,2},{4,5},{5,4},{6,7},{7,6},{8,9},{9,8},{10,11... | collective-permute-start | bytes 2752520 | tf_op jit(solution)/shard_map/ppermute | solution.py:231
  81.8 1.5 %copy-start.3 = (bf16[1,3584,256]{2,1,0:T(8,128)(2,1)S(1)}, bf16[1,3584,256]{2,1,0:T(8,128)(2,1)}, u32[]{:S(2)}) copy-start(bf16[1,3584,256]{2,1,0:T(8,128)(2,1)} %param.18) | copy-start | bytes 5505028
  86.5 7.8 %collective-permute-start.5 = (bf16[288,256]{1,0:T(8,128)(2,1)S(1)}, bf16[288,256]{1,0:T(8,128)(2,1)S(1)}, u32[]{:S(2)}, u32[]{:S(2)}) collective-permute-start(bf16[288,256]{1,0:T(8,128)(2,1)S(1)} %shard_map.118), channel_id=1, source_target_pairs={{0,224},{32,0},{64,32},{96,64},{128,96},{160,128},{192,160},{224,1... | collective-permute-start | bytes 442376 | tf_op jit(solution)/shard_map/ppermute | solution.py:236
  93.8 6.2 %collective-permute-start.7 = (bf16[288,256]{1,0:T(8,128)(2,1)S(1)}, bf16[288,256]{1,0:T(8,128)(2,1)S(1)}, u32[]{:S(2)}, u32[]{:S(2)}) collective-permute-start(bf16[288,256]{1,0:T(8,128)(2,1)S(1)} %shard_map.119), channel_id=1, source_target_pairs={{0,225},{1,224},{2,227},{3,226},{4,229},{5,228},{6,231},{7,230},{8... | collective-permute-start | bytes 442376 | tf_op jit(solution)/shard_map/ppermute | solution.py:244
  104.4 14.8 %copy-start.8 = (bf16[1,128,3584]{2,1,0:T(8,128)(2,1)S(1)}, bf16[1,128,3584]{2,1,0:T(8,128)(2,1)}, u32[]{:S(2)}) copy-start(bf16[1,128,3584]{2,1,0:T(8,128)(2,1)} %param.10) | copy-start | bytes 2752516
  104.4 14.8 %copy-start.14 = (s32[1,1,128,1]{2,3,1,0:T(1,128)S(1)}, s32[1,1,128,1]{2,3,1,0:T(1,128)}, u32[]{:S(2)}) copy-start(s32[1,1,128,1]{2,3,1,0:T(1,128)} %param.12) | copy-start | bytes 1540
  104.4 14.8 %copy-start.15 = (f32[1,1,128,1]{2,3,1,0:T(1,128)S(1)}, f32[1,1,128,1]{2,3,1,0:T(1,128)}, u32[]{:S(2)}) copy-start(f32[1,1,128,1]{2,3,1,0:T(1,128)} %param.14) | copy-start | bytes 1540
  111.3 35.1 %all-to-all-start.3 = ((bf16[16,72,896]{2,1,0:T(8,128)(2,1)}), bf16[16,72,896]{2,1,0:T(8,128)(2,1)S(1)}, u32[]{:S(2)}, u32[]{:S(2)}) async-start(bf16[16,72,896]{2,1,0:T(8,128)(2,1)} %shard_map.120), calls=%async_computation.3 | async-start | bytes 4128768 | tf_op jit(solution)/shard_map/all_to_all | solution.py:249
  119.3 2.7 %copy-start.12 = (bf16[1,128,3584]{2,1,0:T(8,128)(2,1)S(1)}, bf16[1,128,3584]{2,1,0:T(8,128)(2,1)}, u32[]{:S(2)}) copy-start(bf16[1,128,3584]{2,1,0:T(8,128)(2,1)} %param.11) | copy-start | bytes 2752516
  119.3 8.5 %copy-start.17 = (f32[1,1,128,1]{2,3,1,0:T(1,128)S(1)}, f32[1,1,128,1]{2,3,1,0:T(1,128)}, u32[]{:S(2)}) copy-start(f32[1,1,128,1]{2,3,1,0:T(1,128)} %param.15) | copy-start | bytes 1540
  121.9 23.5 %collective-permute-start.10 = (bf16[128,3584]{1,0:T(8,128)(2,1)S(1)}, bf16[128,3584]{1,0:T(8,128)(2,1)S(1)}, u32[]{:S(2)}, u32[]{:S(2)}) collective-permute-start(bf16[128,3584]{1,0:T(8,128)(2,1)S(1)} %shard_map.121), channel_id=1, source_target_pairs={{0,32},{32,64},{64,96},{96,128},{128,160},{160,192},{192,224},{224... | collective-permute-start | bytes 2752520 | tf_op jit(solution)/shard_map/ppermute | solution.py:236
  122.0 24.4 %collective-permute-start.11 = (bf16[128,3584]{1,0:T(8,128)(2,1)S(1)}, bf16[128,3584]{1,0:T(8,128)(2,1)S(1)}, u32[]{:S(2)}, u32[]{:S(2)}) collective-permute-start(bf16[128,3584]{1,0:T(8,128)(2,1)S(1)} %bitcast.28), channel_id=1, source_target_pairs={{0,224},{32,0},{64,32},{96,64},{128,96},{160,128},{192,160},{224,1... | collective-permute-start | bytes 2752520 | tf_op jit(solution)/shard_map/ppermute | solution.py:236
  125.8 20.5 %collective-permute-start.12 = (s32[1,128]{1,0:T(1,128)S(1)}, s32[1,128]{1,0:T(1,128)S(1)}, u32[]{:S(2)}, u32[]{:S(2)}) collective-permute-start(s32[1,128]{1,0:T(1,128)S(1)} %bitcast.33), channel_id=1, source_target_pairs={{0,224},{32,0},{64,32},{96,64},{128,96},{160,128},{192,160},{224,1... | collective-permute-start | bytes 1544 | tf_op jit(solution)/shard_map/ppermute | solution.py:236
  127.8 18.6 %collective-permute-start.13 = (f32[1,128]{1,0:T(1,128)S(1)}, f32[1,128]{1,0:T(1,128)S(1)}, u32[]{:S(2)}, u32[]{:S(2)}) collective-permute-start(f32[1,128]{1,0:T(1,128)S(1)} %bitcast.36), channel_id=1, source_target_pairs={{0,224},{32,0},{64,32},{96,64},{128,96},{160,128},{192,160},{224,1... | collective-permute-start | bytes 1544 | tf_op jit(solution)/shard_map/ppermute | solution.py:236

commit v12 on v11

--- a/solution.py
+++ b/solution.py
@@ -13,7 +13,7 @@
 CHIPS = EP // 2
 MAIN = 16
 LAST = 2
-ORDER = (0, 1, 2, 3, 5, 6, 7, 4, 10, 11, 8, 9, 15, 12, 13, 14)
+ORDER = (0, 1, 2, 3, 7, 4, 5, 6, 10, 11, 8, 9, 13, 14, 15, 12)
 EPSILON = 1e-06
 F32 = jnp.float32
 BF16 = jnp.bfloat16

time: 149 us -> 148 us (level)
  waiting for transfers between devices: 58.9 us -> 56.8 us
    ppermute x7, starting transfers between devices: 20.6 us -> 23 us  [from_behind(): lax.ppermute(value, 'section', [(i, (i + steps) % count) for i in range(c...]
    all_to_all x4, waiting for transfers between devices: 11.9 us -> 9.76 us  [exchange(): lax.all_to_all(blocks, 'ep', split_axis=0, concat_axis=0, axis_index_grou...]
where the time goes in v12:
time: 148 us; the launch traced here: 147 us
  waiting for transfers between devices  56.8 us (38%)
  starting transfers between devices  51.8 us (35%)
  Pallas kernels  29.4 us (20%)
  local copies, waits for them, and re-layouts  8.04 us (5%)
    ppermute x7, waiting for transfers between devices, from_behind(): lax.ppermute(value, 'section', [(i, (i + steps) % count) for i in range(c...  41.3 us
    all_to_all x4, starting transfers between devices, exchange(): lax.all_to_all(blocks, 'ep', split_axis=0, concat_axis=0, axis_index_grou...  27.6 us
    ppermute x7, starting transfers between devices, from_behind(): lax.ppermute(value, 'section', [(i, (i + steps) % count) for i in range(c...  23 us
    pallas_call x4, Pallas kernels, hidden_units(): pl.pallas_call(hidden_kernel, out_shape=jax.ShapeDtypeStruct((count, widt...  13.1 us
    all_to_all x4, waiting for transfers between devices, exchange(): lax.all_to_all(blocks, 'ep', split_axis=0, concat_axis=0, axis_index_grou...  9.76 us
    unnamed x36, local copies, waits for them, and re-layouts  7 us
    pallas_call x2, Pallas kernels, down_product(): pl.pallas_call(functools.partial(down_kernel, len(down)), out_shape=jax.S...  6.46 us
    ppermute x1, waiting for transfers between devices, behind_other_core(): return lax.ppermute(value, ('section', 'ep'), pairs)  5.71 us
  transfers between devices with their start and end apart: 18, of which 6 were waited for; matrix products, arithmetic and copies ran while one was open for 1% of the time, Pallas kernels for 16%

profile of v12, /device:TPU:8, one launch (start us, length us, event | category | flops | bytes accessed | tf_op | source)
XLA Modules:
  0.0 146.9 jit_solution(7169155168537174003)
XLA Ops:
  0.6 3.4 %shard_map.113 = bf16[16,72,896]{2,1,0:T(8,128)(2,1)} custom-call(bf16[128,3584]{1,0:T(8,128)(2,1)} %bitcast.25, s32[1,128]{1,0:T(1,128)} %bitcast.29, f32[1,3584]{1,0:T(1,128)} %gain_hbm.3), custom_call_target="tpu_custom_call" | custom-call | flops 176160768 | bytes 3670016 | tf_op jit(solution)/shard_map/pallas_call | solution.py:85
  4.0 0.0 copy-start.6
  4.0 7.5 %all-to-all-start = ((bf16[16,72,896]{2,1,0:T(8,128)(2,1)}), bf16[16,72,896]{2,1,0:T(8,128)(2,1)}, u32[]{:S(2)}, u32[]{:S(2)}) async-start(bf16[16,72,896]{2,1,0:T(8,128)(2,1)} %shard_map.113), calls=%async_computation | async-start | bytes 4128768 | tf_op jit(solution)/shard_map/all_to_all | solution.py:249
  11.6 0.0 copy-start.13
  11.6 0.0 copy-start.16
  11.6 0.1 collective-permute-start
  11.7 1.0 slice_bitcast_fusion
  12.8 5.9 %collective-permute-start.1 = (bf16[128,3584]{1,0:T(8,128)(2,1)S(1)}, bf16[128,3584]{1,0:T(8,128)(2,1)S(1)}, u32[]{:S(2)}, u32[]{:S(2)}) collective-permute-start(bf16[128,3584]{1,0:T(8,128)(2,1)S(1)} %get-tuple-element.23), channel_id=1, source_target_pairs={{0,224},{32,0},{64,32},{96,64},{128,96},{160,128},{192,160},{224,1... | collective-permute-start | bytes 2752520 | tf_op jit(solution)/shard_map/ppermute | solution.py:236
  18.6 0.0 collective-permute-done.refs_1_
  18.6 1.3 copy-done.9
  19.9 1.2 shard_map.114
  21.1 1.3 copy-done.5
  22.4 16.5 %collective-permute-done.1.refs_0_ = bf16[128,3584]{1,0:T(8,128)(2,1)S(1)} collective-permute-done((bf16[128,3584]{1,0:T(8,128)(2,1)S(1)}, bf16[128,3584]{1,0:T(8,128)(2,1)S(1)}, u32[]{:S(2)}, u32[]{:S(2)}) %collective-permute-start.1) | collective-permute-done | bytes 917536 | tf_op jit(solution)/shard_map/ppermute | solution.py:236
  38.9 7.2 %all-to-all-start.1 = ((bf16[16,72,896]{2,1,0:T(8,128)(2,1)}), bf16[16,72,896]{2,1,0:T(8,128)(2,1)}, u32[]{:S(2)}, u32[]{:S(2)}) async-start(bf16[16,72,896]{2,1,0:T(8,128)(2,1)} %copy-done.5), calls=%async_computation.1 | async-start | bytes 4128768 | tf_op jit(solution)/shard_map/all_to_all | solution.py:249
  46.1 3.7 %collective-permute-start.4 = (bf16[128,3584]{1,0:T(8,128)(2,1)}, bf16[128,3584]{1,0:T(8,128)(2,1)}, u32[]{:S(2)}, u32[]{:S(2)}) collective-permute-start(bf16[128,3584]{1,0:T(8,128)(2,1)} %get-tuple-element.22), channel_id=1, source_target_pairs={{0,224},{32,0},{64,32},{96,64},{128,96},{160,128},{192,160},{224,1... | collective-permute-start | bytes 2752520 | tf_op jit(solution)/shard_map/ppermute | solution.py:236
  49.8 0.0 collective-permute-done.2.received_ref
  49.8 1.5 %copy-done.1 = bf16[1,3584,256]{2,1,0:T(8,128)(2,1)S(1)} copy-done((bf16[1,3584,256]{2,1,0:T(8,128)(2,1)S(1)}, bf16[1,3584,256]{2,1,0:T(8,128)(2,1)}, u32[]{:S(2)}) %copy-start.1) | copy-done | bytes 1835032
  51.3 3.3 %shard_map.116 = bf16[288,256]{1,0:T(8,128)(2,1)S(1)} custom-call(bf16[16,72,896]{2,1,0:T(8,128)(2,1)} %collective-permute-done.2.received_ref, bf16[3584,256]{1,0:T(8,128)(2,1)S(1)} %bitcast.15, bf16[3584,256]{1,0:T(8,128)(2,1)S(1)} %bitcast.19), custom_call_target="tpu_custom_call" | custom-call | flops 1056964608 | bytes 5734400 | tf_op jit(solution)/shard_map/pallas_call | solution.py:124
  54.7 0.0 copy-start.7
  54.7 0.1 collective-permute-start.3
  54.8 3.3 %shard_map.115.mine_ref = bf16[288,256]{1,0:T(8,128)(2,1)S(1)} custom-call(bf16[16,72,896]{2,1,0:T(8,128)(2,1)} %all-to-all-done.received_ref, bf16[3584,256]{1,0:T(8,128)(2,1)S(1)} %bitcast.16, bf16[3584,256]{1,0:T(8,128)(2,1)S(1)} %bitcast.20), custom_call_target="tpu_custom_call" | custom-call | flops 1056964608 | bytes 5734400 | tf_op jit(solution)/shard_map/pallas_call | solution.py:124
  58.2 2.0 %shard_map.117 = bf16[16,72,896]{2,1,0:T(8,128)(2,1)S(1)} custom-call(bf16[288,256]{1,0:T(8,128)(2,1)S(1)} %shard_map.115.mine_ref, bf16[288,256]{1,0:T(8,128)(2,1)S(1)} %collective-permute-done.3.theirs_ref, bf16[256,3584]{1,0:T(8,128)(2,1)S(1)} %bitcast.24, bf16[256,3584]{1,0:T(8,128)(2,1)S(1)} %copy-done.10), custom_call_target="tpu_custom_call" | custom-call | flops 1056964608 | bytes 5734400 | tf_op jit(solution)/shard_map/pallas_call | solution.py:164
  60.1 1.4 copy-done.4
  61.5 8.5 %collective-permute-done.4.refs_1_ = bf16[128,3584]{1,0:T(8,128)(2,1)} collective-permute-done((bf16[128,3584]{1,0:T(8,128)(2,1)}, bf16[128,3584]{1,0:T(8,128)(2,1)}, u32[]{:S(2)}, u32[]{:S(2)}) %collective-permute-start.4) | collective-permute-done | bytes 917536 | tf_op jit(solution)/shard_map/ppermute | solution.py:236
  70.1 5.1 %all-to-all-done.1.received_ref = bf16[16,72,896]{2,1,0:T(8,128)(2,1)} async-done(((bf16[16,72,896]{2,1,0:T(8,128)(2,1)}), bf16[16,72,896]{2,1,0:T(8,128)(2,1)}, u32[]{:S(2)}, u32[]{:S(2)}) %all-to-all-start.1) | async-done | bytes 2064416 | tf_op jit(solution)/shard_map/all_to_all | solution.py:249
  75.2 6.4 %all-to-all-start.2 = ((bf16[16,72,896]{2,1,0:T(8,128)(2,1)}), bf16[16,72,896]{2,1,0:T(8,128)(2,1)}, u32[]{:S(2)}, u32[]{:S(2)}) async-start(bf16[16,72,896]{2,1,0:T(8,128)(2,1)} %copy-done.4), calls=%async_computation.2 | async-start | bytes 4128768 | tf_op jit(solution)/shard_map/all_to_all | solution.py:249
  81.6 0.0 collective-permute-start.8
  81.6 0.5 collective-permute-start.9
  82.1 1.5 %copy-done.3 = bf16[1,3584,256]{2,1,0:T(8,128)(2,1)S(1)} copy-done((bf16[1,3584,256]{2,1,0:T(8,128)(2,1)S(1)}, bf16[1,3584,256]{2,1,0:T(8,128)(2,1)}, u32[]{:S(2)}) %copy-start.3) | copy-done | bytes 1835032
  83.6 3.2 %shard_map.118 = bf16[288,256]{1,0:T(8,128)(2,1)S(1)} custom-call(bf16[16,72,896]{2,1,0:T(8,128)(2,1)} %all-to-all-done.1.received_ref, bf16[3584,256]{1,0:T(8,128)(2,1)S(1)} %bitcast.17, bf16[3584,256]{1,0:T(8,128)(2,1)S(1)} %bitcast.21), custom_call_target="tpu_custom_call" | custom-call | flops 1056964608 | bytes 5734400 | tf_op jit(solution)/shard_map/pallas_call | solution.py:124
  86.8 5.3 %collective-permute-start.5 = (bf16[288,256]{1,0:T(8,128)(2,1)S(1)}, bf16[288,256]{1,0:T(8,128)(2,1)S(1)}, u32[]{:S(2)}, u32[]{:S(2)}) collective-permute-start(bf16[288,256]{1,0:T(8,128)(2,1)S(1)} %shard_map.118), channel_id=1, source_target_pairs={{0,224},{32,0},{64,32},{96,64},{128,96},{160,128},{192,160},{224,1... | collective-permute-start | bytes 442376 | tf_op jit(solution)/shard_map/ppermute | solution.py:236
  92.1 3.2 %shard_map.119 = bf16[288,256]{1,0:T(8,128)(2,1)S(1)} custom-call(bf16[16,72,896]{2,1,0:T(8,128)(2,1)} %collective-permute-done.6.received_ref, bf16[3584,256]{1,0:T(8,128)(2,1)S(1)} %bitcast.18, bf16[3584,256]{1,0:T(8,128)(2,1)S(1)} %bitcast.22), custom_call_target="tpu_custom_call" | custom-call | flops 1056964608 | bytes 5734400 | tf_op jit(solution)/shard_map/pallas_call | solution.py:124
  95.3 0.5 collective-permute-start.7
  95.8 0.0 collective-permute-done.8.refs_2_
  95.8 5.7 %collective-permute-done.7.theirs_ref = bf16[288,256]{1,0:T(8,128)(2,1)S(1)} collective-permute-done((bf16[288,256]{1,0:T(8,128)(2,1)S(1)}, bf16[288,256]{1,0:T(8,128)(2,1)S(1)}, u32[]{:S(2)}, u32[]{:S(2)}) %collective-permute-start.7) | collective-permute-done | bytes 147488 | tf_op jit(solution)/shard_map/ppermute | solution.py:244
  101.5 4.5 %shard_map.120 = bf16[16,72,896]{2,1,0:T(8,128)(2,1)} custom-call(bf16[288,256]{1,0:T(8,128)(2,1)S(1)} %collective-permute-done.5.mine_ref, bf16[288,256]{1,0:T(8,128)(2,1)S(1)} %collective-permute-done.7.theirs_ref, bf16[128,3584]{1,0:T(8,128)(2,1)S(1)} %collective-permute-done.1.refs_0_, bf16[128,3584]{1,0:T(8,128)(2,1)} %collective-permute-done.4.refs_1_, ...), custom_call_target="tpu_custom_call" | custom-call | flops 1056964608 | bytes 5734400 | tf_op jit(solution)/shard_map/pallas_call | solution.py:164
  106.0 4.6 %all-to-all-done.2.back_ref = bf16[16,72,896]{2,1,0:T(8,128)(2,1)} async-done(((bf16[16,72,896]{2,1,0:T(8,128)(2,1)}), bf16[16,72,896]{2,1,0:T(8,128)(2,1)}, u32[]{:S(2)}, u32[]{:S(2)}) %all-to-all-start.2) | async-done | bytes 2064416 | tf_op jit(solution)/shard_map/all_to_all | solution.py:249
  110.7 6.4 %all-to-all-start.3 = ((bf16[16,72,896]{2,1,0:T(8,128)(2,1)}), bf16[16,72,896]{2,1,0:T(8,128)(2,1)S(1)}, u32[]{:S(2)}, u32[]{:S(2)}) async-start(bf16[16,72,896]{2,1,0:T(8,128)(2,1)} %shard_map.120), calls=%async_computation.3 | async-start | bytes 4128768 | tf_op jit(solution)/shard_map/all_to_all | solution.py:249
  117.1 0.0 copy-start.12
  117.1 0.0 copy-start.17
  117.1 2.5 %shard_map.121 = bf16[128,3584]{1,0:T(8,128)(2,1)S(1)} custom-call(bf16[128,3584]{1,0:T(8,128)(2,1)S(1)} %bitcast.26, bf16[16,72,896]{2,1,0:T(8,128)(2,1)} %all-to-all-done.2.back_ref, s32[1,128]{1,0:T(1,128)S(1)} %bitcast.30, f32[1,128]{1,0:T(1,128)S(1)} %bitcast.31), custom_call_target="tpu_custom_call" | custom-call | flops 352321536 | bytes 3670016 | tf_op jit(solution)/shard_map/pallas_call | solution.py:205
  119.7 1.2 collective-permute-start.10
  120.9 4.0 %collective-permute-start.11 = (bf16[128,3584]{1,0:T(8,128)(2,1)S(1)}, bf16[128,3584]{1,0:T(8,128)(2,1)S(1)}, u32[]{:S(2)}, u32[]{:S(2)}) collective-permute-start(bf16[128,3584]{1,0:T(8,128)(2,1)S(1)} %bitcast.28), channel_id=1, source_target_pairs={{0,224},{32,0},{64,32},{96,64},{128,96},{160,128},{192,160},{224,1... | collective-permute-start | bytes 2752520 | tf_op jit(solution)/shard_map/ppermute | solution.py:236
  124.9 1.9 %collective-permute-start.12 = (s32[1,128]{1,0:T(1,128)S(1)}, s32[1,128]{1,0:T(1,128)S(1)}, u32[]{:S(2)}, u32[]{:S(2)}) collective-permute-start(s32[1,128]{1,0:T(1,128)S(1)} %bitcast.33), channel_id=1, source_target_pairs={{0,224},{32,0},{64,32},{96,64},{128,96},{160,128},{192,160},{224,1... | collective-permute-start | bytes 1544 | tf_op jit(solution)/shard_map/ppermute | solution.py:236
  126.8 1.0 collective-permute-start.13
  127.8 16.3 %collective-permute-done.10.value_ref = bf16[128,3584]{1,0:T(8,128)(2,1)S(1)} collective-permute-done((bf16[128,3584]{1,0:T(8,128)(2,1)S(1)}, bf16[128,3584]{1,0:T(8,128)(2,1)S(1)}, u32[]{:S(2)}, u32[]{:S(2)}) %collective-permute-start.10) | collective-permute-done | bytes 917536 | tf_op jit(solution)/shard_map/ppermute | solution.py:236
  144.1 1.0 shard_map.122
  145.1 1.8 %shard_map.123 = bf16[128,3584]{1,0:T(8,128)(2,1)} custom-call(bf16[128,3584]{1,0:T(8,128)(2,1)S(1)} %collective-permute-done.11.current_ref, bf16[16,72,896]{2,1,0:T(8,128)(2,1)S(1)} %all-to-all-done.3.back_ref, s32[1,128]{1,0:T(1,128)S(1)} %collective-permute-done.12.ids_ref, f32[1,128]{1,0:T(1,128)S(1)} %collective-permute-done.13.scores_ref), custom_call_target="tpu_custom_call" | custom-call | flops 352321536 | bytes 3670016 | tf_op jit(solution)/shard_map/pallas_call | solution.py:205
  (36 shorter events, 0.1 us)
Async XLA Ops:
  4.0 7.6 %copy-start.6 = (bf16[1,256,3584]{2,1,0:T(8,128)(2,1)S(1)}, bf16[1,256,3584]{2,1,0:T(8,128)(2,1)}, u32[]{:S(2)}) copy-start(bf16[1,256,3584]{2,1,0:T(8,128)(2,1)} %param.19) | copy-start | bytes 5505028
  4.0 34.8 %all-to-all-start = ((bf16[16,72,896]{2,1,0:T(8,128)(2,1)}), bf16[16,72,896]{2,1,0:T(8,128)(2,1)}, u32[]{:S(2)}, u32[]{:S(2)}) async-start(bf16[16,72,896]{2,1,0:T(8,128)(2,1)} %shard_map.113), calls=%async_computation | async-start | bytes 4128768 | tf_op jit(solution)/shard_map/all_to_all | solution.py:249
  11.6 8.3 %copy-start.11 = (bf16[1,128,3584]{2,1,0:T(8,128)(2,1)S(1)}, bf16[1,128,3584]{2,1,0:T(8,128)(2,1)}, u32[]{:S(2)}) copy-start(bf16[1,128,3584]{2,1,0:T(8,128)(2,1)} %param.11) | copy-start | bytes 2752516
  11.6 8.3 %copy-start.13 = (f32[1,3584]{1,0:T(1,128)S(1)}, f32[1,3584]{1,0:T(1,128)}, u32[]{:S(2)}) copy-start(f32[1,3584]{1,0:T(1,128)} %gain_hbm.3) | copy-start | bytes 43012
  11.6 8.3 %copy-start.16 = (s32[1,1,128,1]{2,3,1,0:T(1,128)S(1)}, s32[1,1,128,1]{2,3,1,0:T(1,128)}, u32[]{:S(2)}) copy-start(s32[1,1,128,1]{2,3,1,0:T(1,128)} %param.13) | copy-start | bytes 1540
  11.6 7.0 %collective-permute-start = (bf16[256,3584]{1,0:T(8,128)(2,1)S(1)}, bf16[256,3584]{1,0:T(8,128)(2,1)S(1)}, u32[]{:S(2)}, u32[]{:S(2)}) collective-permute-start(bf16[256,3584]{1,0:T(8,128)(2,1)S(1)} %bitcast.23), channel_id=1, source_target_pairs={{0,1},{1,0},{2,3},{3,2},{4,5},{5,4},{6,7},{7,6},{8,9},{9,8},{10,11... | collective-permute-start | bytes 5505032 | tf_op jit(solution)/shard_map/ppermute | solution.py:231
  12.8 26.1 %collective-permute-start.1 = (bf16[128,3584]{1,0:T(8,128)(2,1)S(1)}, bf16[128,3584]{1,0:T(8,128)(2,1)S(1)}, u32[]{:S(2)}, u32[]{:S(2)}) collective-permute-start(bf16[128,3584]{1,0:T(8,128)(2,1)S(1)} %get-tuple-element.23), channel_id=1, source_target_pairs={{0,224},{32,0},{64,32},{96,64},{128,96},{160,128},{192,160},{224,1... | collective-permute-start | bytes 2752520 | tf_op jit(solution)/shard_map/ppermute | solution.py:236
  18.6 1.3 copy-start.9
  21.1 1.3 copy-start.5
  22.4 27.4 %copy-start = (bf16[1,3584,256]{2,1,0:T(8,128)(2,1)S(1)}, bf16[1,3584,256]{2,1,0:T(8,128)(2,1)}, u32[]{:S(2)}) copy-start(bf16[1,3584,256]{2,1,0:T(8,128)(2,1)} %param.17) | copy-start | bytes 5505028
  38.9 10.9 %collective-permute-start.2 = (bf16[16,72,896]{2,1,0:T(8,128)(2,1)}, bf16[16,72,896]{2,1,0:T(8,128)(2,1)}, u32[]{:S(2)}, u32[]{:S(2)}) collective-permute-start(bf16[16,72,896]{2,1,0:T(8,128)(2,1)} %all-to-all-done.received_ref), channel_id=1, source_target_pairs={{0,1},{1,0},{2,3},{3,2},{4,5},{5,4},{6,7},{7,6},{8,9},{9,8},{10,11... | collective-permute-start | bytes 6193160 | tf_op jit(solution)/shard_map/ppermute | solution.py:231
  38.9 36.3 %all-to-all-start.1 = ((bf16[16,72,896]{2,1,0:T(8,128)(2,1)}), bf16[16,72,896]{2,1,0:T(8,128)(2,1)}, u32[]{:S(2)}, u32[]{:S(2)}) async-start(bf16[16,72,896]{2,1,0:T(8,128)(2,1)} %copy-done.5), calls=%async_computation.1 | async-start | bytes 4128768 | tf_op jit(solution)/shard_map/all_to_all | solution.py:249
  46.1 23.9 %collective-permute-start.4 = (bf16[128,3584]{1,0:T(8,128)(2,1)}, bf16[128,3584]{1,0:T(8,128)(2,1)}, u32[]{:S(2)}, u32[]{:S(2)}) collective-permute-start(bf16[128,3584]{1,0:T(8,128)(2,1)} %get-tuple-element.22), channel_id=1, source_target_pairs={{0,224},{32,0},{64,32},{96,64},{128,96},{160,128},{192,160},{224,1... | collective-permute-start | bytes 2752520 | tf_op jit(solution)/shard_map/ppermute | solution.py:236
  49.8 1.5 %copy-start.1 = (bf16[1,3584,256]{2,1,0:T(8,128)(2,1)S(1)}, bf16[1,3584,256]{2,1,0:T(8,128)(2,1)}, u32[]{:S(2)}) copy-start(bf16[1,3584,256]{2,1,0:T(8,128)(2,1)} %param.18) | copy-start | bytes 5505028
  51.3 3.5 %copy-start.2 = (bf16[1,3584,256]{2,1,0:T(8,128)(2,1)S(1)}, bf16[1,3584,256]{2,1,0:T(8,128)(2,1)}, u32[]{:S(2)}) copy-start(bf16[1,3584,256]{2,1,0:T(8,128)(2,1)} %param.18) | copy-start | bytes 5505028
  54.7 3.5 %copy-start.7 = (bf16[1,256,3584]{2,1,0:T(8,128)(2,1)S(1)}, bf16[1,256,3584]{2,1,0:T(8,128)(2,1)}, u32[]{:S(2)}) copy-start(bf16[1,256,3584]{2,1,0:T(8,128)(2,1)} %param.19) | copy-start | bytes 5505028
  54.7 3.5 %copy-start.10 = (bf16[256,3584]{1,0:T(8,128)(2,1)S(1)}, bf16[256,3584]{1,0:T(8,128)(2,1)}, u32[]{:S(2)}) copy-start(bf16[256,3584]{1,0:T(8,128)(2,1)} %copy-done.9) | copy-start | bytes 5505028
  54.7 3.5 %collective-permute-start.3 = (bf16[288,256]{1,0:T(8,128)(2,1)S(1)}, bf16[288,256]{1,0:T(8,128)(2,1)S(1)}, u32[]{:S(2)}, u32[]{:S(2)}) collective-permute-start(bf16[288,256]{1,0:T(8,128)(2,1)S(1)} %shard_map.116), channel_id=1, source_target_pairs={{0,1},{1,0},{2,3},{3,2},{4,5},{5,4},{6,7},{7,6},{8,9},{9,8},{10,11... | collective-permute-start | bytes 442376 | tf_op jit(solution)/shard_map/ppermute | solution.py:231
  60.1 1.4 copy-start.4
  75.2 16.9 %collective-permute-start.6 = (bf16[16,72,896]{2,1,0:T(8,128)(2,1)}, bf16[16,72,896]{2,1,0:T(8,128)(2,1)}, u32[]{:S(2)}, u32[]{:S(2)}) collective-permute-start(bf16[16,72,896]{2,1,0:T(8,128)(2,1)} %all-to-all-done.1.received_ref), channel_id=1, source_target_pairs={{0,1},{1,0},{2,3},{3,2},{4,5},{5,4},{6,7},{7,6},{8,9},{9,8},{10,11... | collective-permute-start | bytes 6193160 | tf_op jit(solution)/shard_map/ppermute | solution.py:231
  75.2 35.5 %all-to-all-start.2 = ((bf16[16,72,896]{2,1,0:T(8,128)(2,1)}), bf16[16,72,896]{2,1,0:T(8,128)(2,1)}, u32[]{:S(2)}, u32[]{:S(2)}) async-start(bf16[16,72,896]{2,1,0:T(8,128)(2,1)} %copy-done.4), calls=%async_computation.2 | async-start | bytes 4128768 | tf_op jit(solution)/shard_map/all_to_all | solution.py:249
  81.6 14.2 %collective-permute-start.8 = (bf16[128,3584]{1,0:T(8,128)(2,1)S(1)}, bf16[128,3584]{1,0:T(8,128)(2,1)S(1)}, u32[]{:S(2)}, u32[]{:S(2)}) collective-permute-start(bf16[128,3584]{1,0:T(8,128)(2,1)S(1)} %collective-permute-done.1.refs_0_), channel_id=1, source_target_pairs={{0,1},{1,0},{2,3},{3,2},{4,5},{5,4},{6,7},{7,6},{8,9},{9,8},{10,11... | collective-permute-start | bytes 2752520 | tf_op jit(solution)/shard_map/ppermute | solution.py:231
  81.6 14.2 %collective-permute-start.9 = (bf16[128,3584]{1,0:T(8,128)(2,1)}, bf16[128,3584]{1,0:T(8,128)(2,1)S(1)}, u32[]{:S(2)}, u32[]{:S(2)}) collective-permute-start(bf16[128,3584]{1,0:T(8,128)(2,1)} %collective-permute-done.4.refs_1_), channel_id=1, source_target_pairs={{0,1},{1,0},{2,3},{3,2},{4,5},{5,4},{6,7},{7,6},{8,9},{9,8},{10,11... | collective-permute-start | bytes 2752520 | tf_op jit(solution)/shard_map/ppermute | solution.py:231
  82.1 1.5 %copy-start.3 = (bf16[1,3584,256]{2,1,0:T(8,128)(2,1)S(1)}, bf16[1,3584,256]{2,1,0:T(8,128)(2,1)}, u32[]{:S(2)}) copy-start(bf16[1,3584,256]{2,1,0:T(8,128)(2,1)} %param.18) | copy-start | bytes 5505028
  86.8 9.0 %collective-permute-start.5 = (bf16[288,256]{1,0:T(8,128)(2,1)S(1)}, bf16[288,256]{1,0:T(8,128)(2,1)S(1)}, u32[]{:S(2)}, u32[]{:S(2)}) collective-permute-start(bf16[288,256]{1,0:T(8,128)(2,1)S(1)} %shard_map.118), channel_id=1, source_target_pairs={{0,224},{32,0},{64,32},{96,64},{128,96},{160,128},{192,160},{224,1... | collective-permute-start | bytes 442376 | tf_op jit(solution)/shard_map/ppermute | solution.py:236
  95.3 6.2 %collective-permute-start.7 = (bf16[288,256]{1,0:T(8,128)(2,1)S(1)}, bf16[288,256]{1,0:T(8,128)(2,1)S(1)}, u32[]{:S(2)}, u32[]{:S(2)}) collective-permute-start(bf16[288,256]{1,0:T(8,128)(2,1)S(1)} %shard_map.119), channel_id=1, source_target_pairs={{0,225},{1,224},{2,227},{3,226},{4,229},{5,228},{6,231},{7,230},{8... | collective-permute-start | bytes 442376 | tf_op jit(solution)/shard_map/ppermute | solution.py:244
  106.0 11.1 %copy-start.8 = (bf16[1,128,3584]{2,1,0:T(8,128)(2,1)S(1)}, bf16[1,128,3584]{2,1,0:T(8,128)(2,1)}, u32[]{:S(2)}) copy-start(bf16[1,128,3584]{2,1,0:T(8,128)(2,1)} %param.10) | copy-start | bytes 2752516
  106.0 11.1 %copy-start.14 = (s32[1,1,128,1]{2,3,1,0:T(1,128)S(1)}, s32[1,1,128,1]{2,3,1,0:T(1,128)}, u32[]{:S(2)}) copy-start(s32[1,1,128,1]{2,3,1,0:T(1,128)} %param.12) | copy-start | bytes 1540
  106.0 11.1 %copy-start.15 = (f32[1,1,128,1]{2,3,1,0:T(1,128)S(1)}, f32[1,1,128,1]{2,3,1,0:T(1,128)}, u32[]{:S(2)}) copy-start(f32[1,1,128,1]{2,3,1,0:T(1,128)} %param.14) | copy-start | bytes 1540
  110.7 34.5 %all-to-all-start.3 = ((bf16[16,72,896]{2,1,0:T(8,128)(2,1)}), bf16[16,72,896]{2,1,0:T(8,128)(2,1)S(1)}, u32[]{:S(2)}, u32[]{:S(2)}) async-start(bf16[16,72,896]{2,1,0:T(8,128)(2,1)} %shard_map.120), calls=%async_computation.3 | async-start | bytes 4128768 | tf_op jit(solution)/shard_map/all_to_all | solution.py:249
  117.1 3.8 %copy-start.12 = (bf16[1,128,3584]{2,1,0:T(8,128)(2,1)S(1)}, bf16[1,128,3584]{2,1,0:T(8,128)(2,1)}, u32[]{:S(2)}) copy-start(bf16[1,128,3584]{2,1,0:T(8,128)(2,1)} %param.11) | copy-start | bytes 2752516
  117.1 9.7 %copy-start.17 = (f32[1,1,128,1]{2,3,1,0:T(1,128)S(1)}, f32[1,1,128,1]{2,3,1,0:T(1,128)}, u32[]{:S(2)}) copy-start(f32[1,1,128,1]{2,3,1,0:T(1,128)} %param.15) | copy-start | bytes 1540
  119.7 24.5 %collective-permute-start.10 = (bf16[128,3584]{1,0:T(8,128)(2,1)S(1)}, bf16[128,3584]{1,0:T(8,128)(2,1)S(1)}, u32[]{:S(2)}, u32[]{:S(2)}) collective-permute-start(bf16[128,3584]{1,0:T(8,128)(2,1)S(1)} %shard_map.121), channel_id=1, source_target_pairs={{0,32},{32,64},{64,96},{96,128},{128,160},{160,192},{192,224},{224... | collective-permute-start | bytes 2752520 | tf_op jit(solution)/shard_map/ppermute | solution.py:236
  120.9 24.2 %collective-permute-start.11 = (bf16[128,3584]{1,0:T(8,128)(2,1)S(1)}, bf16[128,3584]{1,0:T(8,128)(2,1)S(1)}, u32[]{:S(2)}, u32[]{:S(2)}) collective-permute-start(bf16[128,3584]{1,0:T(8,128)(2,1)S(1)} %bitcast.28), channel_id=1, source_target_pairs={{0,224},{32,0},{64,32},{96,64},{128,96},{160,128},{192,160},{224,1... | collective-permute-start | bytes 2752520 | tf_op jit(solution)/shard_map/ppermute | solution.py:236
  124.9 20.2 %collective-permute-start.12 = (s32[1,128]{1,0:T(1,128)S(1)}, s32[1,128]{1,0:T(1,128)S(1)}, u32[]{:S(2)}, u32[]{:S(2)}) collective-permute-start(s32[1,128]{1,0:T(1,128)S(1)} %bitcast.33), channel_id=1, source_target_pairs={{0,224},{32,0},{64,32},{96,64},{128,96},{160,128},{192,160},{224,1... | collective-permute-start | bytes 1544 | tf_op jit(solution)/shard_map/ppermute | solution.py:236
  126.8 18.3 %collective-permute-start.13 = (f32[1,128]{1,0:T(1,128)S(1)}, f32[1,128]{1,0:T(1,128)S(1)}, u32[]{:S(2)}, u32[]{:S(2)}) collective-permute-start(f32[1,128]{1,0:T(1,128)S(1)} %bitcast.36), channel_id=1, source_target_pairs={{0,224},{32,0},{64,32},{96,64},{128,96},{160,128},{192,160},{224,1... | collective-permute-start | bytes 1544 | tf_op jit(solution)/shard_map/ppermute | solution.py:236
